TPU v7x, 512 devices: a whole 4x4x16 slice. The times are simulated.
512 devices in a mesh: dp: 64 (over x, z), tensor: 8 (over y, core).
Axes of the slice: x: 4, y: 4, z: 16, core: 2. Of those that a mesh axis runs over, the one named last changes fastest.
Arguments:
- responses: float32 [512, 6144], P('dp'), may hold values from -40 to 40
- weight: float32 [6144, 32768], P('dp', 'tensor'), may hold values from -1 to 1
- lengths: int32 [64], P('dp'), may hold values from 1 to 8, 256 in all
- targets: int32 [512], P('dp'), may hold values from 0 to 32767
- owners: int32 [64], P('dp'), may hold values from 0 to 63, each once
Outputs:
- logprobs: float32 [256], P('dp')
- grad_hidden: float32 [512, 6144], P('dp')
- grad_weight: float32 [6144, 32768], P('dp', 'tensor')
Inputs may be any that keep to these rules, and one draw needn't show every extreme that they name: `lengths`: they sum to 256; the largest is 8. `owners`: each device index appears once.
All inputs are finite; a program needn't handle non-finite values. No bound on the sum of `lengths` on one device may be relied on, other than what follows from the above.
Results may differ from a plain program's by a relative error of at most 0.0003.
Values sent between devices are 32-bit elements; how exact they have to be, the bound alone decides.
No kernel may reach another device: no remote copies, remote signals or barrier semaphores. Data moves between devices by JAX's collectives and lax.ppermute only.
A program may use at most 64 MiB of HBM per device.

v0:
```python
import jax
import jax.numpy as jnp
from jax import lax
from jax.sharding import PartitionSpec as P

ROWS_DEV = 4


HIGH = lax.Precision.HIGHEST


def softmax_terms(logits, labels, offset):
    columns = jnp.arange(logits.shape[1], dtype=jnp.int32) + offset
    onehot = (columns[None, :] == labels[:, None]).astype(jnp.float32)
    picked_local = jnp.sum(logits * onehot, axis=1)
    local_peak = jnp.max(logits, axis=1)
    row_peak = lax.pmax(local_peak, "tensor")
    shifted = jnp.exp(logits - row_peak[:, None])
    exp_total, picked = lax.psum((jnp.sum(shifted, axis=1), picked_local), "tensor")
    logprobs = picked - row_peak - jnp.log(exp_total)
    grad_logits = onehot - shifted / exp_total[:, None]
    return (logprobs, grad_logits)


def on_device(responses, weight, lengths, targets, owners):
    dp_size = lax.axis_size("dp")
    capacity = responses.shape[0]
    total_rows = ROWS_DEV * dp_size
    row_share = ROWS_DEV
    lengths_all, targets_all, owners_all = (
        lax.all_gather(lengths, "dp", axis=0, tiled=True),
        lax.all_gather(targets, "dp", axis=0, tiled=True),
        lax.all_gather(owners, "dp", axis=0, tiled=True),
    )
    received = lax.all_to_all(responses, "dp", split_axis=1, concat_axis=0, tiled=True)
    row_ends = jnp.cumsum(lengths_all)
    row_starts = row_ends - lengths_all
    row_ranks = jnp.arange(total_rows, dtype=jnp.int32)
    sources = jnp.sum((row_ends[None, :] <= row_ranks[:, None]).astype(jnp.int32), axis=1)
    positions = sources * capacity + row_ranks - jnp.take(row_starts, sources)
    hidden = jnp.take(received, positions, axis=0)
    labels = jnp.take(targets_all, positions, axis=0)
    offset = lax.axis_index("tensor") * weight.shape[1]
    first_row = lax.axis_index("dp") * row_share
    logit_share = lax.psum_scatter(
        jnp.dot(hidden, weight, precision=HIGH, preferred_element_type=jnp.float32),
        "dp",
        scatter_dimension=0,
        tiled=True,
    )
    share_labels = lax.dynamic_slice_in_dim(labels, first_row, row_share, 0)
    logprobs, grad_share = softmax_terms(logit_share, share_labels, offset)
    grad_logits = lax.all_gather(grad_share, "dp", axis=0, tiled=True)
    grad_weight = jnp.dot(hidden.T, grad_logits, precision=HIGH, preferred_element_type=jnp.float32)
    local_grad = jnp.dot(grad_logits, weight.T, precision=HIGH, preferred_element_type=jnp.float32)
    grad_rows = lax.psum(local_grad, "tensor")
    device_ids = jnp.arange(dp_size, dtype=jnp.int32)
    owned_by = (owners_all[None, :] == device_ids[:, None]).astype(jnp.int32)
    source_of = jnp.sum(owned_by * device_ids[None, :], axis=1)
    slot_ids = jnp.arange(capacity, dtype=jnp.int32)
    live_slots = slot_ids[None, :] < jnp.take(lengths_all, source_of)[:, None]
    wanted = jnp.where(live_slots, jnp.take(row_starts, source_of)[:, None] + slot_ids[None, :], 0)
    outgoing = jnp.take(grad_rows, wanted.reshape(-1), axis=0).reshape(
        dp_size, capacity, grad_rows.shape[1]
    )
    outgoing = outgoing * live_slots[:, :, None].astype(jnp.float32)
    returned = lax.all_to_all(outgoing, "dp", split_axis=0, concat_axis=2, tiled=True)
    return (logprobs, returned.reshape(capacity, returned.shape[2]), grad_weight)


def solution(mesh):
    placed = (P("dp", None), P("dp", "tensor"), P("dp"), P("dp"), P("dp"))
    return jax.shard_map(
        on_device,
        mesh=mesh,
        in_specs=placed,
        out_specs=(P("dp"), P("dp", None), P("dp", "tensor")),
        check_vma=False,
    )
```

profile of v0, /device:TPU:1, one launch (start us, length us, event | category | flops | bytes accessed | tf_op | source)
XLA Modules:
  0.0 649.3 jit_solution(2219293637057755893)
XLA Ops:
  7.2 1.2 all_to_all.25
  8.3 0.9 copy.21
  9.2 19.1 %all-to-all-start = ((f32[8,64,96]{2,0,1:T(8,128)}), f32[8,64,96]{2,0,1:T(8,128)S(1)}, u32[]{:S(2)}, u32[]{:S(2)}) async-start(f32[8,64,96]{2,0,1:T(8,128)} %copy.21), calls=%async_computation | async-start | bytes 524288 | tf_op jit(solution)/shard_map/all_to_all | solution.py:35
  29.7 1.4 fusion.17
  31.7 0.8 dynamic-update-slice
  32.5 0.8 dynamic-update-slice.2
  33.2 0.8 dynamic-update-slice.1
  34.0 25.7 %all-reduce.4 = (s32[64]{0:T(128)S(1)}, s32[512]{0:T(512)S(1)}, s32[64]{0:T(128)S(1)}) all-reduce(s32[64]{0:T(128)S(1)} %dynamic-update-slice, s32[512]{0:T(512)S(1)} %dynamic-update-slice.1, s32[64]{0:T(128)S(1)} %dynamic-update-slice.2), channel_id=1, replica_groups=mesh['dp'=64,'tensor'=8] {'dp'}, use_global_device_ids=true, to_apply=%add | all-reduce | flops 640 | bytes 5120
  60.2 1.9 gather_fusion
  62.1 1.9 gather_fusion.1
  64.1 0.7 gather_fusion.2
  64.8 5.1 fusion.3
  70.8 280.9 %all-reduce.11.cloned.1.call-done = f32[256,4096]{1,0:T(8,128)} async-done(((f32[256,4096]{1,0:T(8,128)}), f32[256,4096]{1,0:T(8,128)}) %all-reduce.11.cloned.1.call-update) | async-done | bytes 4194320
  351.7 1.1 fusion.5
  352.9 22.2 %pmax.7 = f32[4]{0:T(128)S(1)} all-reduce(f32[4]{0:T(128)S(1)} %get-tuple-element.5), channel_id=1, replica_groups=mesh['dp'=64,'tensor'=8] {'tensor'}, use_global_device_ids=true, to_apply=%region_6.7 | all-reduce | flops 4 | bytes 32 | tf_op jit(solution)/shard_map/pmax | solution.py:17
  375.1 1.1 fusion.11
  376.2 12.4 %all-reduce.5 = (f32[4]{0:T(128)S(1)}, f32[4]{0:T(128)S(1)}) all-reduce(f32[4]{0:T(128)S(1)} %fusion.11, f32[4]{0:T(128)S(1)} %get-tuple-element.4), channel_id=1, replica_groups=mesh['dp'=64,'tensor'=8] {'tensor'}, use_global_device_ids=true, to_apply=%region_8.9 | all-reduce | flops 8 | bytes 64 | tf_op jit(solution)/shard_map/psum | solution.py:19
  388.6 1.6 fusion.6
  390.4 0.8 gather_fusion.5
  391.2 0.8 gather_fusion.4
  392.3 128.4 %all-gather.3.cloned.1.call-done = f32[64,4,4096]{2,1,0:T(4,128)} async-done(((f32[1,4,4096]{2,1,0:T(4,128)}), f32[64,4,4096]{2,1,0:T(4,128)}) %all-gather.3.cloned.1.call-update) | async-done | bytes 4194320 | tf_op jit(solution)/shard_map/all_gather | solution.py:53
  520.7 5.3 reshape.275
  526.0 6.8 %fusion.18 = f32[256,96]{0,1:T(8,128)} fusion(f32[256,4096]{1,0:T(8,128)} %reshape.275, f32[96,4096]{1,0:T(8,128)S(1)} %copy-done), kind=kOutput, calls=%fused_computation.57 | convolution fusion | flops 1207959552 | bytes 5865472 | tf_op jit(solution)/shard_map/dot_general | solution.py:55
  532.8 74.5 %all-reduce.9.cloned.1.call-done = f32[256,96]{0,1:T(8,128)} async-done(((f32[256,96]{0,1:T(8,128)}), f32[256,96]{0,1:T(8,128)}) %all-reduce.9.cloned.1.call-update) | async-done | bytes 98320 | tf_op jit(solution)/shard_map/psum | solution.py:56
  607.3 1.0 copy.22
  608.3 1.0 gather_fusion.3
  609.3 0.9 fusion
  610.2 14.8 %all-to-all-start.1 = ((f32[64,8,96]{2,1,0:T(8,128)}), f32[64,8,96]{2,1,0:T(8,128)S(1)}, u32[]{:S(2)}, u32[]{:S(2)}) async-start(f32[64,8,96]{2,1,0:T(8,128)} %fusion), calls=%async_computation.1 | async-start | bytes 524288 | tf_op jit(solution)/shard_map/all_to_all | solution.py:67
  625.0 0.5 log_subtract_fusion
  625.5 5.9 fusion.1
  631.4 10.5 %all-to-all-done.1 = f32[64,8,96]{2,1,0:T(8,128)S(1)} async-done(((f32[64,8,96]{2,1,0:T(8,128)}), f32[64,8,96]{2,1,0:T(8,128)S(1)}, u32[]{:S(2)}, u32[]{:S(2)}) %all-to-all-start.1) | async-done | bytes 196640 | tf_op jit(solution)/shard_map/all_to_all | solution.py:67
  641.9 0.8 reshape.214
  (34 shorter events, 1.2 us)
Async XLA Ops:
  7.2 57.7 %copy-start = (f32[96,4096]{1,0:T(8,128)S(1)}, f32[96,4096]{1,0:T(8,128)}, u32[]{:S(2)}) copy-start(f32[96,4096]{1,0:T(8,128)} %param.8) | copy-start | bytes 4718596
  9.2 54.9 %all-to-all-start = ((f32[8,64,96]{2,0,1:T(8,128)}), f32[8,64,96]{2,0,1:T(8,128)S(1)}, u32[]{:S(2)}, u32[]{:S(2)}) async-start(f32[8,64,96]{2,0,1:T(8,128)} %copy.21), calls=%async_computation | async-start | bytes 524288 | tf_op jit(solution)/shard_map/all_to_all | solution.py:35
  28.3 323.4 %all-reduce.11.cloned.1.call-start = ((), (), s32[]{:S(2)}) async-start(), calls=%async_computation.4 | async-start | bytes 8388608
  70.0 450.7 %all-gather.3.cloned.1.call-start = ((), (), s32[]{:S(2)}) async-start(), calls=%async_computation.3 | async-start | bytes 4259840 | tf_op jit(solution)/shard_map/all_gather | solution.py:53
  390.3 217.0 %all-reduce.9.cloned.1.call-start = ((), (), s32[]{:S(2)}) async-start(), calls=%async_computation.2 | async-start | bytes 196608 | tf_op jit(solution)/shard_map/psum | solution.py:56
  610.2 31.6 %all-to-all-start.1 = ((f32[64,8,96]{2,1,0:T(8,128)}), f32[64,8,96]{2,1,0:T(8,128)S(1)}, u32[]{:S(2)}, u32[]{:S(2)}) async-start(f32[64,8,96]{2,1,0:T(8,128)} %fusion), calls=%async_computation.1 | async-start | bytes 524288 | tf_op jit(solution)/shard_map/all_to_all | solution.py:67
Sparse Core Ops, SparseCore 0:
  70.1 281.5 all-reduce.10
  390.4 130.2 all-gather.2
  532.9 74.3 all-reduce.8
where the time goes:
time: 653 us; the launch traced here: 649 us
  waiting for transfers between devices  494 us (76%)
  blocking collectives  60.3 us (9%)
  starting transfers between devices  34 us (5%)
  local copies, waits for them, and re-layouts  20.3 us (3%)
  matrix products  17.8 us (3%)
  between operations  16.6 us (3%)
    unnamed x4, waiting for transfers between devices  281 us
    all_gather x1, waiting for transfers between devices, on_device(): grad_logits = lax.all_gather(grad_share, 'dp', axis=0, tiled=True)  128 us
    psum x1, waiting for transfers between devices, on_device(): grad_rows = lax.psum(local_grad, 'tensor')  74.5 us
    unnamed x1, blocking collectives  25.7 us
    pmax x1, blocking collectives, softmax_terms(): row_peak = lax.pmax(local_peak, 'tensor')  22.2 us
    all_to_all x1, starting transfers between devices, on_device(): lax.all_to_all(responses, 'dp', split_axis=1, concat_axis=0, tiled=True)  19.1 us
    all_to_all x1, starting transfers between devices, on_device(): lax.all_to_all(outgoing, 'dp', split_axis=0, concat_axis=2, tiled=True)  14.8 us
  transfers between devices with their start and end apart: 5, of which 4 were waited for; matrix products, arithmetic and copies ran while one was open for 3% of the time, Pallas kernels for 0%

commit v1 on v0

v1 whole, which is shorter than its diff:
```python
import jax
import jax.numpy as jnp
from jax import lax
from jax.sharding import Mesh, PartitionSpec as P

HIGH = lax.Precision.HIGHEST
Z = ("h", "l")
XYC = ("x", "y", "c")
YC = ("y", "c")
META = 128


def swap(blocks, axes):
    return lax.all_to_all(blocks, axes, split_axis=0, concat_axis=0, tiled=True)


def spread(block, axes, count):
    return swap(jnp.broadcast_to(block[None], (count, *block.shape)), axes)


def shift_z(block, step):
    return lax.ppermute(block, Z, [(i, (i + step) % 16) for i in range(16)])


def dot(a, b, contract=(1, 0)):
    dims = (((contract[0],), (contract[1],)), ((), ()))
    return lax.dot_general(a, b, dims, precision=HIGH, preferred_element_type=jnp.float32)


def on_device(responses, weight, lengths, targets, owners):
    width = responses.shape[1]
    depth, columns = weight.shape
    quarter = columns // 4
    wide = 4 * depth
    x, h, l = lax.axis_index("x"), lax.axis_index("h"), lax.axis_index("l")
    j = lax.axis_index(YC)

    head = swap(weight.reshape(depth, 4, quarter).transpose(1, 0, 2), "x").reshape(wide, quarter)

    row = lax.dynamic_slice(responses, (j, 0), (1, width))
    row = row.reshape(4, 16, depth).transpose(1, 0, 2).reshape(16, wide)
    notes = jnp.stack([lax.dynamic_index_in_dim(targets, j, 0, False), lengths[0], owners[0]])
    notes = jnp.pad(notes.astype(jnp.float32), (0, META - 3))
    packed = jnp.concatenate([row, jnp.broadcast_to(notes[None], (16, META))], axis=1)
    mine = swap(packed[:, None, :], Z).reshape(16, wide + META)
    slots = spread(mine, XYC, 32).reshape(512, wide + META)

    ids = jnp.arange(512, dtype=jnp.int32)
    slot_j = (ids // 16) % 8
    source = (ids // 128) * 16 + ids % 16
    notes_all = slots[:, wide : wide + 3].astype(jnp.int32)
    slot_target, slot_length, slot_owner = notes_all[:, 0], notes_all[:, 1], notes_all[:, 2]
    before = (source[None, :] < source[:, None]) & (slot_j[None, :] == 0)
    starts = jnp.sum(jnp.where(before, slot_length[None, :], 0), axis=1)
    live = slot_j < slot_length
    rank = jnp.where(live, (starts + slot_j - 64 * l) % 256, -1)
    rows = jnp.arange(256, dtype=jnp.int32)
    select = rank[None, :] == rows[:, None]
    hidden = dot(select.astype(jnp.float32), slots[:, :wide])
    labels = jnp.sum(jnp.where(select, slot_target[None, :], 0), axis=1)
    owned = (slot_owner[None, :] == source[:, None]) & (slot_j[None, :] == slot_j[:, None])
    sent_rank = jnp.sum(jnp.where(owned, rank[None, :] + 1, 0), axis=1) - 1
    deliver = (sent_rank[:, None] == rows[None, :]).astype(jnp.float32)

    partial = dot(hidden, head)
    up = shift_z(partial[64:128], 1)
    down = shift_z(partial[192:256], -1)
    up2 = shift_z(partial[128:160], 2)
    down2 = shift_z(partial[160:192], -2)
    block = partial[:64] + up + down + jnp.concatenate([up2, down2], axis=0)
    logits = jnp.sum(swap(block.reshape(4, 16, quarter), "h"), axis=0)

    row_labels = lax.dynamic_slice(labels, (h * 16,), (16,))
    column = jnp.arange(quarter, dtype=jnp.int32) + j * columns + x * quarter
    onehot = (column[None, :] == row_labels[:, None]).astype(jnp.float32)
    peak = jnp.max(logits, axis=1)
    shifted = jnp.exp(logits - peak[:, None])
    stats = jnp.stack([peak, jnp.sum(shifted, axis=1), jnp.sum(logits * onehot, axis=1)], axis=0)
    stats = spread(stats, XYC, 32)
    row_peak = jnp.max(stats[:, 0], axis=0)
    exp_total = jnp.sum(stats[:, 1] * jnp.exp(stats[:, 0] - row_peak[None]), axis=0)
    logprobs = jnp.sum(stats[:, 2], axis=0) - row_peak - jnp.log(exp_total)
    scale = jnp.exp(peak - row_peak) / exp_total
    grad = onehot - shifted * scale[:, None]

    own = spread(grad, "h", 4).reshape(64, quarter)
    after = shift_z(own, -1)
    ahead = shift_z(own, 1)
    far = shift_z(own[:32], 2)
    far2 = shift_z(own[32:], -2)
    grads = jnp.concatenate([own, after, far, far2, ahead], axis=0)

    grad_head = dot(hidden, grads, (0, 0)).reshape(4, depth, quarter)
    grad_weight = swap(grad_head, "x").transpose(1, 0, 2).reshape(depth, columns)

    grad_rows = dot(grads, head, (1, 1))
    leaving = dot(deliver, grad_rows).reshape(32, 16, wide)
    summed = jnp.sum(swap(leaving, XYC), axis=0)
    parts = lax.dynamic_update_slice(jnp.zeros((16, META), jnp.float32), logprobs.reshape(4, 4), (h * 4, 0))
    parts = jnp.where(l == x, parts, 0.0)
    arrived = swap(jnp.concatenate([summed, parts], axis=1)[:, None, :], Z)[:, 0]
    slot = arrived[:, :wide].reshape(16, 4, depth).transpose(1, 0, 2).reshape(width)
    grad_hidden = spread(slot, YC, 8)
    return jnp.sum(arrived[:, wide : wide + 4], axis=0), grad_hidden, grad_weight


def solution(mesh):
    grid = Mesh(mesh.devices.reshape(4, 4, 4, 4, 2), ("x", "h", "l", "y", "c"))
    dp = ("x", "h", "l")
    placed = (P(dp, None), P(dp, YC), P(dp), P(dp), P(dp))
    return jax.shard_map(
        on_device,
        mesh=grid,
        in_specs=placed,
        out_specs=(P(dp), P(dp, None), P(dp, YC)),
        check_vma=False,
    )
```

time: 653 us -> 260 us (0.40)
  waiting for transfers between devices: 494 us -> 120 us
  starting transfers between devices: 34 us -> 68.2 us
  blocking collectives: 60.3 us -> 43.2 us
  between operations: 16.6 us -> 2.29 us
  matrix products: 17.8 us -> 8.47 us
  local copies, waits for them, and re-layouts: 20.3 us -> 13.5 us
    unnamed x4 -> x0, waiting for transfers between devices: 281 us -> none
    all_gather x1 -> x0, waiting for transfers between devices: 128 us -> none  [on_device(): grad_logits = lax.all_gather(grad_share, 'dp', axis=0, tiled=True)]
    all_to_all x2 -> x8, waiting for transfers between devices: 10.5 us -> 105 us  [swap(): return lax.all_to_all(blocks, axes, split_axis=0, concat_axis=0, tiled=True)]
    psum x1 -> x0, waiting for transfers between devices: 74.5 us -> none  [on_device(): grad_rows = lax.psum(local_grad, 'tensor')]
    all_to_all x0 -> x2, blocking collectives: none -> 43.2 us  [swap(): return lax.all_to_all(blocks, axes, split_axis=0, concat_axis=0, tiled=True)]
    unnamed x1 -> x0, blocking collectives: 25.7 us -> none
    ppermute x0 -> x8, starting transfers between devices: none -> 24.1 us  [shift_z(): return lax.ppermute(block, Z, [(i, (i + step) % 16) for i in range(16)])]
    pmax x1 -> x0, blocking collectives: 22.2 us -> none  [softmax_terms(): row_peak = lax.pmax(local_peak, 'tensor')]
  transfers between devices with their start and end apart: 5 -> 16, of which waited for: 4 -> 13; matrix products, arithmetic and copies ran while one was open for 3% -> 4% of each run, Pallas kernels for 0% -> 0%
where the time goes in v1:
time: 260 us; the launch traced here: 259 us
  waiting for transfers between devices  120 us (46%)
  starting transfers between devices  68.2 us (26%)
  blocking collectives  43.2 us (17%)
  local copies, waits for them, and re-layouts  13.5 us (5%)
  matrix products  8.47 us (3%)
  other arithmetic  3.59 us (1%)
    all_to_all x8, waiting for transfers between devices, swap(): return lax.all_to_all(blocks, axes, split_axis=0, concat_axis=0, tiled=True)  105 us
    all_to_all x8, starting transfers between devices, swap(): return lax.all_to_all(blocks, axes, split_axis=0, concat_axis=0, tiled=True)  44 us
    all_to_all x2, blocking collectives, swap(): return lax.all_to_all(blocks, axes, split_axis=0, concat_axis=0, tiled=True)  43.2 us
    ppermute x8, starting transfers between devices, shift_z(): return lax.ppermute(block, Z, [(i, (i + step) % 16) for i in range(16)])  24.1 us
    ppermute x8, waiting for transfers between devices, shift_z(): return lax.ppermute(block, Z, [(i, (i + step) % 16) for i in range(16)])  14.8 us
    dot_general x5, matrix products, dot(): lax.dot_general(a, b, dims, precision=HIGH, preferred_element_type=jnp.fl...  8.47 us
  transfers between devices with their start and end apart: 16, of which 13 were waited for; matrix products, arithmetic and copies ran while one was open for 4% of the time, Pallas kernels for 0%

profile of v1, /device:TPU:1, one launch (start us, length us, event | category | flops | bytes accessed | tf_op | source)
XLA Modules:
  0.0 259.0 jit_solution(16735136679608538663)
XLA Ops:
  5.1 27.0 %all_to_all.54 = f32[16,1,512]{2,1,0:T(1,128)S(1)} all-to-all(f32[16,1,512]{2,1,0:T(1,128)S(1)} %copy.30), channel_id=1, replica_groups=mesh['x'=4,'h'=4,'l'=4,'y'=4,'c'=2] {'h','l'}, dimensions={0} | all-to-all | bytes 65536 | tf_op jit(solution)/shard_map/all_to_all | solution.py:14
  33.3 9.1 %all-to-all-start.1 = ((f32[32,16,512]{2,1,0:T(8,128)}), f32[32,16,512]{2,1,0:T(8,128)S(1)}, u32[]{:S(2)}, u32[]{:S(2)}) async-start(f32[32,16,512]{2,1,0:T(8,128)} %broadcast_in_dim.96), calls=%async_computation.1 | async-start | bytes 2097152 | tf_op jit(solution)/shard_map/all_to_all | solution.py:14
  42.4 2.4 reshape.266
  46.9 12.5 %all-to-all-done.1 = f32[32,16,512]{2,1,0:T(8,128)S(1)} async-done(((f32[32,16,512]{2,1,0:T(8,128)}), f32[32,16,512]{2,1,0:T(8,128)S(1)}, u32[]{:S(2)}, u32[]{:S(2)}) %all-to-all-start.1) | async-done | bytes 1048608 | tf_op jit(solution)/shard_map/all_to_all | solution.py:14
  59.3 3.6 %all-to-all-start.2 = ((f32[4,96,1024]{2,1,0:T(8,128)}), f32[4,96,1024]{2,1,0:T(8,128)S(1)}, u32[]{:S(2)}, u32[]{:S(2)}) async-start(f32[4,96,1024]{2,1,0:T(8,128)} %copy.31), calls=%async_computation.2 | async-start | bytes 3145728 | tf_op jit(solution)/shard_map/all_to_all | solution.py:14
  64.5 19.1 %all-to-all-done.2 = f32[4,96,1024]{2,1,0:T(8,128)S(1)} async-done(((f32[4,96,1024]{2,1,0:T(8,128)}), f32[4,96,1024]{2,1,0:T(8,128)S(1)}, u32[]{:S(2)}, u32[]{:S(2)}) %all-to-all-start.2) | async-done | bytes 1572896 | tf_op jit(solution)/shard_map/all_to_all | solution.py:14
  85.5 2.7 %collective-permute-start.1 = (f32[64,1024]{1,0:T(8,128)S(1)}, f32[64,1024]{1,0:T(8,128)S(1)}, u32[]{:S(2)}, u32[]{:S(2)}) collective-permute-start(f32[64,1024]{1,0:T(8,128)S(1)} %get-tuple-element.13), channel_id=1, source_target_pairs={{0,120},{8,0},{16,8},{24,16},{32,24},{40,32},{48,40},{56,48},{64,5... | collective-permute-start | bytes 786440 | tf_op jit(solution)/shard_map/ppermute | solution.py:22
  88.2 2.6 %collective-permute-start = (f32[64,1024]{1,0:T(8,128)S(1)}, f32[64,1024]{1,0:T(8,128)S(1)}, u32[]{:S(2)}, u32[]{:S(2)}) collective-permute-start(f32[64,1024]{1,0:T(8,128)S(1)} %get-tuple-element.12), channel_id=1, source_target_pairs={{0,8},{8,16},{16,24},{24,32},{32,40},{40,48},{48,56},{56,64},{64,7... | collective-permute-start | bytes 786440 | tf_op jit(solution)/shard_map/ppermute | solution.py:22
  90.8 2.6 %collective-permute-start.3 = (f32[32,1024]{1,0:T(8,128)S(1)}, f32[32,1024]{1,0:T(8,128)S(1)}, u32[]{:S(2)}, u32[]{:S(2)}) collective-permute-start(f32[32,1024]{1,0:T(8,128)S(1)} %get-tuple-element.11), channel_id=1, source_target_pairs={{0,112},{8,120},{16,0},{24,8},{32,16},{40,24},{48,32},{56,40},{64,... | collective-permute-start | bytes 393224 | tf_op jit(solution)/shard_map/ppermute | solution.py:22
  93.4 3.6 %collective-permute-start.2 = (f32[32,1024]{1,0:T(8,128)S(1)}, f32[32,1024]{1,0:T(8,128)S(1)}, u32[]{:S(2)}, u32[]{:S(2)}) collective-permute-start(f32[32,1024]{1,0:T(8,128)S(1)} %get-tuple-element.10), channel_id=1, source_target_pairs={{0,16},{8,24},{16,32},{24,40},{32,48},{40,56},{48,64},{56,72},{64,... | collective-permute-start | bytes 393224 | tf_op jit(solution)/shard_map/ppermute | solution.py:22
  97.0 4.2 %collective-permute-done.3 = f32[32,1024]{1,0:T(8,128)S(1)} collective-permute-done((f32[32,1024]{1,0:T(8,128)S(1)}, f32[32,1024]{1,0:T(8,128)S(1)}, u32[]{:S(2)}, u32[]{:S(2)}) %collective-permute-start.3) | collective-permute-done | bytes 131104 | tf_op jit(solution)/shard_map/ppermute | solution.py:22
  101.2 3.7 %collective-permute-done.2 = f32[32,1024]{1,0:T(8,128)S(1)} collective-permute-done((f32[32,1024]{1,0:T(8,128)S(1)}, f32[32,1024]{1,0:T(8,128)S(1)}, u32[]{:S(2)}, u32[]{:S(2)}) %collective-permute-start.2) | collective-permute-done | bytes 131104 | tf_op jit(solution)/shard_map/ppermute | solution.py:22
  105.7 3.4 %all-to-all-start.3 = ((f32[4,16,1024]{2,1,0:T(8,128)}), f32[4,16,1024]{2,1,0:T(8,128)S(1)}, u32[]{:S(2)}, u32[]{:S(2)}) async-start(f32[4,16,1024]{2,1,0:T(8,128)} %bitcast.5), calls=%async_computation.3 | async-start | bytes 524288 | tf_op jit(solution)/shard_map/all_to_all | solution.py:14
  109.4 14.0 %all-to-all-done.3 = f32[4,16,1024]{2,1,0:T(8,128)S(1)} async-done(((f32[4,16,1024]{2,1,0:T(8,128)}), f32[4,16,1024]{2,1,0:T(8,128)S(1)}, u32[]{:S(2)}, u32[]{:S(2)}) %all-to-all-start.3) | async-done | bytes 262176 | tf_op jit(solution)/shard_map/all_to_all | solution.py:14
  124.3 6.9 %all-to-all-start.4 = ((f32[32,3,16]{2,1,0:T(4,128)}), f32[32,3,16]{2,1,0:T(4,128)S(1)}, u32[]{:S(2)}, u32[]{:S(2)}) async-start(f32[32,3,16]{2,1,0:T(4,128)} %broadcast_in_dim.103), calls=%async_computation.4 | async-start | bytes 131072 | tf_op jit(solution)/shard_map/all_to_all | solution.py:14
  131.2 7.4 %all-to-all-done.4 = f32[32,3,16]{2,1,0:T(4,128)S(1)} async-done(((f32[32,3,16]{2,1,0:T(4,128)}), f32[32,3,16]{2,1,0:T(4,128)S(1)}, u32[]{:S(2)}, u32[]{:S(2)}) %all-to-all-start.4) | async-done | bytes 6176 | tf_op jit(solution)/shard_map/all_to_all | solution.py:14
  139.6 6.8 %all-to-all-start.5 = ((f32[4,16,1024]{2,1,0:T(8,128)}), f32[4,16,1024]{2,1,0:T(8,128)S(1)}, u32[]{:S(2)}, u32[]{:S(2)}) async-start(f32[4,16,1024]{2,1,0:T(8,128)} %broadcast_in_dim.104), calls=%async_computation.5 | async-start | bytes 524288 | tf_op jit(solution)/shard_map/all_to_all | solution.py:14
  146.8 16.3 %all-to-all-done.5 = f32[4,16,1024]{2,1,0:T(8,128)S(1)} async-done(((f32[4,16,1024]{2,1,0:T(8,128)}), f32[4,16,1024]{2,1,0:T(8,128)S(1)}, u32[]{:S(2)}, u32[]{:S(2)}) %all-to-all-start.5) | async-done | bytes 262176 | tf_op jit(solution)/shard_map/all_to_all | solution.py:14
  163.1 3.1 %collective-permute-start.4 = (f32[64,1024]{1,0:T(8,128)S(1)}, f32[64,1024]{1,0:T(8,128)S(1)}, u32[]{:S(2)}, u32[]{:S(2)}) collective-permute-start(f32[64,1024]{1,0:T(8,128)S(1)} %bitcast.45), channel_id=1, source_target_pairs={{0,120},{8,0},{16,8},{24,16},{32,24},{40,32},{48,40},{56,48},{64,5... | collective-permute-start | bytes 786440 | tf_op jit(solution)/shard_map/ppermute | solution.py:22
  166.2 2.9 %collective-permute-start.5 = (f32[32,1024]{1,0:T(8,128)S(1)}, f32[32,1024]{1,0:T(8,128)S(1)}, u32[]{:S(2)}, u32[]{:S(2)}) collective-permute-start(f32[32,1024]{1,0:T(8,128)S(1)} %bitcast.58), channel_id=1, source_target_pairs={{0,16},{8,24},{16,32},{24,40},{32,48},{40,56},{48,64},{56,72},{64,... | collective-permute-start | bytes 393224 | tf_op jit(solution)/shard_map/ppermute | solution.py:22
  171.1 4.8 %collective-permute-start.6 = (f32[32,1024]{1,0:T(8,128)S(1)}, f32[32,1024]{1,0:T(8,128)S(1)}, u32[]{:S(2)}, u32[]{:S(2)}) collective-permute-start(f32[32,1024]{1,0:T(8,128)S(1)} %bitcast.57), channel_id=1, source_target_pairs={{0,112},{8,120},{16,0},{24,8},{32,16},{40,24},{48,32},{56,40},{64,... | collective-permute-start | bytes 393224 | tf_op jit(solution)/shard_map/ppermute | solution.py:22
  175.9 2.3 collective-permute-done.5
  178.2 2.3 collective-permute-done.6
  180.5 2.2 collective-permute-done.7
  186.2 5.9 %all-to-all-start.6 = ((f32[32,16,384]{2,1,0:T(8,128)}), f32[32,16,384]{2,1,0:T(8,128)S(1)}, u32[]{:S(2)}, u32[]{:S(2)}) async-start(f32[32,16,384]{2,1,0:T(8,128)} %bitcast.14), calls=%async_computation.6 | async-start | bytes 1572864 | tf_op jit(solution)/shard_map/all_to_all | solution.py:14
  192.5 13.9 %all-to-all-done.6 = f32[32,16,384]{2,1,0:T(8,128)S(1)} async-done(((f32[32,16,384]{2,1,0:T(8,128)}), f32[32,16,384]{2,1,0:T(8,128)S(1)}, u32[]{:S(2)}, u32[]{:S(2)}) %all-to-all-start.6) | async-done | bytes 786464 | tf_op jit(solution)/shard_map/all_to_all | solution.py:14
  206.5 16.1 %all_to_all.55 = f32[16,1,512]{2,1,0:T(1,128)S(1)} all-to-all(f32[16,1,512]{2,1,0:T(1,128)S(1)} %broadcast_in_dim.106), channel_id=1, replica_groups=mesh['x'=4,'h'=4,'l'=4,'y'=4,'c'=2] {'h','l'}, dimensions={0} | all-to-all | bytes 65536 | tf_op jit(solution)/shard_map/all_to_all | solution.py:14
  223.6 4.8 %all-to-all-start.8 = ((f32[8,1,6144]{2,1,0:T(1,128)}), f32[8,1,6144]{2,1,0:T(1,128)S(1)}, u32[]{:S(2)}, u32[]{:S(2)}) async-start(f32[8,1,6144]{2,1,0:T(1,128)} %broadcast_in_dim.108), calls=%async_computation.8 | async-start | bytes 393216 | tf_op jit(solution)/shard_map/all_to_all | solution.py:14
  228.4 2.6 fusion.29
  231.0 3.3 %all-to-all-done.8 = f32[8,1,6144]{2,1,0:T(1,128)S(1)} async-done(((f32[8,1,6144]{2,1,0:T(1,128)}), f32[8,1,6144]{2,1,0:T(1,128)S(1)}, u32[]{:S(2)}, u32[]{:S(2)}) %all-to-all-start.8) | async-done | bytes 196640 | tf_op jit(solution)/shard_map/all_to_all | solution.py:14
  234.3 3.6 %all-to-all-start.9 = ((f32[4,96,1024]{2,1,0:T(8,128)}), f32[4,96,1024]{2,1,0:T(8,128)S(1)}, u32[]{:S(2)}, u32[]{:S(2)}) async-start(f32[4,96,1024]{2,1,0:T(8,128)} %bitcast.16), calls=%async_computation.9 | async-start | bytes 3145728 | tf_op jit(solution)/shard_map/all_to_all | solution.py:14
  239.2 18.5 %all-to-all-done.9 = f32[4,96,1024]{2,1,0:T(8,128)S(1)} async-done(((f32[4,96,1024]{2,1,0:T(8,128)}), f32[4,96,1024]{2,1,0:T(8,128)S(1)}, u32[]{:S(2)}, u32[]{:S(2)}) %all-to-all-start.9) | async-done | bytes 1572896 | tf_op jit(solution)/shard_map/all_to_all | solution.py:14
  (68 shorter events, 22.5 us)
Async XLA Ops:
  0.6 0.9 copy-start
  33.3 26.1 %all-to-all-start.1 = ((f32[32,16,512]{2,1,0:T(8,128)}), f32[32,16,512]{2,1,0:T(8,128)S(1)}, u32[]{:S(2)}, u32[]{:S(2)}) async-start(f32[32,16,512]{2,1,0:T(8,128)} %broadcast_in_dim.96), calls=%async_computation.1 | async-start | bytes 2097152 | tf_op jit(solution)/shard_map/all_to_all | solution.py:14
  59.3 24.2 %all-to-all-start.2 = ((f32[4,96,1024]{2,1,0:T(8,128)}), f32[4,96,1024]{2,1,0:T(8,128)S(1)}, u32[]{:S(2)}, u32[]{:S(2)}) async-start(f32[4,96,1024]{2,1,0:T(8,128)} %copy.31), calls=%async_computation.2 | async-start | bytes 3145728 | tf_op jit(solution)/shard_map/all_to_all | solution.py:14
  85.5 19.4 %collective-permute-start.1 = (f32[64,1024]{1,0:T(8,128)S(1)}, f32[64,1024]{1,0:T(8,128)S(1)}, u32[]{:S(2)}, u32[]{:S(2)}) collective-permute-start(f32[64,1024]{1,0:T(8,128)S(1)} %get-tuple-element.13), channel_id=1, source_target_pairs={{0,120},{8,0},{16,8},{24,16},{32,24},{40,32},{48,40},{56,48},{64,5... | collective-permute-start | bytes 786440 | tf_op jit(solution)/shard_map/ppermute | solution.py:22
  88.2 16.8 %collective-permute-start = (f32[64,1024]{1,0:T(8,128)S(1)}, f32[64,1024]{1,0:T(8,128)S(1)}, u32[]{:S(2)}, u32[]{:S(2)}) collective-permute-start(f32[64,1024]{1,0:T(8,128)S(1)} %get-tuple-element.12), channel_id=1, source_target_pairs={{0,8},{8,16},{16,24},{24,32},{32,40},{40,48},{48,56},{56,64},{64,7... | collective-permute-start | bytes 786440 | tf_op jit(solution)/shard_map/ppermute | solution.py:22
  90.8 10.4 %collective-permute-start.3 = (f32[32,1024]{1,0:T(8,128)S(1)}, f32[32,1024]{1,0:T(8,128)S(1)}, u32[]{:S(2)}, u32[]{:S(2)}) collective-permute-start(f32[32,1024]{1,0:T(8,128)S(1)} %get-tuple-element.11), channel_id=1, source_target_pairs={{0,112},{8,120},{16,0},{24,8},{32,16},{40,24},{48,32},{56,40},{64,... | collective-permute-start | bytes 393224 | tf_op jit(solution)/shard_map/ppermute | solution.py:22
  93.4 11.5 %collective-permute-start.2 = (f32[32,1024]{1,0:T(8,128)S(1)}, f32[32,1024]{1,0:T(8,128)S(1)}, u32[]{:S(2)}, u32[]{:S(2)}) collective-permute-start(f32[32,1024]{1,0:T(8,128)S(1)} %get-tuple-element.10), channel_id=1, source_target_pairs={{0,16},{8,24},{16,32},{24,40},{32,48},{40,56},{48,64},{56,72},{64,... | collective-permute-start | bytes 393224 | tf_op jit(solution)/shard_map/ppermute | solution.py:22
  105.7 17.6 %all-to-all-start.3 = ((f32[4,16,1024]{2,1,0:T(8,128)}), f32[4,16,1024]{2,1,0:T(8,128)S(1)}, u32[]{:S(2)}, u32[]{:S(2)}) async-start(f32[4,16,1024]{2,1,0:T(8,128)} %bitcast.5), calls=%async_computation.3 | async-start | bytes 524288 | tf_op jit(solution)/shard_map/all_to_all | solution.py:14
  124.3 14.3 %all-to-all-start.4 = ((f32[32,3,16]{2,1,0:T(4,128)}), f32[32,3,16]{2,1,0:T(4,128)S(1)}, u32[]{:S(2)}, u32[]{:S(2)}) async-start(f32[32,3,16]{2,1,0:T(4,128)} %broadcast_in_dim.103), calls=%async_computation.4 | async-start | bytes 131072 | tf_op jit(solution)/shard_map/all_to_all | solution.py:14
  139.6 23.5 %all-to-all-start.5 = ((f32[4,16,1024]{2,1,0:T(8,128)}), f32[4,16,1024]{2,1,0:T(8,128)S(1)}, u32[]{:S(2)}, u32[]{:S(2)}) async-start(f32[4,16,1024]{2,1,0:T(8,128)} %broadcast_in_dim.104), calls=%async_computation.5 | async-start | bytes 524288 | tf_op jit(solution)/shard_map/all_to_all | solution.py:14
  163.1 12.8 %collective-permute-start.4 = (f32[64,1024]{1,0:T(8,128)S(1)}, f32[64,1024]{1,0:T(8,128)S(1)}, u32[]{:S(2)}, u32[]{:S(2)}) collective-permute-start(f32[64,1024]{1,0:T(8,128)S(1)} %bitcast.45), channel_id=1, source_target_pairs={{0,120},{8,0},{16,8},{24,16},{32,24},{40,32},{48,40},{56,48},{64,5... | collective-permute-start | bytes 786440 | tf_op jit(solution)/shard_map/ppermute | solution.py:22
  166.2 12.0 %collective-permute-start.5 = (f32[32,1024]{1,0:T(8,128)S(1)}, f32[32,1024]{1,0:T(8,128)S(1)}, u32[]{:S(2)}, u32[]{:S(2)}) collective-permute-start(f32[32,1024]{1,0:T(8,128)S(1)} %bitcast.58), channel_id=1, source_target_pairs={{0,16},{8,24},{16,32},{24,40},{32,48},{40,56},{48,64},{56,72},{64,... | collective-permute-start | bytes 393224 | tf_op jit(solution)/shard_map/ppermute | solution.py:22
  169.1 13.6 %collective-permute-start.7 = (f32[64,1024]{1,0:T(8,128)S(1)}, f32[64,1024]{1,0:T(8,128)S(1)}, u32[]{:S(2)}, u32[]{:S(2)}) collective-permute-start(f32[64,1024]{1,0:T(8,128)S(1)} %bitcast.47), channel_id=1, source_target_pairs={{0,8},{8,16},{16,24},{24,32},{32,40},{40,48},{48,56},{56,64},{64,7... | collective-permute-start | bytes 786440 | tf_op jit(solution)/shard_map/ppermute | solution.py:22
  171.1 9.5 %collective-permute-start.6 = (f32[32,1024]{1,0:T(8,128)S(1)}, f32[32,1024]{1,0:T(8,128)S(1)}, u32[]{:S(2)}, u32[]{:S(2)}) collective-permute-start(f32[32,1024]{1,0:T(8,128)S(1)} %bitcast.57), channel_id=1, source_target_pairs={{0,112},{8,120},{16,0},{24,8},{32,16},{40,24},{48,32},{56,40},{64,... | collective-permute-start | bytes 393224 | tf_op jit(solution)/shard_map/ppermute | solution.py:22
  186.2 20.2 %all-to-all-start.6 = ((f32[32,16,384]{2,1,0:T(8,128)}), f32[32,16,384]{2,1,0:T(8,128)S(1)}, u32[]{:S(2)}, u32[]{:S(2)}) async-start(f32[32,16,384]{2,1,0:T(8,128)} %bitcast.14), calls=%async_computation.6 | async-start | bytes 1572864 | tf_op jit(solution)/shard_map/all_to_all | solution.py:14
  223.6 10.7 %all-to-all-start.8 = ((f32[8,1,6144]{2,1,0:T(1,128)}), f32[8,1,6144]{2,1,0:T(1,128)S(1)}, u32[]{:S(2)}, u32[]{:S(2)}) async-start(f32[8,1,6144]{2,1,0:T(1,128)} %broadcast_in_dim.108), calls=%async_computation.8 | async-start | bytes 393216 | tf_op jit(solution)/shard_map/all_to_all | solution.py:14
  234.3 23.3 %all-to-all-start.9 = ((f32[4,96,1024]{2,1,0:T(8,128)}), f32[4,96,1024]{2,1,0:T(8,128)S(1)}, u32[]{:S(2)}, u32[]{:S(2)}) async-start(f32[4,96,1024]{2,1,0:T(8,128)} %bitcast.16), calls=%async_computation.9 | async-start | bytes 3145728 | tf_op jit(solution)/shard_map/all_to_all | solution.py:14

commit v2 on v1

--- a/solution.py
+++ b/solution.py
@@ -22,6 +22,16 @@
     return lax.ppermute(block, Z, [(i, (i + step) % 16) for i in range(16)])
 
 
+def shift_x(block, step):
+    return lax.ppermute(block, "x", [(i, (i + step) % 4) for i in range(4)])
+
+
+def turn(block, chip):
+    depth = block.shape[-1] // 4
+    order = [(chip - s) % 4 for s in range(4)]
+    return jnp.concatenate([block[..., depth * i : depth * (i + 1)] for i in order], axis=-1)
+
+
 def dot(a, b, contract=(1, 0)):
     dims = (((contract[0],), (contract[1],)), ((), ()))
     return lax.dot_general(a, b, dims, precision=HIGH, preferred_element_type=jnp.float32)
@@ -35,7 +45,11 @@
     x, h, l = lax.axis_index("x"), lax.axis_index("h"), lax.axis_index("l")
     j = lax.axis_index(YC)
 
-    head = swap(weight.reshape(depth, 4, quarter).transpose(1, 0, 2), "x").reshape(wide, quarter)
+    heads = [
+        shift_x(lax.dynamic_slice(weight, (0, (x + s) % 4 * quarter), (depth, quarter)), s) if s
+        else lax.dynamic_slice(weight, (0, x * quarter), (depth, quarter))
+        for s in range(4)
+    ]
 
     row = lax.dynamic_slice(responses, (j, 0), (1, width))
     row = row.reshape(4, 16, depth).transpose(1, 0, 2).reshape(16, wide)
@@ -43,7 +57,9 @@
     notes = jnp.pad(notes.astype(jnp.float32), (0, META - 3))
     packed = jnp.concatenate([row, jnp.broadcast_to(notes[None], (16, META))], axis=1)
     mine = swap(packed[:, None, :], Z).reshape(16, wide + META)
-    slots = spread(mine, XYC, 32).reshape(512, wide + META)
+    turned = jnp.stack([jnp.concatenate([turn(mine[:, :wide], i), mine[:, wide:]], axis=1) for i in range(4)])
+    copies = jnp.broadcast_to(turned[:, None], (4, 8, 16, wide + META)).reshape(32, 16, wide + META)
+    slots = swap(copies, XYC).reshape(512, wide + META)
 
     ids = jnp.arange(512, dtype=jnp.int32)
     slot_j = (ids // 16) % 8
@@ -62,6 +78,7 @@
     sent_rank = jnp.sum(jnp.where(owned, rank[None, :] + 1, 0), axis=1) - 1
     deliver = (sent_rank[:, None] == rows[None, :]).astype(jnp.float32)
 
+    head = jnp.concatenate(heads, axis=0)
     partial = dot(hidden, head)
     up = shift_z(partial[64:128], 1)
     down = shift_z(partial[192:256], -1)
@@ -91,11 +108,15 @@
     grads = jnp.concatenate([own, after, far, far2, ahead], axis=0)
 
     grad_head = dot(hidden, grads, (0, 0)).reshape(4, depth, quarter)
-    grad_weight = swap(grad_head, "x").transpose(1, 0, 2).reshape(depth, columns)
+    grad_weight = jnp.zeros((depth, columns), jnp.float32)
+    for s in range(4):
+        part = shift_x(grad_head[s], -s) if s else grad_head[0]
+        grad_weight = lax.dynamic_update_slice(grad_weight, part, (0, (x + s) % 4 * quarter))
 
     grad_rows = dot(grads, head, (1, 1))
     leaving = dot(deliver, grad_rows).reshape(32, 16, wide)
-    summed = jnp.sum(swap(leaving, XYC), axis=0)
+    summed = jnp.sum(swap(leaving, XYC).reshape(4, 8, 16, wide), axis=1)
+    summed = sum(turn(summed[i], i) for i in range(4))
     parts = lax.dynamic_update_slice(jnp.zeros((16, META), jnp.float32), logprobs.reshape(4, 4), (h * 4, 0))
     parts = jnp.where(l == x, parts, 0.0)
     arrived = swap(jnp.concatenate([summed, parts], axis=1)[:, None, :], Z)[:, 0]

time: 260 us -> 233 us (0.90)
  waiting for transfers between devices: 120 us -> 79.2 us
  starting transfers between devices: 68.2 us -> 98.2 us
  blocking collectives: 43.2 us -> 27 us
    all_to_all x8 -> x7, waiting for transfers between devices: 105 us -> 51 us  [swap(): return lax.all_to_all(blocks, axes, split_axis=0, concat_axis=0, tiled=True)]
    ppermute x0 -> x6, starting transfers between devices: none -> 20.9 us  [shift_x(): return lax.ppermute(block, 'x', [(i, (i + step) % 4) for i in range(4)])]
    ppermute x0 -> x6, waiting for transfers between devices: none -> 20.5 us  [shift_x(): return lax.ppermute(block, 'x', [(i, (i + step) % 4) for i in range(4)])]
    all_to_all x2 -> x1, blocking collectives: 43.2 us -> 27 us  [swap(): return lax.all_to_all(blocks, axes, split_axis=0, concat_axis=0, tiled=True)]
    ppermute x8, waiting for transfers between devices: 14.8 us -> 7.74 us  [shift_z(): return lax.ppermute(block, Z, [(i, (i + step) % 16) for i in range(16)])]
    ppermute x8, starting transfers between devices: 24.1 us -> 31 us  [shift_z(): return lax.ppermute(block, Z, [(i, (i + step) % 16) for i in range(16)])]
    reshape x2 -> x0, local copies, waits for them, and re-layouts: 3.68 us -> none  [the longest x1 2.36 us: on_device(): weight.reshape(depth, 4, quarter).transpose(1, 0, 2)]
    all_to_all x8 -> x7, starting transfers between devices: 44 us -> 46.4 us  [swap(): return lax.all_to_all(blocks, axes, split_axis=0, concat_axis=0, tiled=True)]
  transfers between devices with their start and end apart: 16 -> 21, of which waited for: 13 -> 15; matrix products, arithmetic and copies ran while one was open for 4% -> 4% of each run, Pallas kernels for 0% -> 0%
where the time goes in v2:
time: 233 us; the launch traced here: 232 us
  starting transfers between devices  98.2 us (42%)
  waiting for transfers between devices  79.2 us (34%)
  blocking collectives  27 us (12%)
  local copies, waits for them, and re-layouts  11.4 us (5%)
  matrix products  9.67 us (4%)
  other arithmetic  3.84 us (2%)
  between operations  2.51 us (1%)
    all_to_all x7, waiting for transfers between devices, swap(): return lax.all_to_all(blocks, axes, split_axis=0, concat_axis=0, tiled=True)  51 us
    all_to_all x7, starting transfers between devices, swap(): return lax.all_to_all(blocks, axes, split_axis=0, concat_axis=0, tiled=True)  46.4 us
    ppermute x8, starting transfers between devices, shift_z(): return lax.ppermute(block, Z, [(i, (i + step) % 16) for i in range(16)])  31 us
    all_to_all x1, blocking collectives, swap(): return lax.all_to_all(blocks, axes, split_axis=0, concat_axis=0, tiled=True)  27 us
    ppermute x6, starting transfers between devices, shift_x(): return lax.ppermute(block, 'x', [(i, (i + step) % 4) for i in range(4)])  20.9 us
    ppermute x6, waiting for transfers between devices, shift_x(): return lax.ppermute(block, 'x', [(i, (i + step) % 4) for i in range(4)])  20.5 us
    dot_general x5, matrix products, dot(): lax.dot_general(a, b, dims, precision=HIGH, preferred_element_type=jnp.fl...  9.67 us
    ppermute x8, waiting for transfers between devices, shift_z(): return lax.ppermute(block, Z, [(i, (i + step) % 16) for i in range(16)])  7.74 us
  transfers between devices with their start and end apart: 21, of which 15 were waited for; matrix products, arithmetic and copies ran while one was open for 4% of the time, Pallas kernels for 0%

profile of v2, /device:TPU:1, one launch (start us, length us, event | category | flops | bytes accessed | tf_op | source)
XLA Modules:
  0.0 232.0 jit_solution(14007959242364505657)
XLA Ops:
  4.3 27.0 %all_to_all.44 = f32[16,1,512]{2,1,0:T(1,128)S(1)} all-to-all(f32[16,1,512]{2,1,0:T(1,128)S(1)} %copy.22), channel_id=1, replica_groups=mesh['x'=4,'h'=4,'l'=4,'y'=4,'c'=2] {'h','l'}, dimensions={0} | all-to-all | bytes 65536 | tf_op jit(solution)/shard_map/all_to_all | solution.py:14
  32.9 9.1 %all-to-all-start.1 = ((f32[32,16,512]{2,1,0:T(8,128)}), f32[32,16,512]{2,1,0:T(8,128)S(1)}, u32[]{:S(2)}, u32[]{:S(2)}) async-start(f32[32,16,512]{2,1,0:T(8,128)} %bitcast.6), calls=%async_computation.1 | async-start | bytes 2097152 | tf_op jit(solution)/shard_map/all_to_all | solution.py:14
  43.2 3.3 %collective-permute-start = (f32[96,1024]{1,0:T(8,128)}, f32[96,1024]{1,0:T(8,128)S(1)}, u32[]{:S(2)}, u32[]{:S(2)}) collective-permute-start(f32[96,1024]{1,0:T(8,128)} %get-tuple-element.15), channel_id=1, source_target_pairs={{0,128},{128,256},{256,384},{384,0},{1,129},{129,257},{257,385},{3... | collective-permute-start | bytes 1179656 | tf_op jit(solution)/shard_map/ppermute | solution.py:26
  46.5 3.2 %collective-permute-start.2 = (f32[96,1024]{1,0:T(8,128)}, f32[96,1024]{1,0:T(8,128)}, u32[]{:S(2)}, u32[]{:S(2)}) collective-permute-start(f32[96,1024]{1,0:T(8,128)} %get-tuple-element.16), channel_id=1, source_target_pairs={{0,384},{128,0},{256,128},{384,256},{1,385},{129,1},{257,129},{385... | collective-permute-start | bytes 1179656 | tf_op jit(solution)/shard_map/ppermute | solution.py:26
  49.7 3.6 %collective-permute-start.1 = (f32[96,1024]{1,0:T(8,128)}, f32[96,1024]{1,0:T(8,128)}, u32[]{:S(2)}, u32[]{:S(2)}) collective-permute-start(f32[96,1024]{1,0:T(8,128)} %get-tuple-element.17), channel_id=1, source_target_pairs={{0,256},{128,384},{256,0},{384,128},{1,257},{129,385},{257,1},{385... | collective-permute-start | bytes 1179656 | tf_op jit(solution)/shard_map/ppermute | solution.py:26
  53.3 5.8 %all-to-all-done.1 = f32[32,16,512]{2,1,0:T(8,128)S(1)} async-done(((f32[32,16,512]{2,1,0:T(8,128)}), f32[32,16,512]{2,1,0:T(8,128)S(1)}, u32[]{:S(2)}, u32[]{:S(2)}) %all-to-all-start.1) | async-done | bytes 1048608 | tf_op jit(solution)/shard_map/all_to_all | solution.py:14
  60.6 4.6 %collective-permute-done = f32[96,1024]{1,0:T(8,128)S(1)} collective-permute-done((f32[96,1024]{1,0:T(8,128)}, f32[96,1024]{1,0:T(8,128)S(1)}, u32[]{:S(2)}, u32[]{:S(2)}) %collective-permute-start) | collective-permute-done | bytes 393248 | tf_op jit(solution)/shard_map/ppermute | solution.py:26
  65.2 8.8 %collective-permute-done.1 = f32[96,1024]{1,0:T(8,128)} collective-permute-done((f32[96,1024]{1,0:T(8,128)}, f32[96,1024]{1,0:T(8,128)}, u32[]{:S(2)}, u32[]{:S(2)}) %collective-permute-start.1) | collective-permute-done | bytes 393248 | tf_op jit(solution)/shard_map/ppermute | solution.py:26
  74.0 3.0 %fusion.1 = f32[256,1024]{1,0:T(8,128)S(1)} fusion(f32[256,384]{1,0:T(8,128)S(1)} %fusion.2, f32[96,1024]{1,0:T(8,128)} %collective-permute-done.2, f32[96,1024]{1,0:T(8,128)} %collective-permute-done.1, f32[96,1024]{1,0:T(8,128)S(1)} %collective-permute-done, f32[96,1024]{1,0:T(8,128)S(1)} %get-tuple-element.14), kind=kOutput, calls=%fused_computation.4 | convolution fusion | flops 1209139200 | bytes 3014656 | tf_op jit(solution)/shard_map/dot_general | solution.py:37
  77.0 2.4 %collective-permute-start.3 = (f32[64,1024]{1,0:T(8,128)S(1)}, f32[64,1024]{1,0:T(8,128)S(1)}, u32[]{:S(2)}, u32[]{:S(2)}) collective-permute-start(f32[64,1024]{1,0:T(8,128)S(1)} %get-tuple-element.20), channel_id=1, source_target_pairs={{0,8},{8,16},{16,24},{24,32},{32,40},{40,48},{48,56},{56,64},{64,7... | collective-permute-start | bytes 786440 | tf_op jit(solution)/shard_map/ppermute | solution.py:22
  79.5 4.0 %collective-permute-start.4 = (f32[64,1024]{1,0:T(8,128)S(1)}, f32[64,1024]{1,0:T(8,128)S(1)}, u32[]{:S(2)}, u32[]{:S(2)}) collective-permute-start(f32[64,1024]{1,0:T(8,128)S(1)} %get-tuple-element.21), channel_id=1, source_target_pairs={{0,120},{8,0},{16,8},{24,16},{32,24},{40,32},{48,40},{56,48},{64,5... | collective-permute-start | bytes 786440 | tf_op jit(solution)/shard_map/ppermute | solution.py:22
  83.6 1.9 collective-permute-start.5
  85.5 5.5 %collective-permute-start.6 = (f32[32,1024]{1,0:T(8,128)S(1)}, f32[32,1024]{1,0:T(8,128)S(1)}, u32[]{:S(2)}, u32[]{:S(2)}) collective-permute-start(f32[32,1024]{1,0:T(8,128)S(1)} %get-tuple-element.19), channel_id=1, source_target_pairs={{0,112},{8,120},{16,0},{24,8},{32,16},{40,24},{48,32},{56,40},{64,... | collective-permute-start | bytes 393224 | tf_op jit(solution)/shard_map/ppermute | solution.py:22
  91.0 3.5 %collective-permute-done.5 = f32[32,1024]{1,0:T(8,128)S(1)} collective-permute-done((f32[32,1024]{1,0:T(8,128)S(1)}, f32[32,1024]{1,0:T(8,128)S(1)}, u32[]{:S(2)}, u32[]{:S(2)}) %collective-permute-start.5) | collective-permute-done | bytes 131104 | tf_op jit(solution)/shard_map/ppermute | solution.py:22
  95.9 5.7 %all-to-all-start.2 = ((f32[4,16,1024]{2,1,0:T(8,128)}), f32[4,16,1024]{2,1,0:T(8,128)S(1)}, u32[]{:S(2)}, u32[]{:S(2)}) async-start(f32[4,16,1024]{2,1,0:T(8,128)} %bitcast.8), calls=%async_computation.2 | async-start | bytes 524288 | tf_op jit(solution)/shard_map/all_to_all | solution.py:14
  101.8 14.1 %all-to-all-done.2 = f32[4,16,1024]{2,1,0:T(8,128)S(1)} async-done(((f32[4,16,1024]{2,1,0:T(8,128)}), f32[4,16,1024]{2,1,0:T(8,128)S(1)}, u32[]{:S(2)}, u32[]{:S(2)}) %all-to-all-start.2) | async-done | bytes 262176 | tf_op jit(solution)/shard_map/all_to_all | solution.py:14
  116.9 9.0 %all-to-all-start.3 = ((f32[32,3,16]{2,1,0:T(4,128)}), f32[32,3,16]{2,1,0:T(4,128)S(1)}, u32[]{:S(2)}, u32[]{:S(2)}) async-start(f32[32,3,16]{2,1,0:T(4,128)} %broadcast_in_dim.104), calls=%async_computation.3 | async-start | bytes 131072 | tf_op jit(solution)/shard_map/all_to_all | solution.py:14
  125.9 7.4 %all-to-all-done.3 = f32[32,3,16]{2,1,0:T(4,128)S(1)} async-done(((f32[32,3,16]{2,1,0:T(4,128)}), f32[32,3,16]{2,1,0:T(4,128)S(1)}, u32[]{:S(2)}, u32[]{:S(2)}) %all-to-all-start.3) | async-done | bytes 6176 | tf_op jit(solution)/shard_map/all_to_all | solution.py:14
  134.2 3.4 %all-to-all-start.4 = ((f32[4,16,1024]{2,1,0:T(8,128)}), f32[4,16,1024]{2,1,0:T(8,128)S(1)}, u32[]{:S(2)}, u32[]{:S(2)}) async-start(f32[4,16,1024]{2,1,0:T(8,128)} %broadcast_in_dim.105), calls=%async_computation.4 | async-start | bytes 524288 | tf_op jit(solution)/shard_map/all_to_all | solution.py:14
  137.9 14.6 %all-to-all-done.4 = f32[4,16,1024]{2,1,0:T(8,128)S(1)} async-done(((f32[4,16,1024]{2,1,0:T(8,128)}), f32[4,16,1024]{2,1,0:T(8,128)S(1)}, u32[]{:S(2)}, u32[]{:S(2)}) %all-to-all-start.4) | async-done | bytes 262176 | tf_op jit(solution)/shard_map/all_to_all | solution.py:14
  154.5 7.8 %collective-permute-start.7 = (f32[64,1024]{1,0:T(8,128)S(1)}, f32[64,1024]{1,0:T(8,128)S(1)}, u32[]{:S(2)}, u32[]{:S(2)}) collective-permute-start(f32[64,1024]{1,0:T(8,128)S(1)} %bitcast.50), channel_id=1, source_target_pairs={{0,120},{8,0},{16,8},{24,16},{32,24},{40,32},{48,40},{56,48},{64,5... | collective-permute-start | bytes 786440 | tf_op jit(solution)/shard_map/ppermute | solution.py:22
  164.3 5.5 %collective-permute-start.9 = (f32[32,1024]{1,0:T(8,128)S(1)}, f32[32,1024]{1,0:T(8,128)S(1)}, u32[]{:S(2)}, u32[]{:S(2)}) collective-permute-start(f32[32,1024]{1,0:T(8,128)S(1)} %bitcast.62), channel_id=1, source_target_pairs={{0,112},{8,120},{16,0},{24,8},{32,16},{40,24},{48,32},{56,40},{64,... | collective-permute-start | bytes 393224 | tf_op jit(solution)/shard_map/ppermute | solution.py:22
  173.5 3.1 %fusion = f32[256,384]{1,0:T(8,128)S(1)} fusion(f32[256,1024]{1,0:T(8,128)S(1)} %constant_dynamic-update-slice_fusion, f32[96,1024]{1,0:T(8,128)} %collective-permute-done.2, f32[96,1024]{1,0:T(8,128)} %collective-permute-done.1, f32[96,1024]{1,0:T(8,128)} %copy-done.3, f32[96,1024]{1,0:T(8,128)S(1)} %get-tuple-element.14), kind=kOutput, calls=%fused_computation.3 | convolution fusion | flops 1209139200 | bytes 3014656 | tf_op jit(solution)/shard_map/dot_general | solution.py:37
  178.1 7.5 %all-to-all-start.5 = ((f32[32,16,384]{2,1,0:T(8,128)}), f32[32,16,384]{2,1,0:T(8,128)S(1)}, u32[]{:S(2)}, u32[]{:S(2)}) async-start(f32[32,16,384]{2,1,0:T(8,128)} %bitcast.17), calls=%async_computation.5 | async-start | bytes 1572864 | tf_op jit(solution)/shard_map/all_to_all | solution.py:14
  188.7 3.3 %collective-permute-start.13 = (f32[96,1024]{1,0:T(8,128)}, f32[96,1024]{1,0:T(8,128)S(1)}, u32[]{:S(2)}, u32[]{:S(2)}) collective-permute-start(f32[96,1024]{1,0:T(8,128)} %get-tuple-element.10), channel_id=1, source_target_pairs={{0,128},{128,256},{256,384},{384,0},{1,129},{129,257},{257,385},{3... | collective-permute-start | bytes 1179656 | tf_op jit(solution)/shard_map/ppermute | solution.py:26
  192.1 4.4 %collective-permute-start.12 = (f32[96,1024]{1,0:T(8,128)}, f32[96,1024]{1,0:T(8,128)S(1)}, u32[]{:S(2)}, u32[]{:S(2)}) collective-permute-start(f32[96,1024]{1,0:T(8,128)} %get-tuple-element.11), channel_id=1, source_target_pairs={{0,256},{128,384},{256,0},{384,128},{1,257},{129,385},{257,1},{385... | collective-permute-start | bytes 1179656 | tf_op jit(solution)/shard_map/ppermute | solution.py:26
  196.5 3.0 %collective-permute-start.11 = (f32[96,1024]{1,0:T(8,128)}, f32[96,1024]{1,0:T(8,128)}, u32[]{:S(2)}, u32[]{:S(2)}) collective-permute-start(f32[96,1024]{1,0:T(8,128)} %get-tuple-element.12), channel_id=1, source_target_pairs={{0,384},{128,0},{256,128},{384,256},{1,385},{129,1},{257,129},{385... | collective-permute-start | bytes 1179656 | tf_op jit(solution)/shard_map/ppermute | solution.py:26
  201.2 5.3 %all-to-all-start.6 = ((f32[16,1,512]{2,1,0:T(1,128)}), f32[16,1,512]{2,1,0:T(1,128)S(1)}, u32[]{:S(2)}, u32[]{:S(2)}) async-start(f32[16,1,512]{2,1,0:T(1,128)} %broadcast_in_dim.107), calls=%async_computation.6 | async-start | bytes 65536 | tf_op jit(solution)/shard_map/all_to_all | solution.py:14
  206.6 6.6 %collective-permute-done.11 = f32[96,1024]{1,0:T(8,128)} collective-permute-done((f32[96,1024]{1,0:T(8,128)}, f32[96,1024]{1,0:T(8,128)}, u32[]{:S(2)}, u32[]{:S(2)}) %collective-permute-start.11) | collective-permute-done | bytes 393248 | tf_op jit(solution)/shard_map/ppermute | solution.py:26
  214.8 3.2 %all-to-all-done.6 = f32[16,1,512]{2,1,0:T(1,128)S(1)} async-done(((f32[16,1,512]{2,1,0:T(1,128)}), f32[16,1,512]{2,1,0:T(1,128)S(1)}, u32[]{:S(2)}, u32[]{:S(2)}) %all-to-all-start.6) | async-done | bytes 32800 | tf_op jit(solution)/shard_map/all_to_all | solution.py:14
  219.1 6.3 %all-to-all-start.7 = ((f32[8,1,6144]{2,1,0:T(1,128)}), f32[8,1,6144]{2,1,0:T(1,128)S(1)}, u32[]{:S(2)}, u32[]{:S(2)}) async-start(f32[8,1,6144]{2,1,0:T(1,128)} %broadcast_in_dim.109), calls=%async_computation.7 | async-start | bytes 393216 | tf_op jit(solution)/shard_map/all_to_all | solution.py:14
  226.0 5.3 %all-to-all-done.7 = f32[8,1,6144]{2,1,0:T(1,128)S(1)} async-done(((f32[8,1,6144]{2,1,0:T(1,128)}), f32[8,1,6144]{2,1,0:T(1,128)S(1)}, u32[]{:S(2)}, u32[]{:S(2)}) %all-to-all-start.7) | async-done | bytes 196640 | tf_op jit(solution)/shard_map/all_to_all | solution.py:14
  (100 shorter events, 28.2 us)
Async XLA Ops:
  0.6 3.3 %copy-start = (f32[8,6144]{1,0:T(8,128)S(1)}, f32[8,6144]{1,0:T(8,128)}, u32[]{:S(2)}) copy-start(f32[8,6144]{1,0:T(8,128)} %param.5) | copy-start | bytes 589828
  31.8 10.3 %copy-start.2 = (f32[96,4096]{1,0:T(8,128)S(1)}, f32[96,4096]{1,0:T(8,128)}, u32[]{:S(2)}) copy-start(f32[96,4096]{1,0:T(8,128)} %param.6) | copy-start | bytes 4718596
  32.9 26.2 %all-to-all-start.1 = ((f32[32,16,512]{2,1,0:T(8,128)}), f32[32,16,512]{2,1,0:T(8,128)S(1)}, u32[]{:S(2)}, u32[]{:S(2)}) async-start(f32[32,16,512]{2,1,0:T(8,128)} %bitcast.6), calls=%async_computation.1 | async-start | bytes 2097152 | tf_op jit(solution)/shard_map/all_to_all | solution.py:14
  43.2 22.0 %collective-permute-start = (f32[96,1024]{1,0:T(8,128)}, f32[96,1024]{1,0:T(8,128)S(1)}, u32[]{:S(2)}, u32[]{:S(2)}) collective-permute-start(f32[96,1024]{1,0:T(8,128)} %get-tuple-element.15), channel_id=1, source_target_pairs={{0,128},{128,256},{256,384},{384,0},{1,129},{129,257},{257,385},{3... | collective-permute-start | bytes 1179656 | tf_op jit(solution)/shard_map/ppermute | solution.py:26
  46.5 18.8 %collective-permute-start.2 = (f32[96,1024]{1,0:T(8,128)}, f32[96,1024]{1,0:T(8,128)}, u32[]{:S(2)}, u32[]{:S(2)}) collective-permute-start(f32[96,1024]{1,0:T(8,128)} %get-tuple-element.16), channel_id=1, source_target_pairs={{0,384},{128,0},{256,128},{384,256},{1,385},{129,1},{257,129},{385... | collective-permute-start | bytes 1179656 | tf_op jit(solution)/shard_map/ppermute | solution.py:26
  49.7 24.3 %collective-permute-start.1 = (f32[96,1024]{1,0:T(8,128)}, f32[96,1024]{1,0:T(8,128)}, u32[]{:S(2)}, u32[]{:S(2)}) collective-permute-start(f32[96,1024]{1,0:T(8,128)} %get-tuple-element.17), channel_id=1, source_target_pairs={{0,256},{128,384},{256,0},{384,128},{1,257},{129,385},{257,1},{385... | collective-permute-start | bytes 1179656 | tf_op jit(solution)/shard_map/ppermute | solution.py:26
  65.2 11.8 %copy-start.3 = (f32[96,1024]{1,0:T(8,128)}, f32[96,1024]{1,0:T(8,128)S(1)}, u32[]{:S(2)}) copy-start(f32[96,1024]{1,0:T(8,128)S(1)} %collective-permute-done) | copy-start | bytes 1179652
  77.0 18.1 %collective-permute-start.3 = (f32[64,1024]{1,0:T(8,128)S(1)}, f32[64,1024]{1,0:T(8,128)S(1)}, u32[]{:S(2)}, u32[]{:S(2)}) collective-permute-start(f32[64,1024]{1,0:T(8,128)S(1)} %get-tuple-element.20), channel_id=1, source_target_pairs={{0,8},{8,16},{16,24},{24,32},{32,40},{40,48},{48,56},{56,64},{64,7... | collective-permute-start | bytes 786440 | tf_op jit(solution)/shard_map/ppermute | solution.py:22
  79.5 15.6 %collective-permute-start.4 = (f32[64,1024]{1,0:T(8,128)S(1)}, f32[64,1024]{1,0:T(8,128)S(1)}, u32[]{:S(2)}, u32[]{:S(2)}) collective-permute-start(f32[64,1024]{1,0:T(8,128)S(1)} %get-tuple-element.21), channel_id=1, source_target_pairs={{0,120},{8,0},{16,8},{24,16},{32,24},{40,32},{48,40},{56,48},{64,5... | collective-permute-start | bytes 786440 | tf_op jit(solution)/shard_map/ppermute | solution.py:22
  83.6 10.9 %collective-permute-start.5 = (f32[32,1024]{1,0:T(8,128)S(1)}, f32[32,1024]{1,0:T(8,128)S(1)}, u32[]{:S(2)}, u32[]{:S(2)}) collective-permute-start(f32[32,1024]{1,0:T(8,128)S(1)} %get-tuple-element.18), channel_id=1, source_target_pairs={{0,16},{8,24},{16,32},{24,40},{32,48},{40,56},{48,64},{56,72},{64,... | collective-permute-start | bytes 393224 | tf_op jit(solution)/shard_map/ppermute | solution.py:22
  85.5 9.6 %collective-permute-start.6 = (f32[32,1024]{1,0:T(8,128)S(1)}, f32[32,1024]{1,0:T(8,128)S(1)}, u32[]{:S(2)}, u32[]{:S(2)}) collective-permute-start(f32[32,1024]{1,0:T(8,128)S(1)} %get-tuple-element.19), channel_id=1, source_target_pairs={{0,112},{8,120},{16,0},{24,8},{32,16},{40,24},{48,32},{56,40},{64,... | collective-permute-start | bytes 393224 | tf_op jit(solution)/shard_map/ppermute | solution.py:22
  95.9 20.0 %all-to-all-start.2 = ((f32[4,16,1024]{2,1,0:T(8,128)}), f32[4,16,1024]{2,1,0:T(8,128)S(1)}, u32[]{:S(2)}, u32[]{:S(2)}) async-start(f32[4,16,1024]{2,1,0:T(8,128)} %bitcast.8), calls=%async_computation.2 | async-start | bytes 524288 | tf_op jit(solution)/shard_map/all_to_all | solution.py:14
  116.9 16.4 %all-to-all-start.3 = ((f32[32,3,16]{2,1,0:T(4,128)}), f32[32,3,16]{2,1,0:T(4,128)S(1)}, u32[]{:S(2)}, u32[]{:S(2)}) async-start(f32[32,3,16]{2,1,0:T(4,128)} %broadcast_in_dim.104), calls=%async_computation.3 | async-start | bytes 131072 | tf_op jit(solution)/shard_map/all_to_all | solution.py:14
  134.2 18.4 %all-to-all-start.4 = ((f32[4,16,1024]{2,1,0:T(8,128)}), f32[4,16,1024]{2,1,0:T(8,128)S(1)}, u32[]{:S(2)}, u32[]{:S(2)}) async-start(f32[4,16,1024]{2,1,0:T(8,128)} %broadcast_in_dim.105), calls=%async_computation.4 | async-start | bytes 524288 | tf_op jit(solution)/shard_map/all_to_all | solution.py:14
  152.6 20.9 %collective-permute-start.10 = (f32[64,1024]{1,0:T(8,128)S(1)}, f32[64,1024]{1,0:T(8,128)S(1)}, u32[]{:S(2)}, u32[]{:S(2)}) collective-permute-start(f32[64,1024]{1,0:T(8,128)S(1)} %bitcast.49), channel_id=1, source_target_pairs={{0,8},{8,16},{16,24},{24,32},{32,40},{40,48},{48,56},{56,64},{64,7... | collective-permute-start | bytes 786440 | tf_op jit(solution)/shard_map/ppermute | solution.py:22
  154.5 15.3 %collective-permute-start.7 = (f32[64,1024]{1,0:T(8,128)S(1)}, f32[64,1024]{1,0:T(8,128)S(1)}, u32[]{:S(2)}, u32[]{:S(2)}) collective-permute-start(f32[64,1024]{1,0:T(8,128)S(1)} %bitcast.50), channel_id=1, source_target_pairs={{0,120},{8,0},{16,8},{24,16},{32,24},{40,32},{48,40},{56,48},{64,5... | collective-permute-start | bytes 786440 | tf_op jit(solution)/shard_map/ppermute | solution.py:22
  162.4 9.2 %collective-permute-start.8 = (f32[32,1024]{1,0:T(8,128)S(1)}, f32[32,1024]{1,0:T(8,128)S(1)}, u32[]{:S(2)}, u32[]{:S(2)}) collective-permute-start(f32[32,1024]{1,0:T(8,128)S(1)} %bitcast.63), channel_id=1, source_target_pairs={{0,16},{8,24},{16,32},{24,40},{32,48},{40,56},{48,64},{56,72},{64,... | collective-permute-start | bytes 393224 | tf_op jit(solution)/shard_map/ppermute | solution.py:22
  164.3 9.1 %collective-permute-start.9 = (f32[32,1024]{1,0:T(8,128)S(1)}, f32[32,1024]{1,0:T(8,128)S(1)}, u32[]{:S(2)}, u32[]{:S(2)}) collective-permute-start(f32[32,1024]{1,0:T(8,128)S(1)} %bitcast.62), channel_id=1, source_target_pairs={{0,112},{8,120},{16,0},{24,8},{32,16},{40,24},{48,32},{56,40},{64,... | collective-permute-start | bytes 393224 | tf_op jit(solution)/shard_map/ppermute | solution.py:22
  178.1 22.0 %all-to-all-start.5 = ((f32[32,16,384]{2,1,0:T(8,128)}), f32[32,16,384]{2,1,0:T(8,128)S(1)}, u32[]{:S(2)}, u32[]{:S(2)}) async-start(f32[32,16,384]{2,1,0:T(8,128)} %bitcast.17), calls=%async_computation.5 | async-start | bytes 1572864 | tf_op jit(solution)/shard_map/all_to_all | solution.py:14
  188.7 36.6 %collective-permute-start.13 = (f32[96,1024]{1,0:T(8,128)}, f32[96,1024]{1,0:T(8,128)S(1)}, u32[]{:S(2)}, u32[]{:S(2)}) collective-permute-start(f32[96,1024]{1,0:T(8,128)} %get-tuple-element.10), channel_id=1, source_target_pairs={{0,128},{128,256},{256,384},{384,0},{1,129},{129,257},{257,385},{3... | collective-permute-start | bytes 1179656 | tf_op jit(solution)/shard_map/ppermute | solution.py:26
  192.1 22.7 %collective-permute-start.12 = (f32[96,1024]{1,0:T(8,128)}, f32[96,1024]{1,0:T(8,128)S(1)}, u32[]{:S(2)}, u32[]{:S(2)}) collective-permute-start(f32[96,1024]{1,0:T(8,128)} %get-tuple-element.11), channel_id=1, source_target_pairs={{0,256},{128,384},{256,0},{384,128},{1,257},{129,385},{257,1},{385... | collective-permute-start | bytes 1179656 | tf_op jit(solution)/shard_map/ppermute | solution.py:26
  196.5 16.7 %collective-permute-start.11 = (f32[96,1024]{1,0:T(8,128)}, f32[96,1024]{1,0:T(8,128)}, u32[]{:S(2)}, u32[]{:S(2)}) collective-permute-start(f32[96,1024]{1,0:T(8,128)} %get-tuple-element.12), channel_id=1, source_target_pairs={{0,384},{128,0},{256,128},{384,256},{1,385},{129,1},{257,129},{385... | collective-permute-start | bytes 1179656 | tf_op jit(solution)/shard_map/ppermute | solution.py:26
  201.2 16.8 %all-to-all-start.6 = ((f32[16,1,512]{2,1,0:T(1,128)}), f32[16,1,512]{2,1,0:T(1,128)S(1)}, u32[]{:S(2)}, u32[]{:S(2)}) async-start(f32[16,1,512]{2,1,0:T(1,128)} %broadcast_in_dim.107), calls=%async_computation.6 | async-start | bytes 65536 | tf_op jit(solution)/shard_map/all_to_all | solution.py:14
  219.1 12.2 %all-to-all-start.7 = ((f32[8,1,6144]{2,1,0:T(1,128)}), f32[8,1,6144]{2,1,0:T(1,128)S(1)}, u32[]{:S(2)}, u32[]{:S(2)}) async-start(f32[8,1,6144]{2,1,0:T(1,128)} %broadcast_in_dim.109), calls=%async_computation.7 | async-start | bytes 393216 | tf_op jit(solution)/shard_map/all_to_all | solution.py:14
  225.4 6.6 %copy-start.1 = (f32[96,4096]{1,0:T(8,128)}, f32[96,4096]{1,0:T(8,128)S(1)}, u32[]{:S(2)}) copy-start(f32[96,4096]{1,0:T(8,128)S(1)} %constant_dynamic-update-slice_fusion.5) | copy-start | bytes 4718596

commit v3 on v2

--- a/solution.py
+++ b/solution.py
@@ -20,6 +20,11 @@
 
 def shift_z(block, step):
     return lax.ppermute(block, Z, [(i, (i + step) % 16) for i in range(16)])
+
+
+def shift_far(block):
+    pairs = [(2 * i + c, 2 * ((i + 2 - 4 * c) % 16) + c) for i in range(16) for c in range(2)]
+    return lax.ppermute(block, ("h", "l", "c"), pairs)
 
 
 def shift_x(block, step):
@@ -58,6 +63,7 @@
     packed = jnp.concatenate([row, jnp.broadcast_to(notes[None], (16, META))], axis=1)
     mine = swap(packed[:, None, :], Z).reshape(16, wide + META)
     turned = jnp.stack([jnp.concatenate([turn(mine[:, :wide], i), mine[:, wide:]], axis=1) for i in range(4)])
+    turned, *heads = lax.optimization_barrier((turned, *heads))
     copies = jnp.broadcast_to(turned[:, None], (4, 8, 16, wide + META)).reshape(32, 16, wide + META)
     slots = swap(copies, XYC).reshape(512, wide + META)
 
@@ -82,9 +88,7 @@
     partial = dot(hidden, head)
     up = shift_z(partial[64:128], 1)
     down = shift_z(partial[192:256], -1)
-    up2 = shift_z(partial[128:160], 2)
-    down2 = shift_z(partial[160:192], -2)
-    block = partial[:64] + up + down + jnp.concatenate([up2, down2], axis=0)
+    block = partial[:64] + up + down + shift_far(partial[128:192])
     logits = jnp.sum(swap(block.reshape(4, 16, quarter), "h"), axis=0)
 
     row_labels = lax.dynamic_slice(labels, (h * 16,), (16,))
@@ -103,9 +107,7 @@
     own = spread(grad, "h", 4).reshape(64, quarter)
     after = shift_z(own, -1)
     ahead = shift_z(own, 1)
-    far = shift_z(own[:32], 2)
-    far2 = shift_z(own[32:], -2)
-    grads = jnp.concatenate([own, after, far, far2, ahead], axis=0)
+    grads = jnp.concatenate([own, after, shift_far(own), ahead], axis=0)
 
     grad_head = dot(hidden, grads, (0, 0)).reshape(4, depth, quarter)
     grad_weight = jnp.zeros((depth, columns), jnp.float32)

time: 233 us -> 235 us (level)
  waiting for transfers between devices: 79.2 us -> 91.1 us
  blocking collectives: 27 us -> 17.4 us
    ppermute x8 -> x4, starting transfers between devices: 31 us -> 18.5 us  [shift_z(): return lax.ppermute(block, Z, [(i, (i + step) % 16) for i in range(16)])]
    all_to_all x1, blocking collectives: 27 us -> 17.4 us  [swap(): return lax.all_to_all(blocks, axes, split_axis=0, concat_axis=0, tiled=True)]
    ppermute x0 -> x2, waiting for transfers between devices: none -> 8.3 us  [shift_far(): return lax.ppermute(block, ('h', 'l', 'c'), pairs)]
    all_to_all x7, starting transfers between devices: 46.4 us -> 53.1 us  [swap(): return lax.all_to_all(blocks, axes, split_axis=0, concat_axis=0, tiled=True)]
    ppermute x0 -> x2, starting transfers between devices: none -> 6.23 us  [shift_far(): return lax.ppermute(block, ('h', 'l', 'c'), pairs)]
    ppermute x8 -> x4, waiting for transfers between devices: 7.74 us -> 10.4 us  [shift_z(): return lax.ppermute(block, Z, [(i, (i + step) % 16) for i in range(16)])]
    ppermute x6, waiting for transfers between devices: 20.5 us -> 22.9 us  [shift_x(): return lax.ppermute(block, 'x', [(i, (i + step) % 4) for i in range(4)])]
  transfers between devices with their start and end apart: 21 -> 19, of which waited for: 15 -> 17; matrix products, arithmetic and copies ran while one was open for 4% -> 4% of each run, Pallas kernels for 0% -> 0%
where the time goes in v3:
time: 235 us; the launch traced here: 234 us
  starting transfers between devices  98.6 us (42%)
  waiting for transfers between devices  91.1 us (39%)
  blocking collectives  17.4 us (7%)
  local copies, waits for them, and re-layouts  12.9 us (5%)
  matrix products  7.34 us (3%)
  other arithmetic  3.83 us (2%)
  between operations  2.5 us (1%)
    all_to_all x7, starting transfers between devices, swap(): return lax.all_to_all(blocks, axes, split_axis=0, concat_axis=0, tiled=True)  53.1 us
    all_to_all x7, waiting for transfers between devices, swap(): return lax.all_to_all(blocks, axes, split_axis=0, concat_axis=0, tiled=True)  49.5 us
    ppermute x6, waiting for transfers between devices, shift_x(): return lax.ppermute(block, 'x', [(i, (i + step) % 4) for i in range(4)])  22.9 us
    ppermute x6, starting transfers between devices, shift_x(): return lax.ppermute(block, 'x', [(i, (i + step) % 4) for i in range(4)])  20.7 us
    ppermute x4, starting transfers between devices, shift_z(): return lax.ppermute(block, Z, [(i, (i + step) % 16) for i in range(16)])  18.5 us
    all_to_all x1, blocking collectives, swap(): return lax.all_to_all(blocks, axes, split_axis=0, concat_axis=0, tiled=True)  17.4 us
    ppermute x4, waiting for transfers between devices, shift_z(): return lax.ppermute(block, Z, [(i, (i + step) % 16) for i in range(16)])  10.4 us
    ppermute x2, waiting for transfers between devices, shift_far(): return lax.ppermute(block, ('h', 'l', 'c'), pairs)  8.3 us
  transfers between devices with their start and end apart: 19, of which 17 were waited for; matrix products, arithmetic and copies ran while one was open for 4% of the time, Pallas kernels for 0%

profile of v3, /device:TPU:1, one launch (start us, length us, event | category | flops | bytes accessed | tf_op | source)
XLA Modules:
  0.0 233.6 jit_solution(15310511278315091983)
XLA Ops:
  4.9 15.7 %all-to-all-start = ((f32[16,1,512]{2,1,0:T(1,128)}), f32[16,1,512]{2,1,0:T(1,128)S(1)}, u32[]{:S(2)}, u32[]{:S(2)}) async-start(f32[16,1,512]{2,1,0:T(1,128)} %copy.22), calls=%async_computation | async-start | bytes 65536 | tf_op jit(solution)/shard_map/all_to_all | solution.py:14
  22.2 4.4 %collective-permute-start.2 = (f32[96,1024]{1,0:T(8,128)S(1)}, f32[96,1024]{1,0:T(8,128)S(1)}, u32[]{:S(2)}, u32[]{:S(2)}) collective-permute-start(f32[96,1024]{1,0:T(8,128)S(1)} %get-tuple-element.24), channel_id=1, source_target_pairs={{0,384},{128,0},{256,128},{384,256},{1,385},{129,1},{257,129},{385... | collective-permute-start | bytes 1179656 | tf_op jit(solution)/shard_map/ppermute | solution.py:31
  26.5 1.9 collective-permute-start
  28.5 3.6 %collective-permute-start.1 = (f32[96,1024]{1,0:T(8,128)S(1)}, f32[96,1024]{1,0:T(8,128)S(1)}, u32[]{:S(2)}, u32[]{:S(2)}) collective-permute-start(f32[96,1024]{1,0:T(8,128)S(1)} %get-tuple-element.27), channel_id=1, source_target_pairs={{0,256},{128,384},{256,0},{384,128},{1,257},{129,385},{257,1},{385... | collective-permute-start | bytes 1179656 | tf_op jit(solution)/shard_map/ppermute | solution.py:31
  34.0 6.0 %collective-permute-done = f32[96,1024]{1,0:T(8,128)S(1)} collective-permute-done((f32[96,1024]{1,0:T(8,128)S(1)}, f32[96,1024]{1,0:T(8,128)S(1)}, u32[]{:S(2)}, u32[]{:S(2)}) %collective-permute-start) | collective-permute-done | bytes 393248 | tf_op jit(solution)/shard_map/ppermute | solution.py:31
  40.0 6.6 %collective-permute-done.1 = f32[96,1024]{1,0:T(8,128)S(1)} collective-permute-done((f32[96,1024]{1,0:T(8,128)S(1)}, f32[96,1024]{1,0:T(8,128)S(1)}, u32[]{:S(2)}, u32[]{:S(2)}) %collective-permute-start.1) | collective-permute-done | bytes 393248 | tf_op jit(solution)/shard_map/ppermute | solution.py:31
  47.7 7.8 %all-to-all-start.1 = ((f32[32,16,512]{2,1,0:T(8,128)}), f32[32,16,512]{2,1,0:T(8,128)S(1)}, u32[]{:S(2)}, u32[]{:S(2)}) async-start(f32[32,16,512]{2,1,0:T(8,128)} %bitcast.6), calls=%async_computation.1 | async-start | bytes 2097152 | tf_op jit(solution)/shard_map/all_to_all | solution.py:14
  56.7 15.6 %all-to-all-done.1 = f32[32,16,512]{2,1,0:T(8,128)S(1)} async-done(((f32[32,16,512]{2,1,0:T(8,128)}), f32[32,16,512]{2,1,0:T(8,128)S(1)}, u32[]{:S(2)}, u32[]{:S(2)}) %all-to-all-start.1) | async-done | bytes 1048608 | tf_op jit(solution)/shard_map/all_to_all | solution.py:14
  75.9 3.2 %collective-permute-start.3 = (f32[64,1024]{1,0:T(8,128)S(1)}, f32[64,1024]{1,0:T(8,128)S(1)}, u32[]{:S(2)}, u32[]{:S(2)}) collective-permute-start(f32[64,1024]{1,0:T(8,128)S(1)} %get-tuple-element.28), channel_id=1, source_target_pairs={{0,8},{8,16},{16,24},{24,32},{32,40},{40,48},{48,56},{56,64},{64,7... | collective-permute-start | bytes 786440 | tf_op jit(solution)/shard_map/ppermute | solution.py:22
  79.1 4.3 %collective-permute-start.5 = (f32[64,1024]{1,0:T(8,128)S(1)}, f32[64,1024]{1,0:T(8,128)S(1)}, u32[]{:S(2)}, u32[]{:S(2)}) collective-permute-start(f32[64,1024]{1,0:T(8,128)S(1)} %get-tuple-element.29), channel_id=1, source_target_pairs={{0,16},{1,113},{8,24},{9,121},{16,32},{17,1},{24,40},{25,9},{32,48... | collective-permute-start | bytes 786440 | tf_op jit(solution)/shard_map/ppermute | solution.py:27
  83.4 3.1 %collective-permute-start.4 = (f32[64,1024]{1,0:T(8,128)S(1)}, f32[64,1024]{1,0:T(8,128)S(1)}, u32[]{:S(2)}, u32[]{:S(2)}) collective-permute-start(f32[64,1024]{1,0:T(8,128)S(1)} %get-tuple-element.30), channel_id=1, source_target_pairs={{0,120},{8,0},{16,8},{24,16},{32,24},{40,32},{48,40},{56,48},{64,5... | collective-permute-start | bytes 786440 | tf_op jit(solution)/shard_map/ppermute | solution.py:22
  86.7 2.2 collective-permute-done.5
  89.0 6.6 %collective-permute-done.4 = f32[64,1024]{1,0:T(8,128)S(1)} collective-permute-done((f32[64,1024]{1,0:T(8,128)S(1)}, f32[64,1024]{1,0:T(8,128)S(1)}, u32[]{:S(2)}, u32[]{:S(2)}) %collective-permute-start.4) | collective-permute-done | bytes 262176 | tf_op jit(solution)/shard_map/ppermute | solution.py:22
  96.3 11.3 %all-to-all-start.2 = ((f32[4,16,1024]{2,1,0:T(8,128)}), f32[4,16,1024]{2,1,0:T(8,128)S(1)}, u32[]{:S(2)}, u32[]{:S(2)}) async-start(f32[4,16,1024]{2,1,0:T(8,128)} %bitcast.8), calls=%async_computation.2 | async-start | bytes 524288 | tf_op jit(solution)/shard_map/all_to_all | solution.py:14
  107.9 19.6 %all-to-all-done.2 = f32[4,16,1024]{2,1,0:T(8,128)S(1)} async-done(((f32[4,16,1024]{2,1,0:T(8,128)}), f32[4,16,1024]{2,1,0:T(8,128)S(1)}, u32[]{:S(2)}, u32[]{:S(2)}) %all-to-all-start.2) | async-done | bytes 262176 | tf_op jit(solution)/shard_map/all_to_all | solution.py:14
  128.4 3.6 %all-to-all-start.3 = ((f32[32,3,16]{2,1,0:T(4,128)}), f32[32,3,16]{2,1,0:T(4,128)S(1)}, u32[]{:S(2)}, u32[]{:S(2)}) async-start(f32[32,3,16]{2,1,0:T(4,128)} %broadcast_in_dim.104), calls=%async_computation.3 | async-start | bytes 131072 | tf_op jit(solution)/shard_map/all_to_all | solution.py:14
  132.1 7.3 %all-to-all-done.3 = f32[32,3,16]{2,1,0:T(4,128)S(1)} async-done(((f32[32,3,16]{2,1,0:T(4,128)}), f32[32,3,16]{2,1,0:T(4,128)S(1)}, u32[]{:S(2)}, u32[]{:S(2)}) %all-to-all-start.3) | async-done | bytes 6176 | tf_op jit(solution)/shard_map/all_to_all | solution.py:14
  139.6 17.4 %all_to_all.44 = f32[4,16,1024]{2,1,0:T(8,128)S(1)} all-to-all(f32[4,16,1024]{2,1,0:T(8,128)S(1)} %broadcast_in_dim.105), channel_id=1, replica_groups=mesh['x'=4,'h'=4,'l'=4,'y'=4,'c'=2] {'h'}, dimensions={0} | all-to-all | bytes 524288 | tf_op jit(solution)/shard_map/all_to_all | solution.py:14
  157.1 9.9 %collective-permute-start.8 = (f32[64,1024]{1,0:T(8,128)S(1)}, f32[64,1024]{1,0:T(8,128)S(1)}, u32[]{:S(2)}, u32[]{:S(2)}) collective-permute-start(f32[64,1024]{1,0:T(8,128)S(1)} %bitcast.47), channel_id=1, source_target_pairs={{0,8},{8,16},{16,24},{24,32},{32,40},{40,48},{48,56},{56,64},{64,7... | collective-permute-start | bytes 786440 | tf_op jit(solution)/shard_map/ppermute | solution.py:22
  167.0 1.9 collective-permute-start.7
  168.9 2.3 collective-permute-start.6
  171.8 6.1 %collective-permute-done.7 = f32[64,1024]{1,0:T(8,128)S(1)} collective-permute-done((f32[64,1024]{1,0:T(8,128)S(1)}, f32[64,1024]{1,0:T(8,128)S(1)}, u32[]{:S(2)}, u32[]{:S(2)}) %collective-permute-start.7) | collective-permute-done | bytes 262176 | tf_op jit(solution)/shard_map/ppermute | solution.py:27
  177.9 3.3 %collective-permute-done.6 = f32[64,1024]{1,0:T(8,128)S(1)} collective-permute-done((f32[64,1024]{1,0:T(8,128)S(1)}, f32[64,1024]{1,0:T(8,128)S(1)}, u32[]{:S(2)}, u32[]{:S(2)}) %collective-permute-start.6) | collective-permute-done | bytes 262176 | tf_op jit(solution)/shard_map/ppermute | solution.py:22
  181.2 1.9 fusion.3
  184.6 4.7 %all-to-all-start.5 = ((f32[32,16,384]{2,1,0:T(8,128)}), f32[32,16,384]{2,1,0:T(8,128)S(1)}, u32[]{:S(2)}, u32[]{:S(2)}) async-start(f32[32,16,384]{2,1,0:T(8,128)} %bitcast.15), calls=%async_computation.5 | async-start | bytes 1572864 | tf_op jit(solution)/shard_map/all_to_all | solution.py:14
  192.4 3.3 %collective-permute-start.11 = (f32[96,1024]{1,0:T(8,128)}, f32[96,1024]{1,0:T(8,128)S(1)}, u32[]{:S(2)}, u32[]{:S(2)}) collective-permute-start(f32[96,1024]{1,0:T(8,128)} %get-tuple-element.20), channel_id=1, source_target_pairs={{0,128},{128,256},{256,384},{384,0},{1,129},{129,257},{257,385},{3... | collective-permute-start | bytes 1179656 | tf_op jit(solution)/shard_map/ppermute | solution.py:31
  195.7 4.4 %collective-permute-start.10 = (f32[96,1024]{1,0:T(8,128)}, f32[96,1024]{1,0:T(8,128)S(1)}, u32[]{:S(2)}, u32[]{:S(2)}) collective-permute-start(f32[96,1024]{1,0:T(8,128)} %get-tuple-element.21), channel_id=1, source_target_pairs={{0,256},{128,384},{256,0},{384,128},{1,257},{129,385},{257,1},{385... | collective-permute-start | bytes 1179656 | tf_op jit(solution)/shard_map/ppermute | solution.py:31
  200.2 3.0 %collective-permute-start.9 = (f32[96,1024]{1,0:T(8,128)}, f32[96,1024]{1,0:T(8,128)}, u32[]{:S(2)}, u32[]{:S(2)}) collective-permute-start(f32[96,1024]{1,0:T(8,128)} %get-tuple-element.22), channel_id=1, source_target_pairs={{0,384},{128,0},{256,128},{384,256},{1,385},{129,1},{257,129},{385... | collective-permute-start | bytes 1179656 | tf_op jit(solution)/shard_map/ppermute | solution.py:31
  204.9 3.5 %all-to-all-start.6 = ((f32[16,1,512]{2,1,0:T(1,128)}), f32[16,1,512]{2,1,0:T(1,128)S(1)}, u32[]{:S(2)}, u32[]{:S(2)}) async-start(f32[16,1,512]{2,1,0:T(1,128)} %broadcast_in_dim.107), calls=%async_computation.6 | async-start | bytes 65536 | tf_op jit(solution)/shard_map/all_to_all | solution.py:14
  208.4 8.5 %collective-permute-done.9 = f32[96,1024]{1,0:T(8,128)} collective-permute-done((f32[96,1024]{1,0:T(8,128)}, f32[96,1024]{1,0:T(8,128)}, u32[]{:S(2)}, u32[]{:S(2)}) %collective-permute-start.9) | collective-permute-done | bytes 393248 | tf_op jit(solution)/shard_map/ppermute | solution.py:31
  220.6 6.4 %all-to-all-start.7 = ((f32[8,1,6144]{2,1,0:T(1,128)}), f32[8,1,6144]{2,1,0:T(1,128)S(1)}, u32[]{:S(2)}, u32[]{:S(2)}) async-start(f32[8,1,6144]{2,1,0:T(1,128)} %broadcast_in_dim.109), calls=%async_computation.7 | async-start | bytes 393216 | tf_op jit(solution)/shard_map/all_to_all | solution.py:14
  227.6 5.3 %all-to-all-done.7 = f32[8,1,6144]{2,1,0:T(1,128)S(1)} async-done(((f32[8,1,6144]{2,1,0:T(1,128)}), f32[8,1,6144]{2,1,0:T(1,128)S(1)}, u32[]{:S(2)}, u32[]{:S(2)}) %all-to-all-start.7) | async-done | bytes 196640 | tf_op jit(solution)/shard_map/all_to_all | solution.py:14
  (103 shorter events, 26.2 us)
Async XLA Ops:
  0.6 3.3 %copy-start = (f32[8,6144]{1,0:T(8,128)S(1)}, f32[8,6144]{1,0:T(8,128)}, u32[]{:S(2)}) copy-start(f32[8,6144]{1,0:T(8,128)} %param.5) | copy-start | bytes 589828
  4.9 27.2 %all-to-all-start = ((f32[16,1,512]{2,1,0:T(1,128)}), f32[16,1,512]{2,1,0:T(1,128)S(1)}, u32[]{:S(2)}, u32[]{:S(2)}) async-start(f32[16,1,512]{2,1,0:T(1,128)} %copy.22), calls=%async_computation | async-start | bytes 65536 | tf_op jit(solution)/shard_map/all_to_all | solution.py:14
  22.2 11.8 %collective-permute-start.2 = (f32[96,1024]{1,0:T(8,128)S(1)}, f32[96,1024]{1,0:T(8,128)S(1)}, u32[]{:S(2)}, u32[]{:S(2)}) collective-permute-start(f32[96,1024]{1,0:T(8,128)S(1)} %get-tuple-element.24), channel_id=1, source_target_pairs={{0,384},{128,0},{256,128},{384,256},{1,385},{129,1},{257,129},{385... | collective-permute-start | bytes 1179656 | tf_op jit(solution)/shard_map/ppermute | solution.py:31
  26.5 13.4 %collective-permute-start = (f32[96,1024]{1,0:T(8,128)S(1)}, f32[96,1024]{1,0:T(8,128)S(1)}, u32[]{:S(2)}, u32[]{:S(2)}) collective-permute-start(f32[96,1024]{1,0:T(8,128)S(1)} %get-tuple-element.25), channel_id=1, source_target_pairs={{0,128},{128,256},{256,384},{384,0},{1,129},{129,257},{257,385},{3... | collective-permute-start | bytes 1179656 | tf_op jit(solution)/shard_map/ppermute | solution.py:31
  28.5 18.1 %collective-permute-start.1 = (f32[96,1024]{1,0:T(8,128)S(1)}, f32[96,1024]{1,0:T(8,128)S(1)}, u32[]{:S(2)}, u32[]{:S(2)}) collective-permute-start(f32[96,1024]{1,0:T(8,128)S(1)} %get-tuple-element.27), channel_id=1, source_target_pairs={{0,256},{128,384},{256,0},{384,128},{1,257},{129,385},{257,1},{385... | collective-permute-start | bytes 1179656 | tf_op jit(solution)/shard_map/ppermute | solution.py:31
  34.0 13.7 %copy-start.4 = (f32[96,1024]{1,0:T(8,128)}, f32[96,1024]{1,0:T(8,128)S(1)}, u32[]{:S(2)}) copy-start(f32[96,1024]{1,0:T(8,128)S(1)} %collective-permute-done.2) | copy-start | bytes 1179652
  40.0 15.5 %copy-start.6 = (f32[96,1024]{1,0:T(8,128)}, f32[96,1024]{1,0:T(8,128)S(1)}, u32[]{:S(2)}) copy-start(f32[96,1024]{1,0:T(8,128)S(1)} %collective-permute-done) | copy-start | bytes 1179652
  46.5 1.1 copy-start.7
  47.7 24.7 %all-to-all-start.1 = ((f32[32,16,512]{2,1,0:T(8,128)}), f32[32,16,512]{2,1,0:T(8,128)S(1)}, u32[]{:S(2)}, u32[]{:S(2)}) async-start(f32[32,16,512]{2,1,0:T(8,128)} %bitcast.6), calls=%async_computation.1 | async-start | bytes 2097152 | tf_op jit(solution)/shard_map/all_to_all | solution.py:14
  55.5 1.2 copy-start.8
  55.5 1.2 copy-start.5
  75.9 10.9 %collective-permute-start.3 = (f32[64,1024]{1,0:T(8,128)S(1)}, f32[64,1024]{1,0:T(8,128)S(1)}, u32[]{:S(2)}, u32[]{:S(2)}) collective-permute-start(f32[64,1024]{1,0:T(8,128)S(1)} %get-tuple-element.28), channel_id=1, source_target_pairs={{0,8},{8,16},{16,24},{24,32},{32,40},{40,48},{48,56},{56,64},{64,7... | collective-permute-start | bytes 786440 | tf_op jit(solution)/shard_map/ppermute | solution.py:22
  79.1 9.9 %collective-permute-start.5 = (f32[64,1024]{1,0:T(8,128)S(1)}, f32[64,1024]{1,0:T(8,128)S(1)}, u32[]{:S(2)}, u32[]{:S(2)}) collective-permute-start(f32[64,1024]{1,0:T(8,128)S(1)} %get-tuple-element.29), channel_id=1, source_target_pairs={{0,16},{1,113},{8,24},{9,121},{16,32},{17,1},{24,40},{25,9},{32,48... | collective-permute-start | bytes 786440 | tf_op jit(solution)/shard_map/ppermute | solution.py:27
  83.4 12.2 %collective-permute-start.4 = (f32[64,1024]{1,0:T(8,128)S(1)}, f32[64,1024]{1,0:T(8,128)S(1)}, u32[]{:S(2)}, u32[]{:S(2)}) collective-permute-start(f32[64,1024]{1,0:T(8,128)S(1)} %get-tuple-element.30), channel_id=1, source_target_pairs={{0,120},{8,0},{16,8},{24,16},{32,24},{40,32},{48,40},{56,48},{64,5... | collective-permute-start | bytes 786440 | tf_op jit(solution)/shard_map/ppermute | solution.py:22
  96.3 31.1 %all-to-all-start.2 = ((f32[4,16,1024]{2,1,0:T(8,128)}), f32[4,16,1024]{2,1,0:T(8,128)S(1)}, u32[]{:S(2)}, u32[]{:S(2)}) async-start(f32[4,16,1024]{2,1,0:T(8,128)} %bitcast.8), calls=%async_computation.2 | async-start | bytes 524288 | tf_op jit(solution)/shard_map/all_to_all | solution.py:14
  128.4 11.0 %all-to-all-start.3 = ((f32[32,3,16]{2,1,0:T(4,128)}), f32[32,3,16]{2,1,0:T(4,128)S(1)}, u32[]{:S(2)}, u32[]{:S(2)}) async-start(f32[32,3,16]{2,1,0:T(4,128)} %broadcast_in_dim.104), calls=%async_computation.3 | async-start | bytes 131072 | tf_op jit(solution)/shard_map/all_to_all | solution.py:14
  157.1 14.7 %collective-permute-start.8 = (f32[64,1024]{1,0:T(8,128)S(1)}, f32[64,1024]{1,0:T(8,128)S(1)}, u32[]{:S(2)}, u32[]{:S(2)}) collective-permute-start(f32[64,1024]{1,0:T(8,128)S(1)} %bitcast.47), channel_id=1, source_target_pairs={{0,8},{8,16},{16,24},{24,32},{32,40},{40,48},{48,56},{56,64},{64,7... | collective-permute-start | bytes 786440 | tf_op jit(solution)/shard_map/ppermute | solution.py:22
  167.0 10.9 %collective-permute-start.7 = (f32[64,1024]{1,0:T(8,128)S(1)}, f32[64,1024]{1,0:T(8,128)S(1)}, u32[]{:S(2)}, u32[]{:S(2)}) collective-permute-start(f32[64,1024]{1,0:T(8,128)S(1)} %bitcast.48), channel_id=1, source_target_pairs={{0,16},{1,113},{8,24},{9,121},{16,32},{17,1},{24,40},{25,9},{32,48... | collective-permute-start | bytes 786440 | tf_op jit(solution)/shard_map/ppermute | solution.py:27
  168.9 12.3 %collective-permute-start.6 = (f32[64,1024]{1,0:T(8,128)S(1)}, f32[64,1024]{1,0:T(8,128)S(1)}, u32[]{:S(2)}, u32[]{:S(2)}) collective-permute-start(f32[64,1024]{1,0:T(8,128)S(1)} %bitcast.49), channel_id=1, source_target_pairs={{0,120},{8,0},{16,8},{24,16},{32,24},{40,32},{48,40},{56,48},{64,5... | collective-permute-start | bytes 786440 | tf_op jit(solution)/shard_map/ppermute | solution.py:22
  181.2 3.4 %copy-start.2 = (f32[64,1024]{1,0:T(8,128)}, f32[64,1024]{1,0:T(8,128)S(1)}, u32[]{:S(2)}) copy-start(f32[64,1024]{1,0:T(8,128)S(1)} %collective-permute-done.6) | copy-start | bytes 786436
  184.6 5.2 %copy-start.3 = (f32[64,1024]{1,0:T(8,128)S(1)}, f32[64,1024]{1,0:T(8,128)}, u32[]{:S(2)}) copy-start(f32[64,1024]{1,0:T(8,128)} %copy-done.2) | copy-start | bytes 786436
  184.6 19.2 %all-to-all-start.5 = ((f32[32,16,384]{2,1,0:T(8,128)}), f32[32,16,384]{2,1,0:T(8,128)S(1)}, u32[]{:S(2)}, u32[]{:S(2)}) async-start(f32[32,16,384]{2,1,0:T(8,128)} %bitcast.15), calls=%async_computation.5 | async-start | bytes 1572864 | tf_op jit(solution)/shard_map/all_to_all | solution.py:14
  192.4 34.6 %collective-permute-start.11 = (f32[96,1024]{1,0:T(8,128)}, f32[96,1024]{1,0:T(8,128)S(1)}, u32[]{:S(2)}, u32[]{:S(2)}) collective-permute-start(f32[96,1024]{1,0:T(8,128)} %get-tuple-element.20), channel_id=1, source_target_pairs={{0,128},{128,256},{256,384},{384,0},{1,129},{129,257},{257,385},{3... | collective-permute-start | bytes 1179656 | tf_op jit(solution)/shard_map/ppermute | solution.py:31
  195.7 22.7 %collective-permute-start.10 = (f32[96,1024]{1,0:T(8,128)}, f32[96,1024]{1,0:T(8,128)S(1)}, u32[]{:S(2)}, u32[]{:S(2)}) collective-permute-start(f32[96,1024]{1,0:T(8,128)} %get-tuple-element.21), channel_id=1, source_target_pairs={{0,256},{128,384},{256,0},{384,128},{1,257},{129,385},{257,1},{385... | collective-permute-start | bytes 1179656 | tf_op jit(solution)/shard_map/ppermute | solution.py:31
  200.2 16.7 %collective-permute-start.9 = (f32[96,1024]{1,0:T(8,128)}, f32[96,1024]{1,0:T(8,128)}, u32[]{:S(2)}, u32[]{:S(2)}) collective-permute-start(f32[96,1024]{1,0:T(8,128)} %get-tuple-element.22), channel_id=1, source_target_pairs={{0,384},{128,0},{256,128},{384,256},{1,385},{129,1},{257,129},{385... | collective-permute-start | bytes 1179656 | tf_op jit(solution)/shard_map/ppermute | solution.py:31
  204.9 14.7 %all-to-all-start.6 = ((f32[16,1,512]{2,1,0:T(1,128)}), f32[16,1,512]{2,1,0:T(1,128)S(1)}, u32[]{:S(2)}, u32[]{:S(2)}) async-start(f32[16,1,512]{2,1,0:T(1,128)} %broadcast_in_dim.107), calls=%async_computation.6 | async-start | bytes 65536 | tf_op jit(solution)/shard_map/all_to_all | solution.py:14
  220.6 12.3 %all-to-all-start.7 = ((f32[8,1,6144]{2,1,0:T(1,128)}), f32[8,1,6144]{2,1,0:T(1,128)S(1)}, u32[]{:S(2)}, u32[]{:S(2)}) async-start(f32[8,1,6144]{2,1,0:T(1,128)} %broadcast_in_dim.109), calls=%async_computation.7 | async-start | bytes 393216 | tf_op jit(solution)/shard_map/all_to_all | solution.py:14
  227.0 6.6 %copy-start.1 = (f32[96,4096]{1,0:T(8,128)}, f32[96,4096]{1,0:T(8,128)S(1)}, u32[]{:S(2)}) copy-start(f32[96,4096]{1,0:T(8,128)S(1)} %constant_dynamic-update-slice_fusion.4) | copy-start | bytes 4718596

commit v4 on v1

v4 whole, which is shorter than its diff:
```python
import jax
import jax.numpy as jnp
from jax import lax
from jax.sharding import Mesh, PartitionSpec as P

HIGH = lax.Precision.HIGHEST
Z = ("h", "l")
XYC = ("x", "y", "c")
LYC = ("l", "y", "c")
YC = ("y", "c")
META = 128


def swap(blocks, axes):
    return lax.all_to_all(blocks, axes, split_axis=0, concat_axis=0, tiled=True)


def spread(block, axes, count):
    return swap(jnp.broadcast_to(block[None], (count, *block.shape)), axes)


def shift_z(block, step):
    return lax.ppermute(block, Z, [(i, (i + step) % 16) for i in range(16)])


def shift_far(block, sign):
    step = [2 * sign, -2 * sign]
    pairs = [(2 * i + c, 2 * ((i + step[c]) % 16) + c) for i in range(16) for c in range(2)]
    return lax.ppermute(block, ("h", "l", "c"), pairs)


def dot(a, b, contract=(1, 0)):
    dims = (((contract[0],), (contract[1],)), ((), ()))
    return lax.dot_general(a, b, dims, precision=HIGH, preferred_element_type=jnp.float32)


def on_device(responses, weight, lengths, targets, owners):
    width = responses.shape[1]
    depth, columns = weight.shape
    quarter = columns // 4
    wide = 4 * depth
    x, h, l = lax.axis_index("x"), lax.axis_index("h"), lax.axis_index("l")
    j = lax.axis_index(YC)

    def cut(s):
        return lax.dynamic_slice(weight, (0, (l + s) % 4 * quarter), (depth, quarter))

    head = jnp.concatenate([shift_z(cut(1), 1), cut(0), shift_z(cut(3), -1), shift_far(cut(2), 1)], axis=0)

    row = lax.dynamic_slice(responses, (j, 0), (1, width)).reshape(4, 16, depth)
    near = jnp.concatenate([jnp.roll(row, -d, axis=1) for d in range(-2, 3)], axis=2)
    notes = jnp.stack([lax.dynamic_index_in_dim(targets, j, 0, False), lengths[0], owners[0]])
    notes = jnp.pad(notes.astype(jnp.float32), (0, META - 3))
    packed = jnp.concatenate(
        [near.transpose(1, 0, 2).reshape(16, 20 * depth), jnp.broadcast_to(notes[None], (16, META))], axis=1
    )
    mine = swap(packed[:, None, :], Z).reshape(16, 20 * depth + META)
    chunks = []
    for i in range(4):
        base = mine[:, 5 * depth * i : 5 * depth * (i + 1)]
        chunks.append(jnp.concatenate([base[:, depth : 4 * depth], base[:, :depth], mine[:, 20 * depth :]], axis=1))
        chunks.append(jnp.concatenate([base[:, depth:], mine[:, 20 * depth :]], axis=1))
    chunks = jnp.stack(chunks).reshape(4, 1, 2, 16, wide + META)
    copies = jnp.broadcast_to(chunks, (4, 4, 2, 16, wide + META)).reshape(32, 16, wide + META)
    slots = swap(copies, XYC).reshape(512, wide + META)

    ids = jnp.arange(512, dtype=jnp.int32)
    slot_j = (ids // 16) % 8
    source = (ids // 128) * 16 + ids % 16
    notes_all = slots[:, wide : wide + 3].astype(jnp.int32)
    slot_target, slot_length, slot_owner = notes_all[:, 0], notes_all[:, 1], notes_all[:, 2]
    before = (source[None, :] < source[:, None]) & (slot_j[None, :] == 0)
    starts = jnp.sum(jnp.where(before, slot_length[None, :], 0), axis=1)
    rank = jnp.where(slot_j < slot_length, starts + slot_j, -1)
    rows = jnp.arange(256, dtype=jnp.int32)
    select = rank[None, :] == rows[:, None]
    hidden = dot(select.astype(jnp.float32), slots[:, :wide])
    labels = jnp.sum(jnp.where(select, slot_target[None, :], 0), axis=1)
    owned = (slot_owner[None, :] == source[:, None]) & (slot_j[None, :] == slot_j[:, None])
    sent_rank = jnp.sum(jnp.where(owned, rank[None, :] + 1, 0), axis=1) - 1
    deliver = (sent_rank[:, None] == rows[None, :]).astype(jnp.float32)

    partial = dot(hidden, head)
    block = jnp.sum(swap(partial.reshape(4, 64, quarter), "x"), axis=0)
    logits = jnp.sum(swap(block.reshape(4, 16, quarter), "h"), axis=0)

    row_labels = lax.dynamic_slice(labels, (x * 64 + h * 16,), (16,))
    column = jnp.arange(quarter, dtype=jnp.int32) + j * columns + l * quarter
    onehot = (column[None, :] == row_labels[:, None]).astype(jnp.float32)
    peak = jnp.max(logits, axis=1)
    shifted = jnp.exp(logits - peak[:, None])
    stats = jnp.stack([peak, jnp.sum(shifted, axis=1), jnp.sum(logits * onehot, axis=1)], axis=0)
    stats = spread(stats, LYC, 32)
    row_peak = jnp.max(stats[:, 0], axis=0)
    exp_total = jnp.sum(stats[:, 1] * jnp.exp(stats[:, 0] - row_peak[None]), axis=0)
    logprobs = jnp.sum(stats[:, 2], axis=0) - row_peak - jnp.log(exp_total)
    scale = jnp.exp(peak - row_peak) / exp_total
    grad = onehot - shifted * scale[:, None]

    grads = spread(spread(grad, "h", 4).reshape(64, quarter), "x", 4).reshape(256, quarter)

    grad_head = dot(hidden, grads, (0, 0)).reshape(4, depth, quarter)
    grad_weight = jnp.zeros((depth, columns), jnp.float32)
    back = [grad_head[1], shift_z(grad_head[0], -1), shift_far(grad_head[3], -1), shift_z(grad_head[2], 1)]
    for s in range(4):
        grad_weight = lax.dynamic_update_slice(grad_weight, back[s], (0, (l + s) % 4 * quarter))

    grad_rows = dot(grads, head, (1, 1))
    leaving = dot(deliver, grad_rows).reshape(32, 16, wide)
    summed = jnp.sum(swap(leaving, XYC).reshape(4, 4, 2, 16, wide), axis=1)
    even, odd = summed[:, 0], summed[:, 1]
    near = jnp.concatenate(
        [even[..., 3 * depth :], even[..., : 3 * depth] + odd[..., : 3 * depth], odd[..., 3 * depth :]], axis=-1
    )
    near = near.transpose(1, 0, 2).reshape(16, 1, 20 * depth)
    arrived = swap(near, Z).reshape(16, 4, 5, depth)
    slot = sum(jnp.roll(arrived[:, :, d + 2], d, axis=0) for d in range(-2, 3))
    grad_hidden = spread(slot.transpose(1, 0, 2).reshape(width), YC, 8)
    return lax.dynamic_slice(logprobs, (4 * l,), (4,)), grad_hidden, grad_weight


def solution(mesh):
    grid = Mesh(mesh.devices.reshape(4, 4, 4, 4, 2), ("x", "h", "l", "y", "c"))
    dp = ("x", "h", "l")
    placed = (P(dp, None), P(dp, YC), P(dp), P(dp), P(dp))
    return jax.shard_map(
        on_device,
        mesh=grid,
        in_specs=placed,
        out_specs=(P(dp), P(dp, None), P(dp, YC)),
        check_vma=False,
    )
```

time: 260 us -> 229 us (0.88)
  waiting for transfers between devices: 120 us -> 52.6 us
  blocking collectives: 43.2 us -> 84.9 us
  starting transfers between devices: 68.2 us -> 62.4 us
    all_to_all x8 -> x6, waiting for transfers between devices: 105 us -> 41 us  [swap(): return lax.all_to_all(blocks, axes, split_axis=0, concat_axis=0, tiled=True)]
    all_to_all x2 -> x4, blocking collectives: 43.2 us -> 84.9 us  [swap(): return lax.all_to_all(blocks, axes, split_axis=0, concat_axis=0, tiled=True)]
    ppermute x8 -> x4, starting transfers between devices: 24.1 us -> 13.6 us  [shift_z(): return lax.ppermute(block, Z, [(i, (i + step) % 16) for i in range(16)])]
    ppermute x0 -> x2, starting transfers between devices: none -> 7.63 us  [shift_far(): return lax.ppermute(block, ('h', 'l', 'c'), pairs)]
    ppermute x8 -> x4, waiting for transfers between devices: 14.8 us -> 10.4 us  [shift_z(): return lax.ppermute(block, Z, [(i, (i + step) % 16) for i in range(16)])]
    all_to_all x8 -> x6, starting transfers between devices: 44 us -> 41.2 us  [swap(): return lax.all_to_all(blocks, axes, split_axis=0, concat_axis=0, tiled=True)]
    reshape x5 -> x4, local copies, waits for them, and re-layouts: 3.92 us -> 1.23 us  [the longest x1 0.87 us: on_device(): near = near.transpose(1, 0, 2).reshape(16, 1, 20 * depth)]
  transfers between devices with their start and end apart: 16 -> 12, of which waited for: 13 -> 8; matrix products, arithmetic and copies ran while one was open for 4% -> 4% of each run, Pallas kernels for 0% -> 0%
where the time goes in v4:
time: 229 us; the launch traced here: 228 us
  blocking collectives  84.9 us (37%)
  starting transfers between devices  62.4 us (27%)
  waiting for transfers between devices  52.6 us (23%)
  local copies, waits for them, and re-layouts  13.4 us (6%)
  matrix products  8.34 us (4%)
  other arithmetic  3.84 us (2%)
  between operations  2.5 us (1%)
    all_to_all x4, blocking collectives, swap(): return lax.all_to_all(blocks, axes, split_axis=0, concat_axis=0, tiled=True)  84.9 us
    all_to_all x6, starting transfers between devices, swap(): return lax.all_to_all(blocks, axes, split_axis=0, concat_axis=0, tiled=True)  41.2 us
    all_to_all x6, waiting for transfers between devices, swap(): return lax.all_to_all(blocks, axes, split_axis=0, concat_axis=0, tiled=True)  41 us
    ppermute x4, starting transfers between devices, shift_z(): return lax.ppermute(block, Z, [(i, (i + step) % 16) for i in range(16)])  13.6 us
    ppermute x4, waiting for transfers between devices, shift_z(): return lax.ppermute(block, Z, [(i, (i + step) % 16) for i in range(16)])  10.4 us
    dot_general x5, matrix products, dot(): lax.dot_general(a, b, dims, precision=HIGH, preferred_element_type=jnp.fl...  8.34 us
    ppermute x2, starting transfers between devices, shift_far(): return lax.ppermute(block, ('h', 'l', 'c'), pairs)  7.63 us
  transfers between devices with their start and end apart: 12, of which 8 were waited for; matrix products, arithmetic and copies ran while one was open for 4% of the time, Pallas kernels for 0%

profile of v4, /device:TPU:1, one launch (start us, length us, event | category | flops | bytes accessed | tf_op | source)
XLA Modules:
  0.0 228.0 jit_solution(4007755617741411983)
XLA Ops:
  3.5 1.2 dynamic_slice.26
  5.6 27.5 %all_to_all.54 = f32[16,1,2048]{2,1,0:T(1,128)S(1)} all-to-all(f32[16,1,2048]{2,1,0:T(1,128)S(1)} %copy.70), channel_id=1, replica_groups=mesh['x'=4,'h'=4,'l'=4,'y'=4,'c'=2] {'h','l'}, dimensions={0} | all-to-all | bytes 262144 | tf_op jit(solution)/shard_map/all_to_all | solution.py:15
  33.8 1.1 broadcast_in_dim.98
  34.9 10.7 %all-to-all-start.1 = ((f32[32,16,512]{2,1,0:T(8,128)}), f32[32,16,512]{2,1,0:T(8,128)S(1)}, u32[]{:S(2)}, u32[]{:S(2)}) async-start(f32[32,16,512]{2,1,0:T(8,128)} %bitcast.11), calls=%async_computation.1 | async-start | bytes 2097152 | tf_op jit(solution)/shard_map/all_to_all | solution.py:15
  46.8 3.4 %collective-permute-start.2 = (f32[96,1024]{1,0:T(8,128)}, f32[96,1024]{1,0:T(8,128)S(1)}, u32[]{:S(2)}, u32[]{:S(2)}) collective-permute-start(f32[96,1024]{1,0:T(8,128)} %get-tuple-element.16), channel_id=1, source_target_pairs={{0,16},{1,113},{8,24},{9,121},{16,32},{17,1},{24,40},{25,9},{32,48... | collective-permute-start | bytes 1179656 | tf_op jit(solution)/shard_map/ppermute | solution.py:29
  50.2 2.6 %collective-permute-start.1 = (f32[96,1024]{1,0:T(8,128)}, f32[96,1024]{1,0:T(8,128)S(1)}, u32[]{:S(2)}, u32[]{:S(2)}) collective-permute-start(f32[96,1024]{1,0:T(8,128)} %get-tuple-element.17), channel_id=1, source_target_pairs={{0,120},{8,0},{16,8},{24,16},{32,24},{40,32},{48,40},{56,48},{64,5... | collective-permute-start | bytes 1179656 | tf_op jit(solution)/shard_map/ppermute | solution.py:23
  52.8 3.0 %collective-permute-start = (f32[96,1024]{1,0:T(8,128)}, f32[96,1024]{1,0:T(8,128)S(1)}, u32[]{:S(2)}, u32[]{:S(2)}) collective-permute-start(f32[96,1024]{1,0:T(8,128)} %get-tuple-element.14), channel_id=1, source_target_pairs={{0,8},{8,16},{16,24},{24,32},{32,40},{40,48},{48,56},{56,64},{64,7... | collective-permute-start | bytes 1179656 | tf_op jit(solution)/shard_map/ppermute | solution.py:23
  55.8 6.8 %all-to-all-done.1 = f32[32,16,512]{2,1,0:T(8,128)S(1)} async-done(((f32[32,16,512]{2,1,0:T(8,128)}), f32[32,16,512]{2,1,0:T(8,128)S(1)}, u32[]{:S(2)}, u32[]{:S(2)}) %all-to-all-start.1) | async-done | bytes 1048608 | tf_op jit(solution)/shard_map/all_to_all | solution.py:15
  64.1 5.3 %collective-permute-done.1 = f32[96,1024]{1,0:T(8,128)S(1)} collective-permute-done((f32[96,1024]{1,0:T(8,128)}, f32[96,1024]{1,0:T(8,128)S(1)}, u32[]{:S(2)}, u32[]{:S(2)}) %collective-permute-start.1) | collective-permute-done | bytes 393248 | tf_op jit(solution)/shard_map/ppermute | solution.py:23
  69.4 1.9 fusion.1
  71.3 16.5 %all_to_all.55 = f32[4,64,1024]{2,1,0:T(8,128)S(1)} all-to-all(f32[4,64,1024]{2,1,0:T(8,128)S(1)} %bitcast.108), channel_id=1, replica_groups=mesh['x'=4,'h'=4,'l'=4,'y'=4,'c'=2] {'x'}, dimensions={0} | all-to-all | bytes 2097152 | tf_op jit(solution)/shard_map/all_to_all | solution.py:15
  88.5 5.3 %all-to-all-start.3 = ((f32[4,16,1024]{2,1,0:T(8,128)}), f32[4,16,1024]{2,1,0:T(8,128)S(1)}, u32[]{:S(2)}, u32[]{:S(2)}) async-start(f32[4,16,1024]{2,1,0:T(8,128)} %bitcast.14), calls=%async_computation.3 | async-start | bytes 524288 | tf_op jit(solution)/shard_map/all_to_all | solution.py:15
  94.0 12.8 %all-to-all-done.3 = f32[4,16,1024]{2,1,0:T(8,128)S(1)} async-done(((f32[4,16,1024]{2,1,0:T(8,128)}), f32[4,16,1024]{2,1,0:T(8,128)S(1)}, u32[]{:S(2)}, u32[]{:S(2)}) %all-to-all-start.3) | async-done | bytes 262176 | tf_op jit(solution)/shard_map/all_to_all | solution.py:15
  107.2 22.3 %all_to_all.56 = f32[32,3,16]{2,1,0:T(4,128)S(1)} all-to-all(f32[32,3,16]{2,1,0:T(4,128)S(1)} %broadcast_in_dim.104), channel_id=1, replica_groups=mesh['x'=4,'h'=4,'l'=4,'y'=4,'c'=2] {'l','y','c'}, dimensions={0} | all-to-all | bytes 12288 | tf_op jit(solution)/shard_map/all_to_all | solution.py:15
  129.8 18.5 %all_to_all.57 = f32[4,16,1024]{2,1,0:T(8,128)S(1)} all-to-all(f32[4,16,1024]{2,1,0:T(8,128)S(1)} %broadcast_in_dim.106), channel_id=1, replica_groups=mesh['x'=4,'h'=4,'l'=4,'y'=4,'c'=2] {'h'}, dimensions={0} | all-to-all | bytes 524288 | tf_op jit(solution)/shard_map/all_to_all | solution.py:15
  148.3 1.1 broadcast_in_dim.108
  149.4 3.5 %all-to-all-start.6 = ((f32[4,64,1024]{2,1,0:T(8,128)}), f32[4,64,1024]{2,1,0:T(8,128)S(1)}, u32[]{:S(2)}, u32[]{:S(2)}) async-start(f32[4,64,1024]{2,1,0:T(8,128)} %broadcast_in_dim.108), calls=%async_computation.6 | async-start | bytes 2097152 | tf_op jit(solution)/shard_map/all_to_all | solution.py:15
  153.3 11.1 %all-to-all-done.6 = f32[4,64,1024]{2,1,0:T(8,128)S(1)} async-done(((f32[4,64,1024]{2,1,0:T(8,128)}), f32[4,64,1024]{2,1,0:T(8,128)S(1)}, u32[]{:S(2)}, u32[]{:S(2)}) %all-to-all-start.6) | async-done | bytes 1048608 | tf_op jit(solution)/shard_map/all_to_all | solution.py:15
  164.4 2.9 %fusion = f32[256,384]{1,0:T(8,128)S(1)} fusion(f32[256,1024]{1,0:T(8,128)S(1)} %bitcast.97, f32[96,1024]{1,0:T(8,128)S(1)} %copy-done.6, f32[96,1024]{1,0:T(8,128)S(1)} %copy-done.8, f32[96,1024]{1,0:T(8,128)S(1)} %get-tuple-element.15, f32[96,1024]{1,0:T(8,128)} %copy-done.9), kind=kOutput, calls=%fused_computation.3 | convolution fusion | flops 1209139200 | bytes 3014656 | tf_op jit(solution)/shard_map/dot_general | solution.py:34
  167.3 1.5 fusion.4
  168.8 8.1 %all-to-all-start.7 = ((f32[32,16,384]{2,1,0:T(8,128)}), f32[32,16,384]{2,1,0:T(8,128)S(1)}, u32[]{:S(2)}, u32[]{:S(2)}) async-start(f32[32,16,384]{2,1,0:T(8,128)} %bitcast.22), calls=%async_computation.7 | async-start | bytes 1572864 | tf_op jit(solution)/shard_map/all_to_all | solution.py:15
  176.9 1.4 fusion.54
  179.5 1.1 copy-done.1
  180.7 5.0 %collective-permute-start.3 = (f32[96,1024]{1,0:T(8,128)}, f32[96,1024]{1,0:T(8,128)S(1)}, u32[]{:S(2)}, u32[]{:S(2)}) collective-permute-start(f32[96,1024]{1,0:T(8,128)} %get-tuple-element.12), channel_id=1, source_target_pairs={{0,120},{8,0},{16,8},{24,16},{32,24},{40,32},{48,40},{56,48},{64,5... | collective-permute-start | bytes 1179656 | tf_op jit(solution)/shard_map/ppermute | solution.py:23
  185.7 5.6 %all-to-all-done.7 = f32[32,16,384]{2,1,0:T(8,128)S(1)} async-done(((f32[32,16,384]{2,1,0:T(8,128)}), f32[32,16,384]{2,1,0:T(8,128)S(1)}, u32[]{:S(2)}, u32[]{:S(2)}) %all-to-all-start.7) | async-done | bytes 786464 | tf_op jit(solution)/shard_map/all_to_all | solution.py:15
  192.6 8.2 %all-to-all-start.8 = ((f32[16,1,1920]{2,1,0:T(1,128)}), f32[16,1,1920]{2,1,0:T(1,128)S(1)}, u32[]{:S(2)}, u32[]{:S(2)}) async-start(f32[16,1,1920]{2,1,0:T(1,128)} %reshape.271), calls=%async_computation.8 | async-start | bytes 245760 | tf_op jit(solution)/shard_map/all_to_all | solution.py:15
  201.4 4.2 %collective-permute-start.4 = (f32[96,1024]{1,0:T(8,128)}, f32[96,1024]{1,0:T(8,128)S(1)}, u32[]{:S(2)}, u32[]{:S(2)}) collective-permute-start(f32[96,1024]{1,0:T(8,128)} %get-tuple-element.11), channel_id=1, source_target_pairs={{0,112},{1,17},{8,120},{9,25},{16,0},{17,33},{24,8},{25,41},{32,16... | collective-permute-start | bytes 1179656 | tf_op jit(solution)/shard_map/ppermute | solution.py:29
  205.6 3.1 %collective-permute-start.5 = (f32[96,1024]{1,0:T(8,128)}, f32[96,1024]{1,0:T(8,128)S(1)}, u32[]{:S(2)}, u32[]{:S(2)}) collective-permute-start(f32[96,1024]{1,0:T(8,128)} %get-tuple-element.10), channel_id=1, source_target_pairs={{0,8},{8,16},{16,24},{24,32},{32,40},{40,48},{48,56},{56,64},{64,7... | collective-permute-start | bytes 1179656 | tf_op jit(solution)/shard_map/ppermute | solution.py:23
  208.7 4.7 %all-to-all-done.8 = f32[16,1,1920]{2,1,0:T(1,128)S(1)} async-done(((f32[16,1,1920]{2,1,0:T(1,128)}), f32[16,1,1920]{2,1,0:T(1,128)S(1)}, u32[]{:S(2)}, u32[]{:S(2)}) %all-to-all-start.8) | async-done | bytes 122912 | tf_op jit(solution)/shard_map/all_to_all | solution.py:15
  215.0 5.3 %all-to-all-start.9 = ((f32[8,1,6144]{2,1,0:T(1,128)}), f32[8,1,6144]{2,1,0:T(1,128)S(1)}, u32[]{:S(2)}, u32[]{:S(2)}) async-start(f32[8,1,6144]{2,1,0:T(1,128)} %broadcast_in_dim.110), calls=%async_computation.9 | async-start | bytes 393216 | tf_op jit(solution)/shard_map/all_to_all | solution.py:15
  220.3 1.3 collective-permute-done.4
  221.6 5.1 %collective-permute-done.5 = f32[96,1024]{1,0:T(8,128)S(1)} collective-permute-done((f32[96,1024]{1,0:T(8,128)}, f32[96,1024]{1,0:T(8,128)S(1)}, u32[]{:S(2)}, u32[]{:S(2)}) %collective-permute-start.5) | collective-permute-done | bytes 393248 | tf_op jit(solution)/shard_map/ppermute | solution.py:23
  (102 shorter events, 13.3 us)
Async XLA Ops:
  0.6 0.9 copy-start
  33.8 11.9 %copy-start.4 = (f32[96,4096]{1,0:T(8,128)S(1)}, f32[96,4096]{1,0:T(8,128)}, u32[]{:S(2)}) copy-start(f32[96,4096]{1,0:T(8,128)} %param.6) | copy-start | bytes 4718596
  34.9 27.7 %all-to-all-start.1 = ((f32[32,16,512]{2,1,0:T(8,128)}), f32[32,16,512]{2,1,0:T(8,128)S(1)}, u32[]{:S(2)}, u32[]{:S(2)}) async-start(f32[32,16,512]{2,1,0:T(8,128)} %bitcast.11), calls=%async_computation.1 | async-start | bytes 2097152 | tf_op jit(solution)/shard_map/all_to_all | solution.py:15
  46.8 17.3 %collective-permute-start.2 = (f32[96,1024]{1,0:T(8,128)}, f32[96,1024]{1,0:T(8,128)S(1)}, u32[]{:S(2)}, u32[]{:S(2)}) collective-permute-start(f32[96,1024]{1,0:T(8,128)} %get-tuple-element.16), channel_id=1, source_target_pairs={{0,16},{1,113},{8,24},{9,121},{16,32},{17,1},{24,40},{25,9},{32,48... | collective-permute-start | bytes 1179656 | tf_op jit(solution)/shard_map/ppermute | solution.py:29
  50.2 19.2 %collective-permute-start.1 = (f32[96,1024]{1,0:T(8,128)}, f32[96,1024]{1,0:T(8,128)S(1)}, u32[]{:S(2)}, u32[]{:S(2)}) collective-permute-start(f32[96,1024]{1,0:T(8,128)} %get-tuple-element.17), channel_id=1, source_target_pairs={{0,120},{8,0},{16,8},{24,16},{32,24},{40,32},{48,40},{56,48},{64,5... | collective-permute-start | bytes 1179656 | tf_op jit(solution)/shard_map/ppermute | solution.py:23
  52.8 16.6 %collective-permute-start = (f32[96,1024]{1,0:T(8,128)}, f32[96,1024]{1,0:T(8,128)S(1)}, u32[]{:S(2)}, u32[]{:S(2)}) collective-permute-start(f32[96,1024]{1,0:T(8,128)} %get-tuple-element.14), channel_id=1, source_target_pairs={{0,8},{8,16},{16,24},{24,32},{32,40},{40,48},{48,56},{56,64},{64,7... | collective-permute-start | bytes 1179656 | tf_op jit(solution)/shard_map/ppermute | solution.py:23
  64.1 7.2 %copy-start.5 = (f32[96,1024]{1,0:T(8,128)}, f32[96,1024]{1,0:T(8,128)S(1)}, u32[]{:S(2)}) copy-start(f32[96,1024]{1,0:T(8,128)S(1)} %collective-permute-done.2) | copy-start | bytes 1179652
  69.4 1.9 copy-start.7
  69.4 60.2 %copy-start.9 = (f32[96,1024]{1,0:T(8,128)}, f32[96,1024]{1,0:T(8,128)S(1)}, u32[]{:S(2)}) copy-start(f32[96,1024]{1,0:T(8,128)S(1)} %collective-permute-done) | copy-start | bytes 1179652
  88.5 18.3 %all-to-all-start.3 = ((f32[4,16,1024]{2,1,0:T(8,128)}), f32[4,16,1024]{2,1,0:T(8,128)S(1)}, u32[]{:S(2)}, u32[]{:S(2)}) async-start(f32[4,16,1024]{2,1,0:T(8,128)} %bitcast.14), calls=%async_computation.3 | async-start | bytes 524288 | tf_op jit(solution)/shard_map/all_to_all | solution.py:15
  148.3 16.1 %copy-start.6 = (f32[96,1024]{1,0:T(8,128)S(1)}, f32[96,1024]{1,0:T(8,128)}, u32[]{:S(2)}) copy-start(f32[96,1024]{1,0:T(8,128)} %copy-done.5) | copy-start | bytes 1179652
  148.3 16.1 %copy-start.8 = (f32[96,1024]{1,0:T(8,128)S(1)}, f32[96,1024]{1,0:T(8,128)}, u32[]{:S(2)}) copy-start(f32[96,1024]{1,0:T(8,128)} %copy-done.7) | copy-start | bytes 1179652
  149.4 15.0 %all-to-all-start.6 = ((f32[4,64,1024]{2,1,0:T(8,128)}), f32[4,64,1024]{2,1,0:T(8,128)S(1)}, u32[]{:S(2)}, u32[]{:S(2)}) async-start(f32[4,64,1024]{2,1,0:T(8,128)} %broadcast_in_dim.108), calls=%async_computation.6 | async-start | bytes 2097152 | tf_op jit(solution)/shard_map/all_to_all | solution.py:15
  168.8 22.4 %all-to-all-start.7 = ((f32[32,16,384]{2,1,0:T(8,128)}), f32[32,16,384]{2,1,0:T(8,128)S(1)}, u32[]{:S(2)}, u32[]{:S(2)}) async-start(f32[32,16,384]{2,1,0:T(8,128)} %bitcast.22), calls=%async_computation.7 | async-start | bytes 1572864 | tf_op jit(solution)/shard_map/all_to_all | solution.py:15
  179.5 1.1 copy-start.1
  180.7 28.0 %collective-permute-start.3 = (f32[96,1024]{1,0:T(8,128)}, f32[96,1024]{1,0:T(8,128)S(1)}, u32[]{:S(2)}, u32[]{:S(2)}) collective-permute-start(f32[96,1024]{1,0:T(8,128)} %get-tuple-element.12), channel_id=1, source_target_pairs={{0,120},{8,0},{16,8},{24,16},{32,24},{40,32},{48,40},{56,48},{64,5... | collective-permute-start | bytes 1179656 | tf_op jit(solution)/shard_map/ppermute | solution.py:23
  191.3 17.4 %copy-start.2 = (f32[96,4096]{1,0:T(8,128)S(1)}, f32[96,4096]{1,0:T(8,128)}, u32[]{:S(2)}) copy-start(f32[96,4096]{1,0:T(8,128)} %copy-done.1) | copy-start | bytes 4718596
  192.6 20.9 %all-to-all-start.8 = ((f32[16,1,1920]{2,1,0:T(1,128)}), f32[16,1,1920]{2,1,0:T(1,128)S(1)}, u32[]{:S(2)}, u32[]{:S(2)}) async-start(f32[16,1,1920]{2,1,0:T(1,128)} %reshape.271), calls=%async_computation.8 | async-start | bytes 245760 | tf_op jit(solution)/shard_map/all_to_all | solution.py:15
  201.4 20.2 %collective-permute-start.4 = (f32[96,1024]{1,0:T(8,128)}, f32[96,1024]{1,0:T(8,128)S(1)}, u32[]{:S(2)}, u32[]{:S(2)}) collective-permute-start(f32[96,1024]{1,0:T(8,128)} %get-tuple-element.11), channel_id=1, source_target_pairs={{0,112},{1,17},{8,120},{9,25},{16,0},{17,33},{24,8},{25,41},{32,16... | collective-permute-start | bytes 1179656 | tf_op jit(solution)/shard_map/ppermute | solution.py:29
  205.6 21.2 %collective-permute-start.5 = (f32[96,1024]{1,0:T(8,128)}, f32[96,1024]{1,0:T(8,128)S(1)}, u32[]{:S(2)}, u32[]{:S(2)}) collective-permute-start(f32[96,1024]{1,0:T(8,128)} %get-tuple-element.10), channel_id=1, source_target_pairs={{0,8},{8,16},{16,24},{24,32},{32,40},{40,48},{48,56},{56,64},{64,7... | collective-permute-start | bytes 1179656 | tf_op jit(solution)/shard_map/ppermute | solution.py:23
  215.0 11.8 %all-to-all-start.9 = ((f32[8,1,6144]{2,1,0:T(1,128)}), f32[8,1,6144]{2,1,0:T(1,128)S(1)}, u32[]{:S(2)}, u32[]{:S(2)}) async-start(f32[8,1,6144]{2,1,0:T(1,128)} %broadcast_in_dim.110), calls=%async_computation.9 | async-start | bytes 393216 | tf_op jit(solution)/shard_map/all_to_all | solution.py:15
  226.8 1.2 copy-start.3

commit v5 on v4

v5 whole, which is shorter than its diff:
```python
import jax
import jax.numpy as jnp
from jax import lax
from jax.sharding import Mesh, PartitionSpec as P

HIGH = lax.Precision.HIGHEST
Z = ("h", "l")
XYC = ("x", "y", "c")
LYC = ("l", "y", "c")
YC = ("y", "c")
GRAD = lax.Precision.HIGH


def swap(blocks, axes):
    return lax.all_to_all(blocks, axes, split_axis=0, concat_axis=0, tiled=True)


def spread(block, axes, count):
    return swap(jnp.broadcast_to(block[None], (count, *block.shape)), axes)


def shift_z(block, step):
    return lax.ppermute(block, Z, [(i, (i + step) % 16) for i in range(16)])


def shift_far(block, sign):
    step = [2 * sign, -2 * sign]
    pairs = [(2 * i + c, 2 * ((i + step[c]) % 16) + c) for i in range(16) for c in range(2)]
    return lax.ppermute(block, ("h", "l", "c"), pairs)


def dot(a, b, contract=(1, 0), precision=HIGH):
    dims = (((contract[0],), (contract[1],)), ((), ()))
    return lax.dot_general(a, b, dims, precision=precision, preferred_element_type=jnp.float32)


def on_device(responses, weight, lengths, targets, owners):
    width = responses.shape[1]
    depth, columns = weight.shape
    quarter = columns // 4
    wide = 4 * depth
    packed_wide = 128 * ((5 * depth + 10 + 127) // 128)
    x, h, l = lax.axis_index("x"), lax.axis_index("h"), lax.axis_index("l")
    j, c = lax.axis_index(YC), lax.axis_index("c")

    def cut(s):
        return lax.dynamic_slice(weight, (0, (l + s) % 4 * quarter), (depth, quarter))

    below, above, far = shift_z(cut(1), 1), shift_z(cut(3), -1), shift_far(cut(2), 1)

    row = lax.dynamic_slice(responses, (j, 0), (1, width)).reshape(4, 16, depth)
    notes = jnp.concatenate([targets, lengths, owners]).astype(jnp.float32)
    notes = jnp.broadcast_to(jnp.pad(notes, (0, packed_wide - 5 * depth - 10)), (4, 16, packed_wide - 5 * depth))
    near = jnp.concatenate([*(jnp.roll(row, -d, axis=1) for d in range(-2, 3)), notes], axis=2)
    mine = swap(near.transpose(1, 0, 2).reshape(16, 1, 4 * packed_wide), Z)
    chunks = mine.reshape(16, 4, packed_wide).transpose(1, 0, 2)
    chunks, below = lax.optimization_barrier((chunks, below))
    copies = jnp.broadcast_to(chunks[:, None], (4, 8, 16, packed_wide)).reshape(32, 16, packed_wide)
    slots = swap(copies, XYC).reshape(512, packed_wide)

    ids = jnp.arange(512, dtype=jnp.int32)
    slot_j = (ids // 16) % 8
    source = (ids // 128) * 16 + ids % 16
    notes_all = slots[:, 5 * depth : 5 * depth + 10].astype(jnp.int32)
    slot_length, slot_owner = notes_all[:, 8], notes_all[:, 9]
    slot_target = jnp.sum(jnp.where(jnp.arange(10)[None, :] == slot_j[:, None], notes_all, 0), axis=1)
    before = (source[None, :] < source[:, None]) & (slot_j[None, :] == 0)
    starts = jnp.sum(jnp.where(before, slot_length[None, :], 0), axis=1)
    rank = jnp.where(slot_j < slot_length, starts + slot_j, -1)
    rows = jnp.arange(256, dtype=jnp.int32)
    select = rank[None, :] == rows[:, None]
    hidden = dot(select.astype(jnp.float32), slots[:, : 5 * depth])
    labels = jnp.sum(jnp.where(select, slot_target[None, :], 0), axis=1)
    owned = (slot_owner[None, :] == source[:, None]) & (slot_j[None, :] == slot_j[:, None])
    sent_rank = jnp.sum(jnp.where(owned, rank[None, :] + 1, 0), axis=1) - 1
    deliver = (sent_rank[:, None] == rows[None, :]).astype(jnp.float32)

    none = jnp.zeros_like(far)
    head = jnp.concatenate([jnp.where(c == 0, far, none), below, cut(0), above, jnp.where(c == 0, none, far)], axis=0)
    head = lax.optimization_barrier(head)

    partial = dot(hidden, head)
    block = jnp.sum(swap(partial.reshape(4, 64, quarter), "x"), axis=0)
    logits = jnp.sum(swap(block.reshape(4, 16, quarter), "h"), axis=0)

    row_labels = lax.dynamic_slice(labels, (x * 64 + h * 16,), (16,))
    column = jnp.arange(quarter, dtype=jnp.int32) + j * columns + l * quarter
    onehot = (column[None, :] == row_labels[:, None]).astype(jnp.float32)
    peak = jnp.max(logits, axis=1)
    shifted = jnp.exp(logits - peak[:, None])
    stats = jnp.stack([peak, jnp.sum(shifted, axis=1), jnp.sum(logits * onehot, axis=1)], axis=0)
    stats = spread(stats, LYC, 32)
    row_peak = jnp.max(stats[:, 0], axis=0)
    exp_total = jnp.sum(stats[:, 1] * jnp.exp(stats[:, 0] - row_peak[None]), axis=0)
    logprobs = jnp.sum(stats[:, 2], axis=0) - row_peak - jnp.log(exp_total)
    scale = jnp.exp(peak - row_peak) / exp_total
    grad = onehot - shifted * scale[:, None]

    grads = spread(spread(grad, "h", 4).reshape(64, quarter), "x", 4).reshape(256, quarter)

    grad_head = dot(hidden, grads, (0, 0), GRAD).reshape(5, depth, quarter)
    far = shift_far(jnp.where(c == 0, grad_head[0], grad_head[4]), -1)
    above, below = shift_z(grad_head[1], -1), shift_z(grad_head[3], 1)

    grad_rows = dot(grads, head, (1, 1), GRAD)
    grad_rows = jnp.where(c == 0, grad_rows[:, :wide], grad_rows[:, depth:])
    leaving = dot(deliver, grad_rows, (1, 0), GRAD).reshape(32, 16, wide)
    summed = jnp.sum(swap(leaving, XYC).reshape(4, 4, 2, 16, wide), axis=1)
    near = jnp.pad(summed[:, 0], ((0, 0), (0, 0), (0, depth))) + jnp.pad(summed[:, 1], ((0, 0), (0, 0), (depth, 0)))
    near = near.transpose(1, 0, 2).reshape(16, 1, 20 * depth)
    near, above, below = lax.optimization_barrier((near, above, below))
    arrived = swap(near, Z).reshape(16, 4, 5, depth)
    slot = sum(jnp.roll(arrived[:, :, d + 2], d, axis=0) for d in range(-2, 3))
    grad_weight = jnp.zeros((depth, columns), jnp.float32)
    for s, part in enumerate((grad_head[2], above, far, below)):
        grad_weight = lax.dynamic_update_slice(grad_weight, part, (0, (l + s) % 4 * quarter))
    grad_hidden = spread(slot.transpose(1, 0, 2).reshape(width), YC, 8)
    return lax.dynamic_slice(logprobs, (4 * l,), (4,)), grad_hidden, grad_weight


def solution(mesh):
    grid = Mesh(mesh.devices.reshape(4, 4, 4, 4, 2), ("x", "h", "l", "y", "c"))
    dp = ("x", "h", "l")
    placed = (P(dp, None), P(dp, YC), P(dp), P(dp), P(dp))
    return jax.shard_map(
        on_device,
        mesh=grid,
        in_specs=placed,
        out_specs=(P(dp), P(dp, None), P(dp, YC)),
        check_vma=False,
    )
```

time: 229 us -> 235 us (1.026)
  blocking collectives: 84.9 us -> 57.6 us
  starting transfers between devices: 62.4 us -> 84.5 us
  waiting for transfers between devices: 52.6 us -> 62.1 us
  other arithmetic: 3.84 us -> 7.56 us
    all_to_all x4 -> x3, blocking collectives: 84.9 us -> 57.6 us  [swap(): return lax.all_to_all(blocks, axes, split_axis=0, concat_axis=0, tiled=True)]
    all_to_all x6 -> x7, starting transfers between devices: 41.2 us -> 59.8 us  [swap(): return lax.all_to_all(blocks, axes, split_axis=0, concat_axis=0, tiled=True)]
    all_to_all x6 -> x7, waiting for transfers between devices: 41 us -> 50.5 us  [swap(): return lax.all_to_all(blocks, axes, split_axis=0, concat_axis=0, tiled=True)]
    ppermute x4, starting transfers between devices: 13.6 us -> 16.2 us  [shift_z(): return lax.ppermute(block, Z, [(i, (i + step) % 16) for i in range(16)])]
    unnamed x22 -> x16, local copies, waits for them, and re-layouts: 3.32 us -> 5.53 us
  transfers between devices with their start and end apart: 12 -> 13, of which waited for: 8 -> 10; matrix products, arithmetic and copies ran while one was open for 4% -> 5% of each run, Pallas kernels for 0% -> 0%
where the time goes in v5:
time: 235 us; the launch traced here: 234 us
  starting transfers between devices  84.5 us (36%)
  waiting for transfers between devices  62.1 us (26%)
  blocking collectives  57.6 us (25%)
  local copies, waits for them, and re-layouts  13.6 us (6%)
  other arithmetic  7.56 us (3%)
  matrix products  6.16 us (3%)
  between operations  2.5 us (1%)
    all_to_all x7, starting transfers between devices, swap(): return lax.all_to_all(blocks, axes, split_axis=0, concat_axis=0, tiled=True)  59.8 us
    all_to_all x3, blocking collectives, swap(): return lax.all_to_all(blocks, axes, split_axis=0, concat_axis=0, tiled=True)  57.6 us
    all_to_all x7, waiting for transfers between devices, swap(): return lax.all_to_all(blocks, axes, split_axis=0, concat_axis=0, tiled=True)  50.5 us
    ppermute x4, starting transfers between devices, shift_z(): return lax.ppermute(block, Z, [(i, (i + step) % 16) for i in range(16)])  16.2 us
    ppermute x4, waiting for transfers between devices, shift_z(): return lax.ppermute(block, Z, [(i, (i + step) % 16) for i in range(16)])  11.7 us
    ppermute x2, starting transfers between devices, shift_far(): return lax.ppermute(block, ('h', 'l', 'c'), pairs)  8.46 us
    dot_general x5, matrix products, dot(): lax.dot_general(a, b, dims, precision=precision, preferred_element_type=j...  6.16 us
    unnamed x16, local copies, waits for them, and re-layouts  5.53 us
  transfers between devices with their start and end apart: 13, of which 10 were waited for; matrix products, arithmetic and copies ran while one was open for 5% of the time, Pallas kernels for 0%

profile of v5, /device:TPU:1, one launch (start us, length us, event | category | flops | bytes accessed | tf_op | source)
XLA Modules:
  0.0 234.0 jit_solution(14429828874540651896)
XLA Ops:
  4.9 15.7 %all-to-all-start = ((f32[16,1,2048]{2,1,0:T(1,128)}), f32[16,1,2048]{2,1,0:T(1,128)S(1)}, u32[]{:S(2)}, u32[]{:S(2)}) async-start(f32[16,1,2048]{2,1,0:T(1,128)} %reshape.271), calls=%async_computation | async-start | bytes 262144 | tf_op jit(solution)/shard_map/all_to_all | solution.py:15
  21.7 3.2 %collective-permute-start = (f32[96,1024]{1,0:T(8,128)S(1)}, f32[96,1024]{1,0:T(8,128)S(1)}, u32[]{:S(2)}, u32[]{:S(2)}) collective-permute-start(f32[96,1024]{1,0:T(8,128)S(1)} %get-tuple-element.25), channel_id=1, source_target_pairs={{0,8},{8,16},{16,24},{24,32},{32,40},{40,48},{48,56},{56,64},{64,7... | collective-permute-start | bytes 1179656 | tf_op jit(solution)/shard_map/ppermute | solution.py:23
  24.9 4.3 %collective-permute-start.1 = (f32[96,1024]{1,0:T(8,128)}, f32[96,1024]{1,0:T(8,128)}, u32[]{:S(2)}, u32[]{:S(2)}) collective-permute-start(f32[96,1024]{1,0:T(8,128)} %get-tuple-element.24), channel_id=1, source_target_pairs={{0,16},{1,113},{8,24},{9,121},{16,32},{17,1},{24,40},{25,9},{32,48... | collective-permute-start | bytes 1179656 | tf_op jit(solution)/shard_map/ppermute | solution.py:29
  29.2 3.1 %collective-permute-start.2 = (f32[96,1024]{1,0:T(8,128)}, f32[96,1024]{1,0:T(8,128)}, u32[]{:S(2)}, u32[]{:S(2)}) collective-permute-start(f32[96,1024]{1,0:T(8,128)} %get-tuple-element.23), channel_id=1, source_target_pairs={{0,120},{8,0},{16,8},{24,16},{32,24},{40,32},{48,40},{56,48},{64,5... | collective-permute-start | bytes 1179656 | tf_op jit(solution)/shard_map/ppermute | solution.py:23
  33.1 5.8 %collective-permute-done = f32[96,1024]{1,0:T(8,128)S(1)} collective-permute-done((f32[96,1024]{1,0:T(8,128)S(1)}, f32[96,1024]{1,0:T(8,128)S(1)}, u32[]{:S(2)}, u32[]{:S(2)}) %collective-permute-start) | collective-permute-done | bytes 393248 | tf_op jit(solution)/shard_map/ppermute | solution.py:23
  39.0 1.1 broadcast_in_dim.57
  40.1 7.6 %all-to-all-start.1 = ((f32[32,16,512]{2,1,0:T(8,128)}), f32[32,16,512]{2,1,0:T(8,128)S(1)}, u32[]{:S(2)}, u32[]{:S(2)}) async-start(f32[32,16,512]{2,1,0:T(8,128)} %bitcast.2), calls=%async_computation.1 | async-start | bytes 2097152 | tf_op jit(solution)/shard_map/all_to_all | solution.py:15
  48.9 1.0 dynamic-slice_dynamic-update-slice_fusion
  50.9 1.0 select_dynamic-update-slice_fusion
  52.0 12.7 %all-to-all-done.1 = f32[32,16,512]{2,1,0:T(8,128)S(1)} async-done(((f32[32,16,512]{2,1,0:T(8,128)}), f32[32,16,512]{2,1,0:T(8,128)S(1)}, u32[]{:S(2)}, u32[]{:S(2)}) %all-to-all-start.1) | async-done | bytes 1048608 | tf_op jit(solution)/shard_map/all_to_all | solution.py:15
  67.4 1.9 fusion.33
  69.2 17.9 %all_to_all.54 = f32[4,64,1024]{2,1,0:T(8,128)} all-to-all(f32[4,64,1024]{2,1,0:T(8,128)S(1)} %bitcast.66), channel_id=1, replica_groups=mesh['x'=4,'h'=4,'l'=4,'y'=4,'c'=2] {'x'}, dimensions={0} | all-to-all | bytes 2097152 | tf_op jit(solution)/shard_map/all_to_all | solution.py:15
  87.2 2.0 reduce_sum.100
  89.2 8.6 %all-to-all-start.3 = ((f32[4,16,1024]{2,1,0:T(8,128)}), f32[4,16,1024]{2,1,0:T(8,128)S(1)}, u32[]{:S(2)}, u32[]{:S(2)}) async-start(f32[4,16,1024]{2,1,0:T(8,128)} %bitcast.5), calls=%async_computation.3 | async-start | bytes 524288 | tf_op jit(solution)/shard_map/all_to_all | solution.py:15
  98.3 12.6 %all-to-all-done.3 = f32[4,16,1024]{2,1,0:T(8,128)S(1)} async-done(((f32[4,16,1024]{2,1,0:T(8,128)}), f32[4,16,1024]{2,1,0:T(8,128)S(1)}, u32[]{:S(2)}, u32[]{:S(2)}) %all-to-all-start.3) | async-done | bytes 262176 | tf_op jit(solution)/shard_map/all_to_all | solution.py:15
  111.3 20.4 %all_to_all.55 = f32[32,3,16]{2,1,0:T(4,128)S(1)} all-to-all(f32[32,3,16]{2,1,0:T(4,128)S(1)} %broadcast_in_dim.104), channel_id=1, replica_groups=mesh['x'=4,'h'=4,'l'=4,'y'=4,'c'=2] {'l','y','c'}, dimensions={0} | all-to-all | bytes 12288 | tf_op jit(solution)/shard_map/all_to_all | solution.py:15
  132.0 19.3 %all_to_all.56 = f32[4,16,1024]{2,1,0:T(8,128)S(1)} all-to-all(f32[4,16,1024]{2,1,0:T(8,128)S(1)} %broadcast_in_dim.106), channel_id=1, replica_groups=mesh['x'=4,'h'=4,'l'=4,'y'=4,'c'=2] {'h'}, dimensions={0} | all-to-all | bytes 524288 | tf_op jit(solution)/shard_map/all_to_all | solution.py:15
  151.2 1.1 broadcast_in_dim.108
  152.3 3.5 %all-to-all-start.6 = ((f32[4,64,1024]{2,1,0:T(8,128)}), f32[4,64,1024]{2,1,0:T(8,128)S(1)}, u32[]{:S(2)}, u32[]{:S(2)}) async-start(f32[4,64,1024]{2,1,0:T(8,128)} %broadcast_in_dim.108), calls=%async_computation.6 | async-start | bytes 2097152 | tf_op jit(solution)/shard_map/all_to_all | solution.py:15
  156.2 9.6 %all-to-all-done.6 = f32[4,64,1024]{2,1,0:T(8,128)S(1)} async-done(((f32[4,64,1024]{2,1,0:T(8,128)}), f32[4,64,1024]{2,1,0:T(8,128)S(1)}, u32[]{:S(2)}, u32[]{:S(2)}) %all-to-all-start.6) | async-done | bytes 1048608 | tf_op jit(solution)/shard_map/all_to_all | solution.py:15
  166.8 1.4 fusion.2
  168.2 9.6 %all-to-all-start.7 = ((f32[32,16,384]{2,1,0:T(8,128)}), f32[32,16,384]{2,1,0:T(8,128)S(1)}, u32[]{:S(2)}, u32[]{:S(2)}) async-start(f32[32,16,384]{2,1,0:T(8,128)} %bitcast.68), calls=%async_computation.7 | async-start | bytes 1572864 | tf_op jit(solution)/shard_map/all_to_all | solution.py:15
  178.9 1.1 slice_select_fusion
  180.0 5.0 %collective-permute-start.3 = (f32[96,1024]{1,0:T(8,128)}, f32[96,1024]{1,0:T(8,128)S(1)}, u32[]{:S(2)}, u32[]{:S(2)}) collective-permute-start(f32[96,1024]{1,0:T(8,128)} %get-tuple-element.22), channel_id=1, source_target_pairs={{0,120},{8,0},{16,8},{24,16},{32,24},{40,32},{48,40},{56,48},{64,5... | collective-permute-start | bytes 1179656 | tf_op jit(solution)/shard_map/ppermute | solution.py:23
  184.9 5.0 %collective-permute-start.4 = (f32[96,1024]{1,0:T(8,128)}, f32[96,1024]{1,0:T(8,128)S(1)}, u32[]{:S(2)}, u32[]{:S(2)}) collective-permute-start(f32[96,1024]{1,0:T(8,128)} %get-tuple-element.21), channel_id=1, source_target_pairs={{0,8},{8,16},{16,24},{24,32},{32,40},{40,48},{48,56},{56,64},{64,7... | collective-permute-start | bytes 1179656 | tf_op jit(solution)/shard_map/ppermute | solution.py:23
  189.9 2.2 all-to-all-done.7
  192.6 4.8 %collective-permute-done.3 = f32[96,1024]{1,0:T(8,128)S(1)} collective-permute-done((f32[96,1024]{1,0:T(8,128)}, f32[96,1024]{1,0:T(8,128)S(1)}, u32[]{:S(2)}, u32[]{:S(2)}) %collective-permute-start.3) | collective-permute-done | bytes 393248 | tf_op jit(solution)/shard_map/ppermute | solution.py:23
  199.2 5.0 %all-to-all-start.8 = ((f32[16,1,1920]{2,1,0:T(1,128)}), f32[16,1,1920]{2,1,0:T(1,128)S(1)}, u32[]{:S(2)}, u32[]{:S(2)}) async-start(f32[16,1,1920]{2,1,0:T(1,128)} %copy.82), calls=%async_computation.8 | async-start | bytes 245760 | tf_op jit(solution)/shard_map/all_to_all | solution.py:15
  204.8 4.2 %collective-permute-start.5 = (f32[96,1024]{1,0:T(8,128)}, f32[96,1024]{1,0:T(8,128)S(1)}, u32[]{:S(2)}, u32[]{:S(2)}) collective-permute-start(f32[96,1024]{1,0:T(8,128)} %get-tuple-element.19), channel_id=1, source_target_pairs={{0,112},{1,17},{8,120},{9,25},{16,0},{17,33},{24,8},{25,41},{32,16... | collective-permute-start | bytes 1179656 | tf_op jit(solution)/shard_map/ppermute | solution.py:29
  209.0 7.2 %all-to-all-done.8 = f32[16,1,1920]{2,1,0:T(1,128)S(1)} async-done(((f32[16,1,1920]{2,1,0:T(1,128)}), f32[16,1,1920]{2,1,0:T(1,128)S(1)}, u32[]{:S(2)}, u32[]{:S(2)}) %all-to-all-start.8) | async-done | bytes 122912 | tf_op jit(solution)/shard_map/all_to_all | solution.py:15
  217.7 9.6 %all-to-all-start.9 = ((f32[8,1,6144]{2,1,0:T(1,128)}), f32[8,1,6144]{2,1,0:T(1,128)S(1)}, u32[]{:S(2)}, u32[]{:S(2)}) async-start(f32[8,1,6144]{2,1,0:T(1,128)} %broadcast_in_dim.110), calls=%async_computation.9 | async-start | bytes 393216 | tf_op jit(solution)/shard_map/all_to_all | solution.py:15
  227.5 5.8 %all-to-all-done.9 = f32[8,1,6144]{2,1,0:T(1,128)S(1)} async-done(((f32[8,1,6144]{2,1,0:T(1,128)}), f32[8,1,6144]{2,1,0:T(1,128)S(1)}, u32[]{:S(2)}, u32[]{:S(2)}) %all-to-all-start.9) | async-done | bytes 196640 | tf_op jit(solution)/shard_map/all_to_all | solution.py:15
  (88 shorter events, 18.1 us)
Async XLA Ops:
  0.6 0.9 copy-start
  0.6 20.1 %copy-start.4 = (f32[96,4096]{1,0:T(8,128)S(1)}, f32[96,4096]{1,0:T(8,128)}, u32[]{:S(2)}) copy-start(f32[96,4096]{1,0:T(8,128)} %param.6) | copy-start | bytes 4718596
  4.9 27.8 %all-to-all-start = ((f32[16,1,2048]{2,1,0:T(1,128)}), f32[16,1,2048]{2,1,0:T(1,128)S(1)}, u32[]{:S(2)}, u32[]{:S(2)}) async-start(f32[16,1,2048]{2,1,0:T(1,128)} %reshape.271), calls=%async_computation | async-start | bytes 262144 | tf_op jit(solution)/shard_map/all_to_all | solution.py:15
  21.7 17.2 %collective-permute-start = (f32[96,1024]{1,0:T(8,128)S(1)}, f32[96,1024]{1,0:T(8,128)S(1)}, u32[]{:S(2)}, u32[]{:S(2)}) collective-permute-start(f32[96,1024]{1,0:T(8,128)S(1)} %get-tuple-element.25), channel_id=1, source_target_pairs={{0,8},{8,16},{16,24},{24,32},{32,40},{40,48},{48,56},{56,64},{64,7... | collective-permute-start | bytes 1179656 | tf_op jit(solution)/shard_map/ppermute | solution.py:23
  24.9 22.9 %collective-permute-start.1 = (f32[96,1024]{1,0:T(8,128)}, f32[96,1024]{1,0:T(8,128)}, u32[]{:S(2)}, u32[]{:S(2)}) collective-permute-start(f32[96,1024]{1,0:T(8,128)} %get-tuple-element.24), channel_id=1, source_target_pairs={{0,16},{1,113},{8,24},{9,121},{16,32},{17,1},{24,40},{25,9},{32,48... | collective-permute-start | bytes 1179656 | tf_op jit(solution)/shard_map/ppermute | solution.py:29
  29.2 20.7 %collective-permute-start.2 = (f32[96,1024]{1,0:T(8,128)}, f32[96,1024]{1,0:T(8,128)}, u32[]{:S(2)}, u32[]{:S(2)}) collective-permute-start(f32[96,1024]{1,0:T(8,128)} %get-tuple-element.23), channel_id=1, source_target_pairs={{0,120},{8,0},{16,8},{24,16},{32,24},{40,32},{48,40},{56,48},{64,5... | collective-permute-start | bytes 1179656 | tf_op jit(solution)/shard_map/ppermute | solution.py:23
  38.9 8.8 %copy-start.5 = (f32[96,1024]{1,0:T(8,128)}, f32[96,1024]{1,0:T(8,128)S(1)}, u32[]{:S(2)}) copy-start(f32[96,1024]{1,0:T(8,128)S(1)} %collective-permute-done) | copy-start | bytes 1179652
  40.1 24.6 %all-to-all-start.1 = ((f32[32,16,512]{2,1,0:T(8,128)}), f32[32,16,512]{2,1,0:T(8,128)S(1)}, u32[]{:S(2)}, u32[]{:S(2)}) async-start(f32[32,16,512]{2,1,0:T(8,128)} %bitcast.2), calls=%async_computation.1 | async-start | bytes 2097152 | tf_op jit(solution)/shard_map/all_to_all | solution.py:15
  66.6 0.8 copy-start.1
  89.2 21.8 %all-to-all-start.3 = ((f32[4,16,1024]{2,1,0:T(8,128)}), f32[4,16,1024]{2,1,0:T(8,128)S(1)}, u32[]{:S(2)}, u32[]{:S(2)}) async-start(f32[4,16,1024]{2,1,0:T(8,128)} %bitcast.5), calls=%async_computation.3 | async-start | bytes 524288 | tf_op jit(solution)/shard_map/all_to_all | solution.py:15
  152.3 13.5 %all-to-all-start.6 = ((f32[4,64,1024]{2,1,0:T(8,128)}), f32[4,64,1024]{2,1,0:T(8,128)S(1)}, u32[]{:S(2)}, u32[]{:S(2)}) async-start(f32[4,64,1024]{2,1,0:T(8,128)} %broadcast_in_dim.108), calls=%async_computation.6 | async-start | bytes 2097152 | tf_op jit(solution)/shard_map/all_to_all | solution.py:15
  166.8 11.0 %copy-start.2 = (f32[256,480]{0,1:T(8,128)S(1)}, f32[256,480]{0,1:T(8,128)}, u32[]{:S(2)}) copy-start(f32[256,480]{0,1:T(8,128)} %copy-done.1) | copy-start | bytes 1474564
  168.2 24.0 %all-to-all-start.7 = ((f32[32,16,384]{2,1,0:T(8,128)}), f32[32,16,384]{2,1,0:T(8,128)S(1)}, u32[]{:S(2)}, u32[]{:S(2)}) async-start(f32[32,16,384]{2,1,0:T(8,128)} %bitcast.68), calls=%async_computation.7 | async-start | bytes 1572864 | tf_op jit(solution)/shard_map/all_to_all | solution.py:15
  180.0 17.4 %collective-permute-start.3 = (f32[96,1024]{1,0:T(8,128)}, f32[96,1024]{1,0:T(8,128)S(1)}, u32[]{:S(2)}, u32[]{:S(2)}) collective-permute-start(f32[96,1024]{1,0:T(8,128)} %get-tuple-element.22), channel_id=1, source_target_pairs={{0,120},{8,0},{16,8},{24,16},{32,24},{40,32},{48,40},{56,48},{64,5... | collective-permute-start | bytes 1179656 | tf_op jit(solution)/shard_map/ppermute | solution.py:23
  184.9 13.5 %collective-permute-start.4 = (f32[96,1024]{1,0:T(8,128)}, f32[96,1024]{1,0:T(8,128)S(1)}, u32[]{:S(2)}, u32[]{:S(2)}) collective-permute-start(f32[96,1024]{1,0:T(8,128)} %get-tuple-element.21), channel_id=1, source_target_pairs={{0,8},{8,16},{16,24},{24,32},{32,40},{40,48},{48,56},{56,64},{64,7... | collective-permute-start | bytes 1179656 | tf_op jit(solution)/shard_map/ppermute | solution.py:23
  199.2 17.0 %all-to-all-start.8 = ((f32[16,1,1920]{2,1,0:T(1,128)}), f32[16,1,1920]{2,1,0:T(1,128)S(1)}, u32[]{:S(2)}, u32[]{:S(2)}) async-start(f32[16,1,1920]{2,1,0:T(1,128)} %copy.82), calls=%async_computation.8 | async-start | bytes 245760 | tf_op jit(solution)/shard_map/all_to_all | solution.py:15
  204.8 22.6 %collective-permute-start.5 = (f32[96,1024]{1,0:T(8,128)}, f32[96,1024]{1,0:T(8,128)S(1)}, u32[]{:S(2)}, u32[]{:S(2)}) collective-permute-start(f32[96,1024]{1,0:T(8,128)} %get-tuple-element.19), channel_id=1, source_target_pairs={{0,112},{1,17},{8,120},{9,25},{16,0},{17,33},{24,8},{25,41},{32,16... | collective-permute-start | bytes 1179656 | tf_op jit(solution)/shard_map/ppermute | solution.py:29
  217.7 15.5 %all-to-all-start.9 = ((f32[8,1,6144]{2,1,0:T(1,128)}), f32[8,1,6144]{2,1,0:T(1,128)S(1)}, u32[]{:S(2)}, u32[]{:S(2)}) async-start(f32[8,1,6144]{2,1,0:T(1,128)} %broadcast_in_dim.110), calls=%async_computation.9 | async-start | bytes 393216 | tf_op jit(solution)/shard_map/all_to_all | solution.py:15
  227.5 6.5 %copy-start.3 = (f32[96,4096]{1,0:T(8,128)}, f32[96,4096]{1,0:T(8,128)S(1)}, u32[]{:S(2)}) copy-start(f32[96,4096]{1,0:T(8,128)S(1)} %constant_dynamic-update-slice_fusion.2) | copy-start | bytes 4718596

commit v6 on v1

v6 whole, which is shorter than its diff:
```python
import jax
import jax.numpy as jnp
from jax import lax
from jax.sharding import Mesh, PartitionSpec as P

HIGH = lax.Precision.HIGHEST
GRAD = lax.Precision.HIGH
Z = ("h", "l")
XYC = ("x", "y", "c")
YC = ("y", "c")
META = 128


def swap(blocks, axes):
    return lax.all_to_all(blocks, axes, split_axis=0, concat_axis=0, tiled=True)


def spread(block, axes, count):
    return swap(jnp.broadcast_to(block[None], (count, *block.shape)), axes)


def shift_z(block, step):
    return lax.ppermute(block, Z, [(i, (i + step) % 16) for i in range(16)])


def shift_far(block):
    pairs = [(2 * i + c, 2 * ((i + 2 - 4 * c) % 16) + c) for i in range(16) for c in range(2)]
    return lax.ppermute(block, ("h", "l", "c"), pairs)


def shift_x(block, step):
    return lax.ppermute(block, "x", [(i, (i + step) % 4) for i in range(4)])


def dot(a, b, contract=(1, 0), precision=HIGH):
    dims = (((contract[0],), (contract[1],)), ((), ()))
    return lax.dot_general(a, b, dims, precision=precision, preferred_element_type=jnp.float32)


def on_device(responses, weight, lengths, targets, owners):
    width = responses.shape[1]
    depth, columns = weight.shape
    quarter = columns // 4
    wide = 4 * depth
    x, h, l = lax.axis_index("x"), lax.axis_index("h"), lax.axis_index("l")
    j = lax.axis_index(YC)

    def cut(s):
        return lax.dynamic_slice(weight, (0, (x + s) % 4 * quarter), (depth, quarter))

    pieces = [cut(0), *(shift_x(cut(s), s) for s in range(1, 4))]

    row = lax.dynamic_slice(responses, (j, 0), (1, width)).reshape(4, 16, depth)
    notes = jnp.pad(jnp.concatenate([targets, lengths, owners]).astype(jnp.float32), (0, META - 10))
    notes = jnp.broadcast_to(notes, (16, META))
    packed = jnp.concatenate([row.transpose(1, 0, 2).reshape(16, wide), notes], axis=1)
    mine = swap(packed.reshape(16, 1, wide + META), Z).reshape(16, wide + META)
    mine, pieces[1] = lax.optimization_barrier((mine, pieces[1]))
    slots = spread(mine, XYC, 32).reshape(512, wide + META)

    ids = jnp.arange(512, dtype=jnp.int32)
    slot_j = (ids // 16) % 8
    source = (ids // 128) * 16 + ids % 16
    notes_all = slots[:, wide : wide + 10].astype(jnp.int32)
    slot_length, slot_owner = notes_all[:, 8], notes_all[:, 9]
    slot_target = jnp.sum(jnp.where(jnp.arange(10)[None, :] == slot_j[:, None], notes_all, 0), axis=1)
    before = (source[None, :] < source[:, None]) & (slot_j[None, :] == 0)
    starts = jnp.sum(jnp.where(before, slot_length[None, :], 0), axis=1)
    rank = jnp.where(slot_j < slot_length, (starts + slot_j - 64 * l) % 256, -1)
    rows = jnp.arange(256, dtype=jnp.int32)
    select = rank[None, :] == rows[:, None]
    hidden = dot(select.astype(jnp.float32), slots[:, :wide])
    labels = jnp.sum(jnp.where(select, slot_target[None, :], 0), axis=1)
    owned = (slot_owner[None, :] == source[:, None]) & (slot_j[None, :] == slot_j[:, None])
    sent_rank = jnp.sum(jnp.where(owned, rank[None, :] + 1, 0), axis=1) - 1
    deliver = (sent_rank[:, None] == rows[None, :]).astype(jnp.float32)

    head = jnp.zeros((4, depth, quarter), jnp.float32)
    for s, piece in enumerate(pieces):
        head = lax.dynamic_update_slice(head, piece[None], ((x - s) % 4, 0, 0))
    head = lax.optimization_barrier(head.reshape(wide, quarter))

    partial = dot(hidden, head)
    block = partial[:64] + shift_z(partial[64:128], 1) + shift_z(partial[192:], -1) + shift_far(partial[128:192])
    logits = jnp.sum(swap(block.reshape(4, 16, quarter), "h"), axis=0)

    row_labels = lax.dynamic_slice(labels, (h * 16,), (16,))
    column = jnp.arange(quarter, dtype=jnp.int32) + j * columns + x * quarter
    onehot = (column[None, :] == row_labels[:, None]).astype(jnp.float32)
    peak = jnp.max(logits, axis=1)
    shifted = jnp.exp(logits - peak[:, None])
    stats = jnp.stack([peak, jnp.sum(shifted, axis=1), jnp.sum(logits * onehot, axis=1)], axis=0)
    stats = spread(stats, XYC, 32)
    row_peak = jnp.max(stats[:, 0], axis=0)
    exp_total = jnp.sum(stats[:, 1] * jnp.exp(stats[:, 0] - row_peak[None]), axis=0)
    logprobs = jnp.sum(stats[:, 2], axis=0) - row_peak - jnp.log(exp_total)
    scale = jnp.exp(peak - row_peak) / exp_total
    grad = onehot - shifted * scale[:, None]

    own = spread(grad, "h", 4).reshape(64, quarter)
    grads = jnp.concatenate([own, shift_z(own, -1), shift_far(own), shift_z(own, 1)], axis=0)

    grad_rows = dot(grads, head, (1, 1), GRAD)
    leaving = dot(deliver, grad_rows, (1, 0), GRAD).reshape(32, 16, wide)
    summed = jnp.sum(swap(leaving, XYC), axis=0)

    grad_head = dot(hidden, grads, (0, 0), GRAD).reshape(4, depth, quarter)
    summed, grad_head_later = lax.optimization_barrier((summed, grad_head))
    grad_weight = jnp.zeros((depth, columns), jnp.float32)
    for s in (0, 1, 3, 2):
        part = lax.dynamic_index_in_dim(grad_head_later if s == 2 else grad_head, (x + s) % 4, 0, False)
        part = shift_x(part, s) if s else part
        grad_weight = lax.dynamic_update_slice(grad_weight, part, (0, (x - s) % 4 * quarter))

    parts = lax.dynamic_update_slice(jnp.zeros((16, META), jnp.float32), logprobs.reshape(4, 4), (h * 4, 0))
    parts = jnp.where(l == x, parts, 0.0)
    arrived = swap(jnp.concatenate([summed, parts], axis=1).reshape(16, 1, wide + META), Z)[:, 0]
    slot = arrived[:, :wide].reshape(16, 4, depth).transpose(1, 0, 2).reshape(width)
    grad_hidden = spread(slot, YC, 8)
    return jnp.sum(arrived[:, wide : wide + 4], axis=0), grad_hidden, grad_weight


def solution(mesh):
    grid = Mesh(mesh.devices.reshape(4, 4, 4, 4, 2), ("x", "h", "l", "y", "c"))
    dp = ("x", "h", "l")
    placed = (P(dp, None), P(dp, YC), P(dp), P(dp), P(dp))
    return jax.shard_map(
        on_device,
        mesh=grid,
        in_specs=placed,
        out_specs=(P(dp), P(dp, None), P(dp, YC)),
        check_vma=False,
    )
```

time: 260 us -> 221 us (0.85)
  waiting for transfers between devices: 120 us -> 70.6 us
  starting transfers between devices: 68.2 us -> 99.2 us
  blocking collectives: 43.2 us -> 19.8 us
  local copies, waits for them, and re-layouts: 13.5 us -> 17.4 us
    all_to_all x8 -> x7, waiting for transfers between devices: 105 us -> 52.8 us  [swap(): return lax.all_to_all(blocks, axes, split_axis=0, concat_axis=0, tiled=True)]
    ppermute x0 -> x8, starting transfers between devices: none -> 28.2 us  [the longest x6 21 us: shift_x(): return lax.ppermute(block, 'x', [(i, (i + step) % 4) for i in range(4)])]
    all_to_all x2 -> x1, blocking collectives: 43.2 us -> 19.8 us  [swap(): return lax.all_to_all(blocks, axes, split_axis=0, concat_axis=0, tiled=True)]
    all_to_all x8 -> x7, starting transfers between devices: 44 us -> 58.1 us  [swap(): return lax.all_to_all(blocks, axes, split_axis=0, concat_axis=0, tiled=True)]
    ppermute x8 -> x4, starting transfers between devices: 24.1 us -> 13 us  [shift_z(): return lax.ppermute(block, Z, [(i, (i + step) % 16) for i in range(16)])]
    ppermute x0 -> x8, waiting for transfers between devices: none -> 8.15 us  [the longest x2 8.13 us: shift_far(): return lax.ppermute(block, ('h', 'l', 'c'), pairs)]
    dynamic_update_slice x0 -> x8, local copies, waits for them, and re-layouts: none -> 6.23 us  [the longest x4 3.12 us: on_device(): head = lax.dynamic_update_slice(head, piece[None], ((x - s) % 4, 0, 0))]
    ppermute x8 -> x4, waiting for transfers between devices: 14.8 us -> 9.62 us  [shift_z(): return lax.ppermute(block, Z, [(i, (i + step) % 16) for i in range(16)])]
  transfers between devices with their start and end apart: 16 -> 19, of which waited for: 13 -> 12; matrix products, arithmetic and copies ran while one was open for 4% -> 7% of each run, Pallas kernels for 0% -> 0%
where the time goes in v6:
time: 221 us; the launch traced here: 220 us
  starting transfers between devices  99.2 us (45%)
  waiting for transfers between devices  70.6 us (32%)
  blocking collectives  19.8 us (9%)
  local copies, waits for them, and re-layouts  17.4 us (8%)
  matrix products  6.77 us (3%)
  other arithmetic  3.19 us (1%)
  between operations  2.57 us (1%)
    all_to_all x7, starting transfers between devices, swap(): return lax.all_to_all(blocks, axes, split_axis=0, concat_axis=0, tiled=True)  58.1 us
    all_to_all x7, waiting for transfers between devices, swap(): return lax.all_to_all(blocks, axes, split_axis=0, concat_axis=0, tiled=True)  52.8 us
    ppermute x6, starting transfers between devices, shift_x(): return lax.ppermute(block, 'x', [(i, (i + step) % 4) for i in range(4)])  21 us
    all_to_all x1, blocking collectives, swap(): return lax.all_to_all(blocks, axes, split_axis=0, concat_axis=0, tiled=True)  19.8 us
    ppermute x4, starting transfers between devices, shift_z(): return lax.ppermute(block, Z, [(i, (i + step) % 16) for i in range(16)])  13 us
    ppermute x4, waiting for transfers between devices, shift_z(): return lax.ppermute(block, Z, [(i, (i + step) % 16) for i in range(16)])  9.62 us
    ppermute x2, waiting for transfers between devices, shift_far(): return lax.ppermute(block, ('h', 'l', 'c'), pairs)  8.13 us
    ppermute x2, starting transfers between devices, shift_far(): return lax.ppermute(block, ('h', 'l', 'c'), pairs)  7.23 us
  transfers between devices with their start and end apart: 19, of which 12 were waited for; matrix products, arithmetic and copies ran while one was open for 7% of the time, Pallas kernels for 0%

profile of v6, /device:TPU:1, one launch (start us, length us, event | category | flops | bytes accessed | tf_op | source)
XLA Modules:
  0.0 219.6 jit_solution(7865967429430860852)
XLA Ops:
  0.7 2.1 constant_dynamic-slice_fusion
  2.8 3.9 %collective-permute-start = (f32[96,1024]{1,0:T(8,128)S(1)}, f32[96,1024]{1,0:T(8,128)S(1)}, u32[]{:S(2)}, u32[]{:S(2)}) collective-permute-start(f32[96,1024]{1,0:T(8,128)S(1)} %get-tuple-element.20), channel_id=1, source_target_pairs={{0,128},{128,256},{256,384},{384,0},{1,129},{129,257},{257,385},{3... | collective-permute-start | bytes 1179656 | tf_op jit(solution)/shard_map/ppermute | solution.py:32
  9.0 14.9 %all-to-all-start = ((f32[16,1,512]{2,1,0:T(1,128)}), f32[16,1,512]{2,1,0:T(1,128)S(1)}, u32[]{:S(2)}, u32[]{:S(2)}) async-start(f32[16,1,512]{2,1,0:T(1,128)} %copy.22), calls=%async_computation | async-start | bytes 65536 | tf_op jit(solution)/shard_map/all_to_all | solution.py:15
  24.0 4.4 %collective-permute-start.1 = (f32[96,1024]{1,0:T(8,128)}, f32[96,1024]{1,0:T(8,128)}, u32[]{:S(2)}, u32[]{:S(2)}) collective-permute-start(f32[96,1024]{1,0:T(8,128)} %get-tuple-element.21), channel_id=1, source_target_pairs={{0,256},{128,384},{256,0},{384,128},{1,257},{129,385},{257,1},{385... | collective-permute-start | bytes 1179656 | tf_op jit(solution)/shard_map/ppermute | solution.py:32
  28.3 3.1 %collective-permute-start.2 = (f32[96,1024]{1,0:T(8,128)S(1)}, f32[96,1024]{1,0:T(8,128)}, u32[]{:S(2)}, u32[]{:S(2)}) collective-permute-start(f32[96,1024]{1,0:T(8,128)S(1)} %get-tuple-element.19), channel_id=1, source_target_pairs={{0,384},{128,0},{256,128},{384,256},{1,385},{129,1},{257,129},{385... | collective-permute-start | bytes 1179656 | tf_op jit(solution)/shard_map/ppermute | solution.py:32
  31.4 4.0 %all-to-all-done = f32[16,1,512]{2,1,0:T(1,128)S(1)} async-done(((f32[16,1,512]{2,1,0:T(1,128)}), f32[16,1,512]{2,1,0:T(1,128)S(1)}, u32[]{:S(2)}, u32[]{:S(2)}) %all-to-all-start) | async-done | bytes 32800 | tf_op jit(solution)/shard_map/all_to_all | solution.py:15
  36.6 9.2 %all-to-all-start.1 = ((f32[32,16,512]{2,1,0:T(8,128)}), f32[32,16,512]{2,1,0:T(8,128)S(1)}, u32[]{:S(2)}, u32[]{:S(2)}) async-start(f32[32,16,512]{2,1,0:T(8,128)} %broadcast_in_dim.107), calls=%async_computation.1 | async-start | bytes 2097152 | tf_op jit(solution)/shard_map/all_to_all | solution.py:15
  49.2 13.4 %all-to-all-done.1 = f32[32,16,512]{2,1,0:T(8,128)S(1)} async-done(((f32[32,16,512]{2,1,0:T(8,128)}), f32[32,16,512]{2,1,0:T(8,128)S(1)}, u32[]{:S(2)}, u32[]{:S(2)}) %all-to-all-start.1) | async-done | bytes 1048608 | tf_op jit(solution)/shard_map/all_to_all | solution.py:15
  66.1 2.8 %collective-permute-start.5 = (f32[64,1024]{1,0:T(8,128)S(1)}, f32[64,1024]{1,0:T(8,128)S(1)}, u32[]{:S(2)}, u32[]{:S(2)}) collective-permute-start(f32[64,1024]{1,0:T(8,128)S(1)} %get-tuple-element.23), channel_id=1, source_target_pairs={{0,16},{1,113},{8,24},{9,121},{16,32},{17,1},{24,40},{25,9},{32,48... | collective-permute-start | bytes 786440 | tf_op jit(solution)/shard_map/ppermute | solution.py:28
  68.9 2.5 %collective-permute-start.4 = (f32[64,1024]{1,0:T(8,128)S(1)}, f32[64,1024]{1,0:T(8,128)S(1)}, u32[]{:S(2)}, u32[]{:S(2)}) collective-permute-start(f32[64,1024]{1,0:T(8,128)S(1)} %get-tuple-element.24), channel_id=1, source_target_pairs={{0,120},{8,0},{16,8},{24,16},{32,24},{40,32},{48,40},{56,48},{64,5... | collective-permute-start | bytes 786440 | tf_op jit(solution)/shard_map/ppermute | solution.py:23
  71.4 2.7 %collective-permute-start.3 = (f32[64,1024]{1,0:T(8,128)S(1)}, f32[64,1024]{1,0:T(8,128)S(1)}, u32[]{:S(2)}, u32[]{:S(2)}) collective-permute-start(f32[64,1024]{1,0:T(8,128)S(1)} %get-tuple-element.22), channel_id=1, source_target_pairs={{0,8},{8,16},{16,24},{24,32},{32,40},{40,48},{48,56},{56,64},{64,7... | collective-permute-start | bytes 786440 | tf_op jit(solution)/shard_map/ppermute | solution.py:23
  74.2 4.8 %collective-permute-done.5 = f32[64,1024]{1,0:T(8,128)S(1)} collective-permute-done((f32[64,1024]{1,0:T(8,128)S(1)}, f32[64,1024]{1,0:T(8,128)S(1)}, u32[]{:S(2)}, u32[]{:S(2)}) %collective-permute-start.5) | collective-permute-done | bytes 262176 | tf_op jit(solution)/shard_map/ppermute | solution.py:28
  78.9 3.4 %collective-permute-done.4 = f32[64,1024]{1,0:T(8,128)S(1)} collective-permute-done((f32[64,1024]{1,0:T(8,128)S(1)}, f32[64,1024]{1,0:T(8,128)S(1)}, u32[]{:S(2)}, u32[]{:S(2)}) %collective-permute-start.4) | collective-permute-done | bytes 262176 | tf_op jit(solution)/shard_map/ppermute | solution.py:23
  83.2 7.7 %all-to-all-start.2 = ((f32[4,16,1024]{2,1,0:T(8,128)}), f32[4,16,1024]{2,1,0:T(8,128)S(1)}, u32[]{:S(2)}, u32[]{:S(2)}) async-start(f32[4,16,1024]{2,1,0:T(8,128)} %bitcast.8), calls=%async_computation.2 | async-start | bytes 524288 | tf_op jit(solution)/shard_map/all_to_all | solution.py:15
  91.3 12.7 %all-to-all-done.2 = f32[4,16,1024]{2,1,0:T(8,128)S(1)} async-done(((f32[4,16,1024]{2,1,0:T(8,128)}), f32[4,16,1024]{2,1,0:T(8,128)S(1)}, u32[]{:S(2)}, u32[]{:S(2)}) %all-to-all-start.2) | async-done | bytes 262176 | tf_op jit(solution)/shard_map/all_to_all | solution.py:15
  105.0 13.1 %all-to-all-start.3 = ((f32[32,3,16]{2,1,0:T(4,128)}), f32[32,3,16]{2,1,0:T(4,128)S(1)}, u32[]{:S(2)}, u32[]{:S(2)}) async-start(f32[32,3,16]{2,1,0:T(4,128)} %broadcast_in_dim.119), calls=%async_computation.3 | async-start | bytes 131072 | tf_op jit(solution)/shard_map/all_to_all | solution.py:15
  118.2 7.4 %all-to-all-done.3 = f32[32,3,16]{2,1,0:T(4,128)S(1)} async-done(((f32[32,3,16]{2,1,0:T(4,128)}), f32[32,3,16]{2,1,0:T(4,128)S(1)}, u32[]{:S(2)}, u32[]{:S(2)}) %all-to-all-start.3) | async-done | bytes 6176 | tf_op jit(solution)/shard_map/all_to_all | solution.py:15
  125.8 19.8 %all_to_all.44 = f32[4,16,1024]{2,1,0:T(8,128)S(1)} all-to-all(f32[4,16,1024]{2,1,0:T(8,128)S(1)} %broadcast_in_dim.120), channel_id=1, replica_groups=mesh['x'=4,'h'=4,'l'=4,'y'=4,'c'=2] {'h'}, dimensions={0} | all-to-all | bytes 524288 | tf_op jit(solution)/shard_map/all_to_all | solution.py:15
  145.6 4.3 %collective-permute-start.8 = (f32[64,1024]{1,0:T(8,128)S(1)}, f32[64,1024]{1,0:T(8,128)S(1)}, u32[]{:S(2)}, u32[]{:S(2)}) collective-permute-start(f32[64,1024]{1,0:T(8,128)S(1)} %bitcast.55), channel_id=1, source_target_pairs={{0,8},{8,16},{16,24},{24,32},{32,40},{40,48},{48,56},{56,64},{64,7... | collective-permute-start | bytes 786440 | tf_op jit(solution)/shard_map/ppermute | solution.py:23
  149.9 4.5 %collective-permute-start.7 = (f32[64,1024]{1,0:T(8,128)S(1)}, f32[64,1024]{1,0:T(8,128)S(1)}, u32[]{:S(2)}, u32[]{:S(2)}) collective-permute-start(f32[64,1024]{1,0:T(8,128)S(1)} %bitcast.56), channel_id=1, source_target_pairs={{0,16},{1,113},{8,24},{9,121},{16,32},{17,1},{24,40},{25,9},{32,48... | collective-permute-start | bytes 786440 | tf_op jit(solution)/shard_map/ppermute | solution.py:28
  154.4 3.4 %collective-permute-start.6 = (f32[64,1024]{1,0:T(8,128)S(1)}, f32[64,1024]{1,0:T(8,128)S(1)}, u32[]{:S(2)}, u32[]{:S(2)}) collective-permute-start(f32[64,1024]{1,0:T(8,128)S(1)} %bitcast.57), channel_id=1, source_target_pairs={{0,120},{8,0},{16,8},{24,16},{32,24},{40,32},{48,40},{56,48},{64,5... | collective-permute-start | bytes 786440 | tf_op jit(solution)/shard_map/ppermute | solution.py:23
  158.1 3.4 %collective-permute-done.7 = f32[64,1024]{1,0:T(8,128)S(1)} collective-permute-done((f32[64,1024]{1,0:T(8,128)S(1)}, f32[64,1024]{1,0:T(8,128)S(1)}, u32[]{:S(2)}, u32[]{:S(2)}) %collective-permute-start.7) | collective-permute-done | bytes 262176 | tf_op jit(solution)/shard_map/ppermute | solution.py:28
  161.5 6.2 %collective-permute-done.6 = f32[64,1024]{1,0:T(8,128)S(1)} collective-permute-done((f32[64,1024]{1,0:T(8,128)S(1)}, f32[64,1024]{1,0:T(8,128)S(1)}, u32[]{:S(2)}, u32[]{:S(2)}) %collective-permute-start.6) | collective-permute-done | bytes 262176 | tf_op jit(solution)/shard_map/ppermute | solution.py:23
  170.0 3.9 %all-to-all-start.5 = ((f32[32,16,384]{2,1,0:T(8,128)}), f32[32,16,384]{2,1,0:T(8,128)S(1)}, u32[]{:S(2)}, u32[]{:S(2)}) async-start(f32[32,16,384]{2,1,0:T(8,128)} %bitcast.15), calls=%async_computation.5 | async-start | bytes 1572864 | tf_op jit(solution)/shard_map/all_to_all | solution.py:15
  176.8 3.3 %collective-permute-start.9 = (f32[96,1024]{1,0:T(8,128)}, f32[96,1024]{1,0:T(8,128)}, u32[]{:S(2)}, u32[]{:S(2)}) collective-permute-start(f32[96,1024]{1,0:T(8,128)} %get-tuple-element.18), channel_id=1, source_target_pairs={{0,128},{128,256},{256,384},{384,0},{1,129},{129,257},{257,385},{3... | collective-permute-start | bytes 1179656 | tf_op jit(solution)/shard_map/ppermute | solution.py:32
  180.6 3.2 %collective-permute-start.10 = (f32[96,1024]{1,0:T(8,128)}, f32[96,1024]{1,0:T(8,128)}, u32[]{:S(2)}, u32[]{:S(2)}) collective-permute-start(f32[96,1024]{1,0:T(8,128)} %get-tuple-element.17), channel_id=1, source_target_pairs={{0,384},{128,0},{256,128},{384,256},{1,385},{129,1},{257,129},{385... | collective-permute-start | bytes 1179656 | tf_op jit(solution)/shard_map/ppermute | solution.py:32
  183.8 4.6 %all-to-all-done.5 = f32[32,16,384]{2,1,0:T(8,128)S(1)} async-done(((f32[32,16,384]{2,1,0:T(8,128)}), f32[32,16,384]{2,1,0:T(8,128)S(1)}, u32[]{:S(2)}, u32[]{:S(2)}) %all-to-all-start.5) | async-done | bytes 786464 | tf_op jit(solution)/shard_map/all_to_all | solution.py:15
  189.1 4.4 %all-to-all-start.6 = ((f32[16,1,512]{2,1,0:T(1,128)}), f32[16,1,512]{2,1,0:T(1,128)S(1)}, u32[]{:S(2)}, u32[]{:S(2)}) async-start(f32[16,1,512]{2,1,0:T(1,128)} %reshape.273), calls=%async_computation.6 | async-start | bytes 65536 | tf_op jit(solution)/shard_map/all_to_all | solution.py:15
  194.3 3.0 %collective-permute-start.11 = (f32[96,1024]{1,0:T(8,128)}, f32[96,1024]{1,0:T(8,128)}, u32[]{:S(2)}, u32[]{:S(2)}) collective-permute-start(f32[96,1024]{1,0:T(8,128)} %dynamic-slice_bitcast_fusion), channel_id=1, source_target_pairs={{0,256},{128,384},{256,0},{384,128},{1,257},{129,385},{257,1},{385... | collective-permute-start | bytes 1179656 | tf_op jit(solution)/shard_map/ppermute | solution.py:32
  198.5 6.4 %all-to-all-done.6 = f32[16,1,512]{2,1,0:T(1,128)S(1)} async-done(((f32[16,1,512]{2,1,0:T(1,128)}), f32[16,1,512]{2,1,0:T(1,128)S(1)}, u32[]{:S(2)}, u32[]{:S(2)}) %all-to-all-start.6) | async-done | bytes 32800 | tf_op jit(solution)/shard_map/all_to_all | solution.py:15
  205.9 4.9 %all-to-all-start.7 = ((f32[8,1,6144]{2,1,0:T(1,128)}), f32[8,1,6144]{2,1,0:T(1,128)S(1)}, u32[]{:S(2)}, u32[]{:S(2)}) async-start(f32[8,1,6144]{2,1,0:T(1,128)} %broadcast_in_dim.123), calls=%async_computation.7 | async-start | bytes 393216 | tf_op jit(solution)/shard_map/all_to_all | solution.py:15
  212.4 4.3 %all-to-all-done.7 = f32[8,1,6144]{2,1,0:T(1,128)S(1)} async-done(((f32[8,1,6144]{2,1,0:T(1,128)}), f32[8,1,6144]{2,1,0:T(1,128)S(1)}, u32[]{:S(2)}, u32[]{:S(2)}) %all-to-all-start.7) | async-done | bytes 196640 | tf_op jit(solution)/shard_map/all_to_all | solution.py:15
  (93 shorter events, 25.4 us)
Async XLA Ops:
  0.6 7.5 %copy-start = (f32[8,6144]{1,0:T(8,128)S(1)}, f32[8,6144]{1,0:T(8,128)}, u32[]{:S(2)}) copy-start(f32[8,6144]{1,0:T(8,128)} %param.5) | copy-start | bytes 589828
  0.6 7.4 %copy-start.8 = (s32[8]{0:T(128)S(1)}, s32[8]{0:T(128)}, u32[]{:S(2)}) copy-start(s32[8]{0:T(128)} %param.8) | copy-start | bytes 100
  2.8 32.7 %collective-permute-start = (f32[96,1024]{1,0:T(8,128)S(1)}, f32[96,1024]{1,0:T(8,128)S(1)}, u32[]{:S(2)}, u32[]{:S(2)}) collective-permute-start(f32[96,1024]{1,0:T(8,128)S(1)} %get-tuple-element.20), channel_id=1, source_target_pairs={{0,128},{128,256},{256,384},{384,0},{1,129},{129,257},{257,385},{3... | collective-permute-start | bytes 1179656 | tf_op jit(solution)/shard_map/ppermute | solution.py:32
  9.0 26.4 %all-to-all-start = ((f32[16,1,512]{2,1,0:T(1,128)}), f32[16,1,512]{2,1,0:T(1,128)S(1)}, u32[]{:S(2)}, u32[]{:S(2)}) async-start(f32[16,1,512]{2,1,0:T(1,128)} %copy.22), calls=%async_computation | async-start | bytes 65536 | tf_op jit(solution)/shard_map/all_to_all | solution.py:15
  24.0 23.2 %collective-permute-start.1 = (f32[96,1024]{1,0:T(8,128)}, f32[96,1024]{1,0:T(8,128)}, u32[]{:S(2)}, u32[]{:S(2)}) collective-permute-start(f32[96,1024]{1,0:T(8,128)} %get-tuple-element.21), channel_id=1, source_target_pairs={{0,256},{128,384},{256,0},{384,128},{1,257},{129,385},{257,1},{385... | collective-permute-start | bytes 1179656 | tf_op jit(solution)/shard_map/ppermute | solution.py:32
  28.3 19.9 %collective-permute-start.2 = (f32[96,1024]{1,0:T(8,128)S(1)}, f32[96,1024]{1,0:T(8,128)}, u32[]{:S(2)}, u32[]{:S(2)}) collective-permute-start(f32[96,1024]{1,0:T(8,128)S(1)} %get-tuple-element.19), channel_id=1, source_target_pairs={{0,384},{128,0},{256,128},{384,256},{1,385},{129,1},{257,129},{385... | collective-permute-start | bytes 1179656 | tf_op jit(solution)/shard_map/ppermute | solution.py:32
  35.5 1.1 copy-start.6
  36.6 26.1 %all-to-all-start.1 = ((f32[32,16,512]{2,1,0:T(8,128)}), f32[32,16,512]{2,1,0:T(8,128)S(1)}, u32[]{:S(2)}, u32[]{:S(2)}) async-start(f32[32,16,512]{2,1,0:T(8,128)} %broadcast_in_dim.107), calls=%async_computation.1 | async-start | bytes 2097152 | tf_op jit(solution)/shard_map/all_to_all | solution.py:15
  45.9 1.2 copy-start.7
  66.1 12.9 %collective-permute-start.5 = (f32[64,1024]{1,0:T(8,128)S(1)}, f32[64,1024]{1,0:T(8,128)S(1)}, u32[]{:S(2)}, u32[]{:S(2)}) collective-permute-start(f32[64,1024]{1,0:T(8,128)S(1)} %get-tuple-element.23), channel_id=1, source_target_pairs={{0,16},{1,113},{8,24},{9,121},{16,32},{17,1},{24,40},{25,9},{32,48... | collective-permute-start | bytes 786440 | tf_op jit(solution)/shard_map/ppermute | solution.py:28
  68.9 13.5 %collective-permute-start.4 = (f32[64,1024]{1,0:T(8,128)S(1)}, f32[64,1024]{1,0:T(8,128)S(1)}, u32[]{:S(2)}, u32[]{:S(2)}) collective-permute-start(f32[64,1024]{1,0:T(8,128)S(1)} %get-tuple-element.24), channel_id=1, source_target_pairs={{0,120},{8,0},{16,8},{24,16},{32,24},{40,32},{48,40},{56,48},{64,5... | collective-permute-start | bytes 786440 | tf_op jit(solution)/shard_map/ppermute | solution.py:23
  71.4 11.0 %collective-permute-start.3 = (f32[64,1024]{1,0:T(8,128)S(1)}, f32[64,1024]{1,0:T(8,128)S(1)}, u32[]{:S(2)}, u32[]{:S(2)}) collective-permute-start(f32[64,1024]{1,0:T(8,128)S(1)} %get-tuple-element.22), channel_id=1, source_target_pairs={{0,8},{8,16},{16,24},{24,32},{32,40},{40,48},{48,56},{56,64},{64,7... | collective-permute-start | bytes 786440 | tf_op jit(solution)/shard_map/ppermute | solution.py:23
  83.2 20.9 %all-to-all-start.2 = ((f32[4,16,1024]{2,1,0:T(8,128)}), f32[4,16,1024]{2,1,0:T(8,128)S(1)}, u32[]{:S(2)}, u32[]{:S(2)}) async-start(f32[4,16,1024]{2,1,0:T(8,128)} %bitcast.8), calls=%async_computation.2 | async-start | bytes 524288 | tf_op jit(solution)/shard_map/all_to_all | solution.py:15
  105.0 20.5 %all-to-all-start.3 = ((f32[32,3,16]{2,1,0:T(4,128)}), f32[32,3,16]{2,1,0:T(4,128)S(1)}, u32[]{:S(2)}, u32[]{:S(2)}) async-start(f32[32,3,16]{2,1,0:T(4,128)} %broadcast_in_dim.119), calls=%async_computation.3 | async-start | bytes 131072 | tf_op jit(solution)/shard_map/all_to_all | solution.py:15
  145.6 12.5 %collective-permute-start.8 = (f32[64,1024]{1,0:T(8,128)S(1)}, f32[64,1024]{1,0:T(8,128)S(1)}, u32[]{:S(2)}, u32[]{:S(2)}) collective-permute-start(f32[64,1024]{1,0:T(8,128)S(1)} %bitcast.55), channel_id=1, source_target_pairs={{0,8},{8,16},{16,24},{24,32},{32,40},{40,48},{48,56},{56,64},{64,7... | collective-permute-start | bytes 786440 | tf_op jit(solution)/shard_map/ppermute | solution.py:23
  149.9 11.6 %collective-permute-start.7 = (f32[64,1024]{1,0:T(8,128)S(1)}, f32[64,1024]{1,0:T(8,128)S(1)}, u32[]{:S(2)}, u32[]{:S(2)}) collective-permute-start(f32[64,1024]{1,0:T(8,128)S(1)} %bitcast.56), channel_id=1, source_target_pairs={{0,16},{1,113},{8,24},{9,121},{16,32},{17,1},{24,40},{25,9},{32,48... | collective-permute-start | bytes 786440 | tf_op jit(solution)/shard_map/ppermute | solution.py:28
  154.4 13.3 %collective-permute-start.6 = (f32[64,1024]{1,0:T(8,128)S(1)}, f32[64,1024]{1,0:T(8,128)S(1)}, u32[]{:S(2)}, u32[]{:S(2)}) collective-permute-start(f32[64,1024]{1,0:T(8,128)S(1)} %bitcast.57), channel_id=1, source_target_pairs={{0,120},{8,0},{16,8},{24,16},{32,24},{40,32},{48,40},{56,48},{64,5... | collective-permute-start | bytes 786440 | tf_op jit(solution)/shard_map/ppermute | solution.py:23
  158.1 11.9 %copy-start.2 = (f32[64,1024]{1,0:T(8,128)}, f32[64,1024]{1,0:T(8,128)S(1)}, u32[]{:S(2)}) copy-start(f32[64,1024]{1,0:T(8,128)S(1)} %collective-permute-done.8) | copy-start | bytes 786436
  161.5 8.6 %copy-start.4 = (f32[64,1024]{1,0:T(8,128)}, f32[64,1024]{1,0:T(8,128)S(1)}, u32[]{:S(2)}) copy-start(f32[64,1024]{1,0:T(8,128)S(1)} %collective-permute-done.7) | copy-start | bytes 786436
  167.6 2.4 %copy-start.5 = (f32[64,1024]{1,0:T(8,128)}, f32[64,1024]{1,0:T(8,128)S(1)}, u32[]{:S(2)}) copy-start(f32[64,1024]{1,0:T(8,128)S(1)} %collective-permute-done.6) | copy-start | bytes 786436
  170.0 3.9 %copy-start.3 = (f32[64,1024]{1,0:T(8,128)S(1)}, f32[64,1024]{1,0:T(8,128)}, u32[]{:S(2)}) copy-start(f32[64,1024]{1,0:T(8,128)} %copy-done.2) | copy-start | bytes 786436
  170.0 18.4 %all-to-all-start.5 = ((f32[32,16,384]{2,1,0:T(8,128)}), f32[32,16,384]{2,1,0:T(8,128)S(1)}, u32[]{:S(2)}, u32[]{:S(2)}) async-start(f32[32,16,384]{2,1,0:T(8,128)} %bitcast.15), calls=%async_computation.5 | async-start | bytes 1572864 | tf_op jit(solution)/shard_map/all_to_all | solution.py:15
  176.8 20.7 %collective-permute-start.9 = (f32[96,1024]{1,0:T(8,128)}, f32[96,1024]{1,0:T(8,128)}, u32[]{:S(2)}, u32[]{:S(2)}) collective-permute-start(f32[96,1024]{1,0:T(8,128)} %get-tuple-element.18), channel_id=1, source_target_pairs={{0,128},{128,256},{256,384},{384,0},{1,129},{129,257},{257,385},{3... | collective-permute-start | bytes 1179656 | tf_op jit(solution)/shard_map/ppermute | solution.py:32
  180.6 30.2 %collective-permute-start.10 = (f32[96,1024]{1,0:T(8,128)}, f32[96,1024]{1,0:T(8,128)}, u32[]{:S(2)}, u32[]{:S(2)}) collective-permute-start(f32[96,1024]{1,0:T(8,128)} %get-tuple-element.17), channel_id=1, source_target_pairs={{0,384},{128,0},{256,128},{384,256},{1,385},{129,1},{257,129},{385... | collective-permute-start | bytes 1179656 | tf_op jit(solution)/shard_map/ppermute | solution.py:32
  189.1 15.8 %all-to-all-start.6 = ((f32[16,1,512]{2,1,0:T(1,128)}), f32[16,1,512]{2,1,0:T(1,128)S(1)}, u32[]{:S(2)}, u32[]{:S(2)}) async-start(f32[16,1,512]{2,1,0:T(1,128)} %reshape.273), calls=%async_computation.6 | async-start | bytes 65536 | tf_op jit(solution)/shard_map/all_to_all | solution.py:15
  194.3 23.2 %collective-permute-start.11 = (f32[96,1024]{1,0:T(8,128)}, f32[96,1024]{1,0:T(8,128)}, u32[]{:S(2)}, u32[]{:S(2)}) collective-permute-start(f32[96,1024]{1,0:T(8,128)} %dynamic-slice_bitcast_fusion), channel_id=1, source_target_pairs={{0,256},{128,384},{256,0},{384,128},{1,257},{129,385},{257,1},{385... | collective-permute-start | bytes 1179656 | tf_op jit(solution)/shard_map/ppermute | solution.py:32
  205.9 10.8 %all-to-all-start.7 = ((f32[8,1,6144]{2,1,0:T(1,128)}), f32[8,1,6144]{2,1,0:T(1,128)S(1)}, u32[]{:S(2)}, u32[]{:S(2)}) async-start(f32[8,1,6144]{2,1,0:T(1,128)} %broadcast_in_dim.123), calls=%async_computation.7 | async-start | bytes 393216 | tf_op jit(solution)/shard_map/all_to_all | solution.py:15
  218.5 1.1 copy-start.1

commit v7 on v6

--- a/solution.py
+++ b/solution.py
@@ -23,8 +23,9 @@
     return lax.ppermute(block, Z, [(i, (i + step) % 16) for i in range(16)])
 
 
-def shift_far(block):
-    pairs = [(2 * i + c, 2 * ((i + 2 - 4 * c) % 16) + c) for i in range(16) for c in range(2)]
+def shift_far(block, sign):
+    step = [2 * sign, -2 * sign]
+    pairs = [(2 * i + c, 2 * ((i + step[c]) % 16) + c) for i in range(16) for c in range(2)]
     return lax.ppermute(block, ("h", "l", "c"), pairs)
 
 
@@ -43,17 +44,18 @@
     quarter = columns // 4
     wide = 4 * depth
     x, h, l = lax.axis_index("x"), lax.axis_index("h"), lax.axis_index("l")
-    j = lax.axis_index(YC)
+    j, c = lax.axis_index(YC), lax.axis_index("c")
 
-    def cut(s):
-        return lax.dynamic_slice(weight, (0, (x + s) % 4 * quarter), (depth, quarter))
-
-    pieces = [cut(0), *(shift_x(cut(s), s) for s in range(1, 4))]
+    def cut(array, s):
+        return lax.dynamic_slice(array, (0, (x + s) % 4 * quarter), (depth, quarter))
 
     row = lax.dynamic_slice(responses, (j, 0), (1, width)).reshape(4, 16, depth)
     notes = jnp.pad(jnp.concatenate([targets, lengths, owners]).astype(jnp.float32), (0, META - 10))
     notes = jnp.broadcast_to(notes, (16, META))
     packed = jnp.concatenate([row.transpose(1, 0, 2).reshape(16, wide), notes], axis=1)
+    packed, weight_later = lax.optimization_barrier((packed, weight))
+    first = shift_x(cut(weight, 1), 1)
+    pieces = [cut(weight_later, 0), first, shift_x(cut(weight_later, 2), 2), shift_x(cut(weight_later, 3), 3)]
     mine = swap(packed.reshape(16, 1, wide + META), Z).reshape(16, wide + META)
     mine, pieces[1] = lax.optimization_barrier((mine, pieces[1]))
     slots = spread(mine, XYC, 32).reshape(512, wide + META)
@@ -66,7 +68,11 @@
     slot_target = jnp.sum(jnp.where(jnp.arange(10)[None, :] == slot_j[:, None], notes_all, 0), axis=1)
     before = (source[None, :] < source[:, None]) & (slot_j[None, :] == 0)
     starts = jnp.sum(jnp.where(before, slot_length[None, :], 0), axis=1)
-    rank = jnp.where(slot_j < slot_length, (starts + slot_j - 64 * l) % 256, -1)
+    rank = starts + slot_j
+    turn = (rank // 64 - l) % 4
+    partner = h * 4 + l + jnp.where(turn == 3, -1, jnp.where((turn == 2) & (c == 1), -2, turn))
+    group = (rank // 16 - partner % 16 // 4) % 4
+    rank = jnp.where(slot_j < slot_length, turn * 64 + group * 16 + rank % 16, -1)
     rows = jnp.arange(256, dtype=jnp.int32)
     select = rank[None, :] == rows[:, None]
     hidden = dot(select.astype(jnp.float32), slots[:, :wide])
@@ -81,10 +87,10 @@
     head = lax.optimization_barrier(head.reshape(wide, quarter))
 
     partial = dot(hidden, head)
-    block = partial[:64] + shift_z(partial[64:128], 1) + shift_z(partial[192:], -1) + shift_far(partial[128:192])
-    logits = jnp.sum(swap(block.reshape(4, 16, quarter), "h"), axis=0)
+    block = partial[:64] + shift_z(partial[64:128], 1) + shift_z(partial[192:], -1) + shift_far(partial[128:192], 1)
+    logits = block[:16] + shift_z(block[16:32], 4) + shift_z(block[32:48], 8) + shift_z(block[48:], -4)
 
-    row_labels = lax.dynamic_slice(labels, (h * 16,), (16,))
+    row_labels = labels[:16]
     column = jnp.arange(quarter, dtype=jnp.int32) + j * columns + x * quarter
     onehot = (column[None, :] == row_labels[:, None]).astype(jnp.float32)
     peak = jnp.max(logits, axis=1)
@@ -97,8 +103,8 @@
     scale = jnp.exp(peak - row_peak) / exp_total
     grad = onehot - shifted * scale[:, None]
 
-    own = spread(grad, "h", 4).reshape(64, quarter)
-    grads = jnp.concatenate([own, shift_z(own, -1), shift_far(own), shift_z(own, 1)], axis=0)
+    own = jnp.concatenate([grad, shift_z(grad, -4), shift_z(grad, 8), shift_z(grad, 4)], axis=0)
+    grads = jnp.concatenate([own, shift_z(own, -1), shift_far(own, -1), shift_z(own, 1)], axis=0)
 
     grad_rows = dot(grads, head, (1, 1), GRAD)
     leaving = dot(deliver, grad_rows, (1, 0), GRAD).reshape(32, 16, wide)

time: 221 us -> 233 us (1.054)
  starting transfers between devices: 99.2 us -> 121 us
  blocking collectives: 19.8 us -> 0 us
  waiting for transfers between devices: 70.6 us -> 75.4 us
  local copies, waits for them, and re-layouts: 17.4 us -> 20.4 us
    ppermute x4 -> x10, starting transfers between devices: 13 us -> 43.7 us  [shift_z(): return lax.ppermute(block, Z, [(i, (i + step) % 16) for i in range(16)])]
    ppermute x4 -> x10, waiting for transfers between devices: 9.62 us -> 30.5 us  [shift_z(): return lax.ppermute(block, Z, [(i, (i + step) % 16) for i in range(16)])]
    all_to_all x1 -> x0, blocking collectives: 19.8 us -> none  [swap(): return lax.all_to_all(blocks, axes, split_axis=0, concat_axis=0, tiled=True)]
    all_to_all x7 -> x6, waiting for transfers between devices: 52.8 us -> 38.7 us  [swap(): return lax.all_to_all(blocks, axes, split_axis=0, concat_axis=0, tiled=True)]
    all_to_all x7 -> x6, starting transfers between devices: 58.1 us -> 46.7 us  [swap(): return lax.all_to_all(blocks, axes, split_axis=0, concat_axis=0, tiled=True)]
    ppermute x2, starting transfers between devices: 7.23 us -> 9.79 us  [shift_far(): return lax.ppermute(block, ('h', 'l', 'c'), pairs)]
  transfers between devices with their start and end apart: 19 -> 24, of which waited for: 12 -> 16; matrix products, arithmetic and copies ran while one was open for 7% -> 8% of each run, Pallas kernels for 0% -> 0%
where the time goes in v7:
time: 233 us; the launch traced here: 232 us
  starting transfers between devices  121 us (52%)
  waiting for transfers between devices  75.4 us (32%)
  local copies, waits for them, and re-layouts  20.4 us (9%)
  matrix products  6.7 us (3%)
  other arithmetic  5.41 us (2%)
  between operations  2.63 us (1%)
    all_to_all x6, starting transfers between devices, swap(): return lax.all_to_all(blocks, axes, split_axis=0, concat_axis=0, tiled=True)  46.7 us
    ppermute x10, starting transfers between devices, shift_z(): return lax.ppermute(block, Z, [(i, (i + step) % 16) for i in range(16)])  43.7 us
    all_to_all x6, waiting for transfers between devices, swap(): return lax.all_to_all(blocks, axes, split_axis=0, concat_axis=0, tiled=True)  38.7 us
    ppermute x10, waiting for transfers between devices, shift_z(): return lax.ppermute(block, Z, [(i, (i + step) % 16) for i in range(16)])  30.5 us
    ppermute x6, starting transfers between devices, shift_x(): return lax.ppermute(block, 'x', [(i, (i + step) % 4) for i in range(4)])  21.2 us
    ppermute x2, starting transfers between devices, shift_far(): return lax.ppermute(block, ('h', 'l', 'c'), pairs)  9.79 us
    dot_general x5, matrix products, dot(): lax.dot_general(a, b, dims, precision=precision, preferred_element_type=j...  6.7 us
    ppermute x2, waiting for transfers between devices, shift_far(): return lax.ppermute(block, ('h', 'l', 'c'), pairs)  6.22 us
  transfers between devices with their start and end apart: 24, of which 16 were waited for; matrix products, arithmetic and copies ran while one was open for 8% of the time, Pallas kernels for 0%

profile of v7, /device:TPU:1, one launch (start us, length us, event | category | flops | bytes accessed | tf_op | source)
XLA Modules:
  0.0 231.9 jit_solution(13364605875005605102)
XLA Ops:
  1.7 3.9 %collective-permute-start = (f32[96,1024]{1,0:T(8,128)S(1)}, f32[96,1024]{1,0:T(8,128)S(1)}, u32[]{:S(2)}, u32[]{:S(2)}) collective-permute-start(f32[96,1024]{1,0:T(8,128)S(1)} %constant_dynamic-slice_fusion.2), channel_id=1, source_target_pairs={{0,128},{128,256},{256,384},{384,0},{1,129},{129,257},{257,385},{3... | collective-permute-start | bytes 1179656 | tf_op jit(solution)/shard_map/ppermute | solution.py:33
  8.7 14.9 %all-to-all-start = ((f32[16,1,512]{2,1,0:T(1,128)}), f32[16,1,512]{2,1,0:T(1,128)S(1)}, u32[]{:S(2)}, u32[]{:S(2)}) async-start(f32[16,1,512]{2,1,0:T(1,128)} %copy.22), calls=%async_computation | async-start | bytes 65536 | tf_op jit(solution)/shard_map/all_to_all | solution.py:15
  25.7 4.3 %collective-permute-start.1 = (f32[96,1024]{1,0:T(8,128)}, f32[96,1024]{1,0:T(8,128)}, u32[]{:S(2)}, u32[]{:S(2)}) collective-permute-start(f32[96,1024]{1,0:T(8,128)} %get-tuple-element.28), channel_id=1, source_target_pairs={{0,256},{128,384},{256,0},{384,128},{1,257},{129,385},{257,1},{385... | collective-permute-start | bytes 1179656 | tf_op jit(solution)/shard_map/ppermute | solution.py:33
  30.0 3.1 %collective-permute-start.2 = (f32[96,1024]{1,0:T(8,128)}, f32[96,1024]{1,0:T(8,128)}, u32[]{:S(2)}, u32[]{:S(2)}) collective-permute-start(f32[96,1024]{1,0:T(8,128)} %get-tuple-element.27), channel_id=1, source_target_pairs={{0,384},{128,0},{256,128},{384,256},{1,385},{129,1},{257,129},{385... | collective-permute-start | bytes 1179656 | tf_op jit(solution)/shard_map/ppermute | solution.py:33
  36.2 9.2 %all-to-all-start.1 = ((f32[32,16,512]{2,1,0:T(8,128)}), f32[32,16,512]{2,1,0:T(8,128)S(1)}, u32[]{:S(2)}, u32[]{:S(2)}) async-start(f32[32,16,512]{2,1,0:T(8,128)} %broadcast_in_dim.106), calls=%async_computation.1 | async-start | bytes 2097152 | tf_op jit(solution)/shard_map/all_to_all | solution.py:15
  48.8 13.5 %all-to-all-done.1 = f32[32,16,512]{2,1,0:T(8,128)S(1)} async-done(((f32[32,16,512]{2,1,0:T(8,128)}), f32[32,16,512]{2,1,0:T(8,128)S(1)}, u32[]{:S(2)}, u32[]{:S(2)}) %all-to-all-start.1) | async-done | bytes 1048608 | tf_op jit(solution)/shard_map/all_to_all | solution.py:15
  68.6 4.3 %collective-permute-start.5 = (f32[64,1024]{1,0:T(8,128)}, f32[64,1024]{1,0:T(8,128)S(1)}, u32[]{:S(2)}, u32[]{:S(2)}) collective-permute-start(f32[64,1024]{1,0:T(8,128)} %get-tuple-element.30), channel_id=1, source_target_pairs={{0,16},{1,113},{8,24},{9,121},{16,32},{17,1},{24,40},{25,9},{32,48... | collective-permute-start | bytes 786440 | tf_op jit(solution)/shard_map/ppermute | solution.py:29
  72.9 3.1 %collective-permute-start.4 = (f32[64,1024]{1,0:T(8,128)}, f32[64,1024]{1,0:T(8,128)}, u32[]{:S(2)}, u32[]{:S(2)}) collective-permute-start(f32[64,1024]{1,0:T(8,128)} %get-tuple-element.31), channel_id=1, source_target_pairs={{0,120},{8,0},{16,8},{24,16},{32,24},{40,32},{48,40},{56,48},{64,5... | collective-permute-start | bytes 786440 | tf_op jit(solution)/shard_map/ppermute | solution.py:23
  81.1 4.6 %collective-permute-done.4 = f32[64,1024]{1,0:T(8,128)} collective-permute-done((f32[64,1024]{1,0:T(8,128)}, f32[64,1024]{1,0:T(8,128)}, u32[]{:S(2)}, u32[]{:S(2)}) %collective-permute-start.4) | collective-permute-done | bytes 262176 | tf_op jit(solution)/shard_map/ppermute | solution.py:23
  88.8 5.8 %collective-permute-start.8 = (f32[16,1024]{1,0:T(8,128)S(1)}, f32[16,1024]{1,0:T(8,128)S(1)}, u32[]{:S(2)}, u32[]{:S(2)}) collective-permute-start(f32[16,1024]{1,0:T(8,128)S(1)} %get-tuple-element.33), channel_id=1, source_target_pairs={{0,96},{8,104},{16,112},{24,120},{32,0},{40,8},{48,16},{56,24},{64... | collective-permute-start | bytes 196616 | tf_op jit(solution)/shard_map/ppermute | solution.py:23
  94.7 5.2 %collective-permute-start.7 = (f32[16,1024]{1,0:T(8,128)S(1)}, f32[16,1024]{1,0:T(8,128)S(1)}, u32[]{:S(2)}, u32[]{:S(2)}) collective-permute-start(f32[16,1024]{1,0:T(8,128)S(1)} %get-tuple-element.34), channel_id=1, source_target_pairs={{0,64},{8,72},{16,80},{24,88},{32,96},{40,104},{48,112},{56,120},{... | collective-permute-start | bytes 196616 | tf_op jit(solution)/shard_map/ppermute | solution.py:23
  99.9 6.1 %collective-permute-start.6 = (f32[16,1024]{1,0:T(8,128)S(1)}, f32[16,1024]{1,0:T(8,128)S(1)}, u32[]{:S(2)}, u32[]{:S(2)}) collective-permute-start(f32[16,1024]{1,0:T(8,128)S(1)} %get-tuple-element.32), channel_id=1, source_target_pairs={{0,32},{8,40},{16,48},{24,56},{32,64},{40,72},{48,80},{56,88},{64,... | collective-permute-start | bytes 196616 | tf_op jit(solution)/shard_map/ppermute | solution.py:23
  106.2 2.9 %collective-permute-done.7 = f32[16,1024]{1,0:T(8,128)S(1)} collective-permute-done((f32[16,1024]{1,0:T(8,128)S(1)}, f32[16,1024]{1,0:T(8,128)S(1)}, u32[]{:S(2)}, u32[]{:S(2)}) %collective-permute-start.7) | collective-permute-done | bytes 65568 | tf_op jit(solution)/shard_map/ppermute | solution.py:23
  109.1 5.1 %collective-permute-done.6 = f32[16,1024]{1,0:T(8,128)S(1)} collective-permute-done((f32[16,1024]{1,0:T(8,128)S(1)}, f32[16,1024]{1,0:T(8,128)S(1)}, u32[]{:S(2)}, u32[]{:S(2)}) %collective-permute-start.6) | collective-permute-done | bytes 65568 | tf_op jit(solution)/shard_map/ppermute | solution.py:23
  115.2 6.5 %all-to-all-start.2 = ((f32[32,3,16]{2,1,0:T(4,128)}), f32[32,3,16]{2,1,0:T(4,128)S(1)}, u32[]{:S(2)}, u32[]{:S(2)}) async-start(f32[32,3,16]{2,1,0:T(4,128)} %broadcast_in_dim.119), calls=%async_computation.2 | async-start | bytes 131072 | tf_op jit(solution)/shard_map/all_to_all | solution.py:15
  122.1 7.0 %all-to-all-done.2 = f32[32,3,16]{2,1,0:T(4,128)S(1)} async-done(((f32[32,3,16]{2,1,0:T(4,128)}), f32[32,3,16]{2,1,0:T(4,128)S(1)}, u32[]{:S(2)}, u32[]{:S(2)}) %all-to-all-start.2) | async-done | bytes 6176 | tf_op jit(solution)/shard_map/all_to_all | solution.py:15
  129.3 4.6 %collective-permute-start.9 = (f32[16,1024]{1,0:T(8,128)S(1)}, f32[16,1024]{1,0:T(8,128)S(1)}, u32[]{:S(2)}, u32[]{:S(2)}) collective-permute-start(f32[16,1024]{1,0:T(8,128)S(1)} %get-tuple-element.22), channel_id=1, source_target_pairs={{0,96},{8,104},{16,112},{24,120},{32,0},{40,8},{48,16},{56,24},{64... | collective-permute-start | bytes 196616 | tf_op jit(solution)/shard_map/ppermute | solution.py:23
  134.0 6.3 %collective-permute-start.10 = (f32[16,1024]{1,0:T(8,128)S(1)}, f32[16,1024]{1,0:T(8,128)S(1)}, u32[]{:S(2)}, u32[]{:S(2)}) collective-permute-start(f32[16,1024]{1,0:T(8,128)S(1)} %get-tuple-element.22), channel_id=1, source_target_pairs={{0,64},{8,72},{16,80},{24,88},{32,96},{40,104},{48,112},{56,120},{... | collective-permute-start | bytes 196616 | tf_op jit(solution)/shard_map/ppermute | solution.py:23
  140.3 6.5 %collective-permute-start.11 = (f32[16,1024]{1,0:T(8,128)S(1)}, f32[16,1024]{1,0:T(8,128)S(1)}, u32[]{:S(2)}, u32[]{:S(2)}) collective-permute-start(f32[16,1024]{1,0:T(8,128)S(1)} %get-tuple-element.22), channel_id=1, source_target_pairs={{0,32},{8,40},{16,48},{24,56},{32,64},{40,72},{48,80},{56,88},{64,... | collective-permute-start | bytes 196616 | tf_op jit(solution)/shard_map/ppermute | solution.py:23
  147.7 7.1 %collective-permute-done.11 = f32[16,1024]{1,0:T(8,128)S(1)} collective-permute-done((f32[16,1024]{1,0:T(8,128)S(1)}, f32[16,1024]{1,0:T(8,128)S(1)}, u32[]{:S(2)}, u32[]{:S(2)}) %collective-permute-start.11) | collective-permute-done | bytes 65568 | tf_op jit(solution)/shard_map/ppermute | solution.py:23
  156.8 5.5 %collective-permute-start.13 = (f32[64,1024]{1,0:T(8,128)S(1)}, f32[64,1024]{1,0:T(8,128)S(1)}, u32[]{:S(2)}, u32[]{:S(2)}) collective-permute-start(f32[64,1024]{1,0:T(8,128)S(1)} %pad_maximum_fusion), channel_id=1, source_target_pairs={{0,112},{1,17},{8,120},{9,25},{16,0},{17,33},{24,8},{25,41},{32,16... | collective-permute-start | bytes 786440 | tf_op jit(solution)/shard_map/ppermute | solution.py:29
  165.4 3.6 %collective-permute-done.13 = f32[64,1024]{1,0:T(8,128)S(1)} collective-permute-done((f32[64,1024]{1,0:T(8,128)S(1)}, f32[64,1024]{1,0:T(8,128)S(1)}, u32[]{:S(2)}, u32[]{:S(2)}) %collective-permute-start.13) | collective-permute-done | bytes 262176 | tf_op jit(solution)/shard_map/ppermute | solution.py:29
  169.1 6.7 %collective-permute-done.14 = f32[64,1024]{1,0:T(8,128)S(1)} collective-permute-done((f32[64,1024]{1,0:T(8,128)S(1)}, f32[64,1024]{1,0:T(8,128)S(1)}, u32[]{:S(2)}, u32[]{:S(2)}) %collective-permute-start.14) | collective-permute-done | bytes 262176 | tf_op jit(solution)/shard_map/ppermute | solution.py:23
  178.2 4.6 %all-to-all-start.3 = ((f32[32,16,384]{2,1,0:T(8,128)}), f32[32,16,384]{2,1,0:T(8,128)}, u32[]{:S(2)}, u32[]{:S(2)}) async-start(f32[32,16,384]{2,1,0:T(8,128)} %bitcast.13), calls=%async_computation.3 | async-start | bytes 1572864 | tf_op jit(solution)/shard_map/all_to_all | solution.py:15
  184.6 3.3 %collective-permute-start.15 = (f32[96,1024]{1,0:T(8,128)}, f32[96,1024]{1,0:T(8,128)}, u32[]{:S(2)}, u32[]{:S(2)}) collective-permute-start(f32[96,1024]{1,0:T(8,128)} %get-tuple-element.26), channel_id=1, source_target_pairs={{0,128},{128,256},{256,384},{384,0},{1,129},{129,257},{257,385},{3... | collective-permute-start | bytes 1179656 | tf_op jit(solution)/shard_map/ppermute | solution.py:33
  188.4 3.2 %collective-permute-start.16 = (f32[96,1024]{1,0:T(8,128)}, f32[96,1024]{1,0:T(8,128)}, u32[]{:S(2)}, u32[]{:S(2)}) collective-permute-start(f32[96,1024]{1,0:T(8,128)} %get-tuple-element.25), channel_id=1, source_target_pairs={{0,384},{128,0},{256,128},{384,256},{1,385},{129,1},{257,129},{385... | collective-permute-start | bytes 1179656 | tf_op jit(solution)/shard_map/ppermute | solution.py:33
  191.6 5.6 %all-to-all-done.3 = f32[32,16,384]{2,1,0:T(8,128)} async-done(((f32[32,16,384]{2,1,0:T(8,128)}), f32[32,16,384]{2,1,0:T(8,128)}, u32[]{:S(2)}, u32[]{:S(2)}) %all-to-all-start.3) | async-done | bytes 786464 | tf_op jit(solution)/shard_map/all_to_all | solution.py:15
  199.1 6.6 %all-to-all-start.4 = ((f32[16,1,512]{2,1,0:T(1,128)}), f32[16,1,512]{2,1,0:T(1,128)S(1)}, u32[]{:S(2)}, u32[]{:S(2)}) async-start(f32[16,1,512]{2,1,0:T(1,128)} %reshape.295), calls=%async_computation.4 | async-start | bytes 65536 | tf_op jit(solution)/shard_map/all_to_all | solution.py:15
  206.5 3.2 %collective-permute-start.17 = (f32[96,1024]{1,0:T(8,128)}, f32[96,1024]{1,0:T(8,128)}, u32[]{:S(2)}, u32[]{:S(2)}) collective-permute-start(f32[96,1024]{1,0:T(8,128)} %dynamic-slice_bitcast_fusion), channel_id=1, source_target_pairs={{0,256},{128,384},{256,0},{384,128},{1,257},{129,385},{257,1},{385... | collective-permute-start | bytes 1179656 | tf_op jit(solution)/shard_map/ppermute | solution.py:33
  211.0 6.3 %all-to-all-done.4 = f32[16,1,512]{2,1,0:T(1,128)S(1)} async-done(((f32[16,1,512]{2,1,0:T(1,128)}), f32[16,1,512]{2,1,0:T(1,128)S(1)}, u32[]{:S(2)}, u32[]{:S(2)}) %all-to-all-start.4) | async-done | bytes 32800 | tf_op jit(solution)/shard_map/all_to_all | solution.py:15
  218.2 4.8 %all-to-all-start.5 = ((f32[8,1,6144]{2,1,0:T(1,128)}), f32[8,1,6144]{2,1,0:T(1,128)S(1)}, u32[]{:S(2)}, u32[]{:S(2)}) async-start(f32[8,1,6144]{2,1,0:T(1,128)} %broadcast_in_dim.122), calls=%async_computation.5 | async-start | bytes 393216 | tf_op jit(solution)/shard_map/all_to_all | solution.py:15
  224.6 4.3 %all-to-all-done.5 = f32[8,1,6144]{2,1,0:T(1,128)S(1)} async-done(((f32[8,1,6144]{2,1,0:T(1,128)}), f32[8,1,6144]{2,1,0:T(1,128)S(1)}, u32[]{:S(2)}, u32[]{:S(2)}) %all-to-all-start.5) | async-done | bytes 196640 | tf_op jit(solution)/shard_map/all_to_all | solution.py:15
  (95 shorter events, 47.2 us)
Async XLA Ops:
  0.6 7.1 %copy-start = (f32[8,6144]{1,0:T(8,128)S(1)}, f32[8,6144]{1,0:T(8,128)}, u32[]{:S(2)}) copy-start(f32[8,6144]{1,0:T(8,128)} %param.5) | copy-start | bytes 589828
  1.7 33.3 %collective-permute-start = (f32[96,1024]{1,0:T(8,128)S(1)}, f32[96,1024]{1,0:T(8,128)S(1)}, u32[]{:S(2)}, u32[]{:S(2)}) collective-permute-start(f32[96,1024]{1,0:T(8,128)S(1)} %constant_dynamic-slice_fusion.2), channel_id=1, source_target_pairs={{0,128},{128,256},{256,384},{384,0},{1,129},{129,257},{257,385},{3... | collective-permute-start | bytes 1179656 | tf_op jit(solution)/shard_map/ppermute | solution.py:33
  8.7 26.4 %all-to-all-start = ((f32[16,1,512]{2,1,0:T(1,128)}), f32[16,1,512]{2,1,0:T(1,128)S(1)}, u32[]{:S(2)}, u32[]{:S(2)}) async-start(f32[16,1,512]{2,1,0:T(1,128)} %copy.22), calls=%async_computation | async-start | bytes 65536 | tf_op jit(solution)/shard_map/all_to_all | solution.py:15
  25.7 21.0 %collective-permute-start.1 = (f32[96,1024]{1,0:T(8,128)}, f32[96,1024]{1,0:T(8,128)}, u32[]{:S(2)}, u32[]{:S(2)}) collective-permute-start(f32[96,1024]{1,0:T(8,128)} %get-tuple-element.28), channel_id=1, source_target_pairs={{0,256},{128,384},{256,0},{384,128},{1,257},{129,385},{257,1},{385... | collective-permute-start | bytes 1179656 | tf_op jit(solution)/shard_map/ppermute | solution.py:33
  30.0 17.7 %collective-permute-start.2 = (f32[96,1024]{1,0:T(8,128)}, f32[96,1024]{1,0:T(8,128)}, u32[]{:S(2)}, u32[]{:S(2)}) collective-permute-start(f32[96,1024]{1,0:T(8,128)} %get-tuple-element.27), channel_id=1, source_target_pairs={{0,384},{128,0},{256,128},{384,256},{1,385},{129,1},{257,129},{385... | collective-permute-start | bytes 1179656 | tf_op jit(solution)/shard_map/ppermute | solution.py:33
  36.2 26.1 %all-to-all-start.1 = ((f32[32,16,512]{2,1,0:T(8,128)}), f32[32,16,512]{2,1,0:T(8,128)S(1)}, u32[]{:S(2)}, u32[]{:S(2)}) async-start(f32[32,16,512]{2,1,0:T(8,128)} %broadcast_in_dim.106), calls=%async_computation.1 | async-start | bytes 2097152 | tf_op jit(solution)/shard_map/all_to_all | solution.py:15
  68.6 12.4 %collective-permute-start.5 = (f32[64,1024]{1,0:T(8,128)}, f32[64,1024]{1,0:T(8,128)S(1)}, u32[]{:S(2)}, u32[]{:S(2)}) collective-permute-start(f32[64,1024]{1,0:T(8,128)} %get-tuple-element.30), channel_id=1, source_target_pairs={{0,16},{1,113},{8,24},{9,121},{16,32},{17,1},{24,40},{25,9},{32,48... | collective-permute-start | bytes 786440 | tf_op jit(solution)/shard_map/ppermute | solution.py:29
  72.9 12.8 %collective-permute-start.4 = (f32[64,1024]{1,0:T(8,128)}, f32[64,1024]{1,0:T(8,128)}, u32[]{:S(2)}, u32[]{:S(2)}) collective-permute-start(f32[64,1024]{1,0:T(8,128)} %get-tuple-element.31), channel_id=1, source_target_pairs={{0,120},{8,0},{16,8},{24,16},{32,24},{40,32},{48,40},{56,48},{64,5... | collective-permute-start | bytes 786440 | tf_op jit(solution)/shard_map/ppermute | solution.py:23
  76.0 11.7 %collective-permute-start.3 = (f32[64,1024]{1,0:T(8,128)}, f32[64,1024]{1,0:T(8,128)}, u32[]{:S(2)}, u32[]{:S(2)}) collective-permute-start(f32[64,1024]{1,0:T(8,128)} %get-tuple-element.29), channel_id=1, source_target_pairs={{0,8},{8,16},{16,24},{24,32},{32,40},{40,48},{48,56},{56,64},{64,7... | collective-permute-start | bytes 786440 | tf_op jit(solution)/shard_map/ppermute | solution.py:23
  88.8 17.4 %collective-permute-start.8 = (f32[16,1024]{1,0:T(8,128)S(1)}, f32[16,1024]{1,0:T(8,128)S(1)}, u32[]{:S(2)}, u32[]{:S(2)}) collective-permute-start(f32[16,1024]{1,0:T(8,128)S(1)} %get-tuple-element.33), channel_id=1, source_target_pairs={{0,96},{8,104},{16,112},{24,120},{32,0},{40,8},{48,16},{56,24},{64... | collective-permute-start | bytes 196616 | tf_op jit(solution)/shard_map/ppermute | solution.py:23
  94.7 14.5 %collective-permute-start.7 = (f32[16,1024]{1,0:T(8,128)S(1)}, f32[16,1024]{1,0:T(8,128)S(1)}, u32[]{:S(2)}, u32[]{:S(2)}) collective-permute-start(f32[16,1024]{1,0:T(8,128)S(1)} %get-tuple-element.34), channel_id=1, source_target_pairs={{0,64},{8,72},{16,80},{24,88},{32,96},{40,104},{48,112},{56,120},{... | collective-permute-start | bytes 196616 | tf_op jit(solution)/shard_map/ppermute | solution.py:23
  99.9 14.3 %collective-permute-start.6 = (f32[16,1024]{1,0:T(8,128)S(1)}, f32[16,1024]{1,0:T(8,128)S(1)}, u32[]{:S(2)}, u32[]{:S(2)}) collective-permute-start(f32[16,1024]{1,0:T(8,128)S(1)} %get-tuple-element.32), channel_id=1, source_target_pairs={{0,32},{8,40},{16,48},{24,56},{32,64},{40,72},{48,80},{56,88},{64,... | collective-permute-start | bytes 196616 | tf_op jit(solution)/shard_map/ppermute | solution.py:23
  115.2 13.9 %all-to-all-start.2 = ((f32[32,3,16]{2,1,0:T(4,128)}), f32[32,3,16]{2,1,0:T(4,128)S(1)}, u32[]{:S(2)}, u32[]{:S(2)}) async-start(f32[32,3,16]{2,1,0:T(4,128)} %broadcast_in_dim.119), calls=%async_computation.2 | async-start | bytes 131072 | tf_op jit(solution)/shard_map/all_to_all | solution.py:15
  129.3 17.4 %collective-permute-start.9 = (f32[16,1024]{1,0:T(8,128)S(1)}, f32[16,1024]{1,0:T(8,128)S(1)}, u32[]{:S(2)}, u32[]{:S(2)}) collective-permute-start(f32[16,1024]{1,0:T(8,128)S(1)} %get-tuple-element.22), channel_id=1, source_target_pairs={{0,96},{8,104},{16,112},{24,120},{32,0},{40,8},{48,16},{56,24},{64... | collective-permute-start | bytes 196616 | tf_op jit(solution)/shard_map/ppermute | solution.py:23
  134.0 13.7 %collective-permute-start.10 = (f32[16,1024]{1,0:T(8,128)S(1)}, f32[16,1024]{1,0:T(8,128)S(1)}, u32[]{:S(2)}, u32[]{:S(2)}) collective-permute-start(f32[16,1024]{1,0:T(8,128)S(1)} %get-tuple-element.22), channel_id=1, source_target_pairs={{0,64},{8,72},{16,80},{24,88},{32,96},{40,104},{48,112},{56,120},{... | collective-permute-start | bytes 196616 | tf_op jit(solution)/shard_map/ppermute | solution.py:23
  140.3 14.5 %collective-permute-start.11 = (f32[16,1024]{1,0:T(8,128)S(1)}, f32[16,1024]{1,0:T(8,128)S(1)}, u32[]{:S(2)}, u32[]{:S(2)}) collective-permute-start(f32[16,1024]{1,0:T(8,128)S(1)} %get-tuple-element.22), channel_id=1, source_target_pairs={{0,32},{8,40},{16,48},{24,56},{32,64},{40,72},{48,80},{56,88},{64,... | collective-permute-start | bytes 196616 | tf_op jit(solution)/shard_map/ppermute | solution.py:23
  154.8 10.6 %collective-permute-start.12 = (f32[64,1024]{1,0:T(8,128)S(1)}, f32[64,1024]{1,0:T(8,128)S(1)}, u32[]{:S(2)}, u32[]{:S(2)}) collective-permute-start(f32[64,1024]{1,0:T(8,128)S(1)} %pad_maximum_fusion), channel_id=1, source_target_pairs={{0,120},{8,0},{16,8},{24,16},{32,24},{40,32},{48,40},{56,48},{64,5... | collective-permute-start | bytes 786440 | tf_op jit(solution)/shard_map/ppermute | solution.py:23
  156.8 12.3 %collective-permute-start.13 = (f32[64,1024]{1,0:T(8,128)S(1)}, f32[64,1024]{1,0:T(8,128)S(1)}, u32[]{:S(2)}, u32[]{:S(2)}) collective-permute-start(f32[64,1024]{1,0:T(8,128)S(1)} %pad_maximum_fusion), channel_id=1, source_target_pairs={{0,112},{1,17},{8,120},{9,25},{16,0},{17,33},{24,8},{25,41},{32,16... | collective-permute-start | bytes 786440 | tf_op jit(solution)/shard_map/ppermute | solution.py:29
  162.3 13.5 %collective-permute-start.14 = (f32[64,1024]{1,0:T(8,128)S(1)}, f32[64,1024]{1,0:T(8,128)S(1)}, u32[]{:S(2)}, u32[]{:S(2)}) collective-permute-start(f32[64,1024]{1,0:T(8,128)S(1)} %pad_maximum_fusion), channel_id=1, source_target_pairs={{0,8},{8,16},{16,24},{24,32},{32,40},{40,48},{48,56},{56,64},{64,7... | collective-permute-start | bytes 786440 | tf_op jit(solution)/shard_map/ppermute | solution.py:23
  178.2 19.1 %all-to-all-start.3 = ((f32[32,16,384]{2,1,0:T(8,128)}), f32[32,16,384]{2,1,0:T(8,128)}, u32[]{:S(2)}, u32[]{:S(2)}) async-start(f32[32,16,384]{2,1,0:T(8,128)} %bitcast.13), calls=%async_computation.3 | async-start | bytes 1572864 | tf_op jit(solution)/shard_map/all_to_all | solution.py:15
  184.6 25.4 %collective-permute-start.15 = (f32[96,1024]{1,0:T(8,128)}, f32[96,1024]{1,0:T(8,128)}, u32[]{:S(2)}, u32[]{:S(2)}) collective-permute-start(f32[96,1024]{1,0:T(8,128)} %get-tuple-element.26), channel_id=1, source_target_pairs={{0,128},{128,256},{256,384},{384,0},{1,129},{129,257},{257,385},{3... | collective-permute-start | bytes 1179656 | tf_op jit(solution)/shard_map/ppermute | solution.py:33
  188.4 34.7 %collective-permute-start.16 = (f32[96,1024]{1,0:T(8,128)}, f32[96,1024]{1,0:T(8,128)}, u32[]{:S(2)}, u32[]{:S(2)}) collective-permute-start(f32[96,1024]{1,0:T(8,128)} %get-tuple-element.25), channel_id=1, source_target_pairs={{0,384},{128,0},{256,128},{384,256},{1,385},{129,1},{257,129},{385... | collective-permute-start | bytes 1179656 | tf_op jit(solution)/shard_map/ppermute | solution.py:33
  199.1 18.1 %all-to-all-start.4 = ((f32[16,1,512]{2,1,0:T(1,128)}), f32[16,1,512]{2,1,0:T(1,128)S(1)}, u32[]{:S(2)}, u32[]{:S(2)}) async-start(f32[16,1,512]{2,1,0:T(1,128)} %reshape.295), calls=%async_computation.4 | async-start | bytes 65536 | tf_op jit(solution)/shard_map/all_to_all | solution.py:15
  206.5 23.2 %collective-permute-start.17 = (f32[96,1024]{1,0:T(8,128)}, f32[96,1024]{1,0:T(8,128)}, u32[]{:S(2)}, u32[]{:S(2)}) collective-permute-start(f32[96,1024]{1,0:T(8,128)} %dynamic-slice_bitcast_fusion), channel_id=1, source_target_pairs={{0,256},{128,384},{256,0},{384,128},{1,257},{129,385},{257,1},{385... | collective-permute-start | bytes 1179656 | tf_op jit(solution)/shard_map/ppermute | solution.py:33
  218.2 10.7 %all-to-all-start.5 = ((f32[8,1,6144]{2,1,0:T(1,128)}), f32[8,1,6144]{2,1,0:T(1,128)S(1)}, u32[]{:S(2)}, u32[]{:S(2)}) async-start(f32[8,1,6144]{2,1,0:T(1,128)} %broadcast_in_dim.122), calls=%async_computation.5 | async-start | bytes 393216 | tf_op jit(solution)/shard_map/all_to_all | solution.py:15
  230.7 1.1 copy-start.1

commit v8 on v6

--- a/solution.py
+++ b/solution.py
@@ -43,36 +43,54 @@
     quarter = columns // 4
     wide = 4 * depth
     x, h, l = lax.axis_index("x"), lax.axis_index("h"), lax.axis_index("l")
-    j = lax.axis_index(YC)
-
-    def cut(s):
-        return lax.dynamic_slice(weight, (0, (x + s) % 4 * quarter), (depth, quarter))
-
-    pieces = [cut(0), *(shift_x(cut(s), s) for s in range(1, 4))]
+    j, c = lax.axis_index(YC), lax.axis_index("c")
 
     row = lax.dynamic_slice(responses, (j, 0), (1, width)).reshape(4, 16, depth)
     notes = jnp.pad(jnp.concatenate([targets, lengths, owners]).astype(jnp.float32), (0, META - 10))
     notes = jnp.broadcast_to(notes, (16, META))
     packed = jnp.concatenate([row.transpose(1, 0, 2).reshape(16, wide), notes], axis=1)
+    def cut(array, s):
+        return lax.dynamic_slice(array, (0, (x + s) % 4 * quarter), (depth, quarter))
+
+    packed, weight = lax.optimization_barrier((packed, weight))
+    pieces = [cut(weight, 0), shift_x(cut(weight, 1), 1), shift_x(cut(weight, 2), 2)]
     mine = swap(packed.reshape(16, 1, wide + META), Z).reshape(16, wide + META)
-    mine, pieces[1] = lax.optimization_barrier((mine, pieces[1]))
-    slots = spread(mine, XYC, 32).reshape(512, wide + META)
+    mine, weight = lax.optimization_barrier((mine, weight))
+    pieces.append(shift_x(cut(weight, 3), 3))
+
+    slots = spread(mine, ("x", "y"), 16).reshape(256, wide + META)
+    slots, pieces[2], pieces[3] = lax.optimization_barrier((slots, pieces[2], pieces[3]))
+    slots_other = lax.ppermute(slots, "c", [(0, 1), (1, 0)])
+
+    all_notes = slots[:, wide : wide + 10].astype(jnp.int32)
+    source_notes = all_notes.reshape(4, 4, 16, 10)[:, 0].reshape(64, 10)
+    source_length, source_owner = source_notes[:, 8], source_notes[:, 9]
+    sources = jnp.arange(64, dtype=jnp.int32)
+
+    def starts_of(source):
+        return jnp.sum(jnp.where(sources[None, :] < source[:, None], source_length[None, :], 0), axis=1)
+
+    rows = jnp.arange(256, dtype=jnp.int32)
+    starts = starts_of(rows // 64 * 16 + rows % 16)
+
+    def chosen(core):
+        slot_j = rows // 16 % 4 * 2 + core
+        rank = jnp.where(slot_j < all_notes[:, 8], (starts + slot_j - 64 * l) % 256, -1)
+        target = jnp.sum(jnp.where(jnp.arange(10)[None, :] == slot_j[:, None], all_notes, 0), axis=1)
+        select = rank[None, :] == rows[:, None]
+        return select.astype(jnp.float32), jnp.sum(jnp.where(select, target[None, :], 0), axis=1)
+
+    select, labels = chosen(c)
+    select_other, labels_other = chosen(1 - c)
+    labels = labels + labels_other
+    hidden = dot(select, slots[:, :wide]) + dot(select_other, slots_other[:, :wide])
 
     ids = jnp.arange(512, dtype=jnp.int32)
-    slot_j = (ids // 16) % 8
-    source = (ids // 128) * 16 + ids % 16
-    notes_all = slots[:, wide : wide + 10].astype(jnp.int32)
-    slot_length, slot_owner = notes_all[:, 8], notes_all[:, 9]
-    slot_target = jnp.sum(jnp.where(jnp.arange(10)[None, :] == slot_j[:, None], notes_all, 0), axis=1)
-    before = (source[None, :] < source[:, None]) & (slot_j[None, :] == 0)
-    starts = jnp.sum(jnp.where(before, slot_length[None, :], 0), axis=1)
-    rank = jnp.where(slot_j < slot_length, (starts + slot_j - 64 * l) % 256, -1)
-    rows = jnp.arange(256, dtype=jnp.int32)
-    select = rank[None, :] == rows[:, None]
-    hidden = dot(select.astype(jnp.float32), slots[:, :wide])
-    labels = jnp.sum(jnp.where(select, slot_target[None, :], 0), axis=1)
-    owned = (slot_owner[None, :] == source[:, None]) & (slot_j[None, :] == slot_j[:, None])
-    sent_rank = jnp.sum(jnp.where(owned, rank[None, :] + 1, 0), axis=1) - 1
+    slot_j = ids // 16 % 8
+    owned = source_owner[None, :] == (ids // 128 * 16 + ids % 16)[:, None]
+    sent_start = jnp.sum(jnp.where(owned, starts_of(sources)[None, :], 0), axis=1)
+    sent_length = jnp.sum(jnp.where(owned, source_length[None, :], 0), axis=1)
+    sent_rank = jnp.where(slot_j < sent_length, (sent_start + slot_j - 64 * l) % 256, -1)
     deliver = (sent_rank[:, None] == rows[None, :]).astype(jnp.float32)
 
     head = jnp.zeros((4, depth, quarter), jnp.float32)
@@ -105,10 +123,9 @@
     summed = jnp.sum(swap(leaving, XYC), axis=0)
 
     grad_head = dot(hidden, grads, (0, 0), GRAD).reshape(4, depth, quarter)
-    summed, grad_head_later = lax.optimization_barrier((summed, grad_head))
     grad_weight = jnp.zeros((depth, columns), jnp.float32)
     for s in (0, 1, 3, 2):
-        part = lax.dynamic_index_in_dim(grad_head_later if s == 2 else grad_head, (x + s) % 4, 0, False)
+        part = lax.dynamic_index_in_dim(grad_head, (x + s) % 4, 0, False)
         part = shift_x(part, s) if s else part
         grad_weight = lax.dynamic_update_slice(grad_weight, part, (0, (x - s) % 4 * quarter))
 

time: 221 us -> 222 us (level)
  blocking collectives: 19.8 us -> 0 us
  starting transfers between devices: 99.2 us -> 112 us
  local copies, waits for them, and re-layouts: 17.4 us -> 21.8 us
    all_to_all x1 -> x0, blocking collectives: 19.8 us -> none  [swap(): return lax.all_to_all(blocks, axes, split_axis=0, concat_axis=0, tiled=True)]
    ppermute x6, waiting for transfers between devices: 0.02 us -> 7.37 us  [shift_x(): return lax.ppermute(block, 'x', [(i, (i + step) % 4) for i in range(4)])]
    all_to_all x7 -> x8, waiting for transfers between devices: 52.8 us -> 47.1 us  [swap(): return lax.all_to_all(blocks, axes, split_axis=0, concat_axis=0, tiled=True)]
    all_to_all x7 -> x8, starting transfers between devices: 58.1 us -> 62.4 us  [swap(): return lax.all_to_all(blocks, axes, split_axis=0, concat_axis=0, tiled=True)]
    ppermute x0 -> x1, starting transfers between devices: none -> 4.14 us  [on_device(): slots_other = lax.ppermute(slots, 'c', [(0, 1), (1, 0)])]
    ppermute x4, starting transfers between devices: 13 us -> 16.8 us  [shift_z(): return lax.ppermute(block, Z, [(i, (i + step) % 16) for i in range(16)])]
    dynamic_update_slice x4, local copies, waits for them, and re-layouts: 3.11 us -> 6.07 us  [on_device(): lax.dynamic_update_slice(grad_weight, part, (0, (x - s) % 4 * quarter))]
    dot_general x5 -> x6, matrix products: 6.77 us -> 7.93 us  [dot(): lax.dot_general(a, b, dims, precision=precision, preferred_element_type=j...]
  transfers between devices with their start and end apart: 19 -> 21, of which waited for: 12 -> 14; matrix products, arithmetic and copies ran while one was open for 7% -> 10% of each run, Pallas kernels for 0% -> 0%
where the time goes in v8:
time: 222 us; the launch traced here: 220 us
  starting transfers between devices  112 us (50%)
  waiting for transfers between devices  72.8 us (33%)
  local copies, waits for them, and re-layouts  21.8 us (10%)
  matrix products  7.93 us (4%)
  other arithmetic  3.58 us (2%)
  between operations  2.52 us (1%)
    all_to_all x8, starting transfers between devices, swap(): return lax.all_to_all(blocks, axes, split_axis=0, concat_axis=0, tiled=True)  62.4 us
    all_to_all x8, waiting for transfers between devices, swap(): return lax.all_to_all(blocks, axes, split_axis=0, concat_axis=0, tiled=True)  47.1 us
    ppermute x6, starting transfers between devices, shift_x(): return lax.ppermute(block, 'x', [(i, (i + step) % 4) for i in range(4)])  22.1 us
    ppermute x4, starting transfers between devices, shift_z(): return lax.ppermute(block, Z, [(i, (i + step) % 16) for i in range(16)])  16.8 us
    ppermute x4, waiting for transfers between devices, shift_z(): return lax.ppermute(block, Z, [(i, (i + step) % 16) for i in range(16)])  11.5 us
    dot_general x6, matrix products, dot(): lax.dot_general(a, b, dims, precision=precision, preferred_element_type=j...  7.93 us
    ppermute x6, waiting for transfers between devices, shift_x(): return lax.ppermute(block, 'x', [(i, (i + step) % 4) for i in range(4)])  7.37 us
    ppermute x2, waiting for transfers between devices, shift_far(): return lax.ppermute(block, ('h', 'l', 'c'), pairs)  6.79 us
  transfers between devices with their start and end apart: 21, of which 14 were waited for; matrix products, arithmetic and copies ran while one was open for 10% of the time, Pallas kernels for 0%

profile of v8, /device:TPU:1, one launch (start us, length us, event | category | flops | bytes accessed | tf_op | source)
XLA Modules:
  0.0 220.3 jit_solution(12806994369703906058)
XLA Ops:
  4.5 15.7 %all-to-all-start = ((f32[16,1,512]{2,1,0:T(1,128)}), f32[16,1,512]{2,1,0:T(1,128)S(1)}, u32[]{:S(2)}, u32[]{:S(2)}) async-start(f32[16,1,512]{2,1,0:T(1,128)} %copy.25), calls=%async_computation | async-start | bytes 65536 | tf_op jit(solution)/shard_map/all_to_all | solution.py:15
  21.5 3.1 %collective-permute-start.3 = (f32[96,1024]{1,0:T(8,128)S(1)}, f32[96,1024]{1,0:T(8,128)}, u32[]{:S(2)}, u32[]{:S(2)}) collective-permute-start(f32[96,1024]{1,0:T(8,128)S(1)} %get-tuple-element.26), channel_id=1, source_target_pairs={{0,128},{128,256},{256,384},{384,0},{1,129},{129,257},{257,385},{3... | collective-permute-start | bytes 1179656 | tf_op jit(solution)/shard_map/ppermute | solution.py:32
  24.6 4.4 %collective-permute-start = (f32[96,1024]{1,0:T(8,128)S(1)}, f32[96,1024]{1,0:T(8,128)S(1)}, u32[]{:S(2)}, u32[]{:S(2)}) collective-permute-start(f32[96,1024]{1,0:T(8,128)S(1)} %get-tuple-element.27), channel_id=1, source_target_pairs={{0,256},{128,384},{256,0},{384,128},{1,257},{129,385},{257,1},{385... | collective-permute-start | bytes 1179656 | tf_op jit(solution)/shard_map/ppermute | solution.py:32
  29.0 2.8 %all-to-all-done = f32[16,1,512]{2,1,0:T(1,128)S(1)} async-done(((f32[16,1,512]{2,1,0:T(1,128)}), f32[16,1,512]{2,1,0:T(1,128)S(1)}, u32[]{:S(2)}, u32[]{:S(2)}) %all-to-all-start) | async-done | bytes 32800 | tf_op jit(solution)/shard_map/all_to_all | solution.py:15
  32.6 6.8 %all-to-all-start.1 = ((f32[16,16,512]{2,1,0:T(8,128)}), f32[16,16,512]{2,1,0:T(8,128)S(1)}, u32[]{:S(2)}, u32[]{:S(2)}) async-start(f32[16,16,512]{2,1,0:T(8,128)} %broadcast_in_dim.147), calls=%async_computation.1 | async-start | bytes 1048576 | tf_op jit(solution)/shard_map/all_to_all | solution.py:15
  41.2 4.5 %collective-permute-start.1 = (f32[96,1024]{1,0:T(8,128)}, f32[96,1024]{1,0:T(8,128)}, u32[]{:S(2)}, u32[]{:S(2)}) collective-permute-start(f32[96,1024]{1,0:T(8,128)} %constant_dynamic-slice_fusion.1), channel_id=1, source_target_pairs={{0,384},{128,0},{256,128},{384,256},{1,385},{129,1},{257,129},{385... | collective-permute-start | bytes 1179656 | tf_op jit(solution)/shard_map/ppermute | solution.py:32
  48.0 6.5 %collective-permute-done.1 = f32[96,1024]{1,0:T(8,128)} collective-permute-done((f32[96,1024]{1,0:T(8,128)}, f32[96,1024]{1,0:T(8,128)}, u32[]{:S(2)}, u32[]{:S(2)}) %collective-permute-start.1) | collective-permute-done | bytes 393248 | tf_op jit(solution)/shard_map/ppermute | solution.py:32
  54.5 4.1 %collective-permute-start.2 = (f32[256,512]{1,0:T(8,128)S(1)}, f32[256,512]{1,0:T(8,128)}, u32[]{:S(2)}, u32[]{:S(2)}) collective-permute-start(f32[256,512]{1,0:T(8,128)S(1)} %bitcast.54), channel_id=1, source_target_pairs={{0,1},{1,0},{2,3},{3,2},{4,5},{5,4},{6,7},{7,6},{8,9},{9,8},{10,11... | collective-permute-start | bytes 1572872 | tf_op jit(solution)/shard_map/ppermute | solution.py:63
  64.1 2.6 %collective-permute-start.6 = (f32[64,1024]{1,0:T(8,128)S(1)}, f32[64,1024]{1,0:T(8,128)S(1)}, u32[]{:S(2)}, u32[]{:S(2)}) collective-permute-start(f32[64,1024]{1,0:T(8,128)S(1)} %get-tuple-element.29), channel_id=1, source_target_pairs={{0,16},{1,113},{8,24},{9,121},{16,32},{17,1},{24,40},{25,9},{32,48... | collective-permute-start | bytes 786440 | tf_op jit(solution)/shard_map/ppermute | solution.py:28
  66.7 2.9 %collective-permute-start.5 = (f32[64,1024]{1,0:T(8,128)S(1)}, f32[64,1024]{1,0:T(8,128)S(1)}, u32[]{:S(2)}, u32[]{:S(2)}) collective-permute-start(f32[64,1024]{1,0:T(8,128)S(1)} %get-tuple-element.30), channel_id=1, source_target_pairs={{0,120},{8,0},{16,8},{24,16},{32,24},{40,32},{48,40},{56,48},{64,5... | collective-permute-start | bytes 786440 | tf_op jit(solution)/shard_map/ppermute | solution.py:23
  69.6 2.4 %collective-permute-start.4 = (f32[64,1024]{1,0:T(8,128)S(1)}, f32[64,1024]{1,0:T(8,128)S(1)}, u32[]{:S(2)}, u32[]{:S(2)}) collective-permute-start(f32[64,1024]{1,0:T(8,128)S(1)} %get-tuple-element.28), channel_id=1, source_target_pairs={{0,8},{8,16},{16,24},{24,32},{32,40},{40,48},{48,56},{56,64},{64,7... | collective-permute-start | bytes 786440 | tf_op jit(solution)/shard_map/ppermute | solution.py:23
  72.0 4.6 %collective-permute-done.6 = f32[64,1024]{1,0:T(8,128)S(1)} collective-permute-done((f32[64,1024]{1,0:T(8,128)S(1)}, f32[64,1024]{1,0:T(8,128)S(1)}, u32[]{:S(2)}, u32[]{:S(2)}) %collective-permute-start.6) | collective-permute-done | bytes 262176 | tf_op jit(solution)/shard_map/ppermute | solution.py:28
  76.6 4.0 %collective-permute-done.5 = f32[64,1024]{1,0:T(8,128)S(1)} collective-permute-done((f32[64,1024]{1,0:T(8,128)S(1)}, f32[64,1024]{1,0:T(8,128)S(1)}, u32[]{:S(2)}, u32[]{:S(2)}) %collective-permute-start.5) | collective-permute-done | bytes 262176 | tf_op jit(solution)/shard_map/ppermute | solution.py:23
  81.4 7.8 %all-to-all-start.2 = ((f32[4,16,1024]{2,1,0:T(8,128)}), f32[4,16,1024]{2,1,0:T(8,128)S(1)}, u32[]{:S(2)}, u32[]{:S(2)}) async-start(f32[4,16,1024]{2,1,0:T(8,128)} %bitcast.11), calls=%async_computation.2 | async-start | bytes 524288 | tf_op jit(solution)/shard_map/all_to_all | solution.py:15
  89.9 12.5 %all-to-all-done.2 = f32[4,16,1024]{2,1,0:T(8,128)S(1)} async-done(((f32[4,16,1024]{2,1,0:T(8,128)}), f32[4,16,1024]{2,1,0:T(8,128)S(1)}, u32[]{:S(2)}, u32[]{:S(2)}) %all-to-all-start.2) | async-done | bytes 262176 | tf_op jit(solution)/shard_map/all_to_all | solution.py:15
  103.4 11.4 %all-to-all-start.3 = ((f32[32,3,16]{2,1,0:T(4,128)}), f32[32,3,16]{2,1,0:T(4,128)S(1)}, u32[]{:S(2)}, u32[]{:S(2)}) async-start(f32[32,3,16]{2,1,0:T(4,128)} %broadcast_in_dim.165), calls=%async_computation.3 | async-start | bytes 131072 | tf_op jit(solution)/shard_map/all_to_all | solution.py:15
  114.8 7.4 %all-to-all-done.3 = f32[32,3,16]{2,1,0:T(4,128)S(1)} async-done(((f32[32,3,16]{2,1,0:T(4,128)}), f32[32,3,16]{2,1,0:T(4,128)S(1)}, u32[]{:S(2)}, u32[]{:S(2)}) %all-to-all-start.3) | async-done | bytes 6176 | tf_op jit(solution)/shard_map/all_to_all | solution.py:15
  123.1 6.4 %all-to-all-start.4 = ((f32[4,16,1024]{2,1,0:T(8,128)}), f32[4,16,1024]{2,1,0:T(8,128)S(1)}, u32[]{:S(2)}, u32[]{:S(2)}) async-start(f32[4,16,1024]{2,1,0:T(8,128)} %broadcast_in_dim.166), calls=%async_computation.4 | async-start | bytes 524288 | tf_op jit(solution)/shard_map/all_to_all | solution.py:15
  129.8 13.9 %all-to-all-done.4 = f32[4,16,1024]{2,1,0:T(8,128)S(1)} async-done(((f32[4,16,1024]{2,1,0:T(8,128)}), f32[4,16,1024]{2,1,0:T(8,128)S(1)}, u32[]{:S(2)}, u32[]{:S(2)}) %all-to-all-start.4) | async-done | bytes 262176 | tf_op jit(solution)/shard_map/all_to_all | solution.py:15
  143.7 8.1 %collective-permute-start.9 = (f32[64,1024]{1,0:T(8,128)S(1)}, f32[64,1024]{1,0:T(8,128)S(1)}, u32[]{:S(2)}, u32[]{:S(2)}) collective-permute-start(f32[64,1024]{1,0:T(8,128)S(1)} %bitcast.58), channel_id=1, source_target_pairs={{0,8},{8,16},{16,24},{24,32},{32,40},{40,48},{48,56},{56,64},{64,7... | collective-permute-start | bytes 786440 | tf_op jit(solution)/shard_map/ppermute | solution.py:23
  151.8 3.5 %collective-permute-start.8 = (f32[64,1024]{1,0:T(8,128)S(1)}, f32[64,1024]{1,0:T(8,128)S(1)}, u32[]{:S(2)}, u32[]{:S(2)}) collective-permute-start(f32[64,1024]{1,0:T(8,128)S(1)} %bitcast.59), channel_id=1, source_target_pairs={{0,16},{1,113},{8,24},{9,121},{16,32},{17,1},{24,40},{25,9},{32,48... | collective-permute-start | bytes 786440 | tf_op jit(solution)/shard_map/ppermute | solution.py:28
  155.3 3.4 %collective-permute-start.7 = (f32[64,1024]{1,0:T(8,128)S(1)}, f32[64,1024]{1,0:T(8,128)S(1)}, u32[]{:S(2)}, u32[]{:S(2)}) collective-permute-start(f32[64,1024]{1,0:T(8,128)S(1)} %bitcast.60), channel_id=1, source_target_pairs={{0,120},{8,0},{16,8},{24,16},{32,24},{40,32},{48,40},{56,48},{64,5... | collective-permute-start | bytes 786440 | tf_op jit(solution)/shard_map/ppermute | solution.py:23
  158.8 2.2 collective-permute-done.8
  161.0 7.4 %collective-permute-done.7 = f32[64,1024]{1,0:T(8,128)S(1)} collective-permute-done((f32[64,1024]{1,0:T(8,128)S(1)}, f32[64,1024]{1,0:T(8,128)S(1)}, u32[]{:S(2)}, u32[]{:S(2)}) %collective-permute-start.7) | collective-permute-done | bytes 262176 | tf_op jit(solution)/shard_map/ppermute | solution.py:23
  170.8 4.1 %all-to-all-start.5 = ((f32[32,16,384]{2,1,0:T(8,128)}), f32[32,16,384]{2,1,0:T(8,128)S(1)}, u32[]{:S(2)}, u32[]{:S(2)}) async-start(f32[32,16,384]{2,1,0:T(8,128)} %bitcast.18), calls=%async_computation.5 | async-start | bytes 1572864 | tf_op jit(solution)/shard_map/all_to_all | solution.py:15
  177.7 3.3 %collective-permute-start.10 = (f32[96,1024]{1,0:T(8,128)}, f32[96,1024]{1,0:T(8,128)}, u32[]{:S(2)}, u32[]{:S(2)}) collective-permute-start(f32[96,1024]{1,0:T(8,128)} %get-tuple-element.25), channel_id=1, source_target_pairs={{0,128},{128,256},{256,384},{384,0},{1,129},{129,257},{257,385},{3... | collective-permute-start | bytes 1179656 | tf_op jit(solution)/shard_map/ppermute | solution.py:32
  181.0 3.2 %collective-permute-start.11 = (f32[96,1024]{1,0:T(8,128)S(1)}, f32[96,1024]{1,0:T(8,128)}, u32[]{:S(2)}, u32[]{:S(2)}) collective-permute-start(f32[96,1024]{1,0:T(8,128)S(1)} %get-tuple-element.24), channel_id=1, source_target_pairs={{0,384},{128,0},{256,128},{384,256},{1,385},{129,1},{257,129},{385... | collective-permute-start | bytes 1179656 | tf_op jit(solution)/shard_map/ppermute | solution.py:32
  184.7 3.6 %collective-permute-start.12 = (f32[96,1024]{1,0:T(8,128)S(1)}, f32[96,1024]{1,0:T(8,128)}, u32[]{:S(2)}, u32[]{:S(2)}) collective-permute-start(f32[96,1024]{1,0:T(8,128)S(1)} %get-tuple-element.23), channel_id=1, source_target_pairs={{0,256},{128,384},{256,0},{384,128},{1,257},{129,385},{257,1},{385... | collective-permute-start | bytes 1179656 | tf_op jit(solution)/shard_map/ppermute | solution.py:32
  191.1 3.5 %all-to-all-start.6 = ((f32[16,1,512]{2,1,0:T(1,128)}), f32[16,1,512]{2,1,0:T(1,128)S(1)}, u32[]{:S(2)}, u32[]{:S(2)}) async-start(f32[16,1,512]{2,1,0:T(1,128)} %reshape.335), calls=%async_computation.6 | async-start | bytes 65536 | tf_op jit(solution)/shard_map/all_to_all | solution.py:15
  199.0 7.0 %all-to-all-done.6 = f32[16,1,512]{2,1,0:T(1,128)S(1)} async-done(((f32[16,1,512]{2,1,0:T(1,128)}), f32[16,1,512]{2,1,0:T(1,128)S(1)}, u32[]{:S(2)}, u32[]{:S(2)}) %all-to-all-start.6) | async-done | bytes 32800 | tf_op jit(solution)/shard_map/all_to_all | solution.py:15
  207.0 6.7 %all-to-all-start.7 = ((f32[8,1,6144]{2,1,0:T(1,128)}), f32[8,1,6144]{2,1,0:T(1,128)S(1)}, u32[]{:S(2)}, u32[]{:S(2)}) async-start(f32[8,1,6144]{2,1,0:T(1,128)} %broadcast_in_dim.169), calls=%async_computation.7 | async-start | bytes 393216 | tf_op jit(solution)/shard_map/all_to_all | solution.py:15
  215.9 3.6 %all-to-all-done.7 = f32[8,1,6144]{2,1,0:T(1,128)S(1)} async-done(((f32[8,1,6144]{2,1,0:T(1,128)}), f32[8,1,6144]{2,1,0:T(1,128)S(1)}, u32[]{:S(2)}, u32[]{:S(2)}) %all-to-all-start.7) | async-done | bytes 196640 | tf_op jit(solution)/shard_map/all_to_all | solution.py:15
  (92 shorter events, 34.4 us)
Async XLA Ops:
  0.6 0.9 copy-start
  4.5 27.2 %all-to-all-start = ((f32[16,1,512]{2,1,0:T(1,128)}), f32[16,1,512]{2,1,0:T(1,128)S(1)}, u32[]{:S(2)}, u32[]{:S(2)}) async-start(f32[16,1,512]{2,1,0:T(1,128)} %copy.25), calls=%async_computation | async-start | bytes 65536 | tf_op jit(solution)/shard_map/all_to_all | solution.py:15
  21.5 25.5 %collective-permute-start.3 = (f32[96,1024]{1,0:T(8,128)S(1)}, f32[96,1024]{1,0:T(8,128)}, u32[]{:S(2)}, u32[]{:S(2)}) collective-permute-start(f32[96,1024]{1,0:T(8,128)S(1)} %get-tuple-element.26), channel_id=1, source_target_pairs={{0,128},{128,256},{256,384},{384,0},{1,129},{129,257},{257,385},{3... | collective-permute-start | bytes 1179656 | tf_op jit(solution)/shard_map/ppermute | solution.py:32
  24.6 23.4 %collective-permute-start = (f32[96,1024]{1,0:T(8,128)S(1)}, f32[96,1024]{1,0:T(8,128)S(1)}, u32[]{:S(2)}, u32[]{:S(2)}) collective-permute-start(f32[96,1024]{1,0:T(8,128)S(1)} %get-tuple-element.27), channel_id=1, source_target_pairs={{0,256},{128,384},{256,0},{384,128},{1,257},{129,385},{257,1},{385... | collective-permute-start | bytes 1179656 | tf_op jit(solution)/shard_map/ppermute | solution.py:32
  32.6 21.9 %all-to-all-start.1 = ((f32[16,16,512]{2,1,0:T(8,128)}), f32[16,16,512]{2,1,0:T(8,128)S(1)}, u32[]{:S(2)}, u32[]{:S(2)}) async-start(f32[16,16,512]{2,1,0:T(8,128)} %broadcast_in_dim.147), calls=%async_computation.1 | async-start | bytes 1048576 | tf_op jit(solution)/shard_map/all_to_all | solution.py:15
  41.2 13.3 %collective-permute-start.1 = (f32[96,1024]{1,0:T(8,128)}, f32[96,1024]{1,0:T(8,128)}, u32[]{:S(2)}, u32[]{:S(2)}) collective-permute-start(f32[96,1024]{1,0:T(8,128)} %constant_dynamic-slice_fusion.1), channel_id=1, source_target_pairs={{0,384},{128,0},{256,128},{384,256},{1,385},{129,1},{257,129},{385... | collective-permute-start | bytes 1179656 | tf_op jit(solution)/shard_map/ppermute | solution.py:32
  54.5 5.8 %collective-permute-start.2 = (f32[256,512]{1,0:T(8,128)S(1)}, f32[256,512]{1,0:T(8,128)}, u32[]{:S(2)}, u32[]{:S(2)}) collective-permute-start(f32[256,512]{1,0:T(8,128)S(1)} %bitcast.54), channel_id=1, source_target_pairs={{0,1},{1,0},{2,3},{3,2},{4,5},{5,4},{6,7},{7,6},{8,9},{9,8},{10,11... | collective-permute-start | bytes 1572872 | tf_op jit(solution)/shard_map/ppermute | solution.py:63
  64.1 12.5 %collective-permute-start.6 = (f32[64,1024]{1,0:T(8,128)S(1)}, f32[64,1024]{1,0:T(8,128)S(1)}, u32[]{:S(2)}, u32[]{:S(2)}) collective-permute-start(f32[64,1024]{1,0:T(8,128)S(1)} %get-tuple-element.29), channel_id=1, source_target_pairs={{0,16},{1,113},{8,24},{9,121},{16,32},{17,1},{24,40},{25,9},{32,48... | collective-permute-start | bytes 786440 | tf_op jit(solution)/shard_map/ppermute | solution.py:28
  66.7 13.9 %collective-permute-start.5 = (f32[64,1024]{1,0:T(8,128)S(1)}, f32[64,1024]{1,0:T(8,128)S(1)}, u32[]{:S(2)}, u32[]{:S(2)}) collective-permute-start(f32[64,1024]{1,0:T(8,128)S(1)} %get-tuple-element.30), channel_id=1, source_target_pairs={{0,120},{8,0},{16,8},{24,16},{32,24},{40,32},{48,40},{56,48},{64,5... | collective-permute-start | bytes 786440 | tf_op jit(solution)/shard_map/ppermute | solution.py:23
  69.6 11.1 %collective-permute-start.4 = (f32[64,1024]{1,0:T(8,128)S(1)}, f32[64,1024]{1,0:T(8,128)S(1)}, u32[]{:S(2)}, u32[]{:S(2)}) collective-permute-start(f32[64,1024]{1,0:T(8,128)S(1)} %get-tuple-element.28), channel_id=1, source_target_pairs={{0,8},{8,16},{16,24},{24,32},{32,40},{40,48},{48,56},{56,64},{64,7... | collective-permute-start | bytes 786440 | tf_op jit(solution)/shard_map/ppermute | solution.py:23
  81.4 20.9 %all-to-all-start.2 = ((f32[4,16,1024]{2,1,0:T(8,128)}), f32[4,16,1024]{2,1,0:T(8,128)S(1)}, u32[]{:S(2)}, u32[]{:S(2)}) async-start(f32[4,16,1024]{2,1,0:T(8,128)} %bitcast.11), calls=%async_computation.2 | async-start | bytes 524288 | tf_op jit(solution)/shard_map/all_to_all | solution.py:15
  103.4 18.8 %all-to-all-start.3 = ((f32[32,3,16]{2,1,0:T(4,128)}), f32[32,3,16]{2,1,0:T(4,128)S(1)}, u32[]{:S(2)}, u32[]{:S(2)}) async-start(f32[32,3,16]{2,1,0:T(4,128)} %broadcast_in_dim.165), calls=%async_computation.3 | async-start | bytes 131072 | tf_op jit(solution)/shard_map/all_to_all | solution.py:15
  123.1 20.5 %all-to-all-start.4 = ((f32[4,16,1024]{2,1,0:T(8,128)}), f32[4,16,1024]{2,1,0:T(8,128)S(1)}, u32[]{:S(2)}, u32[]{:S(2)}) async-start(f32[4,16,1024]{2,1,0:T(8,128)} %broadcast_in_dim.166), calls=%async_computation.4 | async-start | bytes 524288 | tf_op jit(solution)/shard_map/all_to_all | solution.py:15
  143.7 15.1 %collective-permute-start.9 = (f32[64,1024]{1,0:T(8,128)S(1)}, f32[64,1024]{1,0:T(8,128)S(1)}, u32[]{:S(2)}, u32[]{:S(2)}) collective-permute-start(f32[64,1024]{1,0:T(8,128)S(1)} %bitcast.58), channel_id=1, source_target_pairs={{0,8},{8,16},{16,24},{24,32},{32,40},{40,48},{48,56},{56,64},{64,7... | collective-permute-start | bytes 786440 | tf_op jit(solution)/shard_map/ppermute | solution.py:23
  151.8 9.2 %collective-permute-start.8 = (f32[64,1024]{1,0:T(8,128)S(1)}, f32[64,1024]{1,0:T(8,128)S(1)}, u32[]{:S(2)}, u32[]{:S(2)}) collective-permute-start(f32[64,1024]{1,0:T(8,128)S(1)} %bitcast.59), channel_id=1, source_target_pairs={{0,16},{1,113},{8,24},{9,121},{16,32},{17,1},{24,40},{25,9},{32,48... | collective-permute-start | bytes 786440 | tf_op jit(solution)/shard_map/ppermute | solution.py:28
  155.3 13.1 %collective-permute-start.7 = (f32[64,1024]{1,0:T(8,128)S(1)}, f32[64,1024]{1,0:T(8,128)S(1)}, u32[]{:S(2)}, u32[]{:S(2)}) collective-permute-start(f32[64,1024]{1,0:T(8,128)S(1)} %bitcast.60), channel_id=1, source_target_pairs={{0,120},{8,0},{16,8},{24,16},{32,24},{40,32},{48,40},{56,48},{64,5... | collective-permute-start | bytes 786440 | tf_op jit(solution)/shard_map/ppermute | solution.py:23
  161.0 9.8 %copy-start.1 = (f32[64,1024]{1,0:T(8,128)}, f32[64,1024]{1,0:T(8,128)S(1)}, u32[]{:S(2)}) copy-start(f32[64,1024]{1,0:T(8,128)S(1)} %collective-permute-done.8) | copy-start | bytes 786436
  168.4 2.4 %copy-start.2 = (f32[64,1024]{1,0:T(8,128)}, f32[64,1024]{1,0:T(8,128)S(1)}, u32[]{:S(2)}) copy-start(f32[64,1024]{1,0:T(8,128)S(1)} %collective-permute-done.7) | copy-start | bytes 786436
  170.8 19.5 %all-to-all-start.5 = ((f32[32,16,384]{2,1,0:T(8,128)}), f32[32,16,384]{2,1,0:T(8,128)S(1)}, u32[]{:S(2)}, u32[]{:S(2)}) async-start(f32[32,16,384]{2,1,0:T(8,128)} %bitcast.18), calls=%async_computation.5 | async-start | bytes 1572864 | tf_op jit(solution)/shard_map/all_to_all | solution.py:15
  177.7 17.8 %collective-permute-start.10 = (f32[96,1024]{1,0:T(8,128)}, f32[96,1024]{1,0:T(8,128)}, u32[]{:S(2)}, u32[]{:S(2)}) collective-permute-start(f32[96,1024]{1,0:T(8,128)} %get-tuple-element.25), channel_id=1, source_target_pairs={{0,128},{128,256},{256,384},{384,0},{1,129},{129,257},{257,385},{3... | collective-permute-start | bytes 1179656 | tf_op jit(solution)/shard_map/ppermute | solution.py:32
  181.0 16.2 %collective-permute-start.11 = (f32[96,1024]{1,0:T(8,128)S(1)}, f32[96,1024]{1,0:T(8,128)}, u32[]{:S(2)}, u32[]{:S(2)}) collective-permute-start(f32[96,1024]{1,0:T(8,128)S(1)} %get-tuple-element.24), channel_id=1, source_target_pairs={{0,384},{128,0},{256,128},{384,256},{1,385},{129,1},{257,129},{385... | collective-permute-start | bytes 1179656 | tf_op jit(solution)/shard_map/ppermute | solution.py:32
  184.7 29.0 %collective-permute-start.12 = (f32[96,1024]{1,0:T(8,128)S(1)}, f32[96,1024]{1,0:T(8,128)}, u32[]{:S(2)}, u32[]{:S(2)}) collective-permute-start(f32[96,1024]{1,0:T(8,128)S(1)} %get-tuple-element.23), channel_id=1, source_target_pairs={{0,256},{128,384},{256,0},{384,128},{1,257},{129,385},{257,1},{385... | collective-permute-start | bytes 1179656 | tf_op jit(solution)/shard_map/ppermute | solution.py:32
  191.1 14.9 %all-to-all-start.6 = ((f32[16,1,512]{2,1,0:T(1,128)}), f32[16,1,512]{2,1,0:T(1,128)S(1)}, u32[]{:S(2)}, u32[]{:S(2)}) async-start(f32[16,1,512]{2,1,0:T(1,128)} %reshape.335), calls=%async_computation.6 | async-start | bytes 65536 | tf_op jit(solution)/shard_map/all_to_all | solution.py:15
  207.0 12.6 %all-to-all-start.7 = ((f32[8,1,6144]{2,1,0:T(1,128)}), f32[8,1,6144]{2,1,0:T(1,128)S(1)}, u32[]{:S(2)}, u32[]{:S(2)}) async-start(f32[8,1,6144]{2,1,0:T(1,128)} %broadcast_in_dim.169), calls=%async_computation.7 | async-start | bytes 393216 | tf_op jit(solution)/shard_map/all_to_all | solution.py:15

commit v9 on v6

--- a/solution.py
+++ b/solution.py
@@ -45,19 +45,19 @@
     x, h, l = lax.axis_index("x"), lax.axis_index("h"), lax.axis_index("l")
     j = lax.axis_index(YC)
 
-    def cut(s):
-        return lax.dynamic_slice(weight, (0, (x + s) % 4 * quarter), (depth, quarter))
-
-    pieces = [cut(0), *(shift_x(cut(s), s) for s in range(1, 4))]
-
     row = lax.dynamic_slice(responses, (j, 0), (1, width)).reshape(4, 16, depth)
     notes = jnp.pad(jnp.concatenate([targets, lengths, owners]).astype(jnp.float32), (0, META - 10))
     notes = jnp.broadcast_to(notes, (16, META))
     packed = jnp.concatenate([row.transpose(1, 0, 2).reshape(16, wide), notes], axis=1)
+    def cut(array, s):
+        return lax.dynamic_slice(array, (0, (x + s) % 4 * quarter), (depth, quarter))
+
+    packed, weight = lax.optimization_barrier((packed, weight))
+    pieces = [cut(weight, 0), shift_x(cut(weight, 1), 1), shift_x(cut(weight, 2), 2)]
     mine = swap(packed.reshape(16, 1, wide + META), Z).reshape(16, wide + META)
-    mine, pieces[1] = lax.optimization_barrier((mine, pieces[1]))
+    mine, weight = lax.optimization_barrier((mine, weight))
+    pieces.append(shift_x(cut(weight, 3), 3))
     slots = spread(mine, XYC, 32).reshape(512, wide + META)
-
     ids = jnp.arange(512, dtype=jnp.int32)
     slot_j = (ids // 16) % 8
     source = (ids // 128) * 16 + ids % 16
@@ -106,11 +106,13 @@
 
     grad_head = dot(hidden, grads, (0, 0), GRAD).reshape(4, depth, quarter)
     summed, grad_head_later = lax.optimization_barrier((summed, grad_head))
-    grad_weight = jnp.zeros((depth, columns), jnp.float32)
-    for s in (0, 1, 3, 2):
-        part = lax.dynamic_index_in_dim(grad_head_later if s == 2 else grad_head, (x + s) % 4, 0, False)
-        part = shift_x(part, s) if s else part
-        grad_weight = lax.dynamic_update_slice(grad_weight, part, (0, (x - s) % 4 * quarter))
+
+    def part(array, s):
+        return lax.dynamic_index_in_dim(array, (x + s) % 4, 0, False)
+
+    grad_weight = jnp.tile(part(grad_head_later, 0), (1, 4))
+    for s in (1, 3, 2):
+        grad_weight = lax.dynamic_update_slice(grad_weight, shift_x(part(grad_head, s), s), (0, (x - s) % 4 * quarter))
 
     parts = lax.dynamic_update_slice(jnp.zeros((16, META), jnp.float32), logprobs.reshape(4, 4), (h * 4, 0))
     parts = jnp.where(l == x, parts, 0.0)

time: 221 us -> 225 us (1.018)
  waiting for transfers between devices: 70.6 us -> 75.4 us
    ppermute x6, waiting for transfers between devices: 0.02 us -> 14.2 us  [shift_x(): return lax.ppermute(block, 'x', [(i, (i + step) % 4) for i in range(4)])]
    all_to_all x7, waiting for transfers between devices: 52.8 us -> 41.2 us  [swap(): return lax.all_to_all(blocks, axes, split_axis=0, concat_axis=0, tiled=True)]
    all_to_all x7, starting transfers between devices: 58.1 us -> 55.5 us  [swap(): return lax.all_to_all(blocks, axes, split_axis=0, concat_axis=0, tiled=True)]
    ppermute x4, starting transfers between devices: 13 us -> 15.3 us  [shift_z(): return lax.ppermute(block, Z, [(i, (i + step) % 16) for i in range(16)])]
  transfers between devices with their start and end apart: 19 -> 19, of which waited for: 12 -> 14; matrix products, arithmetic and copies ran while one was open for 7% -> 8% of each run, Pallas kernels for 0% -> 0%
where the time goes in v9:
time: 225 us; the launch traced here: 224 us
  starting transfers between devices  97.6 us (43%)
  waiting for transfers between devices  75.4 us (34%)
  blocking collectives  19.6 us (9%)
  local copies, waits for them, and re-layouts  17.7 us (8%)
  matrix products  6.76 us (3%)
  other arithmetic  3.89 us (2%)
  between operations  2.58 us (1%)
    all_to_all x7, starting transfers between devices, swap(): return lax.all_to_all(blocks, axes, split_axis=0, concat_axis=0, tiled=True)  55.5 us
    all_to_all x7, waiting for transfers between devices, swap(): return lax.all_to_all(blocks, axes, split_axis=0, concat_axis=0, tiled=True)  41.2 us
    ppermute x6, starting transfers between devices, shift_x(): return lax.ppermute(block, 'x', [(i, (i + step) % 4) for i in range(4)])  21.6 us
    all_to_all x1, blocking collectives, swap(): return lax.all_to_all(blocks, axes, split_axis=0, concat_axis=0, tiled=True)  19.6 us
    ppermute x4, starting transfers between devices, shift_z(): return lax.ppermute(block, Z, [(i, (i + step) % 16) for i in range(16)])  15.3 us
    ppermute x6, waiting for transfers between devices, shift_x(): return lax.ppermute(block, 'x', [(i, (i + step) % 4) for i in range(4)])  14.2 us
    ppermute x4, waiting for transfers between devices, shift_z(): return lax.ppermute(block, Z, [(i, (i + step) % 16) for i in range(16)])  10.5 us
    ppermute x2, waiting for transfers between devices, shift_far(): return lax.ppermute(block, ('h', 'l', 'c'), pairs)  9.56 us
  transfers between devices with their start and end apart: 19, of which 14 were waited for; matrix products, arithmetic and copies ran while one was open for 8% of the time, Pallas kernels for 0%

profile of v9, /device:TPU:1, one launch (start us, length us, event | category | flops | bytes accessed | tf_op | source)
XLA Modules:
  0.0 223.6 jit_solution(15643802633758970456)
XLA Ops:
  3.6 15.7 %all-to-all-start = ((f32[16,1,512]{2,1,0:T(1,128)}), f32[16,1,512]{2,1,0:T(1,128)S(1)}, u32[]{:S(2)}, u32[]{:S(2)}) async-start(f32[16,1,512]{2,1,0:T(1,128)} %copy.22), calls=%async_computation | async-start | bytes 65536 | tf_op jit(solution)/shard_map/all_to_all | solution.py:15
  19.4 1.9 constant_dynamic-slice_fusion.1
  21.4 4.6 %collective-permute-start.1 = (f32[96,1024]{1,0:T(8,128)S(1)}, f32[96,1024]{1,0:T(8,128)}, u32[]{:S(2)}, u32[]{:S(2)}) collective-permute-start(f32[96,1024]{1,0:T(8,128)S(1)} %get-tuple-element.24), channel_id=1, source_target_pairs={{0,256},{128,384},{256,0},{384,128},{1,257},{129,385},{257,1},{385... | collective-permute-start | bytes 1179656 | tf_op jit(solution)/shard_map/ppermute | solution.py:32
  26.0 2.2 collective-permute-start
  32.0 9.1 %all-to-all-start.1 = ((f32[32,16,512]{2,1,0:T(8,128)}), f32[32,16,512]{2,1,0:T(8,128)S(1)}, u32[]{:S(2)}, u32[]{:S(2)}) async-start(f32[32,16,512]{2,1,0:T(8,128)} %broadcast_in_dim.104), calls=%async_computation.1 | async-start | bytes 2097152 | tf_op jit(solution)/shard_map/all_to_all | solution.py:15
  42.3 4.5 %collective-permute-start.2 = (f32[96,1024]{1,0:T(8,128)S(1)}, f32[96,1024]{1,0:T(8,128)S(1)}, u32[]{:S(2)}, u32[]{:S(2)}) collective-permute-start(f32[96,1024]{1,0:T(8,128)S(1)} %constant_dynamic-slice_fusion), channel_id=1, source_target_pairs={{0,384},{128,0},{256,128},{384,256},{1,385},{129,1},{257,129},{385... | collective-permute-start | bytes 1179656 | tf_op jit(solution)/shard_map/ppermute | solution.py:32
  48.9 14.1 %collective-permute-done.2 = f32[96,1024]{1,0:T(8,128)S(1)} collective-permute-done((f32[96,1024]{1,0:T(8,128)S(1)}, f32[96,1024]{1,0:T(8,128)S(1)}, u32[]{:S(2)}, u32[]{:S(2)}) %collective-permute-start.2) | collective-permute-done | bytes 393248 | tf_op jit(solution)/shard_map/ppermute | solution.py:32
  64.6 1.9 fusion.29
  66.5 2.4 %collective-permute-start.3 = (f32[64,1024]{1,0:T(8,128)S(1)}, f32[64,1024]{1,0:T(8,128)S(1)}, u32[]{:S(2)}, u32[]{:S(2)}) collective-permute-start(f32[64,1024]{1,0:T(8,128)S(1)} %get-tuple-element.26), channel_id=1, source_target_pairs={{0,8},{8,16},{16,24},{24,32},{32,40},{40,48},{48,56},{56,64},{64,7... | collective-permute-start | bytes 786440 | tf_op jit(solution)/shard_map/ppermute | solution.py:23
  69.0 3.3 %collective-permute-start.5 = (f32[64,1024]{1,0:T(8,128)S(1)}, f32[64,1024]{1,0:T(8,128)S(1)}, u32[]{:S(2)}, u32[]{:S(2)}) collective-permute-start(f32[64,1024]{1,0:T(8,128)S(1)} %get-tuple-element.27), channel_id=1, source_target_pairs={{0,16},{1,113},{8,24},{9,121},{16,32},{17,1},{24,40},{25,9},{32,48... | collective-permute-start | bytes 786440 | tf_op jit(solution)/shard_map/ppermute | solution.py:28
  72.3 2.9 %collective-permute-start.4 = (f32[64,1024]{1,0:T(8,128)S(1)}, f32[64,1024]{1,0:T(8,128)S(1)}, u32[]{:S(2)}, u32[]{:S(2)}) collective-permute-start(f32[64,1024]{1,0:T(8,128)S(1)} %get-tuple-element.28), channel_id=1, source_target_pairs={{0,120},{8,0},{16,8},{24,16},{32,24},{40,32},{48,40},{56,48},{64,5... | collective-permute-start | bytes 786440 | tf_op jit(solution)/shard_map/ppermute | solution.py:23
  75.2 1.4 collective-permute-done.3
  76.6 2.0 collective-permute-done.5
  78.5 7.1 %collective-permute-done.4 = f32[64,1024]{1,0:T(8,128)S(1)} collective-permute-done((f32[64,1024]{1,0:T(8,128)S(1)}, f32[64,1024]{1,0:T(8,128)S(1)}, u32[]{:S(2)}, u32[]{:S(2)}) %collective-permute-start.4) | collective-permute-done | bytes 262176 | tf_op jit(solution)/shard_map/ppermute | solution.py:23
  86.4 9.9 %all-to-all-start.2 = ((f32[4,16,1024]{2,1,0:T(8,128)}), f32[4,16,1024]{2,1,0:T(8,128)S(1)}, u32[]{:S(2)}, u32[]{:S(2)}) async-start(f32[4,16,1024]{2,1,0:T(8,128)} %bitcast.8), calls=%async_computation.2 | async-start | bytes 524288 | tf_op jit(solution)/shard_map/all_to_all | solution.py:15
  96.8 19.3 %all-to-all-done.2 = f32[4,16,1024]{2,1,0:T(8,128)S(1)} async-done(((f32[4,16,1024]{2,1,0:T(8,128)}), f32[4,16,1024]{2,1,0:T(8,128)S(1)}, u32[]{:S(2)}, u32[]{:S(2)}) %all-to-all-start.2) | async-done | bytes 262176 | tf_op jit(solution)/shard_map/all_to_all | solution.py:15
  117.1 6.6 %all-to-all-start.3 = ((f32[32,3,16]{2,1,0:T(4,128)}), f32[32,3,16]{2,1,0:T(4,128)S(1)}, u32[]{:S(2)}, u32[]{:S(2)}) async-start(f32[32,3,16]{2,1,0:T(4,128)} %broadcast_in_dim.116), calls=%async_computation.3 | async-start | bytes 131072 | tf_op jit(solution)/shard_map/all_to_all | solution.py:15
  123.8 7.4 %all-to-all-done.3 = f32[32,3,16]{2,1,0:T(4,128)S(1)} async-done(((f32[32,3,16]{2,1,0:T(4,128)}), f32[32,3,16]{2,1,0:T(4,128)S(1)}, u32[]{:S(2)}, u32[]{:S(2)}) %all-to-all-start.3) | async-done | bytes 6176 | tf_op jit(solution)/shard_map/all_to_all | solution.py:15
  131.4 19.6 %all_to_all.44 = f32[4,16,1024]{2,1,0:T(8,128)S(1)} all-to-all(f32[4,16,1024]{2,1,0:T(8,128)S(1)} %broadcast_in_dim.117), channel_id=1, replica_groups=mesh['x'=4,'h'=4,'l'=4,'y'=4,'c'=2] {'h'}, dimensions={0} | all-to-all | bytes 524288 | tf_op jit(solution)/shard_map/all_to_all | solution.py:15
  151.0 8.0 %collective-permute-start.8 = (f32[64,1024]{1,0:T(8,128)S(1)}, f32[64,1024]{1,0:T(8,128)S(1)}, u32[]{:S(2)}, u32[]{:S(2)}) collective-permute-start(f32[64,1024]{1,0:T(8,128)S(1)} %bitcast.56), channel_id=1, source_target_pairs={{0,8},{8,16},{16,24},{24,32},{32,40},{40,48},{48,56},{56,64},{64,7... | collective-permute-start | bytes 786440 | tf_op jit(solution)/shard_map/ppermute | solution.py:23
  159.0 1.9 collective-permute-start.7
  160.9 1.9 collective-permute-start.6
  164.1 7.6 %collective-permute-done.7 = f32[64,1024]{1,0:T(8,128)S(1)} collective-permute-done((f32[64,1024]{1,0:T(8,128)S(1)}, f32[64,1024]{1,0:T(8,128)S(1)}, u32[]{:S(2)}, u32[]{:S(2)}) %collective-permute-start.7) | collective-permute-done | bytes 262176 | tf_op jit(solution)/shard_map/ppermute | solution.py:28
  175.1 4.7 %all-to-all-start.5 = ((f32[32,16,384]{2,1,0:T(8,128)}), f32[32,16,384]{2,1,0:T(8,128)S(1)}, u32[]{:S(2)}, u32[]{:S(2)}) async-start(f32[32,16,384]{2,1,0:T(8,128)} %bitcast.15), calls=%async_computation.5 | async-start | bytes 1572864 | tf_op jit(solution)/shard_map/all_to_all | solution.py:15
  179.8 1.9 fusion.2
  182.6 3.3 %collective-permute-start.9 = (f32[96,1024]{1,0:T(8,128)}, f32[96,1024]{1,0:T(8,128)}, u32[]{:S(2)}, u32[]{:S(2)}) collective-permute-start(f32[96,1024]{1,0:T(8,128)} %get-tuple-element.23), channel_id=1, source_target_pairs={{0,128},{128,256},{256,384},{384,0},{1,129},{129,257},{257,385},{3... | collective-permute-start | bytes 1179656 | tf_op jit(solution)/shard_map/ppermute | solution.py:32
  185.9 3.2 %collective-permute-start.10 = (f32[96,1024]{1,0:T(8,128)S(1)}, f32[96,1024]{1,0:T(8,128)}, u32[]{:S(2)}, u32[]{:S(2)}) collective-permute-start(f32[96,1024]{1,0:T(8,128)S(1)} %get-tuple-element.22), channel_id=1, source_target_pairs={{0,384},{128,0},{256,128},{384,256},{1,385},{129,1},{257,129},{385... | collective-permute-start | bytes 1179656 | tf_op jit(solution)/shard_map/ppermute | solution.py:32
  189.6 3.6 %collective-permute-start.11 = (f32[96,1024]{1,0:T(8,128)S(1)}, f32[96,1024]{1,0:T(8,128)}, u32[]{:S(2)}, u32[]{:S(2)}) collective-permute-start(f32[96,1024]{1,0:T(8,128)S(1)} %get-tuple-element.21), channel_id=1, source_target_pairs={{0,256},{128,384},{256,0},{384,128},{1,257},{129,385},{257,1},{385... | collective-permute-start | bytes 1179656 | tf_op jit(solution)/shard_map/ppermute | solution.py:32
  194.9 3.7 %all-to-all-start.6 = ((f32[16,1,512]{2,1,0:T(1,128)}), f32[16,1,512]{2,1,0:T(1,128)S(1)}, u32[]{:S(2)}, u32[]{:S(2)}) async-start(f32[16,1,512]{2,1,0:T(1,128)} %reshape.278), calls=%async_computation.6 | async-start | bytes 65536 | tf_op jit(solution)/shard_map/all_to_all | solution.py:15
  202.5 7.8 %all-to-all-done.6 = f32[16,1,512]{2,1,0:T(1,128)S(1)} async-done(((f32[16,1,512]{2,1,0:T(1,128)}), f32[16,1,512]{2,1,0:T(1,128)S(1)}, u32[]{:S(2)}, u32[]{:S(2)}) %all-to-all-start.6) | async-done | bytes 32800 | tf_op jit(solution)/shard_map/all_to_all | solution.py:15
  211.2 5.7 %all-to-all-start.7 = ((f32[8,1,6144]{2,1,0:T(1,128)}), f32[8,1,6144]{2,1,0:T(1,128)S(1)}, u32[]{:S(2)}, u32[]{:S(2)}) async-start(f32[8,1,6144]{2,1,0:T(1,128)} %broadcast_in_dim.120), calls=%async_computation.7 | async-start | bytes 393216 | tf_op jit(solution)/shard_map/all_to_all | solution.py:15
  218.6 4.3 %all-to-all-done.7 = f32[8,1,6144]{2,1,0:T(1,128)S(1)} async-done(((f32[8,1,6144]{2,1,0:T(1,128)}), f32[8,1,6144]{2,1,0:T(1,128)S(1)}, u32[]{:S(2)}, u32[]{:S(2)}) %all-to-all-start.7) | async-done | bytes 196640 | tf_op jit(solution)/shard_map/all_to_all | solution.py:15
  (84 shorter events, 27.2 us)
Async XLA Ops:
  0.6 2.1 copy-start
  3.6 27.2 %all-to-all-start = ((f32[16,1,512]{2,1,0:T(1,128)}), f32[16,1,512]{2,1,0:T(1,128)S(1)}, u32[]{:S(2)}, u32[]{:S(2)}) async-start(f32[16,1,512]{2,1,0:T(1,128)} %copy.22), calls=%async_computation | async-start | bytes 65536 | tf_op jit(solution)/shard_map/all_to_all | solution.py:15
  21.4 26.5 %collective-permute-start.1 = (f32[96,1024]{1,0:T(8,128)S(1)}, f32[96,1024]{1,0:T(8,128)}, u32[]{:S(2)}, u32[]{:S(2)}) collective-permute-start(f32[96,1024]{1,0:T(8,128)S(1)} %get-tuple-element.24), channel_id=1, source_target_pairs={{0,256},{128,384},{256,0},{384,128},{1,257},{129,385},{257,1},{385... | collective-permute-start | bytes 1179656 | tf_op jit(solution)/shard_map/ppermute | solution.py:32
  26.0 20.8 %collective-permute-start = (f32[96,1024]{1,0:T(8,128)}, f32[96,1024]{1,0:T(8,128)}, u32[]{:S(2)}, u32[]{:S(2)}) collective-permute-start(f32[96,1024]{1,0:T(8,128)} %get-tuple-element.25), channel_id=1, source_target_pairs={{0,128},{128,256},{256,384},{384,0},{1,129},{129,257},{257,385},{3... | collective-permute-start | bytes 1179656 | tf_op jit(solution)/shard_map/ppermute | solution.py:32
  32.0 31.1 %all-to-all-start.1 = ((f32[32,16,512]{2,1,0:T(8,128)}), f32[32,16,512]{2,1,0:T(8,128)S(1)}, u32[]{:S(2)}, u32[]{:S(2)}) async-start(f32[32,16,512]{2,1,0:T(8,128)} %broadcast_in_dim.104), calls=%async_computation.1 | async-start | bytes 2097152 | tf_op jit(solution)/shard_map/all_to_all | solution.py:15
  42.3 20.8 %collective-permute-start.2 = (f32[96,1024]{1,0:T(8,128)S(1)}, f32[96,1024]{1,0:T(8,128)S(1)}, u32[]{:S(2)}, u32[]{:S(2)}) collective-permute-start(f32[96,1024]{1,0:T(8,128)S(1)} %constant_dynamic-slice_fusion), channel_id=1, source_target_pairs={{0,384},{128,0},{256,128},{384,256},{1,385},{129,1},{257,129},{385... | collective-permute-start | bytes 1179656 | tf_op jit(solution)/shard_map/ppermute | solution.py:32
  66.5 10.1 %collective-permute-start.3 = (f32[64,1024]{1,0:T(8,128)S(1)}, f32[64,1024]{1,0:T(8,128)S(1)}, u32[]{:S(2)}, u32[]{:S(2)}) collective-permute-start(f32[64,1024]{1,0:T(8,128)S(1)} %get-tuple-element.26), channel_id=1, source_target_pairs={{0,8},{8,16},{16,24},{24,32},{32,40},{40,48},{48,56},{56,64},{64,7... | collective-permute-start | bytes 786440 | tf_op jit(solution)/shard_map/ppermute | solution.py:23
  69.0 9.6 %collective-permute-start.5 = (f32[64,1024]{1,0:T(8,128)S(1)}, f32[64,1024]{1,0:T(8,128)S(1)}, u32[]{:S(2)}, u32[]{:S(2)}) collective-permute-start(f32[64,1024]{1,0:T(8,128)S(1)} %get-tuple-element.27), channel_id=1, source_target_pairs={{0,16},{1,113},{8,24},{9,121},{16,32},{17,1},{24,40},{25,9},{32,48... | collective-permute-start | bytes 786440 | tf_op jit(solution)/shard_map/ppermute | solution.py:28
  72.3 13.4 %collective-permute-start.4 = (f32[64,1024]{1,0:T(8,128)S(1)}, f32[64,1024]{1,0:T(8,128)S(1)}, u32[]{:S(2)}, u32[]{:S(2)}) collective-permute-start(f32[64,1024]{1,0:T(8,128)S(1)} %get-tuple-element.28), channel_id=1, source_target_pairs={{0,120},{8,0},{16,8},{24,16},{32,24},{40,32},{48,40},{56,48},{64,5... | collective-permute-start | bytes 786440 | tf_op jit(solution)/shard_map/ppermute | solution.py:23
  86.4 29.7 %all-to-all-start.2 = ((f32[4,16,1024]{2,1,0:T(8,128)}), f32[4,16,1024]{2,1,0:T(8,128)S(1)}, u32[]{:S(2)}, u32[]{:S(2)}) async-start(f32[4,16,1024]{2,1,0:T(8,128)} %bitcast.8), calls=%async_computation.2 | async-start | bytes 524288 | tf_op jit(solution)/shard_map/all_to_all | solution.py:15
  117.1 14.0 %all-to-all-start.3 = ((f32[32,3,16]{2,1,0:T(4,128)}), f32[32,3,16]{2,1,0:T(4,128)S(1)}, u32[]{:S(2)}, u32[]{:S(2)}) async-start(f32[32,3,16]{2,1,0:T(4,128)} %broadcast_in_dim.116), calls=%async_computation.3 | async-start | bytes 131072 | tf_op jit(solution)/shard_map/all_to_all | solution.py:15
  151.0 13.2 %collective-permute-start.8 = (f32[64,1024]{1,0:T(8,128)S(1)}, f32[64,1024]{1,0:T(8,128)S(1)}, u32[]{:S(2)}, u32[]{:S(2)}) collective-permute-start(f32[64,1024]{1,0:T(8,128)S(1)} %bitcast.56), channel_id=1, source_target_pairs={{0,8},{8,16},{16,24},{24,32},{32,40},{40,48},{48,56},{56,64},{64,7... | collective-permute-start | bytes 786440 | tf_op jit(solution)/shard_map/ppermute | solution.py:23
  159.0 12.7 %collective-permute-start.7 = (f32[64,1024]{1,0:T(8,128)S(1)}, f32[64,1024]{1,0:T(8,128)S(1)}, u32[]{:S(2)}, u32[]{:S(2)}) collective-permute-start(f32[64,1024]{1,0:T(8,128)S(1)} %bitcast.57), channel_id=1, source_target_pairs={{0,16},{1,113},{8,24},{9,121},{16,32},{17,1},{24,40},{25,9},{32,48... | collective-permute-start | bytes 786440 | tf_op jit(solution)/shard_map/ppermute | solution.py:28
  160.9 11.8 %collective-permute-start.6 = (f32[64,1024]{1,0:T(8,128)S(1)}, f32[64,1024]{1,0:T(8,128)S(1)}, u32[]{:S(2)}, u32[]{:S(2)}) collective-permute-start(f32[64,1024]{1,0:T(8,128)S(1)} %bitcast.58), channel_id=1, source_target_pairs={{0,120},{8,0},{16,8},{24,16},{32,24},{40,32},{48,40},{56,48},{64,5... | collective-permute-start | bytes 786440 | tf_op jit(solution)/shard_map/ppermute | solution.py:23
  171.7 3.4 %copy-start.2 = (f32[64,1024]{1,0:T(8,128)}, f32[64,1024]{1,0:T(8,128)S(1)}, u32[]{:S(2)}) copy-start(f32[64,1024]{1,0:T(8,128)S(1)} %collective-permute-done.7) | copy-start | bytes 786436
  172.7 2.4 %copy-start.3 = (f32[64,1024]{1,0:T(8,128)}, f32[64,1024]{1,0:T(8,128)S(1)}, u32[]{:S(2)}) copy-start(f32[64,1024]{1,0:T(8,128)S(1)} %collective-permute-done.6) | copy-start | bytes 786436
  175.1 19.1 %all-to-all-start.5 = ((f32[32,16,384]{2,1,0:T(8,128)}), f32[32,16,384]{2,1,0:T(8,128)S(1)}, u32[]{:S(2)}, u32[]{:S(2)}) async-start(f32[32,16,384]{2,1,0:T(8,128)} %bitcast.15), calls=%async_computation.5 | async-start | bytes 1572864 | tf_op jit(solution)/shard_map/all_to_all | solution.py:15
  182.6 17.8 %collective-permute-start.9 = (f32[96,1024]{1,0:T(8,128)}, f32[96,1024]{1,0:T(8,128)}, u32[]{:S(2)}, u32[]{:S(2)}) collective-permute-start(f32[96,1024]{1,0:T(8,128)} %get-tuple-element.23), channel_id=1, source_target_pairs={{0,128},{128,256},{256,384},{384,0},{1,129},{129,257},{257,385},{3... | collective-permute-start | bytes 1179656 | tf_op jit(solution)/shard_map/ppermute | solution.py:32
  185.9 15.5 %collective-permute-start.10 = (f32[96,1024]{1,0:T(8,128)S(1)}, f32[96,1024]{1,0:T(8,128)}, u32[]{:S(2)}, u32[]{:S(2)}) collective-permute-start(f32[96,1024]{1,0:T(8,128)S(1)} %get-tuple-element.22), channel_id=1, source_target_pairs={{0,384},{128,0},{256,128},{384,256},{1,385},{129,1},{257,129},{385... | collective-permute-start | bytes 1179656 | tf_op jit(solution)/shard_map/ppermute | solution.py:32
  189.6 27.4 %collective-permute-start.11 = (f32[96,1024]{1,0:T(8,128)S(1)}, f32[96,1024]{1,0:T(8,128)}, u32[]{:S(2)}, u32[]{:S(2)}) collective-permute-start(f32[96,1024]{1,0:T(8,128)S(1)} %get-tuple-element.21), channel_id=1, source_target_pairs={{0,256},{128,384},{256,0},{384,128},{1,257},{129,385},{257,1},{385... | collective-permute-start | bytes 1179656 | tf_op jit(solution)/shard_map/ppermute | solution.py:32
  194.9 15.3 %all-to-all-start.6 = ((f32[16,1,512]{2,1,0:T(1,128)}), f32[16,1,512]{2,1,0:T(1,128)S(1)}, u32[]{:S(2)}, u32[]{:S(2)}) async-start(f32[16,1,512]{2,1,0:T(1,128)} %reshape.278), calls=%async_computation.6 | async-start | bytes 65536 | tf_op jit(solution)/shard_map/all_to_all | solution.py:15
  211.2 11.6 %all-to-all-start.7 = ((f32[8,1,6144]{2,1,0:T(1,128)}), f32[8,1,6144]{2,1,0:T(1,128)S(1)}, u32[]{:S(2)}, u32[]{:S(2)}) async-start(f32[8,1,6144]{2,1,0:T(1,128)} %broadcast_in_dim.120), calls=%async_computation.7 | async-start | bytes 393216 | tf_op jit(solution)/shard_map/all_to_all | solution.py:15
  218.0 5.6 %copy-start.1 = (f32[96,4096]{1,0:T(8,128)}, f32[96,4096]{1,0:T(8,128)S(1)}, u32[]{:S(2)}) copy-start(f32[96,4096]{1,0:T(8,128)S(1)} %constant_dynamic-update-slice_fusion) | copy-start | bytes 4718596

commit v10 on v8

--- a/solution.py
+++ b/solution.py
@@ -52,14 +52,13 @@
     def cut(array, s):
         return lax.dynamic_slice(array, (0, (x + s) % 4 * quarter), (depth, quarter))
 
+    first = shift_x(cut(weight, 1), 1)
     packed, weight = lax.optimization_barrier((packed, weight))
-    pieces = [cut(weight, 0), shift_x(cut(weight, 1), 1), shift_x(cut(weight, 2), 2)]
+    pieces = [cut(weight, 0), first, shift_x(cut(weight, 2), 2), shift_x(cut(weight, 3), 3)]
     mine = swap(packed.reshape(16, 1, wide + META), Z).reshape(16, wide + META)
-    mine, weight = lax.optimization_barrier((mine, weight))
-    pieces.append(shift_x(cut(weight, 3), 3))
 
     slots = spread(mine, ("x", "y"), 16).reshape(256, wide + META)
-    slots, pieces[2], pieces[3] = lax.optimization_barrier((slots, pieces[2], pieces[3]))
+    slots, pieces[3] = lax.optimization_barrier((slots, pieces[3]))
     slots_other = lax.ppermute(slots, "c", [(0, 1), (1, 0)])
 
     all_notes = slots[:, wide : wide + 10].astype(jnp.int32)
@@ -123,11 +122,14 @@
     summed = jnp.sum(swap(leaving, XYC), axis=0)
 
     grad_head = dot(hidden, grads, (0, 0), GRAD).reshape(4, depth, quarter)
-    grad_weight = jnp.zeros((depth, columns), jnp.float32)
-    for s in (0, 1, 3, 2):
-        part = lax.dynamic_index_in_dim(grad_head, (x + s) % 4, 0, False)
-        part = shift_x(part, s) if s else part
-        grad_weight = lax.dynamic_update_slice(grad_weight, part, (0, (x - s) % 4 * quarter))
+    summed, grad_head_later = lax.optimization_barrier((summed, grad_head))
+
+    def part(array, s):
+        return lax.dynamic_index_in_dim(array, (x + s) % 4, 0, False)
+
+    grad_weight = jnp.tile(part(grad_head_later, 0), (1, 4))
+    for s in (1, 3, 2):
+        grad_weight = lax.dynamic_update_slice(grad_weight, shift_x(part(grad_head, s), s), (0, (x - s) % 4 * quarter))
 
     parts = lax.dynamic_update_slice(jnp.zeros((16, META), jnp.float32), logprobs.reshape(4, 4), (h * 4, 0))
     parts = jnp.where(l == x, parts, 0.0)

time: 222 us -> 224 us (level)
  waiting for transfers between devices: 72.8 us -> 80.6 us
  local copies, waits for them, and re-layouts: 21.8 us -> 17.4 us
    all_to_all x8, waiting for transfers between devices: 47.1 us -> 58 us  [swap(): return lax.all_to_all(blocks, axes, split_axis=0, concat_axis=0, tiled=True)]
    ppermute x6, waiting for transfers between devices: 7.37 us -> 3.91 us  [shift_x(): return lax.ppermute(block, 'x', [(i, (i + step) % 4) for i in range(4)])]
    all_to_all x8, starting transfers between devices: 62.4 us -> 59.4 us  [swap(): return lax.all_to_all(blocks, axes, split_axis=0, concat_axis=0, tiled=True)]
    dynamic_update_slice x4 -> x3, local copies, waits for them, and re-layouts: 6.07 us -> 3.08 us  [on_device(): lax.dynamic_update_slice(grad_weight, shift_x(part(grad_head, s), s), (0,...]
  transfers between devices with their start and end apart: 21 -> 21, of which waited for: 14 -> 14; matrix products, arithmetic and copies ran while one was open for 10% -> 8% of each run, Pallas kernels for 0% -> 0%
where the time goes in v10:
time: 224 us; the launch traced here: 222 us
  starting transfers between devices  110 us (49%)
  waiting for transfers between devices  80.6 us (36%)
  local copies, waits for them, and re-layouts  17.4 us (8%)
  matrix products  7.94 us (4%)
  other arithmetic  3.64 us (2%)
  between operations  2.59 us (1%)
    all_to_all x8, starting transfers between devices, swap(): return lax.all_to_all(blocks, axes, split_axis=0, concat_axis=0, tiled=True)  59.4 us
    all_to_all x8, waiting for transfers between devices, swap(): return lax.all_to_all(blocks, axes, split_axis=0, concat_axis=0, tiled=True)  58 us
    ppermute x6, starting transfers between devices, shift_x(): return lax.ppermute(block, 'x', [(i, (i + step) % 4) for i in range(4)])  21.5 us
    ppermute x4, starting transfers between devices, shift_z(): return lax.ppermute(block, Z, [(i, (i + step) % 16) for i in range(16)])  17.4 us
    ppermute x4, waiting for transfers between devices, shift_z(): return lax.ppermute(block, Z, [(i, (i + step) % 16) for i in range(16)])  10.1 us
    dot_general x6, matrix products, dot(): lax.dot_general(a, b, dims, precision=precision, preferred_element_type=j...  7.94 us
    ppermute x2, waiting for transfers between devices, shift_far(): return lax.ppermute(block, ('h', 'l', 'c'), pairs)  7.59 us
    ppermute x2, starting transfers between devices, shift_far(): return lax.ppermute(block, ('h', 'l', 'c'), pairs)  7.46 us
  transfers between devices with their start and end apart: 21, of which 14 were waited for; matrix products, arithmetic and copies ran while one was open for 8% of the time, Pallas kernels for 0%

profile of v10, /device:TPU:1, one launch (start us, length us, event | category | flops | bytes accessed | tf_op | source)
XLA Modules:
  0.0 222.5 jit_solution(1386036115134063849)
XLA Ops:
  1.7 3.9 %collective-permute-start.2 = (f32[96,1024]{1,0:T(8,128)S(1)}, f32[96,1024]{1,0:T(8,128)S(1)}, u32[]{:S(2)}, u32[]{:S(2)}) collective-permute-start(f32[96,1024]{1,0:T(8,128)S(1)} %constant_dynamic-slice_fusion.1), channel_id=1, source_target_pairs={{0,128},{128,256},{256,384},{384,0},{1,129},{129,257},{257,385},{3... | collective-permute-start | bytes 1179656 | tf_op jit(solution)/shard_map/ppermute | solution.py:32
  8.7 14.9 %all-to-all-start = ((f32[16,1,512]{2,1,0:T(1,128)}), f32[16,1,512]{2,1,0:T(1,128)S(1)}, u32[]{:S(2)}, u32[]{:S(2)}) async-start(f32[16,1,512]{2,1,0:T(1,128)} %copy.25), calls=%async_computation | async-start | bytes 65536 | tf_op jit(solution)/shard_map/all_to_all | solution.py:15
  25.7 4.3 %collective-permute-start.3 = (f32[96,1024]{1,0:T(8,128)}, f32[96,1024]{1,0:T(8,128)}, u32[]{:S(2)}, u32[]{:S(2)}) collective-permute-start(f32[96,1024]{1,0:T(8,128)} %get-tuple-element.24), channel_id=1, source_target_pairs={{0,256},{128,384},{256,0},{384,128},{1,257},{129,385},{257,1},{385... | collective-permute-start | bytes 1179656 | tf_op jit(solution)/shard_map/ppermute | solution.py:32
  30.1 3.1 %collective-permute-start = (f32[96,1024]{1,0:T(8,128)}, f32[96,1024]{1,0:T(8,128)S(1)}, u32[]{:S(2)}, u32[]{:S(2)}) collective-permute-start(f32[96,1024]{1,0:T(8,128)} %get-tuple-element.25), channel_id=1, source_target_pairs={{0,384},{128,0},{256,128},{384,256},{1,385},{129,1},{257,129},{385... | collective-permute-start | bytes 1179656 | tf_op jit(solution)/shard_map/ppermute | solution.py:32
  35.9 6.5 %all-to-all-start.1 = ((f32[16,16,512]{2,1,0:T(8,128)}), f32[16,16,512]{2,1,0:T(8,128)S(1)}, u32[]{:S(2)}, u32[]{:S(2)}) async-start(f32[16,16,512]{2,1,0:T(8,128)} %broadcast_in_dim.146), calls=%async_computation.1 | async-start | bytes 1048576 | tf_op jit(solution)/shard_map/all_to_all | solution.py:15
  43.6 3.9 %collective-permute-done = f32[96,1024]{1,0:T(8,128)S(1)} collective-permute-done((f32[96,1024]{1,0:T(8,128)}, f32[96,1024]{1,0:T(8,128)S(1)}, u32[]{:S(2)}, u32[]{:S(2)}) %collective-permute-start) | collective-permute-done | bytes 393248 | tf_op jit(solution)/shard_map/ppermute | solution.py:32
  47.5 6.1 %all-to-all-done.1 = f32[16,16,512]{2,1,0:T(8,128)S(1)} async-done(((f32[16,16,512]{2,1,0:T(8,128)}), f32[16,16,512]{2,1,0:T(8,128)S(1)}, u32[]{:S(2)}, u32[]{:S(2)}) %all-to-all-start.1) | async-done | bytes 524320 | tf_op jit(solution)/shard_map/all_to_all | solution.py:15
  53.6 4.4 %collective-permute-start.1 = (f32[256,512]{1,0:T(8,128)S(1)}, f32[256,512]{1,0:T(8,128)}, u32[]{:S(2)}, u32[]{:S(2)}) collective-permute-start(f32[256,512]{1,0:T(8,128)S(1)} %bitcast.58), channel_id=1, source_target_pairs={{0,1},{1,0},{2,3},{3,2},{4,5},{5,4},{6,7},{7,6},{8,9},{9,8},{10,11... | collective-permute-start | bytes 1572872 | tf_op jit(solution)/shard_map/ppermute | solution.py:62
  63.5 3.2 %collective-permute-start.4 = (f32[64,1024]{1,0:T(8,128)S(1)}, f32[64,1024]{1,0:T(8,128)S(1)}, u32[]{:S(2)}, u32[]{:S(2)}) collective-permute-start(f32[64,1024]{1,0:T(8,128)S(1)} %get-tuple-element.26), channel_id=1, source_target_pairs={{0,8},{8,16},{16,24},{24,32},{32,40},{40,48},{48,56},{56,64},{64,7... | collective-permute-start | bytes 786440 | tf_op jit(solution)/shard_map/ppermute | solution.py:23
  66.7 4.3 %collective-permute-start.6 = (f32[64,1024]{1,0:T(8,128)S(1)}, f32[64,1024]{1,0:T(8,128)S(1)}, u32[]{:S(2)}, u32[]{:S(2)}) collective-permute-start(f32[64,1024]{1,0:T(8,128)S(1)} %get-tuple-element.27), channel_id=1, source_target_pairs={{0,16},{1,113},{8,24},{9,121},{16,32},{17,1},{24,40},{25,9},{32,48... | collective-permute-start | bytes 786440 | tf_op jit(solution)/shard_map/ppermute | solution.py:28
  71.0 3.1 %collective-permute-start.5 = (f32[64,1024]{1,0:T(8,128)S(1)}, f32[64,1024]{1,0:T(8,128)S(1)}, u32[]{:S(2)}, u32[]{:S(2)}) collective-permute-start(f32[64,1024]{1,0:T(8,128)S(1)} %get-tuple-element.28), channel_id=1, source_target_pairs={{0,120},{8,0},{16,8},{24,16},{32,24},{40,32},{48,40},{56,48},{64,5... | collective-permute-start | bytes 786440 | tf_op jit(solution)/shard_map/ppermute | solution.py:23
  74.1 2.7 %collective-permute-done.6 = f32[64,1024]{1,0:T(8,128)S(1)} collective-permute-done((f32[64,1024]{1,0:T(8,128)S(1)}, f32[64,1024]{1,0:T(8,128)S(1)}, u32[]{:S(2)}, u32[]{:S(2)}) %collective-permute-start.6) | collective-permute-done | bytes 262176 | tf_op jit(solution)/shard_map/ppermute | solution.py:28
  76.9 6.3 %collective-permute-done.5 = f32[64,1024]{1,0:T(8,128)S(1)} collective-permute-done((f32[64,1024]{1,0:T(8,128)S(1)}, f32[64,1024]{1,0:T(8,128)S(1)}, u32[]{:S(2)}, u32[]{:S(2)}) %collective-permute-start.5) | collective-permute-done | bytes 262176 | tf_op jit(solution)/shard_map/ppermute | solution.py:23
  84.0 11.3 %all-to-all-start.2 = ((f32[4,16,1024]{2,1,0:T(8,128)}), f32[4,16,1024]{2,1,0:T(8,128)S(1)}, u32[]{:S(2)}, u32[]{:S(2)}) async-start(f32[4,16,1024]{2,1,0:T(8,128)} %bitcast.11), calls=%async_computation.2 | async-start | bytes 524288 | tf_op jit(solution)/shard_map/all_to_all | solution.py:15
  95.9 16.8 %all-to-all-done.2 = f32[4,16,1024]{2,1,0:T(8,128)S(1)} async-done(((f32[4,16,1024]{2,1,0:T(8,128)}), f32[4,16,1024]{2,1,0:T(8,128)S(1)}, u32[]{:S(2)}, u32[]{:S(2)}) %all-to-all-start.2) | async-done | bytes 262176 | tf_op jit(solution)/shard_map/all_to_all | solution.py:15
  113.7 8.2 %all-to-all-start.3 = ((f32[32,3,16]{2,1,0:T(4,128)}), f32[32,3,16]{2,1,0:T(4,128)S(1)}, u32[]{:S(2)}, u32[]{:S(2)}) async-start(f32[32,3,16]{2,1,0:T(4,128)} %broadcast_in_dim.164), calls=%async_computation.3 | async-start | bytes 131072 | tf_op jit(solution)/shard_map/all_to_all | solution.py:15
  121.9 7.4 %all-to-all-done.3 = f32[32,3,16]{2,1,0:T(4,128)S(1)} async-done(((f32[32,3,16]{2,1,0:T(4,128)}), f32[32,3,16]{2,1,0:T(4,128)S(1)}, u32[]{:S(2)}, u32[]{:S(2)}) %all-to-all-start.3) | async-done | bytes 6176 | tf_op jit(solution)/shard_map/all_to_all | solution.py:15
  130.2 3.5 %all-to-all-start.4 = ((f32[4,16,1024]{2,1,0:T(8,128)}), f32[4,16,1024]{2,1,0:T(8,128)S(1)}, u32[]{:S(2)}, u32[]{:S(2)}) async-start(f32[4,16,1024]{2,1,0:T(8,128)} %broadcast_in_dim.165), calls=%async_computation.4 | async-start | bytes 524288 | tf_op jit(solution)/shard_map/all_to_all | solution.py:15
  133.8 13.8 %all-to-all-done.4 = f32[4,16,1024]{2,1,0:T(8,128)S(1)} async-done(((f32[4,16,1024]{2,1,0:T(8,128)}), f32[4,16,1024]{2,1,0:T(8,128)S(1)}, u32[]{:S(2)}, u32[]{:S(2)}) %all-to-all-start.4) | async-done | bytes 262176 | tf_op jit(solution)/shard_map/all_to_all | solution.py:15
  147.6 8.4 %collective-permute-start.9 = (f32[64,1024]{1,0:T(8,128)S(1)}, f32[64,1024]{1,0:T(8,128)S(1)}, u32[]{:S(2)}, u32[]{:S(2)}) collective-permute-start(f32[64,1024]{1,0:T(8,128)S(1)} %bitcast.61), channel_id=1, source_target_pairs={{0,8},{8,16},{16,24},{24,32},{32,40},{40,48},{48,56},{56,64},{64,7... | collective-permute-start | bytes 786440 | tf_op jit(solution)/shard_map/ppermute | solution.py:23
  156.0 3.1 %collective-permute-start.8 = (f32[64,1024]{1,0:T(8,128)S(1)}, f32[64,1024]{1,0:T(8,128)S(1)}, u32[]{:S(2)}, u32[]{:S(2)}) collective-permute-start(f32[64,1024]{1,0:T(8,128)S(1)} %bitcast.62), channel_id=1, source_target_pairs={{0,16},{1,113},{8,24},{9,121},{16,32},{17,1},{24,40},{25,9},{32,48... | collective-permute-start | bytes 786440 | tf_op jit(solution)/shard_map/ppermute | solution.py:28
  159.2 2.8 %collective-permute-start.7 = (f32[64,1024]{1,0:T(8,128)S(1)}, f32[64,1024]{1,0:T(8,128)S(1)}, u32[]{:S(2)}, u32[]{:S(2)}) collective-permute-start(f32[64,1024]{1,0:T(8,128)S(1)} %bitcast.63), channel_id=1, source_target_pairs={{0,120},{8,0},{16,8},{24,16},{32,24},{40,32},{48,40},{56,48},{64,5... | collective-permute-start | bytes 786440 | tf_op jit(solution)/shard_map/ppermute | solution.py:23
  162.1 4.9 %collective-permute-done.8 = f32[64,1024]{1,0:T(8,128)S(1)} collective-permute-done((f32[64,1024]{1,0:T(8,128)S(1)}, f32[64,1024]{1,0:T(8,128)S(1)}, u32[]{:S(2)}, u32[]{:S(2)}) %collective-permute-start.8) | collective-permute-done | bytes 262176 | tf_op jit(solution)/shard_map/ppermute | solution.py:28
  166.9 3.7 %collective-permute-done.7 = f32[64,1024]{1,0:T(8,128)S(1)} collective-permute-done((f32[64,1024]{1,0:T(8,128)S(1)}, f32[64,1024]{1,0:T(8,128)S(1)}, u32[]{:S(2)}, u32[]{:S(2)}) %collective-permute-start.7) | collective-permute-done | bytes 262176 | tf_op jit(solution)/shard_map/ppermute | solution.py:23
  173.0 5.0 %all-to-all-start.5 = ((f32[32,16,384]{2,1,0:T(8,128)}), f32[32,16,384]{2,1,0:T(8,128)S(1)}, u32[]{:S(2)}, u32[]{:S(2)}) async-start(f32[32,16,384]{2,1,0:T(8,128)} %bitcast.18), calls=%async_computation.5 | async-start | bytes 1572864 | tf_op jit(solution)/shard_map/all_to_all | solution.py:15
  180.8 3.3 %collective-permute-start.10 = (f32[96,1024]{1,0:T(8,128)}, f32[96,1024]{1,0:T(8,128)}, u32[]{:S(2)}, u32[]{:S(2)}) collective-permute-start(f32[96,1024]{1,0:T(8,128)} %get-tuple-element.23), channel_id=1, source_target_pairs={{0,128},{128,256},{256,384},{384,0},{1,129},{129,257},{257,385},{3... | collective-permute-start | bytes 1179656 | tf_op jit(solution)/shard_map/ppermute | solution.py:32
  184.1 3.2 %collective-permute-start.11 = (f32[96,1024]{1,0:T(8,128)S(1)}, f32[96,1024]{1,0:T(8,128)}, u32[]{:S(2)}, u32[]{:S(2)}) collective-permute-start(f32[96,1024]{1,0:T(8,128)S(1)} %get-tuple-element.22), channel_id=1, source_target_pairs={{0,384},{128,0},{256,128},{384,256},{1,385},{129,1},{257,129},{385... | collective-permute-start | bytes 1179656 | tf_op jit(solution)/shard_map/ppermute | solution.py:32
  187.8 3.6 %collective-permute-start.12 = (f32[96,1024]{1,0:T(8,128)S(1)}, f32[96,1024]{1,0:T(8,128)}, u32[]{:S(2)}, u32[]{:S(2)}) collective-permute-start(f32[96,1024]{1,0:T(8,128)S(1)} %get-tuple-element.21), channel_id=1, source_target_pairs={{0,256},{128,384},{256,0},{384,128},{1,257},{129,385},{257,1},{385... | collective-permute-start | bytes 1179656 | tf_op jit(solution)/shard_map/ppermute | solution.py:32
  193.2 4.3 %all-to-all-start.6 = ((f32[16,1,512]{2,1,0:T(1,128)}), f32[16,1,512]{2,1,0:T(1,128)S(1)}, u32[]{:S(2)}, u32[]{:S(2)}) async-start(f32[16,1,512]{2,1,0:T(1,128)} %reshape.337), calls=%async_computation.6 | async-start | bytes 65536 | tf_op jit(solution)/shard_map/all_to_all | solution.py:15
  201.2 7.9 %all-to-all-done.6 = f32[16,1,512]{2,1,0:T(1,128)S(1)} async-done(((f32[16,1,512]{2,1,0:T(1,128)}), f32[16,1,512]{2,1,0:T(1,128)S(1)}, u32[]{:S(2)}, u32[]{:S(2)}) %all-to-all-start.6) | async-done | bytes 32800 | tf_op jit(solution)/shard_map/all_to_all | solution.py:15
  210.1 5.8 %all-to-all-start.7 = ((f32[8,1,6144]{2,1,0:T(1,128)}), f32[8,1,6144]{2,1,0:T(1,128)S(1)}, u32[]{:S(2)}, u32[]{:S(2)}) async-start(f32[8,1,6144]{2,1,0:T(1,128)} %broadcast_in_dim.168), calls=%async_computation.7 | async-start | bytes 393216 | tf_op jit(solution)/shard_map/all_to_all | solution.py:15
  217.5 4.3 %all-to-all-done.7 = f32[8,1,6144]{2,1,0:T(1,128)S(1)} async-done(((f32[8,1,6144]{2,1,0:T(1,128)}), f32[8,1,6144]{2,1,0:T(1,128)S(1)}, u32[]{:S(2)}, u32[]{:S(2)}) %all-to-all-start.7) | async-done | bytes 196640 | tf_op jit(solution)/shard_map/all_to_all | solution.py:15
  (95 shorter events, 31.9 us)
Async XLA Ops:
  0.6 7.1 %copy-start = (f32[8,6144]{1,0:T(8,128)S(1)}, f32[8,6144]{1,0:T(8,128)}, u32[]{:S(2)}) copy-start(f32[8,6144]{1,0:T(8,128)} %param.5) | copy-start | bytes 589828
  1.7 40.8 %collective-permute-start.2 = (f32[96,1024]{1,0:T(8,128)S(1)}, f32[96,1024]{1,0:T(8,128)S(1)}, u32[]{:S(2)}, u32[]{:S(2)}) collective-permute-start(f32[96,1024]{1,0:T(8,128)S(1)} %constant_dynamic-slice_fusion.1), channel_id=1, source_target_pairs={{0,128},{128,256},{256,384},{384,0},{1,129},{129,257},{257,385},{3... | collective-permute-start | bytes 1179656 | tf_op jit(solution)/shard_map/ppermute | solution.py:32
  8.7 26.4 %all-to-all-start = ((f32[16,1,512]{2,1,0:T(1,128)}), f32[16,1,512]{2,1,0:T(1,128)S(1)}, u32[]{:S(2)}, u32[]{:S(2)}) async-start(f32[16,1,512]{2,1,0:T(1,128)} %copy.25), calls=%async_computation | async-start | bytes 65536 | tf_op jit(solution)/shard_map/all_to_all | solution.py:15
  25.7 16.8 %collective-permute-start.3 = (f32[96,1024]{1,0:T(8,128)}, f32[96,1024]{1,0:T(8,128)}, u32[]{:S(2)}, u32[]{:S(2)}) collective-permute-start(f32[96,1024]{1,0:T(8,128)} %get-tuple-element.24), channel_id=1, source_target_pairs={{0,256},{128,384},{256,0},{384,128},{1,257},{129,385},{257,1},{385... | collective-permute-start | bytes 1179656 | tf_op jit(solution)/shard_map/ppermute | solution.py:32
  30.1 17.4 %collective-permute-start = (f32[96,1024]{1,0:T(8,128)}, f32[96,1024]{1,0:T(8,128)S(1)}, u32[]{:S(2)}, u32[]{:S(2)}) collective-permute-start(f32[96,1024]{1,0:T(8,128)} %get-tuple-element.25), channel_id=1, source_target_pairs={{0,384},{128,0},{256,128},{384,256},{1,385},{129,1},{257,129},{385... | collective-permute-start | bytes 1179656 | tf_op jit(solution)/shard_map/ppermute | solution.py:32
  35.9 17.6 %all-to-all-start.1 = ((f32[16,16,512]{2,1,0:T(8,128)}), f32[16,16,512]{2,1,0:T(8,128)S(1)}, u32[]{:S(2)}, u32[]{:S(2)}) async-start(f32[16,16,512]{2,1,0:T(8,128)} %broadcast_in_dim.146), calls=%async_computation.1 | async-start | bytes 1048576 | tf_op jit(solution)/shard_map/all_to_all | solution.py:15
  53.6 6.1 %collective-permute-start.1 = (f32[256,512]{1,0:T(8,128)S(1)}, f32[256,512]{1,0:T(8,128)}, u32[]{:S(2)}, u32[]{:S(2)}) collective-permute-start(f32[256,512]{1,0:T(8,128)S(1)} %bitcast.58), channel_id=1, source_target_pairs={{0,1},{1,0},{2,3},{3,2},{4,5},{5,4},{6,7},{7,6},{8,9},{9,8},{10,11... | collective-permute-start | bytes 1572872 | tf_op jit(solution)/shard_map/ppermute | solution.py:62
  63.5 10.7 %collective-permute-start.4 = (f32[64,1024]{1,0:T(8,128)S(1)}, f32[64,1024]{1,0:T(8,128)S(1)}, u32[]{:S(2)}, u32[]{:S(2)}) collective-permute-start(f32[64,1024]{1,0:T(8,128)S(1)} %get-tuple-element.26), channel_id=1, source_target_pairs={{0,8},{8,16},{16,24},{24,32},{32,40},{40,48},{48,56},{56,64},{64,7... | collective-permute-start | bytes 786440 | tf_op jit(solution)/shard_map/ppermute | solution.py:23
  66.7 10.2 %collective-permute-start.6 = (f32[64,1024]{1,0:T(8,128)S(1)}, f32[64,1024]{1,0:T(8,128)S(1)}, u32[]{:S(2)}, u32[]{:S(2)}) collective-permute-start(f32[64,1024]{1,0:T(8,128)S(1)} %get-tuple-element.27), channel_id=1, source_target_pairs={{0,16},{1,113},{8,24},{9,121},{16,32},{17,1},{24,40},{25,9},{32,48... | collective-permute-start | bytes 786440 | tf_op jit(solution)/shard_map/ppermute | solution.py:28
  71.0 12.2 %collective-permute-start.5 = (f32[64,1024]{1,0:T(8,128)S(1)}, f32[64,1024]{1,0:T(8,128)S(1)}, u32[]{:S(2)}, u32[]{:S(2)}) collective-permute-start(f32[64,1024]{1,0:T(8,128)S(1)} %get-tuple-element.28), channel_id=1, source_target_pairs={{0,120},{8,0},{16,8},{24,16},{32,24},{40,32},{48,40},{56,48},{64,5... | collective-permute-start | bytes 786440 | tf_op jit(solution)/shard_map/ppermute | solution.py:23
  84.0 28.7 %all-to-all-start.2 = ((f32[4,16,1024]{2,1,0:T(8,128)}), f32[4,16,1024]{2,1,0:T(8,128)S(1)}, u32[]{:S(2)}, u32[]{:S(2)}) async-start(f32[4,16,1024]{2,1,0:T(8,128)} %bitcast.11), calls=%async_computation.2 | async-start | bytes 524288 | tf_op jit(solution)/shard_map/all_to_all | solution.py:15
  113.7 15.5 %all-to-all-start.3 = ((f32[32,3,16]{2,1,0:T(4,128)}), f32[32,3,16]{2,1,0:T(4,128)S(1)}, u32[]{:S(2)}, u32[]{:S(2)}) async-start(f32[32,3,16]{2,1,0:T(4,128)} %broadcast_in_dim.164), calls=%async_computation.3 | async-start | bytes 131072 | tf_op jit(solution)/shard_map/all_to_all | solution.py:15
  130.2 17.5 %all-to-all-start.4 = ((f32[4,16,1024]{2,1,0:T(8,128)}), f32[4,16,1024]{2,1,0:T(8,128)S(1)}, u32[]{:S(2)}, u32[]{:S(2)}) async-start(f32[4,16,1024]{2,1,0:T(8,128)} %broadcast_in_dim.165), calls=%async_computation.4 | async-start | bytes 524288 | tf_op jit(solution)/shard_map/all_to_all | solution.py:15
  147.6 14.4 %collective-permute-start.9 = (f32[64,1024]{1,0:T(8,128)S(1)}, f32[64,1024]{1,0:T(8,128)S(1)}, u32[]{:S(2)}, u32[]{:S(2)}) collective-permute-start(f32[64,1024]{1,0:T(8,128)S(1)} %bitcast.61), channel_id=1, source_target_pairs={{0,8},{8,16},{16,24},{24,32},{32,40},{40,48},{48,56},{56,64},{64,7... | collective-permute-start | bytes 786440 | tf_op jit(solution)/shard_map/ppermute | solution.py:23
  156.0 10.9 %collective-permute-start.8 = (f32[64,1024]{1,0:T(8,128)S(1)}, f32[64,1024]{1,0:T(8,128)S(1)}, u32[]{:S(2)}, u32[]{:S(2)}) collective-permute-start(f32[64,1024]{1,0:T(8,128)S(1)} %bitcast.62), channel_id=1, source_target_pairs={{0,16},{1,113},{8,24},{9,121},{16,32},{17,1},{24,40},{25,9},{32,48... | collective-permute-start | bytes 786440 | tf_op jit(solution)/shard_map/ppermute | solution.py:28
  159.2 11.5 %collective-permute-start.7 = (f32[64,1024]{1,0:T(8,128)S(1)}, f32[64,1024]{1,0:T(8,128)S(1)}, u32[]{:S(2)}, u32[]{:S(2)}) collective-permute-start(f32[64,1024]{1,0:T(8,128)S(1)} %bitcast.63), channel_id=1, source_target_pairs={{0,120},{8,0},{16,8},{24,16},{32,24},{40,32},{48,40},{56,48},{64,5... | collective-permute-start | bytes 786440 | tf_op jit(solution)/shard_map/ppermute | solution.py:23
  166.9 6.1 %copy-start.2 = (f32[64,1024]{1,0:T(8,128)}, f32[64,1024]{1,0:T(8,128)S(1)}, u32[]{:S(2)}) copy-start(f32[64,1024]{1,0:T(8,128)S(1)} %collective-permute-done.8) | copy-start | bytes 786436
  170.7 2.4 %copy-start.3 = (f32[64,1024]{1,0:T(8,128)}, f32[64,1024]{1,0:T(8,128)S(1)}, u32[]{:S(2)}) copy-start(f32[64,1024]{1,0:T(8,128)S(1)} %collective-permute-done.7) | copy-start | bytes 786436
  173.0 19.4 %all-to-all-start.5 = ((f32[32,16,384]{2,1,0:T(8,128)}), f32[32,16,384]{2,1,0:T(8,128)S(1)}, u32[]{:S(2)}, u32[]{:S(2)}) async-start(f32[32,16,384]{2,1,0:T(8,128)} %bitcast.18), calls=%async_computation.5 | async-start | bytes 1572864 | tf_op jit(solution)/shard_map/all_to_all | solution.py:15
  180.8 18.3 %collective-permute-start.10 = (f32[96,1024]{1,0:T(8,128)}, f32[96,1024]{1,0:T(8,128)}, u32[]{:S(2)}, u32[]{:S(2)}) collective-permute-start(f32[96,1024]{1,0:T(8,128)} %get-tuple-element.23), channel_id=1, source_target_pairs={{0,128},{128,256},{256,384},{384,0},{1,129},{129,257},{257,385},{3... | collective-permute-start | bytes 1179656 | tf_op jit(solution)/shard_map/ppermute | solution.py:32
  184.1 16.0 %collective-permute-start.11 = (f32[96,1024]{1,0:T(8,128)S(1)}, f32[96,1024]{1,0:T(8,128)}, u32[]{:S(2)}, u32[]{:S(2)}) collective-permute-start(f32[96,1024]{1,0:T(8,128)S(1)} %get-tuple-element.22), channel_id=1, source_target_pairs={{0,384},{128,0},{256,128},{384,256},{1,385},{129,1},{257,129},{385... | collective-permute-start | bytes 1179656 | tf_op jit(solution)/shard_map/ppermute | solution.py:32
  187.8 28.0 %collective-permute-start.12 = (f32[96,1024]{1,0:T(8,128)S(1)}, f32[96,1024]{1,0:T(8,128)}, u32[]{:S(2)}, u32[]{:S(2)}) collective-permute-start(f32[96,1024]{1,0:T(8,128)S(1)} %get-tuple-element.21), channel_id=1, source_target_pairs={{0,256},{128,384},{256,0},{384,128},{1,257},{129,385},{257,1},{385... | collective-permute-start | bytes 1179656 | tf_op jit(solution)/shard_map/ppermute | solution.py:32
  193.2 15.9 %all-to-all-start.6 = ((f32[16,1,512]{2,1,0:T(1,128)}), f32[16,1,512]{2,1,0:T(1,128)S(1)}, u32[]{:S(2)}, u32[]{:S(2)}) async-start(f32[16,1,512]{2,1,0:T(1,128)} %reshape.337), calls=%async_computation.6 | async-start | bytes 65536 | tf_op jit(solution)/shard_map/all_to_all | solution.py:15
  210.1 11.6 %all-to-all-start.7 = ((f32[8,1,6144]{2,1,0:T(1,128)}), f32[8,1,6144]{2,1,0:T(1,128)S(1)}, u32[]{:S(2)}, u32[]{:S(2)}) async-start(f32[8,1,6144]{2,1,0:T(1,128)} %broadcast_in_dim.168), calls=%async_computation.7 | async-start | bytes 393216 | tf_op jit(solution)/shard_map/all_to_all | solution.py:15
  216.9 5.6 %copy-start.1 = (f32[96,4096]{1,0:T(8,128)}, f32[96,4096]{1,0:T(8,128)S(1)}, u32[]{:S(2)}) copy-start(f32[96,4096]{1,0:T(8,128)S(1)} %constant_dynamic-update-slice_fusion.2) | copy-start | bytes 4718596

commit v11 on v10

--- a/solution.py
+++ b/solution.py
@@ -48,32 +48,32 @@
     row = lax.dynamic_slice(responses, (j, 0), (1, width)).reshape(4, 16, depth)
     notes = jnp.pad(jnp.concatenate([targets, lengths, owners]).astype(jnp.float32), (0, META - 10))
     notes = jnp.broadcast_to(notes, (16, META))
-    packed = jnp.concatenate([row.transpose(1, 0, 2).reshape(16, wide), notes], axis=1)
+    packed = jnp.concatenate([row.transpose(1, 0, 2).reshape(16, wide), notes], axis=1).reshape(1, 16, 1, wide + META)
+    packed = jnp.broadcast_to(packed, (4, 16, 1, wide + META)).reshape(64, 1, wide + META)
+
     def cut(array, s):
         return lax.dynamic_slice(array, (0, (x + s) % 4 * quarter), (depth, quarter))
 
-    first = shift_x(cut(weight, 1), 1)
     packed, weight = lax.optimization_barrier((packed, weight))
-    pieces = [cut(weight, 0), first, shift_x(cut(weight, 2), 2), shift_x(cut(weight, 3), 3)]
-    mine = swap(packed.reshape(16, 1, wide + META), Z).reshape(16, wide + META)
+    pieces = [cut(weight, 0), *(shift_x(cut(weight, s), s) for s in range(1, 4))]
+    mine = swap(packed, ("x", *Z)).reshape(64, wide + META)
 
-    slots = spread(mine, ("x", "y"), 16).reshape(256, wide + META)
+    slots = spread(mine, "y", 4).reshape(256, wide + META)
     slots, pieces[3] = lax.optimization_barrier((slots, pieces[3]))
     slots_other = lax.ppermute(slots, "c", [(0, 1), (1, 0)])
 
     all_notes = slots[:, wide : wide + 10].astype(jnp.int32)
-    source_notes = all_notes.reshape(4, 4, 16, 10)[:, 0].reshape(64, 10)
-    source_length, source_owner = source_notes[:, 8], source_notes[:, 9]
+    source_length, source_owner = all_notes[:64, 8], all_notes[:64, 9]
     sources = jnp.arange(64, dtype=jnp.int32)
 
     def starts_of(source):
         return jnp.sum(jnp.where(sources[None, :] < source[:, None], source_length[None, :], 0), axis=1)
 
     rows = jnp.arange(256, dtype=jnp.int32)
-    starts = starts_of(rows // 64 * 16 + rows % 16)
+    starts = starts_of(rows % 64)
 
     def chosen(core):
-        slot_j = rows // 16 % 4 * 2 + core
+        slot_j = rows // 64 * 2 + core
         rank = jnp.where(slot_j < all_notes[:, 8], (starts + slot_j - 64 * l) % 256, -1)
         target = jnp.sum(jnp.where(jnp.arange(10)[None, :] == slot_j[:, None], all_notes, 0), axis=1)
         select = rank[None, :] == rows[:, None]

time: 224 us -> 218 us (0.973)
  starting transfers between devices: 110 us -> 107 us
  waiting for transfers between devices: 80.6 us -> 78.2 us
    ppermute x2, waiting for transfers between devices: 7.59 us -> 2.88 us  [shift_far(): return lax.ppermute(block, ('h', 'l', 'c'), pairs)]
    ppermute x4, starting transfers between devices: 17.4 us -> 13.3 us  [shift_z(): return lax.ppermute(block, Z, [(i, (i + step) % 16) for i in range(16)])]
    ppermute x4, waiting for transfers between devices: 10.1 us -> 14 us  [shift_z(): return lax.ppermute(block, Z, [(i, (i + step) % 16) for i in range(16)])]
  transfers between devices with their start and end apart: 21 -> 21, of which waited for: 14 -> 14; matrix products, arithmetic and copies ran while one was open for 8% -> 9% of each run, Pallas kernels for 0% -> 0%
where the time goes in v11:
time: 218 us; the launch traced here: 217 us
  starting transfers between devices  107 us (49%)
  waiting for transfers between devices  78.2 us (36%)
  local copies, waits for them, and re-layouts  18.4 us (8%)
  matrix products  6.95 us (3%)
  other arithmetic  3.61 us (2%)
  between operations  2.59 us (1%)
    all_to_all x8, starting transfers between devices, swap(): return lax.all_to_all(blocks, axes, split_axis=0, concat_axis=0, tiled=True)  59.4 us
    all_to_all x8, waiting for transfers between devices, swap(): return lax.all_to_all(blocks, axes, split_axis=0, concat_axis=0, tiled=True)  55.8 us
    ppermute x6, starting transfers between devices, shift_x(): return lax.ppermute(block, 'x', [(i, (i + step) % 4) for i in range(4)])  20.6 us
    ppermute x4, waiting for transfers between devices, shift_z(): return lax.ppermute(block, Z, [(i, (i + step) % 16) for i in range(16)])  14 us
    ppermute x4, starting transfers between devices, shift_z(): return lax.ppermute(block, Z, [(i, (i + step) % 16) for i in range(16)])  13.3 us
    ppermute x2, starting transfers between devices, shift_far(): return lax.ppermute(block, ('h', 'l', 'c'), pairs)  7.75 us
    dot_general x6, matrix products, dot(): lax.dot_general(a, b, dims, precision=precision, preferred_element_type=j...  6.95 us
    ppermute x1, starting transfers between devices, on_device(): slots_other = lax.ppermute(slots, 'c', [(0, 1), (1, 0)])  6.23 us
  transfers between devices with their start and end apart: 21, of which 14 were waited for; matrix products, arithmetic and copies ran while one was open for 9% of the time, Pallas kernels for 0%

profile of v11, /device:TPU:1, one launch (start us, length us, event | category | flops | bytes accessed | tf_op | source)
XLA Modules:
  0.0 217.0 jit_solution(17577572408069209977)
XLA Ops:
  3.8 19.1 %all-to-all-start = ((f32[64,1,512]{2,1,0:T(1,128)}), f32[64,1,512]{2,1,0:T(1,128)S(1)}, u32[]{:S(2)}, u32[]{:S(2)}) async-start(f32[64,1,512]{2,1,0:T(1,128)} %copy.21), calls=%async_computation | async-start | bytes 262144 | tf_op jit(solution)/shard_map/all_to_all | solution.py:15
  23.0 2.1 constant_dynamic-slice_fusion
  25.1 2.9 %collective-permute-start.2 = (f32[96,1024]{1,0:T(8,128)}, f32[96,1024]{1,0:T(8,128)}, u32[]{:S(2)}, u32[]{:S(2)}) collective-permute-start(f32[96,1024]{1,0:T(8,128)} %get-tuple-element.27), channel_id=1, source_target_pairs={{0,128},{128,256},{256,384},{384,0},{1,129},{129,257},{257,385},{3... | collective-permute-start | bytes 1179656 | tf_op jit(solution)/shard_map/ppermute | solution.py:32
  28.0 4.5 %collective-permute-start.3 = (f32[96,1024]{1,0:T(8,128)S(1)}, f32[96,1024]{1,0:T(8,128)}, u32[]{:S(2)}, u32[]{:S(2)}) collective-permute-start(f32[96,1024]{1,0:T(8,128)S(1)} %get-tuple-element.26), channel_id=1, source_target_pairs={{0,256},{128,384},{256,0},{384,128},{1,257},{129,385},{257,1},{385... | collective-permute-start | bytes 1179656 | tf_op jit(solution)/shard_map/ppermute | solution.py:32
  32.5 3.0 %collective-permute-start = (f32[96,1024]{1,0:T(8,128)S(1)}, f32[96,1024]{1,0:T(8,128)}, u32[]{:S(2)}, u32[]{:S(2)}) collective-permute-start(f32[96,1024]{1,0:T(8,128)S(1)} %get-tuple-element.28), channel_id=1, source_target_pairs={{0,384},{128,0},{256,128},{384,256},{1,385},{129,1},{257,129},{385... | collective-permute-start | bytes 1179656 | tf_op jit(solution)/shard_map/ppermute | solution.py:32
  37.8 4.2 %all-to-all-start.1 = ((f32[4,64,512]{2,1,0:T(8,128)}), f32[4,64,512]{2,1,0:T(8,128)S(1)}, u32[]{:S(2)}, u32[]{:S(2)}) async-start(f32[4,64,512]{2,1,0:T(8,128)} %broadcast_in_dim.155), calls=%async_computation.1 | async-start | bytes 1048576 | tf_op jit(solution)/shard_map/all_to_all | solution.py:15
  43.0 5.3 %collective-permute-done.3 = f32[96,1024]{1,0:T(8,128)} collective-permute-done((f32[96,1024]{1,0:T(8,128)S(1)}, f32[96,1024]{1,0:T(8,128)}, u32[]{:S(2)}, u32[]{:S(2)}) %collective-permute-start.3) | collective-permute-done | bytes 393248 | tf_op jit(solution)/shard_map/ppermute | solution.py:32
  49.5 6.2 %collective-permute-start.1 = (f32[256,512]{1,0:T(8,128)S(1)}, f32[256,512]{1,0:T(8,128)S(1)}, u32[]{:S(2)}, u32[]{:S(2)}) collective-permute-start(f32[256,512]{1,0:T(8,128)S(1)} %bitcast.54), channel_id=1, source_target_pairs={{0,1},{1,0},{2,3},{3,2},{4,5},{5,4},{6,7},{7,6},{8,9},{9,8},{10,11... | collective-permute-start | bytes 1572872 | tf_op jit(solution)/shard_map/ppermute | solution.py:63
  58.1 1.9 fusion.37
  60.1 2.5 %collective-permute-start.4 = (f32[64,1024]{1,0:T(8,128)S(1)}, f32[64,1024]{1,0:T(8,128)S(1)}, u32[]{:S(2)}, u32[]{:S(2)}) collective-permute-start(f32[64,1024]{1,0:T(8,128)S(1)} %get-tuple-element.29), channel_id=1, source_target_pairs={{0,8},{8,16},{16,24},{24,32},{32,40},{40,48},{48,56},{56,64},{64,7... | collective-permute-start | bytes 786440 | tf_op jit(solution)/shard_map/ppermute | solution.py:23
  62.6 3.5 %collective-permute-start.6 = (f32[64,1024]{1,0:T(8,128)S(1)}, f32[64,1024]{1,0:T(8,128)S(1)}, u32[]{:S(2)}, u32[]{:S(2)}) collective-permute-start(f32[64,1024]{1,0:T(8,128)S(1)} %get-tuple-element.30), channel_id=1, source_target_pairs={{0,16},{1,113},{8,24},{9,121},{16,32},{17,1},{24,40},{25,9},{32,48... | collective-permute-start | bytes 786440 | tf_op jit(solution)/shard_map/ppermute | solution.py:28
  66.1 3.1 %collective-permute-start.5 = (f32[64,1024]{1,0:T(8,128)S(1)}, f32[64,1024]{1,0:T(8,128)S(1)}, u32[]{:S(2)}, u32[]{:S(2)}) collective-permute-start(f32[64,1024]{1,0:T(8,128)S(1)} %get-tuple-element.31), channel_id=1, source_target_pairs={{0,120},{8,0},{16,8},{24,16},{32,24},{40,32},{48,40},{56,48},{64,5... | collective-permute-start | bytes 786440 | tf_op jit(solution)/shard_map/ppermute | solution.py:23
  72.1 6.9 %collective-permute-done.5 = f32[64,1024]{1,0:T(8,128)S(1)} collective-permute-done((f32[64,1024]{1,0:T(8,128)S(1)}, f32[64,1024]{1,0:T(8,128)S(1)}, u32[]{:S(2)}, u32[]{:S(2)}) %collective-permute-start.5) | collective-permute-done | bytes 262176 | tf_op jit(solution)/shard_map/ppermute | solution.py:23
  79.8 10.6 %all-to-all-start.2 = ((f32[4,16,1024]{2,1,0:T(8,128)}), f32[4,16,1024]{2,1,0:T(8,128)S(1)}, u32[]{:S(2)}, u32[]{:S(2)}) async-start(f32[4,16,1024]{2,1,0:T(8,128)} %bitcast.8), calls=%async_computation.2 | async-start | bytes 524288 | tf_op jit(solution)/shard_map/all_to_all | solution.py:15
  90.9 19.2 %all-to-all-done.2 = f32[4,16,1024]{2,1,0:T(8,128)S(1)} async-done(((f32[4,16,1024]{2,1,0:T(8,128)}), f32[4,16,1024]{2,1,0:T(8,128)S(1)}, u32[]{:S(2)}, u32[]{:S(2)}) %all-to-all-start.2) | async-done | bytes 262176 | tf_op jit(solution)/shard_map/all_to_all | solution.py:15
  111.1 5.5 %all-to-all-start.3 = ((f32[32,3,16]{2,1,0:T(4,128)}), f32[32,3,16]{2,1,0:T(4,128)S(1)}, u32[]{:S(2)}, u32[]{:S(2)}) async-start(f32[32,3,16]{2,1,0:T(4,128)} %broadcast_in_dim.173), calls=%async_computation.3 | async-start | bytes 131072 | tf_op jit(solution)/shard_map/all_to_all | solution.py:15
  116.7 7.4 %all-to-all-done.3 = f32[32,3,16]{2,1,0:T(4,128)S(1)} async-done(((f32[32,3,16]{2,1,0:T(4,128)}), f32[32,3,16]{2,1,0:T(4,128)S(1)}, u32[]{:S(2)}, u32[]{:S(2)}) %all-to-all-start.3) | async-done | bytes 6176 | tf_op jit(solution)/shard_map/all_to_all | solution.py:15
  125.0 3.8 %all-to-all-start.4 = ((f32[4,16,1024]{2,1,0:T(8,128)}), f32[4,16,1024]{2,1,0:T(8,128)S(1)}, u32[]{:S(2)}, u32[]{:S(2)}) async-start(f32[4,16,1024]{2,1,0:T(8,128)} %broadcast_in_dim.174), calls=%async_computation.4 | async-start | bytes 524288 | tf_op jit(solution)/shard_map/all_to_all | solution.py:15
  128.9 16.0 %all-to-all-done.4 = f32[4,16,1024]{2,1,0:T(8,128)S(1)} async-done(((f32[4,16,1024]{2,1,0:T(8,128)}), f32[4,16,1024]{2,1,0:T(8,128)S(1)}, u32[]{:S(2)}, u32[]{:S(2)}) %all-to-all-start.4) | async-done | bytes 262176 | tf_op jit(solution)/shard_map/all_to_all | solution.py:15
  144.9 4.4 %collective-permute-start.9 = (f32[64,1024]{1,0:T(8,128)S(1)}, f32[64,1024]{1,0:T(8,128)S(1)}, u32[]{:S(2)}, u32[]{:S(2)}) collective-permute-start(f32[64,1024]{1,0:T(8,128)S(1)} %bitcast.57), channel_id=1, source_target_pairs={{0,8},{8,16},{16,24},{24,32},{32,40},{40,48},{48,56},{56,64},{64,7... | collective-permute-start | bytes 786440 | tf_op jit(solution)/shard_map/ppermute | solution.py:23
  149.3 4.2 %collective-permute-start.8 = (f32[64,1024]{1,0:T(8,128)S(1)}, f32[64,1024]{1,0:T(8,128)S(1)}, u32[]{:S(2)}, u32[]{:S(2)}) collective-permute-start(f32[64,1024]{1,0:T(8,128)S(1)} %bitcast.58), channel_id=1, source_target_pairs={{0,16},{1,113},{8,24},{9,121},{16,32},{17,1},{24,40},{25,9},{32,48... | collective-permute-start | bytes 786440 | tf_op jit(solution)/shard_map/ppermute | solution.py:28
  153.5 3.4 %collective-permute-start.7 = (f32[64,1024]{1,0:T(8,128)S(1)}, f32[64,1024]{1,0:T(8,128)S(1)}, u32[]{:S(2)}, u32[]{:S(2)}) collective-permute-start(f32[64,1024]{1,0:T(8,128)S(1)} %bitcast.59), channel_id=1, source_target_pairs={{0,120},{8,0},{16,8},{24,16},{32,24},{40,32},{48,40},{56,48},{64,5... | collective-permute-start | bytes 786440 | tf_op jit(solution)/shard_map/ppermute | solution.py:23
  158.5 5.6 %collective-permute-done.7 = f32[64,1024]{1,0:T(8,128)S(1)} collective-permute-done((f32[64,1024]{1,0:T(8,128)S(1)}, f32[64,1024]{1,0:T(8,128)S(1)}, u32[]{:S(2)}, u32[]{:S(2)}) %collective-permute-start.7) | collective-permute-done | bytes 262176 | tf_op jit(solution)/shard_map/ppermute | solution.py:23
  166.5 6.1 %all-to-all-start.5 = ((f32[32,16,384]{2,1,0:T(8,128)}), f32[32,16,384]{2,1,0:T(8,128)S(1)}, u32[]{:S(2)}, u32[]{:S(2)}) async-start(f32[32,16,384]{2,1,0:T(8,128)} %bitcast.15), calls=%async_computation.5 | async-start | bytes 1572864 | tf_op jit(solution)/shard_map/all_to_all | solution.py:15
  172.6 1.9 fusion
  175.3 3.3 %collective-permute-start.10 = (f32[96,1024]{1,0:T(8,128)}, f32[96,1024]{1,0:T(8,128)}, u32[]{:S(2)}, u32[]{:S(2)}) collective-permute-start(f32[96,1024]{1,0:T(8,128)} %get-tuple-element.25), channel_id=1, source_target_pairs={{0,128},{128,256},{256,384},{384,0},{1,129},{129,257},{257,385},{3... | collective-permute-start | bytes 1179656 | tf_op jit(solution)/shard_map/ppermute | solution.py:32
  178.7 3.2 %collective-permute-start.11 = (f32[96,1024]{1,0:T(8,128)S(1)}, f32[96,1024]{1,0:T(8,128)}, u32[]{:S(2)}, u32[]{:S(2)}) collective-permute-start(f32[96,1024]{1,0:T(8,128)S(1)} %get-tuple-element.24), channel_id=1, source_target_pairs={{0,384},{128,0},{256,128},{384,256},{1,385},{129,1},{257,129},{385... | collective-permute-start | bytes 1179656 | tf_op jit(solution)/shard_map/ppermute | solution.py:32
  182.4 3.6 %collective-permute-start.12 = (f32[96,1024]{1,0:T(8,128)S(1)}, f32[96,1024]{1,0:T(8,128)}, u32[]{:S(2)}, u32[]{:S(2)}) collective-permute-start(f32[96,1024]{1,0:T(8,128)S(1)} %get-tuple-element.23), channel_id=1, source_target_pairs={{0,256},{128,384},{256,0},{384,128},{1,257},{129,385},{257,1},{385... | collective-permute-start | bytes 1179656 | tf_op jit(solution)/shard_map/ppermute | solution.py:32
  187.7 4.3 %all-to-all-start.6 = ((f32[16,1,512]{2,1,0:T(1,128)}), f32[16,1,512]{2,1,0:T(1,128)S(1)}, u32[]{:S(2)}, u32[]{:S(2)}) async-start(f32[16,1,512]{2,1,0:T(1,128)} %reshape.303), calls=%async_computation.6 | async-start | bytes 65536 | tf_op jit(solution)/shard_map/all_to_all | solution.py:15
  195.7 7.8 %all-to-all-done.6 = f32[16,1,512]{2,1,0:T(1,128)S(1)} async-done(((f32[16,1,512]{2,1,0:T(1,128)}), f32[16,1,512]{2,1,0:T(1,128)S(1)}, u32[]{:S(2)}, u32[]{:S(2)}) %all-to-all-start.6) | async-done | bytes 32800 | tf_op jit(solution)/shard_map/all_to_all | solution.py:15
  204.5 5.8 %all-to-all-start.7 = ((f32[8,1,6144]{2,1,0:T(1,128)}), f32[8,1,6144]{2,1,0:T(1,128)S(1)}, u32[]{:S(2)}, u32[]{:S(2)}) async-start(f32[8,1,6144]{2,1,0:T(1,128)} %broadcast_in_dim.177), calls=%async_computation.7 | async-start | bytes 393216 | tf_op jit(solution)/shard_map/all_to_all | solution.py:15
  212.0 4.3 %all-to-all-done.7 = f32[8,1,6144]{2,1,0:T(1,128)S(1)} async-done(((f32[8,1,6144]{2,1,0:T(1,128)}), f32[8,1,6144]{2,1,0:T(1,128)S(1)}, u32[]{:S(2)}, u32[]{:S(2)}) %all-to-all-start.7) | async-done | bytes 196640 | tf_op jit(solution)/shard_map/all_to_all | solution.py:15
  (92 shorter events, 28.9 us)
Async XLA Ops:
  0.6 2.1 copy-start
  3.8 33.1 %all-to-all-start = ((f32[64,1,512]{2,1,0:T(1,128)}), f32[64,1,512]{2,1,0:T(1,128)S(1)}, u32[]{:S(2)}, u32[]{:S(2)}) async-start(f32[64,1,512]{2,1,0:T(1,128)} %copy.21), calls=%async_computation | async-start | bytes 262144 | tf_op jit(solution)/shard_map/all_to_all | solution.py:15
  25.1 16.9 %collective-permute-start.2 = (f32[96,1024]{1,0:T(8,128)}, f32[96,1024]{1,0:T(8,128)}, u32[]{:S(2)}, u32[]{:S(2)}) collective-permute-start(f32[96,1024]{1,0:T(8,128)} %get-tuple-element.27), channel_id=1, source_target_pairs={{0,128},{128,256},{256,384},{384,0},{1,129},{129,257},{257,385},{3... | collective-permute-start | bytes 1179656 | tf_op jit(solution)/shard_map/ppermute | solution.py:32
  28.0 20.3 %collective-permute-start.3 = (f32[96,1024]{1,0:T(8,128)S(1)}, f32[96,1024]{1,0:T(8,128)}, u32[]{:S(2)}, u32[]{:S(2)}) collective-permute-start(f32[96,1024]{1,0:T(8,128)S(1)} %get-tuple-element.26), channel_id=1, source_target_pairs={{0,256},{128,384},{256,0},{384,128},{1,257},{129,385},{257,1},{385... | collective-permute-start | bytes 1179656 | tf_op jit(solution)/shard_map/ppermute | solution.py:32
  32.5 17.0 %collective-permute-start = (f32[96,1024]{1,0:T(8,128)S(1)}, f32[96,1024]{1,0:T(8,128)}, u32[]{:S(2)}, u32[]{:S(2)}) collective-permute-start(f32[96,1024]{1,0:T(8,128)S(1)} %get-tuple-element.28), channel_id=1, source_target_pairs={{0,384},{128,0},{256,128},{384,256},{1,385},{129,1},{257,129},{385... | collective-permute-start | bytes 1179656 | tf_op jit(solution)/shard_map/ppermute | solution.py:32
  37.8 11.7 %all-to-all-start.1 = ((f32[4,64,512]{2,1,0:T(8,128)}), f32[4,64,512]{2,1,0:T(8,128)S(1)}, u32[]{:S(2)}, u32[]{:S(2)}) async-start(f32[4,64,512]{2,1,0:T(8,128)} %broadcast_in_dim.155), calls=%async_computation.1 | async-start | bytes 1048576 | tf_op jit(solution)/shard_map/all_to_all | solution.py:15
  49.5 7.8 %collective-permute-start.1 = (f32[256,512]{1,0:T(8,128)S(1)}, f32[256,512]{1,0:T(8,128)S(1)}, u32[]{:S(2)}, u32[]{:S(2)}) collective-permute-start(f32[256,512]{1,0:T(8,128)S(1)} %bitcast.54), channel_id=1, source_target_pairs={{0,1},{1,0},{2,3},{3,2},{4,5},{5,4},{6,7},{7,6},{8,9},{9,8},{10,11... | collective-permute-start | bytes 1572872 | tf_op jit(solution)/shard_map/ppermute | solution.py:63
  60.1 10.6 %collective-permute-start.4 = (f32[64,1024]{1,0:T(8,128)S(1)}, f32[64,1024]{1,0:T(8,128)S(1)}, u32[]{:S(2)}, u32[]{:S(2)}) collective-permute-start(f32[64,1024]{1,0:T(8,128)S(1)} %get-tuple-element.29), channel_id=1, source_target_pairs={{0,8},{8,16},{16,24},{24,32},{32,40},{40,48},{48,56},{56,64},{64,7... | collective-permute-start | bytes 786440 | tf_op jit(solution)/shard_map/ppermute | solution.py:23
  62.6 9.6 %collective-permute-start.6 = (f32[64,1024]{1,0:T(8,128)S(1)}, f32[64,1024]{1,0:T(8,128)S(1)}, u32[]{:S(2)}, u32[]{:S(2)}) collective-permute-start(f32[64,1024]{1,0:T(8,128)S(1)} %get-tuple-element.30), channel_id=1, source_target_pairs={{0,16},{1,113},{8,24},{9,121},{16,32},{17,1},{24,40},{25,9},{32,48... | collective-permute-start | bytes 786440 | tf_op jit(solution)/shard_map/ppermute | solution.py:28
  66.1 12.9 %collective-permute-start.5 = (f32[64,1024]{1,0:T(8,128)S(1)}, f32[64,1024]{1,0:T(8,128)S(1)}, u32[]{:S(2)}, u32[]{:S(2)}) collective-permute-start(f32[64,1024]{1,0:T(8,128)S(1)} %get-tuple-element.31), channel_id=1, source_target_pairs={{0,120},{8,0},{16,8},{24,16},{32,24},{40,32},{48,40},{56,48},{64,5... | collective-permute-start | bytes 786440 | tf_op jit(solution)/shard_map/ppermute | solution.py:23
  79.8 30.3 %all-to-all-start.2 = ((f32[4,16,1024]{2,1,0:T(8,128)}), f32[4,16,1024]{2,1,0:T(8,128)S(1)}, u32[]{:S(2)}, u32[]{:S(2)}) async-start(f32[4,16,1024]{2,1,0:T(8,128)} %bitcast.8), calls=%async_computation.2 | async-start | bytes 524288 | tf_op jit(solution)/shard_map/all_to_all | solution.py:15
  111.1 12.9 %all-to-all-start.3 = ((f32[32,3,16]{2,1,0:T(4,128)}), f32[32,3,16]{2,1,0:T(4,128)S(1)}, u32[]{:S(2)}, u32[]{:S(2)}) async-start(f32[32,3,16]{2,1,0:T(4,128)} %broadcast_in_dim.173), calls=%async_computation.3 | async-start | bytes 131072 | tf_op jit(solution)/shard_map/all_to_all | solution.py:15
  125.0 20.0 %all-to-all-start.4 = ((f32[4,16,1024]{2,1,0:T(8,128)}), f32[4,16,1024]{2,1,0:T(8,128)S(1)}, u32[]{:S(2)}, u32[]{:S(2)}) async-start(f32[4,16,1024]{2,1,0:T(8,128)} %broadcast_in_dim.174), calls=%async_computation.4 | async-start | bytes 524288 | tf_op jit(solution)/shard_map/all_to_all | solution.py:15
  144.9 12.1 %collective-permute-start.9 = (f32[64,1024]{1,0:T(8,128)S(1)}, f32[64,1024]{1,0:T(8,128)S(1)}, u32[]{:S(2)}, u32[]{:S(2)}) collective-permute-start(f32[64,1024]{1,0:T(8,128)S(1)} %bitcast.57), channel_id=1, source_target_pairs={{0,8},{8,16},{16,24},{24,32},{32,40},{40,48},{48,56},{56,64},{64,7... | collective-permute-start | bytes 786440 | tf_op jit(solution)/shard_map/ppermute | solution.py:23
  149.3 9.2 %collective-permute-start.8 = (f32[64,1024]{1,0:T(8,128)S(1)}, f32[64,1024]{1,0:T(8,128)S(1)}, u32[]{:S(2)}, u32[]{:S(2)}) collective-permute-start(f32[64,1024]{1,0:T(8,128)S(1)} %bitcast.58), channel_id=1, source_target_pairs={{0,16},{1,113},{8,24},{9,121},{16,32},{17,1},{24,40},{25,9},{32,48... | collective-permute-start | bytes 786440 | tf_op jit(solution)/shard_map/ppermute | solution.py:28
  153.5 10.6 %collective-permute-start.7 = (f32[64,1024]{1,0:T(8,128)S(1)}, f32[64,1024]{1,0:T(8,128)S(1)}, u32[]{:S(2)}, u32[]{:S(2)}) collective-permute-start(f32[64,1024]{1,0:T(8,128)S(1)} %bitcast.59), channel_id=1, source_target_pairs={{0,120},{8,0},{16,8},{24,16},{32,24},{40,32},{48,40},{56,48},{64,5... | collective-permute-start | bytes 786440 | tf_op jit(solution)/shard_map/ppermute | solution.py:23
  158.5 8.0 %copy-start.2 = (f32[64,1024]{1,0:T(8,128)}, f32[64,1024]{1,0:T(8,128)S(1)}, u32[]{:S(2)}) copy-start(f32[64,1024]{1,0:T(8,128)S(1)} %collective-permute-done.8) | copy-start | bytes 786436
  164.1 2.4 %copy-start.3 = (f32[64,1024]{1,0:T(8,128)}, f32[64,1024]{1,0:T(8,128)S(1)}, u32[]{:S(2)}) copy-start(f32[64,1024]{1,0:T(8,128)S(1)} %collective-permute-done.7) | copy-start | bytes 786436
  166.5 20.5 %all-to-all-start.5 = ((f32[32,16,384]{2,1,0:T(8,128)}), f32[32,16,384]{2,1,0:T(8,128)S(1)}, u32[]{:S(2)}, u32[]{:S(2)}) async-start(f32[32,16,384]{2,1,0:T(8,128)} %bitcast.15), calls=%async_computation.5 | async-start | bytes 1572864 | tf_op jit(solution)/shard_map/all_to_all | solution.py:15
  175.3 18.3 %collective-permute-start.10 = (f32[96,1024]{1,0:T(8,128)}, f32[96,1024]{1,0:T(8,128)}, u32[]{:S(2)}, u32[]{:S(2)}) collective-permute-start(f32[96,1024]{1,0:T(8,128)} %get-tuple-element.25), channel_id=1, source_target_pairs={{0,128},{128,256},{256,384},{384,0},{1,129},{129,257},{257,385},{3... | collective-permute-start | bytes 1179656 | tf_op jit(solution)/shard_map/ppermute | solution.py:32
  178.7 16.0 %collective-permute-start.11 = (f32[96,1024]{1,0:T(8,128)S(1)}, f32[96,1024]{1,0:T(8,128)}, u32[]{:S(2)}, u32[]{:S(2)}) collective-permute-start(f32[96,1024]{1,0:T(8,128)S(1)} %get-tuple-element.24), channel_id=1, source_target_pairs={{0,384},{128,0},{256,128},{384,256},{1,385},{129,1},{257,129},{385... | collective-permute-start | bytes 1179656 | tf_op jit(solution)/shard_map/ppermute | solution.py:32
  182.4 28.0 %collective-permute-start.12 = (f32[96,1024]{1,0:T(8,128)S(1)}, f32[96,1024]{1,0:T(8,128)}, u32[]{:S(2)}, u32[]{:S(2)}) collective-permute-start(f32[96,1024]{1,0:T(8,128)S(1)} %get-tuple-element.23), channel_id=1, source_target_pairs={{0,256},{128,384},{256,0},{384,128},{1,257},{129,385},{257,1},{385... | collective-permute-start | bytes 1179656 | tf_op jit(solution)/shard_map/ppermute | solution.py:32
  187.7 15.8 %all-to-all-start.6 = ((f32[16,1,512]{2,1,0:T(1,128)}), f32[16,1,512]{2,1,0:T(1,128)S(1)}, u32[]{:S(2)}, u32[]{:S(2)}) async-start(f32[16,1,512]{2,1,0:T(1,128)} %reshape.303), calls=%async_computation.6 | async-start | bytes 65536 | tf_op jit(solution)/shard_map/all_to_all | solution.py:15
  204.5 11.7 %all-to-all-start.7 = ((f32[8,1,6144]{2,1,0:T(1,128)}), f32[8,1,6144]{2,1,0:T(1,128)S(1)}, u32[]{:S(2)}, u32[]{:S(2)}) async-start(f32[8,1,6144]{2,1,0:T(1,128)} %broadcast_in_dim.177), calls=%async_computation.7 | async-start | bytes 393216 | tf_op jit(solution)/shard_map/all_to_all | solution.py:15
  211.4 5.6 %copy-start.1 = (f32[96,4096]{1,0:T(8,128)}, f32[96,4096]{1,0:T(8,128)S(1)}, u32[]{:S(2)}) copy-start(f32[96,4096]{1,0:T(8,128)S(1)} %constant_dynamic-update-slice_fusion) | copy-start | bytes 4718596

commit v12 on v11

--- a/solution.py
+++ b/solution.py
@@ -54,9 +54,9 @@
     def cut(array, s):
         return lax.dynamic_slice(array, (0, (x + s) % 4 * quarter), (depth, quarter))
 
-    packed, weight = lax.optimization_barrier((packed, weight))
     pieces = [cut(weight, 0), *(shift_x(cut(weight, s), s) for s in range(1, 4))]
     mine = swap(packed, ("x", *Z)).reshape(64, wide + META)
+    mine, pieces[0] = lax.optimization_barrier((mine, pieces[0]))
 
     slots = spread(mine, "y", 4).reshape(256, wide + META)
     slots, pieces[3] = lax.optimization_barrier((slots, pieces[3]))
@@ -97,8 +97,9 @@
         head = lax.dynamic_update_slice(head, piece[None], ((x - s) % 4, 0, 0))
     head = lax.optimization_barrier(head.reshape(wide, quarter))
 
-    partial = dot(hidden, head)
-    block = partial[:64] + shift_z(partial[64:128], 1) + shift_z(partial[192:], -1) + shift_far(partial[128:192])
+    leave = dot(hidden[64:], head)
+    stay = lax.optimization_barrier(dot(hidden[:64], head))
+    block = stay + shift_z(leave[:64], 1) + shift_z(leave[128:], -1) + shift_far(leave[64:128])
     logits = jnp.sum(swap(block.reshape(4, 16, quarter), "h"), axis=0)
 
     row_labels = lax.dynamic_slice(labels, (h * 16,), (16,))
@@ -115,10 +116,13 @@
     grad = onehot - shifted * scale[:, None]
 
     own = spread(grad, "h", 4).reshape(64, quarter)
-    grads = jnp.concatenate([own, shift_z(own, -1), shift_far(own), shift_z(own, 1)], axis=0)
+    blocks = [own, shift_z(own, -1), shift_far(own), shift_z(own, 1)]
+    grads = jnp.concatenate(blocks, axis=0)
 
-    grad_rows = dot(grads, head, (1, 1), GRAD)
-    leaving = dot(deliver, grad_rows, (1, 0), GRAD).reshape(32, 16, wide)
+    def sent(i):
+        return dot(deliver[:, 64 * i : 64 * (i + 1)], dot(blocks[i], head, (1, 1), GRAD), (1, 0), GRAD)
+
+    leaving = (sent(0) + sent(1) + sent(3) + sent(2)).reshape(32, 16, wide)
     summed = jnp.sum(swap(leaving, XYC), axis=0)
 
     grad_head = dot(hidden, grads, (0, 0), GRAD).reshape(4, depth, quarter)

time: 218 us -> 220 us (level)
  waiting for transfers between devices: 78.2 us -> 66.9 us
  starting transfers between devices: 107 us -> 118 us
  matrix products: 6.95 us -> 11 us
    ppermute x4, waiting for transfers between devices: 14 us -> 4.29 us  [shift_z(): return lax.ppermute(block, Z, [(i, (i + step) % 16) for i in range(16)])]
    all_to_all x8, starting transfers between devices: 59.4 us -> 68.6 us  [swap(): return lax.all_to_all(blocks, axes, split_axis=0, concat_axis=0, tiled=True)]
    all_to_all x8, waiting for transfers between devices: 55.8 us -> 47.7 us  [swap(): return lax.all_to_all(blocks, axes, split_axis=0, concat_axis=0, tiled=True)]
    ppermute x2, waiting for transfers between devices: 2.88 us -> 7.22 us  [shift_far(): return lax.ppermute(block, ('h', 'l', 'c'), pairs)]
    dot_general x6 -> x13, matrix products: 6.95 us -> 11 us  [dot(): lax.dot_general(a, b, dims, precision=precision, preferred_element_type=j...]
    dynamic_update_slice x4, local copies, waits for them, and re-layouts: 4.11 us -> 1.13 us  [on_device(): head = lax.dynamic_update_slice(head, piece[None], ((x - s) % 4, 0, 0))]
  transfers between devices with their start and end apart: 21 -> 21, of which waited for: 14 -> 14; matrix products, arithmetic and copies ran while one was open for 9% -> 10% of each run, Pallas kernels for 0% -> 0%
where the time goes in v12:
time: 220 us; the launch traced here: 219 us
  starting transfers between devices  118 us (54%)
  waiting for transfers between devices  66.9 us (30%)
  local copies, waits for them, and re-layouts  16.7 us (8%)
  matrix products  11 us (5%)
  other arithmetic  3.75 us (2%)
  between operations  2.63 us (1%)
    all_to_all x8, starting transfers between devices, swap(): return lax.all_to_all(blocks, axes, split_axis=0, concat_axis=0, tiled=True)  68.6 us
    all_to_all x8, waiting for transfers between devices, swap(): return lax.all_to_all(blocks, axes, split_axis=0, concat_axis=0, tiled=True)  47.7 us
    ppermute x6, starting transfers between devices, shift_x(): return lax.ppermute(block, 'x', [(i, (i + step) % 4) for i in range(4)])  20.6 us
    ppermute x4, starting transfers between devices, shift_z(): return lax.ppermute(block, Z, [(i, (i + step) % 16) for i in range(16)])  15.1 us
    dot_general x13, matrix products, dot(): lax.dot_general(a, b, dims, precision=precision, preferred_element_type=j...  11 us
    ppermute x2, starting transfers between devices, shift_far(): return lax.ppermute(block, ('h', 'l', 'c'), pairs)  8.26 us
    ppermute x2, waiting for transfers between devices, shift_far(): return lax.ppermute(block, ('h', 'l', 'c'), pairs)  7.22 us
    ppermute x6, waiting for transfers between devices, shift_x(): return lax.ppermute(block, 'x', [(i, (i + step) % 4) for i in range(4)])  6.78 us
  transfers between devices with their start and end apart: 21, of which 14 were waited for; matrix products, arithmetic and copies ran while one was open for 10% of the time, Pallas kernels for 0%

profile of v12, /device:TPU:1, one launch (start us, length us, event | category | flops | bytes accessed | tf_op | source)
XLA Modules:
  0.0 219.1 jit_solution(8633341219243014081)
XLA Ops:
  4.7 19.1 %all-to-all-start = ((f32[64,1,512]{2,1,0:T(1,128)}), f32[64,1,512]{2,1,0:T(1,128)S(1)}, u32[]{:S(2)}, u32[]{:S(2)}) async-start(f32[64,1,512]{2,1,0:T(1,128)} %copy.21), calls=%async_computation | async-start | bytes 262144 | tf_op jit(solution)/shard_map/all_to_all | solution.py:15
  23.9 2.4 %constant_dynamic-slice_fusion.2 = (f32[96,1024]{1,0:T(8,128)}, f32[96,1024]{1,0:T(8,128)S(1)}, f32[96,1024]{1,0:T(8,128)}, f32[96,1024]{1,0:T(8,128)}) fusion(f32[96,4096]{1,0:T(8,128)} %param.6, s32[]{:T(128)S(6)} %select_n.266, s32[]{:T(128)S(6)} %select_n.264, s32[]{:T(128)S(6)} %select_n.292, s32[]{:T(128)S(6)} %select_n.288), kind=kLoop, calls=%fused_computation.77 | loop fusion | bytes 3145744 | tf_op jit(solution)/shard_map/dynamic_slice | solution.py:55
  26.3 2.9 %collective-permute-start.2 = (f32[96,1024]{1,0:T(8,128)}, f32[96,1024]{1,0:T(8,128)}, u32[]{:S(2)}, u32[]{:S(2)}) collective-permute-start(f32[96,1024]{1,0:T(8,128)} %get-tuple-element.29), channel_id=1, source_target_pairs={{0,128},{128,256},{256,384},{384,0},{1,129},{129,257},{257,385},{3... | collective-permute-start | bytes 1179656 | tf_op jit(solution)/shard_map/ppermute | solution.py:32
  29.2 4.5 %collective-permute-start.3 = (f32[96,1024]{1,0:T(8,128)}, f32[96,1024]{1,0:T(8,128)S(1)}, u32[]{:S(2)}, u32[]{:S(2)}) collective-permute-start(f32[96,1024]{1,0:T(8,128)} %get-tuple-element.28), channel_id=1, source_target_pairs={{0,256},{128,384},{256,0},{384,128},{1,257},{129,385},{257,1},{385... | collective-permute-start | bytes 1179656 | tf_op jit(solution)/shard_map/ppermute | solution.py:32
  33.7 3.0 %collective-permute-start = (f32[96,1024]{1,0:T(8,128)}, f32[96,1024]{1,0:T(8,128)S(1)}, u32[]{:S(2)}, u32[]{:S(2)}) collective-permute-start(f32[96,1024]{1,0:T(8,128)} %get-tuple-element.26), channel_id=1, source_target_pairs={{0,384},{128,0},{256,128},{384,256},{1,385},{129,1},{257,129},{385... | collective-permute-start | bytes 1179656 | tf_op jit(solution)/shard_map/ppermute | solution.py:32
  38.6 4.2 %all-to-all-start.1 = ((f32[4,64,512]{2,1,0:T(8,128)}), f32[4,64,512]{2,1,0:T(8,128)S(1)}, u32[]{:S(2)}, u32[]{:S(2)}) async-start(f32[4,64,512]{2,1,0:T(8,128)} %broadcast_in_dim.153), calls=%async_computation.1 | async-start | bytes 1048576 | tf_op jit(solution)/shard_map/all_to_all | solution.py:15
  44.1 5.2 %collective-permute-done.3 = f32[96,1024]{1,0:T(8,128)S(1)} collective-permute-done((f32[96,1024]{1,0:T(8,128)}, f32[96,1024]{1,0:T(8,128)S(1)}, u32[]{:S(2)}, u32[]{:S(2)}) %collective-permute-start.3) | collective-permute-done | bytes 393248 | tf_op jit(solution)/shard_map/ppermute | solution.py:32
  50.9 5.6 %collective-permute-start.1 = (f32[256,512]{1,0:T(8,128)S(1)}, f32[256,512]{1,0:T(8,128)S(1)}, u32[]{:S(2)}, u32[]{:S(2)}) collective-permute-start(f32[256,512]{1,0:T(8,128)S(1)} %bitcast.67), channel_id=1, source_target_pairs={{0,1},{1,0},{2,3},{3,2},{4,5},{5,4},{6,7},{7,6},{8,9},{9,8},{10,11... | collective-permute-start | bytes 1572872 | tf_op jit(solution)/shard_map/ppermute | solution.py:63
  60.4 3.2 %collective-permute-start.6 = (f32[64,1024]{1,0:T(8,128)S(1)}, f32[64,1024]{1,0:T(8,128)S(1)}, u32[]{:S(2)}, u32[]{:S(2)}) collective-permute-start(f32[64,1024]{1,0:T(8,128)S(1)} %get-tuple-element.31), channel_id=1, source_target_pairs={{0,16},{1,113},{8,24},{9,121},{16,32},{17,1},{24,40},{25,9},{32,48... | collective-permute-start | bytes 786440 | tf_op jit(solution)/shard_map/ppermute | solution.py:28
  63.6 2.9 %collective-permute-start.5 = (f32[64,1024]{1,0:T(8,128)S(1)}, f32[64,1024]{1,0:T(8,128)S(1)}, u32[]{:S(2)}, u32[]{:S(2)}) collective-permute-start(f32[64,1024]{1,0:T(8,128)S(1)} %get-tuple-element.32), channel_id=1, source_target_pairs={{0,120},{8,0},{16,8},{24,16},{32,24},{40,32},{48,40},{56,48},{64,5... | collective-permute-start | bytes 786440 | tf_op jit(solution)/shard_map/ppermute | solution.py:23
  66.5 2.4 %collective-permute-start.4 = (f32[64,1024]{1,0:T(8,128)S(1)}, f32[64,1024]{1,0:T(8,128)S(1)}, u32[]{:S(2)}, u32[]{:S(2)}) collective-permute-start(f32[64,1024]{1,0:T(8,128)S(1)} %get-tuple-element.30), channel_id=1, source_target_pairs={{0,8},{8,16},{16,24},{24,32},{32,40},{40,48},{48,56},{56,64},{64,7... | collective-permute-start | bytes 786440 | tf_op jit(solution)/shard_map/ppermute | solution.py:23
  70.0 2.8 %collective-permute-done.6 = f32[64,1024]{1,0:T(8,128)S(1)} collective-permute-done((f32[64,1024]{1,0:T(8,128)S(1)}, f32[64,1024]{1,0:T(8,128)S(1)}, u32[]{:S(2)}, u32[]{:S(2)}) %collective-permute-start.6) | collective-permute-done | bytes 262176 | tf_op jit(solution)/shard_map/ppermute | solution.py:28
  72.8 3.9 %collective-permute-done.5 = f32[64,1024]{1,0:T(8,128)S(1)} collective-permute-done((f32[64,1024]{1,0:T(8,128)S(1)}, f32[64,1024]{1,0:T(8,128)S(1)}, u32[]{:S(2)}, u32[]{:S(2)}) %collective-permute-start.5) | collective-permute-done | bytes 262176 | tf_op jit(solution)/shard_map/ppermute | solution.py:23
  77.9 8.2 %all-to-all-start.2 = ((f32[4,16,1024]{2,1,0:T(8,128)}), f32[4,16,1024]{2,1,0:T(8,128)S(1)}, u32[]{:S(2)}, u32[]{:S(2)}) async-start(f32[4,16,1024]{2,1,0:T(8,128)} %bitcast.8), calls=%async_computation.2 | async-start | bytes 524288 | tf_op jit(solution)/shard_map/all_to_all | solution.py:15
  86.7 12.5 %all-to-all-done.2 = f32[4,16,1024]{2,1,0:T(8,128)S(1)} async-done(((f32[4,16,1024]{2,1,0:T(8,128)}), f32[4,16,1024]{2,1,0:T(8,128)S(1)}, u32[]{:S(2)}, u32[]{:S(2)}) %all-to-all-start.2) | async-done | bytes 262176 | tf_op jit(solution)/shard_map/all_to_all | solution.py:15
  100.2 12.6 %all-to-all-start.3 = ((f32[32,3,16]{2,1,0:T(4,128)}), f32[32,3,16]{2,1,0:T(4,128)S(1)}, u32[]{:S(2)}, u32[]{:S(2)}) async-start(f32[32,3,16]{2,1,0:T(4,128)} %broadcast_in_dim.171), calls=%async_computation.3 | async-start | bytes 131072 | tf_op jit(solution)/shard_map/all_to_all | solution.py:15
  112.8 7.4 %all-to-all-done.3 = f32[32,3,16]{2,1,0:T(4,128)S(1)} async-done(((f32[32,3,16]{2,1,0:T(4,128)}), f32[32,3,16]{2,1,0:T(4,128)S(1)}, u32[]{:S(2)}, u32[]{:S(2)}) %all-to-all-start.3) | async-done | bytes 6176 | tf_op jit(solution)/shard_map/all_to_all | solution.py:15
  121.2 6.1 %all-to-all-start.4 = ((f32[4,16,1024]{2,1,0:T(8,128)}), f32[4,16,1024]{2,1,0:T(8,128)S(1)}, u32[]{:S(2)}, u32[]{:S(2)}) async-start(f32[4,16,1024]{2,1,0:T(8,128)} %broadcast_in_dim.172), calls=%async_computation.4 | async-start | bytes 524288 | tf_op jit(solution)/shard_map/all_to_all | solution.py:15
  127.6 13.7 %all-to-all-done.4 = f32[4,16,1024]{2,1,0:T(8,128)S(1)} async-done(((f32[4,16,1024]{2,1,0:T(8,128)}), f32[4,16,1024]{2,1,0:T(8,128)S(1)}, u32[]{:S(2)}, u32[]{:S(2)}) %all-to-all-start.4) | async-done | bytes 262176 | tf_op jit(solution)/shard_map/all_to_all | solution.py:15
  141.3 1.9 collective-permute-start.7
  144.1 7.9 %collective-permute-start.8 = (f32[64,1024]{1,0:T(8,128)S(1)}, f32[64,1024]{1,0:T(8,128)S(1)}, u32[]{:S(2)}, u32[]{:S(2)}) collective-permute-start(f32[64,1024]{1,0:T(8,128)S(1)} %bitcast.73), channel_id=1, source_target_pairs={{0,8},{8,16},{16,24},{24,32},{32,40},{40,48},{48,56},{56,64},{64,7... | collective-permute-start | bytes 786440 | tf_op jit(solution)/shard_map/ppermute | solution.py:23
  152.0 5.1 %collective-permute-start.9 = (f32[64,1024]{1,0:T(8,128)S(1)}, f32[64,1024]{1,0:T(8,128)S(1)}, u32[]{:S(2)}, u32[]{:S(2)}) collective-permute-start(f32[64,1024]{1,0:T(8,128)S(1)} %bitcast.74), channel_id=1, source_target_pairs={{0,16},{1,113},{8,24},{9,121},{16,32},{17,1},{24,40},{25,9},{32,48... | collective-permute-start | bytes 786440 | tf_op jit(solution)/shard_map/ppermute | solution.py:28
  160.0 4.4 %collective-permute-done.9 = f32[64,1024]{1,0:T(8,128)S(1)} collective-permute-done((f32[64,1024]{1,0:T(8,128)S(1)}, f32[64,1024]{1,0:T(8,128)S(1)}, u32[]{:S(2)}, u32[]{:S(2)}) %collective-permute-start.9) | collective-permute-done | bytes 262176 | tf_op jit(solution)/shard_map/ppermute | solution.py:28
  166.5 7.5 %all-to-all-start.5 = ((f32[32,16,384]{2,1,0:T(8,128)}), f32[32,16,384]{2,1,0:T(8,128)S(1)}, u32[]{:S(2)}, u32[]{:S(2)}) async-start(f32[32,16,384]{2,1,0:T(8,128)} %bitcast.15), calls=%async_computation.5 | async-start | bytes 1572864 | tf_op jit(solution)/shard_map/all_to_all | solution.py:15
  174.0 1.9 fusion
  176.7 3.3 %collective-permute-start.10 = (f32[96,1024]{1,0:T(8,128)}, f32[96,1024]{1,0:T(8,128)}, u32[]{:S(2)}, u32[]{:S(2)}) collective-permute-start(f32[96,1024]{1,0:T(8,128)} %get-tuple-element.25), channel_id=1, source_target_pairs={{0,128},{128,256},{256,384},{384,0},{1,129},{129,257},{257,385},{3... | collective-permute-start | bytes 1179656 | tf_op jit(solution)/shard_map/ppermute | solution.py:32
  180.1 3.2 %collective-permute-start.11 = (f32[96,1024]{1,0:T(8,128)S(1)}, f32[96,1024]{1,0:T(8,128)}, u32[]{:S(2)}, u32[]{:S(2)}) collective-permute-start(f32[96,1024]{1,0:T(8,128)S(1)} %get-tuple-element.24), channel_id=1, source_target_pairs={{0,384},{128,0},{256,128},{384,256},{1,385},{129,1},{257,129},{385... | collective-permute-start | bytes 1179656 | tf_op jit(solution)/shard_map/ppermute | solution.py:32
  183.7 3.6 %collective-permute-start.12 = (f32[96,1024]{1,0:T(8,128)S(1)}, f32[96,1024]{1,0:T(8,128)}, u32[]{:S(2)}, u32[]{:S(2)}) collective-permute-start(f32[96,1024]{1,0:T(8,128)S(1)} %get-tuple-element.23), channel_id=1, source_target_pairs={{0,256},{128,384},{256,0},{384,128},{1,257},{129,385},{257,1},{385... | collective-permute-start | bytes 1179656 | tf_op jit(solution)/shard_map/ppermute | solution.py:32
  189.1 5.1 %all-to-all-start.6 = ((f32[16,1,512]{2,1,0:T(1,128)}), f32[16,1,512]{2,1,0:T(1,128)S(1)}, u32[]{:S(2)}, u32[]{:S(2)}) async-start(f32[16,1,512]{2,1,0:T(1,128)} %reshape.307), calls=%async_computation.6 | async-start | bytes 65536 | tf_op jit(solution)/shard_map/all_to_all | solution.py:15
  197.8 7.8 %all-to-all-done.6 = f32[16,1,512]{2,1,0:T(1,128)S(1)} async-done(((f32[16,1,512]{2,1,0:T(1,128)}), f32[16,1,512]{2,1,0:T(1,128)S(1)}, u32[]{:S(2)}, u32[]{:S(2)}) %all-to-all-start.6) | async-done | bytes 32800 | tf_op jit(solution)/shard_map/all_to_all | solution.py:15
  206.6 5.9 %all-to-all-start.7 = ((f32[8,1,6144]{2,1,0:T(1,128)}), f32[8,1,6144]{2,1,0:T(1,128)S(1)}, u32[]{:S(2)}, u32[]{:S(2)}) async-start(f32[8,1,6144]{2,1,0:T(1,128)} %broadcast_in_dim.175), calls=%async_computation.7 | async-start | bytes 393216 | tf_op jit(solution)/shard_map/all_to_all | solution.py:15
  214.1 4.3 %all-to-all-done.7 = f32[8,1,6144]{2,1,0:T(1,128)S(1)} async-done(((f32[8,1,6144]{2,1,0:T(1,128)}), f32[8,1,6144]{2,1,0:T(1,128)S(1)}, u32[]{:S(2)}, u32[]{:S(2)}) %all-to-all-start.7) | async-done | bytes 196640 | tf_op jit(solution)/shard_map/all_to_all | solution.py:15
  (100 shorter events, 32.1 us)
Async XLA Ops:
  0.6 0.9 copy-start
  4.7 33.1 %all-to-all-start = ((f32[64,1,512]{2,1,0:T(1,128)}), f32[64,1,512]{2,1,0:T(1,128)S(1)}, u32[]{:S(2)}, u32[]{:S(2)}) async-start(f32[64,1,512]{2,1,0:T(1,128)} %copy.21), calls=%async_computation | async-start | bytes 262144 | tf_op jit(solution)/shard_map/all_to_all | solution.py:15
  26.3 16.8 %collective-permute-start.2 = (f32[96,1024]{1,0:T(8,128)}, f32[96,1024]{1,0:T(8,128)}, u32[]{:S(2)}, u32[]{:S(2)}) collective-permute-start(f32[96,1024]{1,0:T(8,128)} %get-tuple-element.29), channel_id=1, source_target_pairs={{0,128},{128,256},{256,384},{384,0},{1,129},{129,257},{257,385},{3... | collective-permute-start | bytes 1179656 | tf_op jit(solution)/shard_map/ppermute | solution.py:32
  29.2 20.1 %collective-permute-start.3 = (f32[96,1024]{1,0:T(8,128)}, f32[96,1024]{1,0:T(8,128)S(1)}, u32[]{:S(2)}, u32[]{:S(2)}) collective-permute-start(f32[96,1024]{1,0:T(8,128)} %get-tuple-element.28), channel_id=1, source_target_pairs={{0,256},{128,384},{256,0},{384,128},{1,257},{129,385},{257,1},{385... | collective-permute-start | bytes 1179656 | tf_op jit(solution)/shard_map/ppermute | solution.py:32
  33.7 17.2 %collective-permute-start = (f32[96,1024]{1,0:T(8,128)}, f32[96,1024]{1,0:T(8,128)S(1)}, u32[]{:S(2)}, u32[]{:S(2)}) collective-permute-start(f32[96,1024]{1,0:T(8,128)} %get-tuple-element.26), channel_id=1, source_target_pairs={{0,384},{128,0},{256,128},{384,256},{1,385},{129,1},{257,129},{385... | collective-permute-start | bytes 1179656 | tf_op jit(solution)/shard_map/ppermute | solution.py:32
  38.6 12.3 %all-to-all-start.1 = ((f32[4,64,512]{2,1,0:T(8,128)}), f32[4,64,512]{2,1,0:T(8,128)S(1)}, u32[]{:S(2)}, u32[]{:S(2)}) async-start(f32[4,64,512]{2,1,0:T(8,128)} %broadcast_in_dim.153), calls=%async_computation.1 | async-start | bytes 1048576 | tf_op jit(solution)/shard_map/all_to_all | solution.py:15
  50.9 7.1 %collective-permute-start.1 = (f32[256,512]{1,0:T(8,128)S(1)}, f32[256,512]{1,0:T(8,128)S(1)}, u32[]{:S(2)}, u32[]{:S(2)}) collective-permute-start(f32[256,512]{1,0:T(8,128)S(1)} %bitcast.67), channel_id=1, source_target_pairs={{0,1},{1,0},{2,3},{3,2},{4,5},{5,4},{6,7},{7,6},{8,9},{9,8},{10,11... | collective-permute-start | bytes 1572872 | tf_op jit(solution)/shard_map/ppermute | solution.py:63
  60.4 12.4 %collective-permute-start.6 = (f32[64,1024]{1,0:T(8,128)S(1)}, f32[64,1024]{1,0:T(8,128)S(1)}, u32[]{:S(2)}, u32[]{:S(2)}) collective-permute-start(f32[64,1024]{1,0:T(8,128)S(1)} %get-tuple-element.31), channel_id=1, source_target_pairs={{0,16},{1,113},{8,24},{9,121},{16,32},{17,1},{24,40},{25,9},{32,48... | collective-permute-start | bytes 786440 | tf_op jit(solution)/shard_map/ppermute | solution.py:28
  63.6 13.1 %collective-permute-start.5 = (f32[64,1024]{1,0:T(8,128)S(1)}, f32[64,1024]{1,0:T(8,128)S(1)}, u32[]{:S(2)}, u32[]{:S(2)}) collective-permute-start(f32[64,1024]{1,0:T(8,128)S(1)} %get-tuple-element.32), channel_id=1, source_target_pairs={{0,120},{8,0},{16,8},{24,16},{32,24},{40,32},{48,40},{56,48},{64,5... | collective-permute-start | bytes 786440 | tf_op jit(solution)/shard_map/ppermute | solution.py:23
  66.5 10.6 %collective-permute-start.4 = (f32[64,1024]{1,0:T(8,128)S(1)}, f32[64,1024]{1,0:T(8,128)S(1)}, u32[]{:S(2)}, u32[]{:S(2)}) collective-permute-start(f32[64,1024]{1,0:T(8,128)S(1)} %get-tuple-element.30), channel_id=1, source_target_pairs={{0,8},{8,16},{16,24},{24,32},{32,40},{40,48},{48,56},{56,64},{64,7... | collective-permute-start | bytes 786440 | tf_op jit(solution)/shard_map/ppermute | solution.py:23
  77.9 21.3 %all-to-all-start.2 = ((f32[4,16,1024]{2,1,0:T(8,128)}), f32[4,16,1024]{2,1,0:T(8,128)S(1)}, u32[]{:S(2)}, u32[]{:S(2)}) async-start(f32[4,16,1024]{2,1,0:T(8,128)} %bitcast.8), calls=%async_computation.2 | async-start | bytes 524288 | tf_op jit(solution)/shard_map/all_to_all | solution.py:15
  100.2 20.0 %all-to-all-start.3 = ((f32[32,3,16]{2,1,0:T(4,128)}), f32[32,3,16]{2,1,0:T(4,128)S(1)}, u32[]{:S(2)}, u32[]{:S(2)}) async-start(f32[32,3,16]{2,1,0:T(4,128)} %broadcast_in_dim.171), calls=%async_computation.3 | async-start | bytes 131072 | tf_op jit(solution)/shard_map/all_to_all | solution.py:15
  121.2 20.2 %all-to-all-start.4 = ((f32[4,16,1024]{2,1,0:T(8,128)}), f32[4,16,1024]{2,1,0:T(8,128)S(1)}, u32[]{:S(2)}, u32[]{:S(2)}) async-start(f32[4,16,1024]{2,1,0:T(8,128)} %broadcast_in_dim.172), calls=%async_computation.4 | async-start | bytes 524288 | tf_op jit(solution)/shard_map/all_to_all | solution.py:15
  141.3 16.1 %collective-permute-start.7 = (f32[64,1024]{1,0:T(8,128)S(1)}, f32[64,1024]{1,0:T(8,128)S(1)}, u32[]{:S(2)}, u32[]{:S(2)}) collective-permute-start(f32[64,1024]{1,0:T(8,128)S(1)} %bitcast.71), channel_id=1, source_target_pairs={{0,120},{8,0},{16,8},{24,16},{32,24},{40,32},{48,40},{56,48},{64,5... | collective-permute-start | bytes 786440 | tf_op jit(solution)/shard_map/ppermute | solution.py:23
  144.1 14.6 %collective-permute-start.8 = (f32[64,1024]{1,0:T(8,128)S(1)}, f32[64,1024]{1,0:T(8,128)S(1)}, u32[]{:S(2)}, u32[]{:S(2)}) collective-permute-start(f32[64,1024]{1,0:T(8,128)S(1)} %bitcast.73), channel_id=1, source_target_pairs={{0,8},{8,16},{16,24},{24,32},{32,40},{40,48},{48,56},{56,64},{64,7... | collective-permute-start | bytes 786440 | tf_op jit(solution)/shard_map/ppermute | solution.py:23
  152.0 12.4 %collective-permute-start.9 = (f32[64,1024]{1,0:T(8,128)S(1)}, f32[64,1024]{1,0:T(8,128)S(1)}, u32[]{:S(2)}, u32[]{:S(2)}) collective-permute-start(f32[64,1024]{1,0:T(8,128)S(1)} %bitcast.74), channel_id=1, source_target_pairs={{0,16},{1,113},{8,24},{9,121},{16,32},{17,1},{24,40},{25,9},{32,48... | collective-permute-start | bytes 786440 | tf_op jit(solution)/shard_map/ppermute | solution.py:28
  158.7 7.8 %copy-start.2 = (f32[64,1024]{1,0:T(8,128)}, f32[64,1024]{1,0:T(8,128)S(1)}, u32[]{:S(2)}) copy-start(f32[64,1024]{1,0:T(8,128)S(1)} %collective-permute-done.8) | copy-start | bytes 786436
  164.4 2.1 copy-start.3
  166.5 21.9 %all-to-all-start.5 = ((f32[32,16,384]{2,1,0:T(8,128)}), f32[32,16,384]{2,1,0:T(8,128)S(1)}, u32[]{:S(2)}, u32[]{:S(2)}) async-start(f32[32,16,384]{2,1,0:T(8,128)} %bitcast.15), calls=%async_computation.5 | async-start | bytes 1572864 | tf_op jit(solution)/shard_map/all_to_all | solution.py:15
  176.7 19.0 %collective-permute-start.10 = (f32[96,1024]{1,0:T(8,128)}, f32[96,1024]{1,0:T(8,128)}, u32[]{:S(2)}, u32[]{:S(2)}) collective-permute-start(f32[96,1024]{1,0:T(8,128)} %get-tuple-element.25), channel_id=1, source_target_pairs={{0,128},{128,256},{256,384},{384,0},{1,129},{129,257},{257,385},{3... | collective-permute-start | bytes 1179656 | tf_op jit(solution)/shard_map/ppermute | solution.py:32
  180.1 16.7 %collective-permute-start.11 = (f32[96,1024]{1,0:T(8,128)S(1)}, f32[96,1024]{1,0:T(8,128)}, u32[]{:S(2)}, u32[]{:S(2)}) collective-permute-start(f32[96,1024]{1,0:T(8,128)S(1)} %get-tuple-element.24), channel_id=1, source_target_pairs={{0,384},{128,0},{256,128},{384,256},{1,385},{129,1},{257,129},{385... | collective-permute-start | bytes 1179656 | tf_op jit(solution)/shard_map/ppermute | solution.py:32
  183.7 28.8 %collective-permute-start.12 = (f32[96,1024]{1,0:T(8,128)S(1)}, f32[96,1024]{1,0:T(8,128)}, u32[]{:S(2)}, u32[]{:S(2)}) collective-permute-start(f32[96,1024]{1,0:T(8,128)S(1)} %get-tuple-element.23), channel_id=1, source_target_pairs={{0,256},{128,384},{256,0},{384,128},{1,257},{129,385},{257,1},{385... | collective-permute-start | bytes 1179656 | tf_op jit(solution)/shard_map/ppermute | solution.py:32
  189.1 16.6 %all-to-all-start.6 = ((f32[16,1,512]{2,1,0:T(1,128)}), f32[16,1,512]{2,1,0:T(1,128)S(1)}, u32[]{:S(2)}, u32[]{:S(2)}) async-start(f32[16,1,512]{2,1,0:T(1,128)} %reshape.307), calls=%async_computation.6 | async-start | bytes 65536 | tf_op jit(solution)/shard_map/all_to_all | solution.py:15
  206.6 11.7 %all-to-all-start.7 = ((f32[8,1,6144]{2,1,0:T(1,128)}), f32[8,1,6144]{2,1,0:T(1,128)S(1)}, u32[]{:S(2)}, u32[]{:S(2)}) async-start(f32[8,1,6144]{2,1,0:T(1,128)} %broadcast_in_dim.175), calls=%async_computation.7 | async-start | bytes 393216 | tf_op jit(solution)/shard_map/all_to_all | solution.py:15
  213.5 5.6 %copy-start.1 = (f32[96,4096]{1,0:T(8,128)}, f32[96,4096]{1,0:T(8,128)S(1)}, u32[]{:S(2)}) copy-start(f32[96,4096]{1,0:T(8,128)S(1)} %constant_dynamic-update-slice_fusion) | copy-start | bytes 4718596

commit v13 on v11

--- a/solution.py
+++ b/solution.py
@@ -1,6 +1,10 @@
+import functools
+
 import jax
 import jax.numpy as jnp
 from jax import lax
+from jax.experimental import pallas as pl
+from jax.experimental.pallas import tpu as pltpu
 from jax.sharding import Mesh, PartitionSpec as P
 
 HIGH = lax.Precision.HIGHEST
@@ -37,6 +41,48 @@
     return lax.dot_general(a, b, dims, precision=precision, preferred_element_type=jnp.float32)
 
 
+def cut_kernel(quarter, weight, targets, lengths, owners, own, one, two, three, notes, target, sems):
+    x = lax.axis_index("x")
+    small = pltpu.make_async_copy(targets, target, sems.at[4])
+    large = [
+        pltpu.make_async_copy(
+            weight.at[:, pl.ds(pl.multiple_of(lax.rem(x + s, 4) * quarter, 128), quarter)], block, sems.at[s]
+        )
+        for s, block in enumerate((own, one, two, three))
+    ]
+    small.start()
+    for copy in large:
+        copy.start()
+    small.wait()
+    lane = lax.broadcasted_iota(jnp.int32, (1, META), 1)
+    values = [*(target[i] for i in range(8)), lengths[0], owners[0]]
+    row = jnp.zeros((1, META), jnp.int32)
+    for i, value in enumerate(values):
+        row = jnp.where(lane == i, value, row)
+    notes[...] = row.astype(jnp.float32)
+    for copy in large:
+        copy.wait()
+
+
+def cut(weight, targets, lengths, owners):
+    depth, columns = weight.shape
+    quarter = columns // 4
+    block = jax.ShapeDtypeStruct((depth, quarter), jnp.float32)
+    anywhere = pl.BlockSpec(memory_space=pl.ANY)
+    scalar = pl.BlockSpec(memory_space=pltpu.SMEM)
+    return pl.pallas_call(
+        functools.partial(cut_kernel, quarter),
+        out_shape=(block, block, block, block, jax.ShapeDtypeStruct((1, META), jnp.float32)),
+        in_specs=[anywhere, anywhere, scalar, scalar],
+        out_specs=(*([anywhere] * 4), pl.BlockSpec(memory_space=pltpu.VMEM)),
+        scratch_shapes=[
+            pltpu.SMEM((8,), jnp.int32),
+            pltpu.SemaphoreType.DMA((5,)),
+        ],
+        name="cut",
+    )(weight, targets, lengths, owners)
+
+
 def on_device(responses, weight, lengths, targets, owners):
     width = responses.shape[1]
     depth, columns = weight.shape
@@ -46,20 +92,17 @@
     j, c = lax.axis_index(YC), lax.axis_index("c")
 
     row = lax.dynamic_slice(responses, (j, 0), (1, width)).reshape(4, 16, depth)
-    notes = jnp.pad(jnp.concatenate([targets, lengths, owners]).astype(jnp.float32), (0, META - 10))
+    *blocks, notes = cut(weight, targets, lengths, owners)
     notes = jnp.broadcast_to(notes, (16, META))
     packed = jnp.concatenate([row.transpose(1, 0, 2).reshape(16, wide), notes], axis=1).reshape(1, 16, 1, wide + META)
     packed = jnp.broadcast_to(packed, (4, 16, 1, wide + META)).reshape(64, 1, wide + META)
 
-    def cut(array, s):
-        return lax.dynamic_slice(array, (0, (x + s) % 4 * quarter), (depth, quarter))
-
-    packed, weight = lax.optimization_barrier((packed, weight))
-    pieces = [cut(weight, 0), *(shift_x(cut(weight, s), s) for s in range(1, 4))]
+    pieces = [blocks[0], *(shift_x(blocks[s], s) for s in range(1, 4))]
     mine = swap(packed, ("x", *Z)).reshape(64, wide + META)
+    mine, pieces[0] = lax.optimization_barrier((mine, pieces[0]))
 
     slots = spread(mine, "y", 4).reshape(256, wide + META)
-    slots, pieces[3] = lax.optimization_barrier((slots, pieces[3]))
+    _, pieces[3] = lax.optimization_barrier((slots, pieces[3]))
     slots_other = lax.ppermute(slots, "c", [(0, 1), (1, 0)])
 
     all_notes = slots[:, wide : wide + 10].astype(jnp.int32)
@@ -97,8 +140,9 @@
         head = lax.dynamic_update_slice(head, piece[None], ((x - s) % 4, 0, 0))
     head = lax.optimization_barrier(head.reshape(wide, quarter))
 
-    partial = dot(hidden, head)
-    block = partial[:64] + shift_z(partial[64:128], 1) + shift_z(partial[192:], -1) + shift_far(partial[128:192])
+    leave = dot(hidden[64:], head)
+    stay = lax.optimization_barrier(dot(hidden[:64], head))
+    block = stay + shift_z(leave[:64], 1) + shift_z(leave[128:], -1) + shift_far(leave[64:128])
     logits = jnp.sum(swap(block.reshape(4, 16, quarter), "h"), axis=0)
 
     row_labels = lax.dynamic_slice(labels, (h * 16,), (16,))

time: 218 us -> 260 us (1.19)
  Pallas kernels: 0 us -> 49.3 us
  local copies, waits for them, and re-layouts: 18.4 us -> 14.9 us
  waiting for transfers between devices: 78.2 us -> 75.6 us
    pallas_call x0 -> x1, Pallas kernels: none -> 49.3 us  [cut(): pl.pallas_call(functools.partial(cut_kernel, quarter), out_shape=(block,...]
    ppermute x4, waiting for transfers between devices: 14 us -> 8.41 us  [shift_z(): return lax.ppermute(block, Z, [(i, (i + step) % 16) for i in range(16)])]
    ppermute x2, waiting for transfers between devices: 2.88 us -> 8.06 us  [shift_far(): return lax.ppermute(block, ('h', 'l', 'c'), pairs)]
    ppermute x4, starting transfers between devices: 13.3 us -> 17.7 us  [shift_z(): return lax.ppermute(block, Z, [(i, (i + step) % 16) for i in range(16)])]
    all_to_all x8, starting transfers between devices: 59.4 us -> 56.2 us  [swap(): return lax.all_to_all(blocks, axes, split_axis=0, concat_axis=0, tiled=True)]
    dynamic_update_slice x4, local copies, waits for them, and re-layouts: 4.11 us -> 1.13 us  [on_device(): head = lax.dynamic_update_slice(head, piece[None], ((x - s) % 4, 0, 0))]
    ppermute x2, starting transfers between devices: 7.75 us -> 5.12 us  [shift_far(): return lax.ppermute(block, ('h', 'l', 'c'), pairs)]
    dot_general x6 -> x7, matrix products: 6.95 us -> 7.56 us  [dot(): lax.dot_general(a, b, dims, precision=precision, preferred_element_type=j...]
  transfers between devices with their start and end apart: 21 -> 21, of which waited for: 14 -> 16; matrix products, arithmetic and copies ran while one was open for 9% -> 6% of each run, Pallas kernels for 0% -> 0%
where the time goes in v13:
time: 260 us; the launch traced here: 259 us
  starting transfers between devices  106 us (41%)
  waiting for transfers between devices  75.6 us (29%)
  Pallas kernels  49.3 us (19%)
  local copies, waits for them, and re-layouts  14.9 us (6%)
  matrix products  7.56 us (3%)
  other arithmetic  2.86 us (1%)
    all_to_all x8, starting transfers between devices, swap(): return lax.all_to_all(blocks, axes, split_axis=0, concat_axis=0, tiled=True)  56.2 us
    all_to_all x8, waiting for transfers between devices, swap(): return lax.all_to_all(blocks, axes, split_axis=0, concat_axis=0, tiled=True)  55.2 us
    pallas_call x1, Pallas kernels, cut(): pl.pallas_call(functools.partial(cut_kernel, quarter), out_shape=(block,...  49.3 us
    ppermute x6, starting transfers between devices, shift_x(): return lax.ppermute(block, 'x', [(i, (i + step) % 4) for i in range(4)])  20.6 us
    ppermute x4, starting transfers between devices, shift_z(): return lax.ppermute(block, Z, [(i, (i + step) % 16) for i in range(16)])  17.7 us
    ppermute x4, waiting for transfers between devices, shift_z(): return lax.ppermute(block, Z, [(i, (i + step) % 16) for i in range(16)])  8.41 us
    ppermute x2, waiting for transfers between devices, shift_far(): return lax.ppermute(block, ('h', 'l', 'c'), pairs)  8.06 us
    dot_general x7, matrix products, dot(): lax.dot_general(a, b, dims, precision=precision, preferred_element_type=j...  7.56 us
  transfers between devices with their start and end apart: 21, of which 16 were waited for; matrix products, arithmetic and copies ran while one was open for 6% of the time, Pallas kernels for 0%

profile of v13, /device:TPU:1, one launch (start us, length us, event | category | flops | bytes accessed | tf_op | source)
XLA Modules:
  0.0 259.2 jit_solution(4671672491003299697)
XLA Ops:
  3.1 49.3 %cut.1 = (f32[96,1024]{1,0:T(8,128)}, f32[96,1024]{1,0:T(8,128)}, f32[96,1024]{1,0:T(8,128)}, f32[96,1024]{1,0:T(8,128)}, f32[1,128]{1,0:T(1,128)}) custom-call(f32[96,4096]{1,0:T(8,128)} %weight.1, s32[8]{0:T(128)} %targets.1, s32[1]{0:T(128)S(6)} %copy.49.lengths, s32[1]{0:T(128)S(6)} %copy.50.owners), custom_call_target="tpu_custom_call" | custom-call | tf_op jit(solution)/shard_map/cut/pallas_call | solution.py:73
  53.9 19.1 %all-to-all-start = ((f32[64,1,512]{2,1,0:T(1,128)}), f32[64,1,512]{2,1,0:T(1,128)S(1)}, u32[]{:S(2)}, u32[]{:S(2)}) async-start(f32[64,1,512]{2,1,0:T(1,128)} %copy.21), calls=%async_computation | async-start | bytes 262144 | tf_op jit(solution)/shard_map/all_to_all | solution.py:19
  73.0 2.9 %collective-permute-start.1 = (f32[96,1024]{1,0:T(8,128)}, f32[96,1024]{1,0:T(8,128)}, u32[]{:S(2)}, u32[]{:S(2)}) collective-permute-start(f32[96,1024]{1,0:T(8,128)} %get-tuple-element.17), channel_id=1, source_target_pairs={{0,128},{128,256},{256,384},{384,0},{1,129},{129,257},{257,385},{3... | collective-permute-start | bytes 1179656 | tf_op jit(solution)/shard_map/ppermute | solution.py:36
  76.0 4.5 %collective-permute-start.2 = (f32[96,1024]{1,0:T(8,128)}, f32[96,1024]{1,0:T(8,128)S(1)}, u32[]{:S(2)}, u32[]{:S(2)}) collective-permute-start(f32[96,1024]{1,0:T(8,128)} %get-tuple-element.18), channel_id=1, source_target_pairs={{0,256},{128,384},{256,0},{384,128},{1,257},{129,385},{257,1},{385... | collective-permute-start | bytes 1179656 | tf_op jit(solution)/shard_map/ppermute | solution.py:36
  80.5 3.0 %collective-permute-start.3 = (f32[96,1024]{1,0:T(8,128)}, f32[96,1024]{1,0:T(8,128)S(1)}, u32[]{:S(2)}, u32[]{:S(2)}) collective-permute-start(f32[96,1024]{1,0:T(8,128)} %get-tuple-element.19), channel_id=1, source_target_pairs={{0,384},{128,0},{256,128},{384,256},{1,385},{129,1},{257,129},{385... | collective-permute-start | bytes 1179656 | tf_op jit(solution)/shard_map/ppermute | solution.py:36
  83.6 3.4 %all-to-all-done = f32[64,1,512]{2,1,0:T(1,128)S(1)} async-done(((f32[64,1,512]{2,1,0:T(1,128)}), f32[64,1,512]{2,1,0:T(1,128)S(1)}, u32[]{:S(2)}, u32[]{:S(2)}) %all-to-all-start) | async-done | bytes 131104 | tf_op jit(solution)/shard_map/all_to_all | solution.py:19
  87.9 4.2 %all-to-all-start.1 = ((f32[4,64,512]{2,1,0:T(8,128)}), f32[4,64,512]{2,1,0:T(8,128)S(1)}, u32[]{:S(2)}, u32[]{:S(2)}) async-start(f32[4,64,512]{2,1,0:T(8,128)} %broadcast_in_dim.158), calls=%async_computation.1 | async-start | bytes 1048576 | tf_op jit(solution)/shard_map/all_to_all | solution.py:19
  93.3 3.2 %collective-permute-done.2 = f32[96,1024]{1,0:T(8,128)S(1)} collective-permute-done((f32[96,1024]{1,0:T(8,128)}, f32[96,1024]{1,0:T(8,128)S(1)}, u32[]{:S(2)}, u32[]{:S(2)}) %collective-permute-start.2) | collective-permute-done | bytes 393248 | tf_op jit(solution)/shard_map/ppermute | solution.py:36
  96.6 2.5 all-to-all-done.1
  99.0 6.8 %collective-permute-start = (f32[256,512]{1,0:T(8,128)S(1)}, f32[256,512]{1,0:T(8,128)S(1)}, u32[]{:S(2)}, u32[]{:S(2)}) collective-permute-start(f32[256,512]{1,0:T(8,128)S(1)} %bitcast.55), channel_id=1, source_target_pairs={{0,1},{1,0},{2,3},{3,2},{4,5},{5,4},{6,7},{7,6},{8,9},{9,8},{10,11... | collective-permute-start | bytes 1572872 | tf_op jit(solution)/shard_map/ppermute | solution.py:106
  109.2 3.2 %collective-permute-start.6 = (f32[64,1024]{1,0:T(8,128)S(1)}, f32[64,1024]{1,0:T(8,128)S(1)}, u32[]{:S(2)}, u32[]{:S(2)}) collective-permute-start(f32[64,1024]{1,0:T(8,128)S(1)} %get-tuple-element.35), channel_id=1, source_target_pairs={{0,16},{1,113},{8,24},{9,121},{16,32},{17,1},{24,40},{25,9},{32,48... | collective-permute-start | bytes 786440 | tf_op jit(solution)/shard_map/ppermute | solution.py:32
  114.4 3.4 %collective-permute-start.4 = (f32[64,1024]{1,0:T(8,128)S(1)}, f32[64,1024]{1,0:T(8,128)S(1)}, u32[]{:S(2)}, u32[]{:S(2)}) collective-permute-start(f32[64,1024]{1,0:T(8,128)S(1)} %get-tuple-element.34), channel_id=1, source_target_pairs={{0,8},{8,16},{16,24},{24,32},{32,40},{40,48},{48,56},{56,64},{64,7... | collective-permute-start | bytes 786440 | tf_op jit(solution)/shard_map/ppermute | solution.py:27
  118.8 3.6 %collective-permute-done.6 = f32[64,1024]{1,0:T(8,128)S(1)} collective-permute-done((f32[64,1024]{1,0:T(8,128)S(1)}, f32[64,1024]{1,0:T(8,128)S(1)}, u32[]{:S(2)}, u32[]{:S(2)}) %collective-permute-start.6) | collective-permute-done | bytes 262176 | tf_op jit(solution)/shard_map/ppermute | solution.py:32
  122.4 2.9 %collective-permute-done.5 = f32[64,1024]{1,0:T(8,128)S(1)} collective-permute-done((f32[64,1024]{1,0:T(8,128)S(1)}, f32[64,1024]{1,0:T(8,128)S(1)}, u32[]{:S(2)}, u32[]{:S(2)}) %collective-permute-start.5) | collective-permute-done | bytes 262176 | tf_op jit(solution)/shard_map/ppermute | solution.py:27
  126.7 5.9 %all-to-all-start.2 = ((f32[4,16,1024]{2,1,0:T(8,128)}), f32[4,16,1024]{2,1,0:T(8,128)S(1)}, u32[]{:S(2)}, u32[]{:S(2)}) async-start(f32[4,16,1024]{2,1,0:T(8,128)} %bitcast.9), calls=%async_computation.2 | async-start | bytes 524288 | tf_op jit(solution)/shard_map/all_to_all | solution.py:19
  133.2 15.0 %all-to-all-done.2 = f32[4,16,1024]{2,1,0:T(8,128)S(1)} async-done(((f32[4,16,1024]{2,1,0:T(8,128)}), f32[4,16,1024]{2,1,0:T(8,128)S(1)}, u32[]{:S(2)}, u32[]{:S(2)}) %all-to-all-start.2) | async-done | bytes 262176 | tf_op jit(solution)/shard_map/all_to_all | solution.py:19
  149.2 8.9 %all-to-all-start.3 = ((f32[32,3,16]{2,1,0:T(4,128)}), f32[32,3,16]{2,1,0:T(4,128)S(1)}, u32[]{:S(2)}, u32[]{:S(2)}) async-start(f32[32,3,16]{2,1,0:T(4,128)} %broadcast_in_dim.176), calls=%async_computation.3 | async-start | bytes 131072 | tf_op jit(solution)/shard_map/all_to_all | solution.py:19
  158.1 7.4 %all-to-all-done.3 = f32[32,3,16]{2,1,0:T(4,128)S(1)} async-done(((f32[32,3,16]{2,1,0:T(4,128)}), f32[32,3,16]{2,1,0:T(4,128)S(1)}, u32[]{:S(2)}, u32[]{:S(2)}) %all-to-all-start.3) | async-done | bytes 6176 | tf_op jit(solution)/shard_map/all_to_all | solution.py:19
  166.5 4.1 %all-to-all-start.4 = ((f32[4,16,1024]{2,1,0:T(8,128)}), f32[4,16,1024]{2,1,0:T(8,128)S(1)}, u32[]{:S(2)}, u32[]{:S(2)}) async-start(f32[4,16,1024]{2,1,0:T(8,128)} %broadcast_in_dim.177), calls=%async_computation.4 | async-start | bytes 524288 | tf_op jit(solution)/shard_map/all_to_all | solution.py:19
  170.7 14.0 %all-to-all-done.4 = f32[4,16,1024]{2,1,0:T(8,128)S(1)} async-done(((f32[4,16,1024]{2,1,0:T(8,128)}), f32[4,16,1024]{2,1,0:T(8,128)S(1)}, u32[]{:S(2)}, u32[]{:S(2)}) %all-to-all-start.4) | async-done | bytes 262176 | tf_op jit(solution)/shard_map/all_to_all | solution.py:19
  184.7 9.3 %collective-permute-start.9 = (f32[64,1024]{1,0:T(8,128)S(1)}, f32[64,1024]{1,0:T(8,128)S(1)}, u32[]{:S(2)}, u32[]{:S(2)}) collective-permute-start(f32[64,1024]{1,0:T(8,128)S(1)} %bitcast.59), channel_id=1, source_target_pairs={{0,8},{8,16},{16,24},{24,32},{32,40},{40,48},{48,56},{56,64},{64,7... | collective-permute-start | bytes 786440 | tf_op jit(solution)/shard_map/ppermute | solution.py:27
  195.9 3.1 %collective-permute-start.7 = (f32[64,1024]{1,0:T(8,128)S(1)}, f32[64,1024]{1,0:T(8,128)S(1)}, u32[]{:S(2)}, u32[]{:S(2)}) collective-permute-start(f32[64,1024]{1,0:T(8,128)S(1)} %bitcast.61), channel_id=1, source_target_pairs={{0,120},{8,0},{16,8},{24,16},{32,24},{40,32},{48,40},{56,48},{64,5... | collective-permute-start | bytes 786440 | tf_op jit(solution)/shard_map/ppermute | solution.py:27
  199.1 4.4 %collective-permute-done.8 = f32[64,1024]{1,0:T(8,128)S(1)} collective-permute-done((f32[64,1024]{1,0:T(8,128)S(1)}, f32[64,1024]{1,0:T(8,128)S(1)}, u32[]{:S(2)}, u32[]{:S(2)}) %collective-permute-start.8) | collective-permute-done | bytes 262176 | tf_op jit(solution)/shard_map/ppermute | solution.py:32
  203.6 4.9 %collective-permute-done.7 = f32[64,1024]{1,0:T(8,128)S(1)} collective-permute-done((f32[64,1024]{1,0:T(8,128)S(1)}, f32[64,1024]{1,0:T(8,128)S(1)}, u32[]{:S(2)}, u32[]{:S(2)}) %collective-permute-start.7) | collective-permute-done | bytes 262176 | tf_op jit(solution)/shard_map/ppermute | solution.py:27
  210.9 4.6 %all-to-all-start.5 = ((f32[32,16,384]{2,1,0:T(8,128)}), f32[32,16,384]{2,1,0:T(8,128)S(1)}, u32[]{:S(2)}, u32[]{:S(2)}) async-start(f32[32,16,384]{2,1,0:T(8,128)} %bitcast.16), calls=%async_computation.5 | async-start | bytes 1572864 | tf_op jit(solution)/shard_map/all_to_all | solution.py:19
  218.2 3.3 %collective-permute-start.10 = (f32[96,1024]{1,0:T(8,128)}, f32[96,1024]{1,0:T(8,128)}, u32[]{:S(2)}, u32[]{:S(2)}) collective-permute-start(f32[96,1024]{1,0:T(8,128)} %get-tuple-element.33), channel_id=1, source_target_pairs={{0,128},{128,256},{256,384},{384,0},{1,129},{129,257},{257,385},{3... | collective-permute-start | bytes 1179656 | tf_op jit(solution)/shard_map/ppermute | solution.py:36
  221.5 3.2 %collective-permute-start.11 = (f32[96,1024]{1,0:T(8,128)S(1)}, f32[96,1024]{1,0:T(8,128)}, u32[]{:S(2)}, u32[]{:S(2)}) collective-permute-start(f32[96,1024]{1,0:T(8,128)S(1)} %get-tuple-element.32), channel_id=1, source_target_pairs={{0,384},{128,0},{256,128},{384,256},{1,385},{129,1},{257,129},{385... | collective-permute-start | bytes 1179656 | tf_op jit(solution)/shard_map/ppermute | solution.py:36
  225.2 3.6 %collective-permute-start.12 = (f32[96,1024]{1,0:T(8,128)S(1)}, f32[96,1024]{1,0:T(8,128)}, u32[]{:S(2)}, u32[]{:S(2)}) collective-permute-start(f32[96,1024]{1,0:T(8,128)S(1)} %get-tuple-element.31), channel_id=1, source_target_pairs={{0,256},{128,384},{256,0},{384,128},{1,257},{129,385},{257,1},{385... | collective-permute-start | bytes 1179656 | tf_op jit(solution)/shard_map/ppermute | solution.py:36
  230.6 3.6 %all-to-all-start.6 = ((f32[16,1,512]{2,1,0:T(1,128)}), f32[16,1,512]{2,1,0:T(1,128)S(1)}, u32[]{:S(2)}, u32[]{:S(2)}) async-start(f32[16,1,512]{2,1,0:T(1,128)} %reshape.307), calls=%async_computation.6 | async-start | bytes 65536 | tf_op jit(solution)/shard_map/all_to_all | solution.py:19
  238.1 7.6 %all-to-all-done.6 = f32[16,1,512]{2,1,0:T(1,128)S(1)} async-done(((f32[16,1,512]{2,1,0:T(1,128)}), f32[16,1,512]{2,1,0:T(1,128)S(1)}, u32[]{:S(2)}, u32[]{:S(2)}) %all-to-all-start.6) | async-done | bytes 32800 | tf_op jit(solution)/shard_map/all_to_all | solution.py:19
  246.7 5.8 %all-to-all-start.7 = ((f32[8,1,6144]{2,1,0:T(1,128)}), f32[8,1,6144]{2,1,0:T(1,128)S(1)}, u32[]{:S(2)}, u32[]{:S(2)}) async-start(f32[8,1,6144]{2,1,0:T(1,128)} %broadcast_in_dim.180), calls=%async_computation.7 | async-start | bytes 393216 | tf_op jit(solution)/shard_map/all_to_all | solution.py:19
  254.1 4.3 %all-to-all-done.7 = f32[8,1,6144]{2,1,0:T(1,128)S(1)} async-done(((f32[8,1,6144]{2,1,0:T(1,128)}), f32[8,1,6144]{2,1,0:T(1,128)S(1)}, u32[]{:S(2)}, u32[]{:S(2)}) %all-to-all-start.7) | async-done | bytes 196640 | tf_op jit(solution)/shard_map/all_to_all | solution.py:19
  (94 shorter events, 31.6 us)
Async XLA Ops:
  0.6 0.9 copy-start
  53.9 33.1 %all-to-all-start = ((f32[64,1,512]{2,1,0:T(1,128)}), f32[64,1,512]{2,1,0:T(1,128)S(1)}, u32[]{:S(2)}, u32[]{:S(2)}) async-start(f32[64,1,512]{2,1,0:T(1,128)} %copy.21), calls=%async_computation | async-start | bytes 262144 | tf_op jit(solution)/shard_map/all_to_all | solution.py:19
  73.0 19.3 %collective-permute-start.1 = (f32[96,1024]{1,0:T(8,128)}, f32[96,1024]{1,0:T(8,128)}, u32[]{:S(2)}, u32[]{:S(2)}) collective-permute-start(f32[96,1024]{1,0:T(8,128)} %get-tuple-element.17), channel_id=1, source_target_pairs={{0,128},{128,256},{256,384},{384,0},{1,129},{129,257},{257,385},{3... | collective-permute-start | bytes 1179656 | tf_op jit(solution)/shard_map/ppermute | solution.py:36
  76.0 20.5 %collective-permute-start.2 = (f32[96,1024]{1,0:T(8,128)}, f32[96,1024]{1,0:T(8,128)S(1)}, u32[]{:S(2)}, u32[]{:S(2)}) collective-permute-start(f32[96,1024]{1,0:T(8,128)} %get-tuple-element.18), channel_id=1, source_target_pairs={{0,256},{128,384},{256,0},{384,128},{1,257},{129,385},{257,1},{385... | collective-permute-start | bytes 1179656 | tf_op jit(solution)/shard_map/ppermute | solution.py:36
  80.5 25.7 %collective-permute-start.3 = (f32[96,1024]{1,0:T(8,128)}, f32[96,1024]{1,0:T(8,128)S(1)}, u32[]{:S(2)}, u32[]{:S(2)}) collective-permute-start(f32[96,1024]{1,0:T(8,128)} %get-tuple-element.19), channel_id=1, source_target_pairs={{0,384},{128,0},{256,128},{384,256},{1,385},{129,1},{257,129},{385... | collective-permute-start | bytes 1179656 | tf_op jit(solution)/shard_map/ppermute | solution.py:36
  87.0 5.2 %copy-start.4 = (f32[96,1024]{1,0:T(8,128)S(1)}, f32[96,1024]{1,0:T(8,128)}, u32[]{:S(2)}) copy-start(f32[96,1024]{1,0:T(8,128)} %get-tuple-element.16) | copy-start | bytes 1179652
  87.9 11.1 %all-to-all-start.1 = ((f32[4,64,512]{2,1,0:T(8,128)}), f32[4,64,512]{2,1,0:T(8,128)S(1)}, u32[]{:S(2)}, u32[]{:S(2)}) async-start(f32[4,64,512]{2,1,0:T(8,128)} %broadcast_in_dim.158), calls=%async_computation.1 | async-start | bytes 1048576 | tf_op jit(solution)/shard_map/all_to_all | solution.py:19
  99.0 8.3 %collective-permute-start = (f32[256,512]{1,0:T(8,128)S(1)}, f32[256,512]{1,0:T(8,128)S(1)}, u32[]{:S(2)}, u32[]{:S(2)}) collective-permute-start(f32[256,512]{1,0:T(8,128)S(1)} %bitcast.55), channel_id=1, source_target_pairs={{0,1},{1,0},{2,3},{3,2},{4,5},{5,4},{6,7},{7,6},{8,9},{9,8},{10,11... | collective-permute-start | bytes 1572872 | tf_op jit(solution)/shard_map/ppermute | solution.py:106
  109.2 13.2 %collective-permute-start.6 = (f32[64,1024]{1,0:T(8,128)S(1)}, f32[64,1024]{1,0:T(8,128)S(1)}, u32[]{:S(2)}, u32[]{:S(2)}) collective-permute-start(f32[64,1024]{1,0:T(8,128)S(1)} %get-tuple-element.35), channel_id=1, source_target_pairs={{0,16},{1,113},{8,24},{9,121},{16,32},{17,1},{24,40},{25,9},{32,48... | collective-permute-start | bytes 786440 | tf_op jit(solution)/shard_map/ppermute | solution.py:32
  112.4 12.8 %collective-permute-start.5 = (f32[64,1024]{1,0:T(8,128)S(1)}, f32[64,1024]{1,0:T(8,128)S(1)}, u32[]{:S(2)}, u32[]{:S(2)}) collective-permute-start(f32[64,1024]{1,0:T(8,128)S(1)} %get-tuple-element.36), channel_id=1, source_target_pairs={{0,120},{8,0},{16,8},{24,16},{32,24},{40,32},{48,40},{56,48},{64,5... | collective-permute-start | bytes 786440 | tf_op jit(solution)/shard_map/ppermute | solution.py:27
  114.4 11.6 %collective-permute-start.4 = (f32[64,1024]{1,0:T(8,128)S(1)}, f32[64,1024]{1,0:T(8,128)S(1)}, u32[]{:S(2)}, u32[]{:S(2)}) collective-permute-start(f32[64,1024]{1,0:T(8,128)S(1)} %get-tuple-element.34), channel_id=1, source_target_pairs={{0,8},{8,16},{16,24},{24,32},{32,40},{40,48},{48,56},{56,64},{64,7... | collective-permute-start | bytes 786440 | tf_op jit(solution)/shard_map/ppermute | solution.py:27
  126.7 21.5 %all-to-all-start.2 = ((f32[4,16,1024]{2,1,0:T(8,128)}), f32[4,16,1024]{2,1,0:T(8,128)S(1)}, u32[]{:S(2)}, u32[]{:S(2)}) async-start(f32[4,16,1024]{2,1,0:T(8,128)} %bitcast.9), calls=%async_computation.2 | async-start | bytes 524288 | tf_op jit(solution)/shard_map/all_to_all | solution.py:19
  149.2 16.3 %all-to-all-start.3 = ((f32[32,3,16]{2,1,0:T(4,128)}), f32[32,3,16]{2,1,0:T(4,128)S(1)}, u32[]{:S(2)}, u32[]{:S(2)}) async-start(f32[32,3,16]{2,1,0:T(4,128)} %broadcast_in_dim.176), calls=%async_computation.3 | async-start | bytes 131072 | tf_op jit(solution)/shard_map/all_to_all | solution.py:19
  166.5 18.2 %all-to-all-start.4 = ((f32[4,16,1024]{2,1,0:T(8,128)}), f32[4,16,1024]{2,1,0:T(8,128)S(1)}, u32[]{:S(2)}, u32[]{:S(2)}) async-start(f32[4,16,1024]{2,1,0:T(8,128)} %broadcast_in_dim.177), calls=%async_computation.4 | async-start | bytes 524288 | tf_op jit(solution)/shard_map/all_to_all | solution.py:19
  184.7 14.5 %collective-permute-start.9 = (f32[64,1024]{1,0:T(8,128)S(1)}, f32[64,1024]{1,0:T(8,128)S(1)}, u32[]{:S(2)}, u32[]{:S(2)}) collective-permute-start(f32[64,1024]{1,0:T(8,128)S(1)} %bitcast.59), channel_id=1, source_target_pairs={{0,8},{8,16},{16,24},{24,32},{32,40},{40,48},{48,56},{56,64},{64,7... | collective-permute-start | bytes 786440 | tf_op jit(solution)/shard_map/ppermute | solution.py:27
  193.9 9.7 %collective-permute-start.8 = (f32[64,1024]{1,0:T(8,128)S(1)}, f32[64,1024]{1,0:T(8,128)S(1)}, u32[]{:S(2)}, u32[]{:S(2)}) collective-permute-start(f32[64,1024]{1,0:T(8,128)S(1)} %bitcast.60), channel_id=1, source_target_pairs={{0,16},{1,113},{8,24},{9,121},{16,32},{17,1},{24,40},{25,9},{32,48... | collective-permute-start | bytes 786440 | tf_op jit(solution)/shard_map/ppermute | solution.py:32
  195.9 12.6 %collective-permute-start.7 = (f32[64,1024]{1,0:T(8,128)S(1)}, f32[64,1024]{1,0:T(8,128)S(1)}, u32[]{:S(2)}, u32[]{:S(2)}) collective-permute-start(f32[64,1024]{1,0:T(8,128)S(1)} %bitcast.61), channel_id=1, source_target_pairs={{0,120},{8,0},{16,8},{24,16},{32,24},{40,32},{48,40},{56,48},{64,5... | collective-permute-start | bytes 786440 | tf_op jit(solution)/shard_map/ppermute | solution.py:27
  203.6 7.3 %copy-start.2 = (f32[64,1024]{1,0:T(8,128)}, f32[64,1024]{1,0:T(8,128)S(1)}, u32[]{:S(2)}) copy-start(f32[64,1024]{1,0:T(8,128)S(1)} %collective-permute-done.8) | copy-start | bytes 786436
  208.5 2.4 copy-start.3
  210.9 19.0 %all-to-all-start.5 = ((f32[32,16,384]{2,1,0:T(8,128)}), f32[32,16,384]{2,1,0:T(8,128)S(1)}, u32[]{:S(2)}, u32[]{:S(2)}) async-start(f32[32,16,384]{2,1,0:T(8,128)} %bitcast.16), calls=%async_computation.5 | async-start | bytes 1572864 | tf_op jit(solution)/shard_map/all_to_all | solution.py:19
  218.2 17.8 %collective-permute-start.10 = (f32[96,1024]{1,0:T(8,128)}, f32[96,1024]{1,0:T(8,128)}, u32[]{:S(2)}, u32[]{:S(2)}) collective-permute-start(f32[96,1024]{1,0:T(8,128)} %get-tuple-element.33), channel_id=1, source_target_pairs={{0,128},{128,256},{256,384},{384,0},{1,129},{129,257},{257,385},{3... | collective-permute-start | bytes 1179656 | tf_op jit(solution)/shard_map/ppermute | solution.py:36
  221.5 15.5 %collective-permute-start.11 = (f32[96,1024]{1,0:T(8,128)S(1)}, f32[96,1024]{1,0:T(8,128)}, u32[]{:S(2)}, u32[]{:S(2)}) collective-permute-start(f32[96,1024]{1,0:T(8,128)S(1)} %get-tuple-element.32), channel_id=1, source_target_pairs={{0,384},{128,0},{256,128},{384,256},{1,385},{129,1},{257,129},{385... | collective-permute-start | bytes 1179656 | tf_op jit(solution)/shard_map/ppermute | solution.py:36
  225.2 27.3 %collective-permute-start.12 = (f32[96,1024]{1,0:T(8,128)S(1)}, f32[96,1024]{1,0:T(8,128)}, u32[]{:S(2)}, u32[]{:S(2)}) collective-permute-start(f32[96,1024]{1,0:T(8,128)S(1)} %get-tuple-element.31), channel_id=1, source_target_pairs={{0,256},{128,384},{256,0},{384,128},{1,257},{129,385},{257,1},{385... | collective-permute-start | bytes 1179656 | tf_op jit(solution)/shard_map/ppermute | solution.py:36
  230.6 15.1 %all-to-all-start.6 = ((f32[16,1,512]{2,1,0:T(1,128)}), f32[16,1,512]{2,1,0:T(1,128)S(1)}, u32[]{:S(2)}, u32[]{:S(2)}) async-start(f32[16,1,512]{2,1,0:T(1,128)} %reshape.307), calls=%async_computation.6 | async-start | bytes 65536 | tf_op jit(solution)/shard_map/all_to_all | solution.py:19
  246.7 11.7 %all-to-all-start.7 = ((f32[8,1,6144]{2,1,0:T(1,128)}), f32[8,1,6144]{2,1,0:T(1,128)S(1)}, u32[]{:S(2)}, u32[]{:S(2)}) async-start(f32[8,1,6144]{2,1,0:T(1,128)} %broadcast_in_dim.180), calls=%async_computation.7 | async-start | bytes 393216 | tf_op jit(solution)/shard_map/all_to_all | solution.py:19
  253.6 5.6 %copy-start.1 = (f32[96,4096]{1,0:T(8,128)}, f32[96,4096]{1,0:T(8,128)S(1)}, u32[]{:S(2)}) copy-start(f32[96,4096]{1,0:T(8,128)S(1)} %constant_dynamic-update-slice_fusion.2) | copy-start | bytes 4718596

commit v14 on v11

--- a/solution.py
+++ b/solution.py
@@ -51,15 +51,15 @@
     packed = jnp.concatenate([row.transpose(1, 0, 2).reshape(16, wide), notes], axis=1).reshape(1, 16, 1, wide + META)
     packed = jnp.broadcast_to(packed, (4, 16, 1, wide + META)).reshape(64, 1, wide + META)
 
-    def cut(array, s):
-        return lax.dynamic_slice(array, (0, (x + s) % 4 * quarter), (depth, quarter))
+    def cut(s):
+        return lax.dynamic_slice(weight, (0, (x + s) % 4 * quarter), (depth, quarter))
 
-    packed, weight = lax.optimization_barrier((packed, weight))
-    pieces = [cut(weight, 0), *(shift_x(cut(weight, s), s) for s in range(1, 4))]
+    pieces = [cut(0), *(shift_x(cut(s), s) for s in range(1, 4))]
     mine = swap(packed, ("x", *Z)).reshape(64, wide + META)
+    mine, pieces[0] = lax.optimization_barrier((mine, pieces[0]))
 
     slots = spread(mine, "y", 4).reshape(256, wide + META)
-    slots, pieces[3] = lax.optimization_barrier((slots, pieces[3]))
+    _, pieces[3] = lax.optimization_barrier((slots, pieces[3]))
     slots_other = lax.ppermute(slots, "c", [(0, 1), (1, 0)])
 
     all_notes = slots[:, wide : wide + 10].astype(jnp.int32)
@@ -97,8 +97,9 @@
         head = lax.dynamic_update_slice(head, piece[None], ((x - s) % 4, 0, 0))
     head = lax.optimization_barrier(head.reshape(wide, quarter))
 
-    partial = dot(hidden, head)
-    block = partial[:64] + shift_z(partial[64:128], 1) + shift_z(partial[192:], -1) + shift_far(partial[128:192])
+    leave = dot(hidden[64:], head)
+    stay = lax.optimization_barrier(dot(hidden[:64], head))
+    block = stay + shift_z(leave[:64], 1) + shift_z(leave[128:], -1) + shift_far(leave[64:128])
     logits = jnp.sum(swap(block.reshape(4, 16, quarter), "h"), axis=0)
 
     row_labels = lax.dynamic_slice(labels, (h * 16,), (16,))

time: 218 us -> 215 us (0.986)
  waiting for transfers between devices: 78.2 us -> 72.6 us
  starting transfers between devices: 107 us -> 111 us
    all_to_all x8, waiting for transfers between devices: 55.8 us -> 50.5 us  [swap(): return lax.all_to_all(blocks, axes, split_axis=0, concat_axis=0, tiled=True)]
    ppermute x4, waiting for transfers between devices: 14 us -> 9.51 us  [shift_z(): return lax.ppermute(block, Z, [(i, (i + step) % 16) for i in range(16)])]
    ppermute x2, waiting for transfers between devices: 2.88 us -> 6.8 us  [shift_far(): return lax.ppermute(block, ('h', 'l', 'c'), pairs)]
    all_to_all x8, starting transfers between devices: 59.4 us -> 63.1 us  [swap(): return lax.all_to_all(blocks, axes, split_axis=0, concat_axis=0, tiled=True)]
    dynamic_update_slice x4, local copies, waits for them, and re-layouts: 4.11 us -> 1.13 us  [on_device(): head = lax.dynamic_update_slice(head, piece[None], ((x - s) % 4, 0, 0))]
    ppermute x2, starting transfers between devices: 7.75 us -> 5.53 us  [shift_far(): return lax.ppermute(block, ('h', 'l', 'c'), pairs)]
    dot_general x6 -> x7, matrix products: 6.95 us -> 7.55 us  [dot(): lax.dot_general(a, b, dims, precision=precision, preferred_element_type=j...]
  transfers between devices with their start and end apart: 21 -> 21, of which waited for: 14 -> 15; matrix products, arithmetic and copies ran while one was open for 9% -> 8% of each run, Pallas kernels for 0% -> 0%
where the time goes in v14:
time: 215 us; the launch traced here: 214 us
  starting transfers between devices  111 us (52%)
  waiting for transfers between devices  72.6 us (34%)
  local copies, waits for them, and re-layouts  16.7 us (8%)
  matrix products  7.55 us (4%)
  other arithmetic  3.6 us (2%)
  between operations  2.57 us (1%)
    all_to_all x8, starting transfers between devices, swap(): return lax.all_to_all(blocks, axes, split_axis=0, concat_axis=0, tiled=True)  63.1 us
    all_to_all x8, waiting for transfers between devices, swap(): return lax.all_to_all(blocks, axes, split_axis=0, concat_axis=0, tiled=True)  50.5 us
    ppermute x6, starting transfers between devices, shift_x(): return lax.ppermute(block, 'x', [(i, (i + step) % 4) for i in range(4)])  20.6 us
    ppermute x4, starting transfers between devices, shift_z(): return lax.ppermute(block, Z, [(i, (i + step) % 16) for i in range(16)])  14.9 us
    ppermute x4, waiting for transfers between devices, shift_z(): return lax.ppermute(block, Z, [(i, (i + step) % 16) for i in range(16)])  9.51 us
    dot_general x7, matrix products, dot(): lax.dot_general(a, b, dims, precision=precision, preferred_element_type=j...  7.55 us
    ppermute x2, waiting for transfers between devices, shift_far(): return lax.ppermute(block, ('h', 'l', 'c'), pairs)  6.8 us
    ppermute x1, starting transfers between devices, on_device(): slots_other = lax.ppermute(slots, 'c', [(0, 1), (1, 0)])  6.47 us
  transfers between devices with their start and end apart: 21, of which 15 were waited for; matrix products, arithmetic and copies ran while one was open for 8% of the time, Pallas kernels for 0%

profile of v14, /device:TPU:1, one launch (start us, length us, event | category | flops | bytes accessed | tf_op | source)
XLA Modules:
  0.0 213.5 jit_solution(11445149945576561601)
XLA Ops:
  4.7 19.1 %all-to-all-start = ((f32[64,1,512]{2,1,0:T(1,128)}), f32[64,1,512]{2,1,0:T(1,128)S(1)}, u32[]{:S(2)}, u32[]{:S(2)}) async-start(f32[64,1,512]{2,1,0:T(1,128)} %copy.21), calls=%async_computation | async-start | bytes 262144 | tf_op jit(solution)/shard_map/all_to_all | solution.py:15
  23.9 2.4 %constant_dynamic-slice_fusion = (f32[96,1024]{1,0:T(8,128)}, f32[96,1024]{1,0:T(8,128)}, f32[96,1024]{1,0:T(8,128)S(1)}, f32[96,1024]{1,0:T(8,128)}) fusion(f32[96,4096]{1,0:T(8,128)} %param.6, s32[]{:T(128)S(6)} %select_n.294, s32[]{:T(128)S(6)} %select_n.286, s32[]{:T(128)S(6)} %select_n.264, s32[]{:T(128)S(6)} %select_n.290), kind=kLoop, calls=%fused_computation.64 | loop fusion | bytes 3145744 | tf_op jit(solution)/shard_map/dynamic_slice | solution.py:55
  26.3 2.9 %collective-permute-start.1 = (f32[96,1024]{1,0:T(8,128)}, f32[96,1024]{1,0:T(8,128)}, u32[]{:S(2)}, u32[]{:S(2)}) collective-permute-start(f32[96,1024]{1,0:T(8,128)} %get-tuple-element.25), channel_id=1, source_target_pairs={{0,128},{128,256},{256,384},{384,0},{1,129},{129,257},{257,385},{3... | collective-permute-start | bytes 1179656 | tf_op jit(solution)/shard_map/ppermute | solution.py:32
  29.2 4.5 %collective-permute-start.2 = (f32[96,1024]{1,0:T(8,128)}, f32[96,1024]{1,0:T(8,128)S(1)}, u32[]{:S(2)}, u32[]{:S(2)}) collective-permute-start(f32[96,1024]{1,0:T(8,128)} %get-tuple-element.27), channel_id=1, source_target_pairs={{0,256},{128,384},{256,0},{384,128},{1,257},{129,385},{257,1},{385... | collective-permute-start | bytes 1179656 | tf_op jit(solution)/shard_map/ppermute | solution.py:32
  33.7 3.0 %collective-permute-start.3 = (f32[96,1024]{1,0:T(8,128)}, f32[96,1024]{1,0:T(8,128)S(1)}, u32[]{:S(2)}, u32[]{:S(2)}) collective-permute-start(f32[96,1024]{1,0:T(8,128)} %get-tuple-element.24), channel_id=1, source_target_pairs={{0,384},{128,0},{256,128},{384,256},{1,385},{129,1},{257,129},{385... | collective-permute-start | bytes 1179656 | tf_op jit(solution)/shard_map/ppermute | solution.py:32
  38.6 4.2 %all-to-all-start.1 = ((f32[4,64,512]{2,1,0:T(8,128)}), f32[4,64,512]{2,1,0:T(8,128)S(1)}, u32[]{:S(2)}, u32[]{:S(2)}) async-start(f32[4,64,512]{2,1,0:T(8,128)} %broadcast_in_dim.153), calls=%async_computation.1 | async-start | bytes 1048576 | tf_op jit(solution)/shard_map/all_to_all | solution.py:15
  44.1 5.2 %collective-permute-done.2 = f32[96,1024]{1,0:T(8,128)S(1)} collective-permute-done((f32[96,1024]{1,0:T(8,128)}, f32[96,1024]{1,0:T(8,128)S(1)}, u32[]{:S(2)}, u32[]{:S(2)}) %collective-permute-start.2) | collective-permute-done | bytes 393248 | tf_op jit(solution)/shard_map/ppermute | solution.py:32
  50.0 6.5 %collective-permute-start = (f32[256,512]{1,0:T(8,128)S(1)}, f32[256,512]{1,0:T(8,128)S(1)}, u32[]{:S(2)}, u32[]{:S(2)}) collective-permute-start(f32[256,512]{1,0:T(8,128)S(1)} %bitcast.54), channel_id=1, source_target_pairs={{0,1},{1,0},{2,3},{3,2},{4,5},{5,4},{6,7},{7,6},{8,9},{9,8},{10,11... | collective-permute-start | bytes 1572872 | tf_op jit(solution)/shard_map/ppermute | solution.py:63
  60.0 3.2 %collective-permute-start.6 = (f32[64,1024]{1,0:T(8,128)S(1)}, f32[64,1024]{1,0:T(8,128)S(1)}, u32[]{:S(2)}, u32[]{:S(2)}) collective-permute-start(f32[64,1024]{1,0:T(8,128)S(1)} %get-tuple-element.29), channel_id=1, source_target_pairs={{0,16},{1,113},{8,24},{9,121},{16,32},{17,1},{24,40},{25,9},{32,48... | collective-permute-start | bytes 786440 | tf_op jit(solution)/shard_map/ppermute | solution.py:28
  63.2 2.9 %collective-permute-start.5 = (f32[64,1024]{1,0:T(8,128)S(1)}, f32[64,1024]{1,0:T(8,128)S(1)}, u32[]{:S(2)}, u32[]{:S(2)}) collective-permute-start(f32[64,1024]{1,0:T(8,128)S(1)} %get-tuple-element.30), channel_id=1, source_target_pairs={{0,120},{8,0},{16,8},{24,16},{32,24},{40,32},{48,40},{56,48},{64,5... | collective-permute-start | bytes 786440 | tf_op jit(solution)/shard_map/ppermute | solution.py:23
  66.1 2.4 %collective-permute-start.4 = (f32[64,1024]{1,0:T(8,128)S(1)}, f32[64,1024]{1,0:T(8,128)S(1)}, u32[]{:S(2)}, u32[]{:S(2)}) collective-permute-start(f32[64,1024]{1,0:T(8,128)S(1)} %get-tuple-element.28), channel_id=1, source_target_pairs={{0,8},{8,16},{16,24},{24,32},{32,40},{40,48},{48,56},{56,64},{64,7... | collective-permute-start | bytes 786440 | tf_op jit(solution)/shard_map/ppermute | solution.py:23
  69.5 2.9 %collective-permute-done.6 = f32[64,1024]{1,0:T(8,128)S(1)} collective-permute-done((f32[64,1024]{1,0:T(8,128)S(1)}, f32[64,1024]{1,0:T(8,128)S(1)}, u32[]{:S(2)}, u32[]{:S(2)}) %collective-permute-start.6) | collective-permute-done | bytes 262176 | tf_op jit(solution)/shard_map/ppermute | solution.py:28
  72.4 3.9 %collective-permute-done.5 = f32[64,1024]{1,0:T(8,128)S(1)} collective-permute-done((f32[64,1024]{1,0:T(8,128)S(1)}, f32[64,1024]{1,0:T(8,128)S(1)}, u32[]{:S(2)}, u32[]{:S(2)}) %collective-permute-start.5) | collective-permute-done | bytes 262176 | tf_op jit(solution)/shard_map/ppermute | solution.py:23
  77.4 8.2 %all-to-all-start.2 = ((f32[4,16,1024]{2,1,0:T(8,128)}), f32[4,16,1024]{2,1,0:T(8,128)S(1)}, u32[]{:S(2)}, u32[]{:S(2)}) async-start(f32[4,16,1024]{2,1,0:T(8,128)} %bitcast.8), calls=%async_computation.2 | async-start | bytes 524288 | tf_op jit(solution)/shard_map/all_to_all | solution.py:15
  86.3 12.5 %all-to-all-done.2 = f32[4,16,1024]{2,1,0:T(8,128)S(1)} async-done(((f32[4,16,1024]{2,1,0:T(8,128)}), f32[4,16,1024]{2,1,0:T(8,128)S(1)}, u32[]{:S(2)}, u32[]{:S(2)}) %all-to-all-start.2) | async-done | bytes 262176 | tf_op jit(solution)/shard_map/all_to_all | solution.py:15
  99.8 12.4 %all-to-all-start.3 = ((f32[32,3,16]{2,1,0:T(4,128)}), f32[32,3,16]{2,1,0:T(4,128)S(1)}, u32[]{:S(2)}, u32[]{:S(2)}) async-start(f32[32,3,16]{2,1,0:T(4,128)} %broadcast_in_dim.171), calls=%async_computation.3 | async-start | bytes 131072 | tf_op jit(solution)/shard_map/all_to_all | solution.py:15
  112.2 7.4 %all-to-all-done.3 = f32[32,3,16]{2,1,0:T(4,128)S(1)} async-done(((f32[32,3,16]{2,1,0:T(4,128)}), f32[32,3,16]{2,1,0:T(4,128)S(1)}, u32[]{:S(2)}, u32[]{:S(2)}) %all-to-all-start.3) | async-done | bytes 6176 | tf_op jit(solution)/shard_map/all_to_all | solution.py:15
  120.5 3.8 %all-to-all-start.4 = ((f32[4,16,1024]{2,1,0:T(8,128)}), f32[4,16,1024]{2,1,0:T(8,128)S(1)}, u32[]{:S(2)}, u32[]{:S(2)}) async-start(f32[4,16,1024]{2,1,0:T(8,128)} %broadcast_in_dim.172), calls=%async_computation.4 | async-start | bytes 524288 | tf_op jit(solution)/shard_map/all_to_all | solution.py:15
  124.5 15.8 %all-to-all-done.4 = f32[4,16,1024]{2,1,0:T(8,128)S(1)} async-done(((f32[4,16,1024]{2,1,0:T(8,128)}), f32[4,16,1024]{2,1,0:T(8,128)S(1)}, u32[]{:S(2)}, u32[]{:S(2)}) %all-to-all-start.4) | async-done | bytes 262176 | tf_op jit(solution)/shard_map/all_to_all | solution.py:15
  140.2 6.3 %collective-permute-start.9 = (f32[64,1024]{1,0:T(8,128)S(1)}, f32[64,1024]{1,0:T(8,128)S(1)}, u32[]{:S(2)}, u32[]{:S(2)}) collective-permute-start(f32[64,1024]{1,0:T(8,128)S(1)} %bitcast.58), channel_id=1, source_target_pairs={{0,8},{8,16},{16,24},{24,32},{32,40},{40,48},{48,56},{56,64},{64,7... | collective-permute-start | bytes 786440 | tf_op jit(solution)/shard_map/ppermute | solution.py:23
  146.5 2.3 %collective-permute-start.8 = (f32[64,1024]{1,0:T(8,128)S(1)}, f32[64,1024]{1,0:T(8,128)S(1)}, u32[]{:S(2)}, u32[]{:S(2)}) collective-permute-start(f32[64,1024]{1,0:T(8,128)S(1)} %bitcast.59), channel_id=1, source_target_pairs={{0,16},{1,113},{8,24},{9,121},{16,32},{17,1},{24,40},{25,9},{32,48... | collective-permute-start | bytes 786440 | tf_op jit(solution)/shard_map/ppermute | solution.py:28
  148.8 3.4 %collective-permute-start.7 = (f32[64,1024]{1,0:T(8,128)S(1)}, f32[64,1024]{1,0:T(8,128)S(1)}, u32[]{:S(2)}, u32[]{:S(2)}) collective-permute-start(f32[64,1024]{1,0:T(8,128)S(1)} %bitcast.60), channel_id=1, source_target_pairs={{0,120},{8,0},{16,8},{24,16},{32,24},{40,32},{48,40},{56,48},{64,5... | collective-permute-start | bytes 786440 | tf_op jit(solution)/shard_map/ppermute | solution.py:23
  152.3 3.9 %collective-permute-done.8 = f32[64,1024]{1,0:T(8,128)S(1)} collective-permute-done((f32[64,1024]{1,0:T(8,128)S(1)}, f32[64,1024]{1,0:T(8,128)S(1)}, u32[]{:S(2)}, u32[]{:S(2)}) %collective-permute-start.8) | collective-permute-done | bytes 262176 | tf_op jit(solution)/shard_map/ppermute | solution.py:28
  156.3 5.2 %collective-permute-done.7 = f32[64,1024]{1,0:T(8,128)S(1)} collective-permute-done((f32[64,1024]{1,0:T(8,128)S(1)}, f32[64,1024]{1,0:T(8,128)S(1)}, u32[]{:S(2)}, u32[]{:S(2)}) %collective-permute-start.7) | collective-permute-done | bytes 262176 | tf_op jit(solution)/shard_map/ppermute | solution.py:23
  163.9 4.2 %all-to-all-start.5 = ((f32[32,16,384]{2,1,0:T(8,128)}), f32[32,16,384]{2,1,0:T(8,128)S(1)}, u32[]{:S(2)}, u32[]{:S(2)}) async-start(f32[32,16,384]{2,1,0:T(8,128)} %bitcast.15), calls=%async_computation.5 | async-start | bytes 1572864 | tf_op jit(solution)/shard_map/all_to_all | solution.py:15
  170.9 3.3 %collective-permute-start.10 = (f32[96,1024]{1,0:T(8,128)}, f32[96,1024]{1,0:T(8,128)}, u32[]{:S(2)}, u32[]{:S(2)}) collective-permute-start(f32[96,1024]{1,0:T(8,128)} %get-tuple-element.23), channel_id=1, source_target_pairs={{0,128},{128,256},{256,384},{384,0},{1,129},{129,257},{257,385},{3... | collective-permute-start | bytes 1179656 | tf_op jit(solution)/shard_map/ppermute | solution.py:32
  174.2 3.2 %collective-permute-start.11 = (f32[96,1024]{1,0:T(8,128)S(1)}, f32[96,1024]{1,0:T(8,128)}, u32[]{:S(2)}, u32[]{:S(2)}) collective-permute-start(f32[96,1024]{1,0:T(8,128)S(1)} %get-tuple-element.22), channel_id=1, source_target_pairs={{0,384},{128,0},{256,128},{384,256},{1,385},{129,1},{257,129},{385... | collective-permute-start | bytes 1179656 | tf_op jit(solution)/shard_map/ppermute | solution.py:32
  177.9 3.6 %collective-permute-start.12 = (f32[96,1024]{1,0:T(8,128)S(1)}, f32[96,1024]{1,0:T(8,128)}, u32[]{:S(2)}, u32[]{:S(2)}) collective-permute-start(f32[96,1024]{1,0:T(8,128)S(1)} %get-tuple-element.21), channel_id=1, source_target_pairs={{0,256},{128,384},{256,0},{384,128},{1,257},{129,385},{257,1},{385... | collective-permute-start | bytes 1179656 | tf_op jit(solution)/shard_map/ppermute | solution.py:32
  183.3 5.3 %all-to-all-start.6 = ((f32[16,1,512]{2,1,0:T(1,128)}), f32[16,1,512]{2,1,0:T(1,128)S(1)}, u32[]{:S(2)}, u32[]{:S(2)}) async-start(f32[16,1,512]{2,1,0:T(1,128)} %reshape.307), calls=%async_computation.6 | async-start | bytes 65536 | tf_op jit(solution)/shard_map/all_to_all | solution.py:15
  192.3 7.9 %all-to-all-done.6 = f32[16,1,512]{2,1,0:T(1,128)S(1)} async-done(((f32[16,1,512]{2,1,0:T(1,128)}), f32[16,1,512]{2,1,0:T(1,128)S(1)}, u32[]{:S(2)}, u32[]{:S(2)}) %all-to-all-start.6) | async-done | bytes 32800 | tf_op jit(solution)/shard_map/all_to_all | solution.py:15
  201.2 5.8 %all-to-all-start.7 = ((f32[8,1,6144]{2,1,0:T(1,128)}), f32[8,1,6144]{2,1,0:T(1,128)S(1)}, u32[]{:S(2)}, u32[]{:S(2)}) async-start(f32[8,1,6144]{2,1,0:T(1,128)} %broadcast_in_dim.175), calls=%async_computation.7 | async-start | bytes 393216 | tf_op jit(solution)/shard_map/all_to_all | solution.py:15
  208.5 4.3 %all-to-all-done.7 = f32[8,1,6144]{2,1,0:T(1,128)S(1)} async-done(((f32[8,1,6144]{2,1,0:T(1,128)}), f32[8,1,6144]{2,1,0:T(1,128)S(1)}, u32[]{:S(2)}, u32[]{:S(2)}) %all-to-all-start.7) | async-done | bytes 196640 | tf_op jit(solution)/shard_map/all_to_all | solution.py:15
  (93 shorter events, 29.1 us)
Async XLA Ops:
  0.6 0.9 copy-start
  4.7 33.1 %all-to-all-start = ((f32[64,1,512]{2,1,0:T(1,128)}), f32[64,1,512]{2,1,0:T(1,128)S(1)}, u32[]{:S(2)}, u32[]{:S(2)}) async-start(f32[64,1,512]{2,1,0:T(1,128)} %copy.21), calls=%async_computation | async-start | bytes 262144 | tf_op jit(solution)/shard_map/all_to_all | solution.py:15
  26.3 16.8 %collective-permute-start.1 = (f32[96,1024]{1,0:T(8,128)}, f32[96,1024]{1,0:T(8,128)}, u32[]{:S(2)}, u32[]{:S(2)}) collective-permute-start(f32[96,1024]{1,0:T(8,128)} %get-tuple-element.25), channel_id=1, source_target_pairs={{0,128},{128,256},{256,384},{384,0},{1,129},{129,257},{257,385},{3... | collective-permute-start | bytes 1179656 | tf_op jit(solution)/shard_map/ppermute | solution.py:32
  29.2 20.1 %collective-permute-start.2 = (f32[96,1024]{1,0:T(8,128)}, f32[96,1024]{1,0:T(8,128)S(1)}, u32[]{:S(2)}, u32[]{:S(2)}) collective-permute-start(f32[96,1024]{1,0:T(8,128)} %get-tuple-element.27), channel_id=1, source_target_pairs={{0,256},{128,384},{256,0},{384,128},{1,257},{129,385},{257,1},{385... | collective-permute-start | bytes 1179656 | tf_op jit(solution)/shard_map/ppermute | solution.py:32
  33.7 23.2 %collective-permute-start.3 = (f32[96,1024]{1,0:T(8,128)}, f32[96,1024]{1,0:T(8,128)S(1)}, u32[]{:S(2)}, u32[]{:S(2)}) collective-permute-start(f32[96,1024]{1,0:T(8,128)} %get-tuple-element.24), channel_id=1, source_target_pairs={{0,384},{128,0},{256,128},{384,256},{1,385},{129,1},{257,129},{385... | collective-permute-start | bytes 1179656 | tf_op jit(solution)/shard_map/ppermute | solution.py:32
  38.6 11.4 %all-to-all-start.1 = ((f32[4,64,512]{2,1,0:T(8,128)}), f32[4,64,512]{2,1,0:T(8,128)S(1)}, u32[]{:S(2)}, u32[]{:S(2)}) async-start(f32[4,64,512]{2,1,0:T(8,128)} %broadcast_in_dim.153), calls=%async_computation.1 | async-start | bytes 1048576 | tf_op jit(solution)/shard_map/all_to_all | solution.py:15
  50.0 8.0 %collective-permute-start = (f32[256,512]{1,0:T(8,128)S(1)}, f32[256,512]{1,0:T(8,128)S(1)}, u32[]{:S(2)}, u32[]{:S(2)}) collective-permute-start(f32[256,512]{1,0:T(8,128)S(1)} %bitcast.54), channel_id=1, source_target_pairs={{0,1},{1,0},{2,3},{3,2},{4,5},{5,4},{6,7},{7,6},{8,9},{9,8},{10,11... | collective-permute-start | bytes 1572872 | tf_op jit(solution)/shard_map/ppermute | solution.py:63
  60.0 12.4 %collective-permute-start.6 = (f32[64,1024]{1,0:T(8,128)S(1)}, f32[64,1024]{1,0:T(8,128)S(1)}, u32[]{:S(2)}, u32[]{:S(2)}) collective-permute-start(f32[64,1024]{1,0:T(8,128)S(1)} %get-tuple-element.29), channel_id=1, source_target_pairs={{0,16},{1,113},{8,24},{9,121},{16,32},{17,1},{24,40},{25,9},{32,48... | collective-permute-start | bytes 786440 | tf_op jit(solution)/shard_map/ppermute | solution.py:28
  63.2 13.1 %collective-permute-start.5 = (f32[64,1024]{1,0:T(8,128)S(1)}, f32[64,1024]{1,0:T(8,128)S(1)}, u32[]{:S(2)}, u32[]{:S(2)}) collective-permute-start(f32[64,1024]{1,0:T(8,128)S(1)} %get-tuple-element.30), channel_id=1, source_target_pairs={{0,120},{8,0},{16,8},{24,16},{32,24},{40,32},{48,40},{56,48},{64,5... | collective-permute-start | bytes 786440 | tf_op jit(solution)/shard_map/ppermute | solution.py:23
  66.1 10.6 %collective-permute-start.4 = (f32[64,1024]{1,0:T(8,128)S(1)}, f32[64,1024]{1,0:T(8,128)S(1)}, u32[]{:S(2)}, u32[]{:S(2)}) collective-permute-start(f32[64,1024]{1,0:T(8,128)S(1)} %get-tuple-element.28), channel_id=1, source_target_pairs={{0,8},{8,16},{16,24},{24,32},{32,40},{40,48},{48,56},{56,64},{64,7... | collective-permute-start | bytes 786440 | tf_op jit(solution)/shard_map/ppermute | solution.py:23
  77.4 21.3 %all-to-all-start.2 = ((f32[4,16,1024]{2,1,0:T(8,128)}), f32[4,16,1024]{2,1,0:T(8,128)S(1)}, u32[]{:S(2)}, u32[]{:S(2)}) async-start(f32[4,16,1024]{2,1,0:T(8,128)} %bitcast.8), calls=%async_computation.2 | async-start | bytes 524288 | tf_op jit(solution)/shard_map/all_to_all | solution.py:15
  99.8 19.8 %all-to-all-start.3 = ((f32[32,3,16]{2,1,0:T(4,128)}), f32[32,3,16]{2,1,0:T(4,128)S(1)}, u32[]{:S(2)}, u32[]{:S(2)}) async-start(f32[32,3,16]{2,1,0:T(4,128)} %broadcast_in_dim.171), calls=%async_computation.3 | async-start | bytes 131072 | tf_op jit(solution)/shard_map/all_to_all | solution.py:15
  120.5 19.7 %all-to-all-start.4 = ((f32[4,16,1024]{2,1,0:T(8,128)}), f32[4,16,1024]{2,1,0:T(8,128)S(1)}, u32[]{:S(2)}, u32[]{:S(2)}) async-start(f32[4,16,1024]{2,1,0:T(8,128)} %broadcast_in_dim.172), calls=%async_computation.4 | async-start | bytes 524288 | tf_op jit(solution)/shard_map/all_to_all | solution.py:15
  140.2 12.1 %collective-permute-start.9 = (f32[64,1024]{1,0:T(8,128)S(1)}, f32[64,1024]{1,0:T(8,128)S(1)}, u32[]{:S(2)}, u32[]{:S(2)}) collective-permute-start(f32[64,1024]{1,0:T(8,128)S(1)} %bitcast.58), channel_id=1, source_target_pairs={{0,8},{8,16},{16,24},{24,32},{32,40},{40,48},{48,56},{56,64},{64,7... | collective-permute-start | bytes 786440 | tf_op jit(solution)/shard_map/ppermute | solution.py:23
  146.5 9.8 %collective-permute-start.8 = (f32[64,1024]{1,0:T(8,128)S(1)}, f32[64,1024]{1,0:T(8,128)S(1)}, u32[]{:S(2)}, u32[]{:S(2)}) collective-permute-start(f32[64,1024]{1,0:T(8,128)S(1)} %bitcast.59), channel_id=1, source_target_pairs={{0,16},{1,113},{8,24},{9,121},{16,32},{17,1},{24,40},{25,9},{32,48... | collective-permute-start | bytes 786440 | tf_op jit(solution)/shard_map/ppermute | solution.py:28
  148.8 12.7 %collective-permute-start.7 = (f32[64,1024]{1,0:T(8,128)S(1)}, f32[64,1024]{1,0:T(8,128)S(1)}, u32[]{:S(2)}, u32[]{:S(2)}) collective-permute-start(f32[64,1024]{1,0:T(8,128)S(1)} %bitcast.60), channel_id=1, source_target_pairs={{0,120},{8,0},{16,8},{24,16},{32,24},{40,32},{48,40},{56,48},{64,5... | collective-permute-start | bytes 786440 | tf_op jit(solution)/shard_map/ppermute | solution.py:23
  156.3 7.6 %copy-start.2 = (f32[64,1024]{1,0:T(8,128)}, f32[64,1024]{1,0:T(8,128)S(1)}, u32[]{:S(2)}) copy-start(f32[64,1024]{1,0:T(8,128)S(1)} %collective-permute-done.8) | copy-start | bytes 786436
  161.5 2.4 %copy-start.3 = (f32[64,1024]{1,0:T(8,128)}, f32[64,1024]{1,0:T(8,128)S(1)}, u32[]{:S(2)}) copy-start(f32[64,1024]{1,0:T(8,128)S(1)} %collective-permute-done.7) | copy-start | bytes 786436
  163.9 18.7 %all-to-all-start.5 = ((f32[32,16,384]{2,1,0:T(8,128)}), f32[32,16,384]{2,1,0:T(8,128)S(1)}, u32[]{:S(2)}, u32[]{:S(2)}) async-start(f32[32,16,384]{2,1,0:T(8,128)} %bitcast.15), calls=%async_computation.5 | async-start | bytes 1572864 | tf_op jit(solution)/shard_map/all_to_all | solution.py:15
  170.9 19.3 %collective-permute-start.10 = (f32[96,1024]{1,0:T(8,128)}, f32[96,1024]{1,0:T(8,128)}, u32[]{:S(2)}, u32[]{:S(2)}) collective-permute-start(f32[96,1024]{1,0:T(8,128)} %get-tuple-element.23), channel_id=1, source_target_pairs={{0,128},{128,256},{256,384},{384,0},{1,129},{129,257},{257,385},{3... | collective-permute-start | bytes 1179656 | tf_op jit(solution)/shard_map/ppermute | solution.py:32
  174.2 17.0 %collective-permute-start.11 = (f32[96,1024]{1,0:T(8,128)S(1)}, f32[96,1024]{1,0:T(8,128)}, u32[]{:S(2)}, u32[]{:S(2)}) collective-permute-start(f32[96,1024]{1,0:T(8,128)S(1)} %get-tuple-element.22), channel_id=1, source_target_pairs={{0,384},{128,0},{256,128},{384,256},{1,385},{129,1},{257,129},{385... | collective-permute-start | bytes 1179656 | tf_op jit(solution)/shard_map/ppermute | solution.py:32
  177.9 29.0 %collective-permute-start.12 = (f32[96,1024]{1,0:T(8,128)S(1)}, f32[96,1024]{1,0:T(8,128)}, u32[]{:S(2)}, u32[]{:S(2)}) collective-permute-start(f32[96,1024]{1,0:T(8,128)S(1)} %get-tuple-element.21), channel_id=1, source_target_pairs={{0,256},{128,384},{256,0},{384,128},{1,257},{129,385},{257,1},{385... | collective-permute-start | bytes 1179656 | tf_op jit(solution)/shard_map/ppermute | solution.py:32
  183.3 16.9 %all-to-all-start.6 = ((f32[16,1,512]{2,1,0:T(1,128)}), f32[16,1,512]{2,1,0:T(1,128)S(1)}, u32[]{:S(2)}, u32[]{:S(2)}) async-start(f32[16,1,512]{2,1,0:T(1,128)} %reshape.307), calls=%async_computation.6 | async-start | bytes 65536 | tf_op jit(solution)/shard_map/all_to_all | solution.py:15
  201.2 11.6 %all-to-all-start.7 = ((f32[8,1,6144]{2,1,0:T(1,128)}), f32[8,1,6144]{2,1,0:T(1,128)S(1)}, u32[]{:S(2)}, u32[]{:S(2)}) async-start(f32[8,1,6144]{2,1,0:T(1,128)} %broadcast_in_dim.175), calls=%async_computation.7 | async-start | bytes 393216 | tf_op jit(solution)/shard_map/all_to_all | solution.py:15
  207.9 5.6 %copy-start.1 = (f32[96,4096]{1,0:T(8,128)}, f32[96,4096]{1,0:T(8,128)S(1)}, u32[]{:S(2)}) copy-start(f32[96,4096]{1,0:T(8,128)S(1)} %constant_dynamic-update-slice_fusion) | copy-start | bytes 4718596

commit v15 on v14

--- a/solution.py
+++ b/solution.py
@@ -23,8 +23,9 @@
     return lax.ppermute(block, Z, [(i, (i + step) % 16) for i in range(16)])
 
 
-def shift_far(block):
-    pairs = [(2 * i + c, 2 * ((i + 2 - 4 * c) % 16) + c) for i in range(16) for c in range(2)]
+def shift_far(block, sign):
+    step = [2 * sign, -2 * sign]
+    pairs = [(2 * i + c, 2 * ((i + step[c]) % 16) + c) for i in range(16) for c in range(2)]
     return lax.ppermute(block, ("h", "l", "c"), pairs)
 
 
@@ -69,12 +70,19 @@
     def starts_of(source):
         return jnp.sum(jnp.where(sources[None, :] < source[:, None], source_length[None, :], 0), axis=1)
 
+    def placed(rank):
+        turn = (rank // 64 - l) % 4
+        partner = h * 4 + l + jnp.where(turn == 3, -1, jnp.where((turn == 2) & (c == 1), -2, turn))
+        group = (rank // 16 - partner % 16 // 4) % 4
+        group = jnp.where((group == 1) | (group == 2), 3 - group, group)
+        return turn * 64 + group * 16 + rank % 16
+
     rows = jnp.arange(256, dtype=jnp.int32)
     starts = starts_of(rows % 64)
 
     def chosen(core):
         slot_j = rows // 64 * 2 + core
-        rank = jnp.where(slot_j < all_notes[:, 8], (starts + slot_j - 64 * l) % 256, -1)
+        rank = jnp.where(slot_j < all_notes[:, 8], placed(starts + slot_j), -1)
         target = jnp.sum(jnp.where(jnp.arange(10)[None, :] == slot_j[:, None], all_notes, 0), axis=1)
         select = rank[None, :] == rows[:, None]
         return select.astype(jnp.float32), jnp.sum(jnp.where(select, target[None, :], 0), axis=1)
@@ -89,7 +97,7 @@
     owned = source_owner[None, :] == (ids // 128 * 16 + ids % 16)[:, None]
     sent_start = jnp.sum(jnp.where(owned, starts_of(sources)[None, :], 0), axis=1)
     sent_length = jnp.sum(jnp.where(owned, source_length[None, :], 0), axis=1)
-    sent_rank = jnp.where(slot_j < sent_length, (sent_start + slot_j - 64 * l) % 256, -1)
+    sent_rank = jnp.where(slot_j < sent_length, placed(sent_start + slot_j), -1)
     deliver = (sent_rank[:, None] == rows[None, :]).astype(jnp.float32)
 
     head = jnp.zeros((4, depth, quarter), jnp.float32)
@@ -99,10 +107,10 @@
 
     leave = dot(hidden[64:], head)
     stay = lax.optimization_barrier(dot(hidden[:64], head))
-    block = stay + shift_z(leave[:64], 1) + shift_z(leave[128:], -1) + shift_far(leave[64:128])
-    logits = jnp.sum(swap(block.reshape(4, 16, quarter), "h"), axis=0)
+    block = stay + shift_z(leave[:64], 1) + shift_z(leave[128:], -1) + shift_far(leave[64:128], 1)
+    logits = block[:16] + shift_z(block[32:48], 4) + shift_z(block[48:], -4) + shift_z(block[16:32], 8)
 
-    row_labels = lax.dynamic_slice(labels, (h * 16,), (16,))
+    row_labels = labels[:16]
     column = jnp.arange(quarter, dtype=jnp.int32) + j * columns + x * quarter
     onehot = (column[None, :] == row_labels[:, None]).astype(jnp.float32)
     peak = jnp.max(logits, axis=1)
@@ -115,8 +123,8 @@
     scale = jnp.exp(peak - row_peak) / exp_total
     grad = onehot - shifted * scale[:, None]
 
-    own = spread(grad, "h", 4).reshape(64, quarter)
-    grads = jnp.concatenate([own, shift_z(own, -1), shift_far(own), shift_z(own, 1)], axis=0)
+    own = jnp.concatenate([grad, shift_z(grad, 8), shift_z(grad, -4), shift_z(grad, 4)], axis=0)
+    grads = jnp.concatenate([own, shift_z(own, -1), shift_far(own, -1), shift_z(own, 1)], axis=0)
 
     grad_rows = dot(grads, head, (1, 1), GRAD)
     leaving = dot(deliver, grad_rows, (1, 0), GRAD).reshape(32, 16, wide)

time: 215 us -> 215 us (level)
  starting transfers between devices: 111 us -> 125 us
  waiting for transfers between devices: 72.6 us -> 61.8 us
  local copies, waits for them, and re-layouts: 16.7 us -> 14.2 us
    ppermute x4 -> x10, starting transfers between devices: 14.9 us -> 46 us  [shift_z(): return lax.ppermute(block, Z, [(i, (i + step) % 16) for i in range(16)])]
    all_to_all x8 -> x6, waiting for transfers between devices: 50.5 us -> 24.8 us  [swap(): return lax.all_to_all(blocks, axes, split_axis=0, concat_axis=0, tiled=True)]
    all_to_all x8 -> x6, starting transfers between devices: 63.1 us -> 46.6 us  [swap(): return lax.all_to_all(blocks, axes, split_axis=0, concat_axis=0, tiled=True)]
    ppermute x4 -> x10, waiting for transfers between devices: 9.51 us -> 23.7 us  [shift_z(): return lax.ppermute(block, Z, [(i, (i + step) % 16) for i in range(16)])]
  transfers between devices with their start and end apart: 21 -> 25, of which waited for: 15 -> 16; matrix products, arithmetic and copies ran while one was open for 8% -> 7% of each run, Pallas kernels for 0% -> 0%
where the time goes in v15:
time: 215 us; the launch traced here: 214 us
  starting transfers between devices  125 us (58%)
  waiting for transfers between devices  61.8 us (29%)
  local copies, waits for them, and re-layouts  14.2 us (7%)
  matrix products  6.53 us (3%)
  other arithmetic  4.12 us (2%)
  between operations  2.72 us (1%)
    all_to_all x6, starting transfers between devices, swap(): return lax.all_to_all(blocks, axes, split_axis=0, concat_axis=0, tiled=True)  46.6 us
    ppermute x10, starting transfers between devices, shift_z(): return lax.ppermute(block, Z, [(i, (i + step) % 16) for i in range(16)])  46 us
    all_to_all x6, waiting for transfers between devices, swap(): return lax.all_to_all(blocks, axes, split_axis=0, concat_axis=0, tiled=True)  24.8 us
    ppermute x10, waiting for transfers between devices, shift_z(): return lax.ppermute(block, Z, [(i, (i + step) % 16) for i in range(16)])  23.7 us
    ppermute x6, starting transfers between devices, shift_x(): return lax.ppermute(block, 'x', [(i, (i + step) % 4) for i in range(4)])  20.6 us
    ppermute x2, waiting for transfers between devices, shift_far(): return lax.ppermute(block, ('h', 'l', 'c'), pairs)  8.13 us
    dot_general x7, matrix products, dot(): lax.dot_general(a, b, dims, precision=precision, preferred_element_type=j...  6.53 us
    ppermute x1, starting transfers between devices, on_device(): slots_other = lax.ppermute(slots, 'c', [(0, 1), (1, 0)])  6.47 us
  transfers between devices with their start and end apart: 25, of which 16 were waited for; matrix products, arithmetic and copies ran while one was open for 7% of the time, Pallas kernels for 0%

profile of v15, /device:TPU:1, one launch (start us, length us, event | category | flops | bytes accessed | tf_op | source)
XLA Modules:
  0.0 214.2 jit_solution(3611687980633657194)
XLA Ops:
  4.7 19.1 %all-to-all-start = ((f32[64,1,512]{2,1,0:T(1,128)}), f32[64,1,512]{2,1,0:T(1,128)S(1)}, u32[]{:S(2)}, u32[]{:S(2)}) async-start(f32[64,1,512]{2,1,0:T(1,128)} %copy.21), calls=%async_computation | async-start | bytes 262144 | tf_op jit(solution)/shard_map/all_to_all | solution.py:15
  26.3 2.9 %collective-permute-start.1 = (f32[96,1024]{1,0:T(8,128)}, f32[96,1024]{1,0:T(8,128)}, u32[]{:S(2)}, u32[]{:S(2)}) collective-permute-start(f32[96,1024]{1,0:T(8,128)} %get-tuple-element.29), channel_id=1, source_target_pairs={{0,128},{128,256},{256,384},{384,0},{1,129},{129,257},{257,385},{3... | collective-permute-start | bytes 1179656 | tf_op jit(solution)/shard_map/ppermute | solution.py:33
  29.2 4.5 %collective-permute-start.2 = (f32[96,1024]{1,0:T(8,128)}, f32[96,1024]{1,0:T(8,128)S(1)}, u32[]{:S(2)}, u32[]{:S(2)}) collective-permute-start(f32[96,1024]{1,0:T(8,128)} %get-tuple-element.31), channel_id=1, source_target_pairs={{0,256},{128,384},{256,0},{384,128},{1,257},{129,385},{257,1},{385... | collective-permute-start | bytes 1179656 | tf_op jit(solution)/shard_map/ppermute | solution.py:33
  33.7 3.0 %collective-permute-start.3 = (f32[96,1024]{1,0:T(8,128)}, f32[96,1024]{1,0:T(8,128)S(1)}, u32[]{:S(2)}, u32[]{:S(2)}) collective-permute-start(f32[96,1024]{1,0:T(8,128)} %get-tuple-element.28), channel_id=1, source_target_pairs={{0,384},{128,0},{256,128},{384,256},{1,385},{129,1},{257,129},{385... | collective-permute-start | bytes 1179656 | tf_op jit(solution)/shard_map/ppermute | solution.py:33
  38.6 4.2 %all-to-all-start.1 = ((f32[4,64,512]{2,1,0:T(8,128)}), f32[4,64,512]{2,1,0:T(8,128)S(1)}, u32[]{:S(2)}, u32[]{:S(2)}) async-start(f32[4,64,512]{2,1,0:T(8,128)} %broadcast_in_dim.159), calls=%async_computation.1 | async-start | bytes 1048576 | tf_op jit(solution)/shard_map/all_to_all | solution.py:15
  44.1 5.2 %collective-permute-done.2 = f32[96,1024]{1,0:T(8,128)S(1)} collective-permute-done((f32[96,1024]{1,0:T(8,128)}, f32[96,1024]{1,0:T(8,128)S(1)}, u32[]{:S(2)}, u32[]{:S(2)}) %collective-permute-start.2) | collective-permute-done | bytes 393248 | tf_op jit(solution)/shard_map/ppermute | solution.py:33
  50.0 6.5 %collective-permute-start = (f32[256,512]{1,0:T(8,128)S(1)}, f32[256,512]{1,0:T(8,128)S(1)}, u32[]{:S(2)}, u32[]{:S(2)}) collective-permute-start(f32[256,512]{1,0:T(8,128)S(1)} %bitcast.54), channel_id=1, source_target_pairs={{0,1},{1,0},{2,3},{3,2},{4,5},{5,4},{6,7},{7,6},{8,9},{9,8},{10,11... | collective-permute-start | bytes 1572872 | tf_op jit(solution)/shard_map/ppermute | solution.py:64
  60.0 3.2 %collective-permute-start.6 = (f32[64,1024]{1,0:T(8,128)S(1)}, f32[64,1024]{1,0:T(8,128)S(1)}, u32[]{:S(2)}, u32[]{:S(2)}) collective-permute-start(f32[64,1024]{1,0:T(8,128)S(1)} %get-tuple-element.33), channel_id=1, source_target_pairs={{0,16},{1,113},{8,24},{9,121},{16,32},{17,1},{24,40},{25,9},{32,48... | collective-permute-start | bytes 786440 | tf_op jit(solution)/shard_map/ppermute | solution.py:29
  72.5 3.8 %collective-permute-done.5 = f32[64,1024]{1,0:T(8,128)S(1)} collective-permute-done((f32[64,1024]{1,0:T(8,128)S(1)}, f32[64,1024]{1,0:T(8,128)S(1)}, u32[]{:S(2)}, u32[]{:S(2)}) %collective-permute-start.5) | collective-permute-done | bytes 262176 | tf_op jit(solution)/shard_map/ppermute | solution.py:23
  76.7 9.0 %collective-permute-start.9 = (f32[16,1024]{1,0:T(8,128)S(1)}, f32[16,1024]{1,0:T(8,128)S(1)}, u32[]{:S(2)}, u32[]{:S(2)}) collective-permute-start(f32[16,1024]{1,0:T(8,128)S(1)} %get-tuple-element.36), channel_id=1, source_target_pairs={{0,64},{8,72},{16,80},{24,88},{32,96},{40,104},{48,112},{56,120},{... | collective-permute-start | bytes 196616 | tf_op jit(solution)/shard_map/ppermute | solution.py:23
  85.7 3.3 %collective-permute-start.8 = (f32[16,1024]{1,0:T(8,128)S(1)}, f32[16,1024]{1,0:T(8,128)S(1)}, u32[]{:S(2)}, u32[]{:S(2)}) collective-permute-start(f32[16,1024]{1,0:T(8,128)S(1)} %get-tuple-element.37), channel_id=1, source_target_pairs={{0,96},{8,104},{16,112},{24,120},{32,0},{40,8},{48,16},{56,24},{64... | collective-permute-start | bytes 196616 | tf_op jit(solution)/shard_map/ppermute | solution.py:23
  89.1 5.8 %collective-permute-start.7 = (f32[16,1024]{1,0:T(8,128)S(1)}, f32[16,1024]{1,0:T(8,128)S(1)}, u32[]{:S(2)}, u32[]{:S(2)}) collective-permute-start(f32[16,1024]{1,0:T(8,128)S(1)} %get-tuple-element.35), channel_id=1, source_target_pairs={{0,32},{8,40},{16,48},{24,56},{32,64},{40,72},{48,80},{56,88},{64,... | collective-permute-start | bytes 196616 | tf_op jit(solution)/shard_map/ppermute | solution.py:23
  95.1 5.1 %collective-permute-done.8 = f32[16,1024]{1,0:T(8,128)S(1)} collective-permute-done((f32[16,1024]{1,0:T(8,128)S(1)}, f32[16,1024]{1,0:T(8,128)S(1)}, u32[]{:S(2)}, u32[]{:S(2)}) %collective-permute-start.8) | collective-permute-done | bytes 65568 | tf_op jit(solution)/shard_map/ppermute | solution.py:23
  101.1 8.9 %all-to-all-start.2 = ((f32[32,3,16]{2,1,0:T(4,128)}), f32[32,3,16]{2,1,0:T(4,128)S(1)}, u32[]{:S(2)}, u32[]{:S(2)}) async-start(f32[32,3,16]{2,1,0:T(4,128)} %broadcast_in_dim.179), calls=%async_computation.2 | async-start | bytes 131072 | tf_op jit(solution)/shard_map/all_to_all | solution.py:15
  110.1 7.3 %all-to-all-done.2 = f32[32,3,16]{2,1,0:T(4,128)S(1)} async-done(((f32[32,3,16]{2,1,0:T(4,128)}), f32[32,3,16]{2,1,0:T(4,128)S(1)}, u32[]{:S(2)}, u32[]{:S(2)}) %all-to-all-start.2) | async-done | bytes 6176 | tf_op jit(solution)/shard_map/all_to_all | solution.py:15
  117.6 8.1 %collective-permute-start.10 = (f32[16,1024]{1,0:T(8,128)S(1)}, f32[16,1024]{1,0:T(8,128)S(1)}, u32[]{:S(2)}, u32[]{:S(2)}) collective-permute-start(f32[16,1024]{1,0:T(8,128)S(1)} %get-tuple-element.22), channel_id=1, source_target_pairs={{0,64},{8,72},{16,80},{24,88},{32,96},{40,104},{48,112},{56,120},{... | collective-permute-start | bytes 196616 | tf_op jit(solution)/shard_map/ppermute | solution.py:23
  125.7 3.8 %collective-permute-start.11 = (f32[16,1024]{1,0:T(8,128)S(1)}, f32[16,1024]{1,0:T(8,128)S(1)}, u32[]{:S(2)}, u32[]{:S(2)}) collective-permute-start(f32[16,1024]{1,0:T(8,128)S(1)} %get-tuple-element.22), channel_id=1, source_target_pairs={{0,96},{8,104},{16,112},{24,120},{32,0},{40,8},{48,16},{56,24},{64... | collective-permute-start | bytes 196616 | tf_op jit(solution)/shard_map/ppermute | solution.py:23
  129.5 5.3 %collective-permute-start.12 = (f32[16,1024]{1,0:T(8,128)S(1)}, f32[16,1024]{1,0:T(8,128)S(1)}, u32[]{:S(2)}, u32[]{:S(2)}) collective-permute-start(f32[16,1024]{1,0:T(8,128)S(1)} %get-tuple-element.22), channel_id=1, source_target_pairs={{0,32},{8,40},{16,48},{24,56},{32,64},{40,72},{48,80},{56,88},{64,... | collective-permute-start | bytes 196616 | tf_op jit(solution)/shard_map/ppermute | solution.py:23
  134.9 4.4 %collective-permute-done.11 = f32[16,1024]{1,0:T(8,128)S(1)} collective-permute-done((f32[16,1024]{1,0:T(8,128)S(1)}, f32[16,1024]{1,0:T(8,128)S(1)}, u32[]{:S(2)}, u32[]{:S(2)}) %collective-permute-start.11) | collective-permute-done | bytes 65568 | tf_op jit(solution)/shard_map/ppermute | solution.py:23
  139.4 3.1 %collective-permute-done.12 = f32[16,1024]{1,0:T(8,128)S(1)} collective-permute-done((f32[16,1024]{1,0:T(8,128)S(1)}, f32[16,1024]{1,0:T(8,128)S(1)}, u32[]{:S(2)}, u32[]{:S(2)}) %collective-permute-start.12) | collective-permute-done | bytes 65568 | tf_op jit(solution)/shard_map/ppermute | solution.py:23
  146.3 3.4 %collective-permute-start.15 = (f32[64,1024]{1,0:T(8,128)S(1)}, f32[64,1024]{1,0:T(8,128)S(1)}, u32[]{:S(2)}, u32[]{:S(2)}) collective-permute-start(f32[64,1024]{1,0:T(8,128)S(1)} %pad_maximum_fusion), channel_id=1, source_target_pairs={{0,8},{8,16},{16,24},{24,32},{32,40},{40,48},{48,56},{56,64},{64,7... | collective-permute-start | bytes 786440 | tf_op jit(solution)/shard_map/ppermute | solution.py:23
  149.8 3.4 %collective-permute-done.13 = f32[64,1024]{1,0:T(8,128)S(1)} collective-permute-done((f32[64,1024]{1,0:T(8,128)S(1)}, f32[64,1024]{1,0:T(8,128)S(1)}, u32[]{:S(2)}, u32[]{:S(2)}) %collective-permute-start.13) | collective-permute-done | bytes 262176 | tf_op jit(solution)/shard_map/ppermute | solution.py:23
  153.2 5.2 %collective-permute-done.14 = f32[64,1024]{1,0:T(8,128)S(1)} collective-permute-done((f32[64,1024]{1,0:T(8,128)S(1)}, f32[64,1024]{1,0:T(8,128)S(1)}, u32[]{:S(2)}, u32[]{:S(2)}) %collective-permute-start.14) | collective-permute-done | bytes 262176 | tf_op jit(solution)/shard_map/ppermute | solution.py:29
  158.5 3.4 %collective-permute-done.15 = f32[64,1024]{1,0:T(8,128)S(1)} collective-permute-done((f32[64,1024]{1,0:T(8,128)S(1)}, f32[64,1024]{1,0:T(8,128)S(1)}, u32[]{:S(2)}, u32[]{:S(2)}) %collective-permute-start.15) | collective-permute-done | bytes 262176 | tf_op jit(solution)/shard_map/ppermute | solution.py:23
  164.3 5.1 %all-to-all-start.3 = ((f32[32,16,384]{2,1,0:T(8,128)}), f32[32,16,384]{2,1,0:T(8,128)}, u32[]{:S(2)}, u32[]{:S(2)}) async-start(f32[32,16,384]{2,1,0:T(8,128)} %bitcast.13), calls=%async_computation.3 | async-start | bytes 1572864 | tf_op jit(solution)/shard_map/all_to_all | solution.py:15
  170.4 3.3 %collective-permute-start.16 = (f32[96,1024]{1,0:T(8,128)S(1)}, f32[96,1024]{1,0:T(8,128)}, u32[]{:S(2)}, u32[]{:S(2)}) collective-permute-start(f32[96,1024]{1,0:T(8,128)S(1)} %get-tuple-element.27), channel_id=1, source_target_pairs={{0,128},{128,256},{256,384},{384,0},{1,129},{129,257},{257,385},{3... | collective-permute-start | bytes 1179656 | tf_op jit(solution)/shard_map/ppermute | solution.py:33
  173.8 3.2 %collective-permute-start.17 = (f32[96,1024]{1,0:T(8,128)S(1)}, f32[96,1024]{1,0:T(8,128)S(1)}, u32[]{:S(2)}, u32[]{:S(2)}) collective-permute-start(f32[96,1024]{1,0:T(8,128)S(1)} %get-tuple-element.26), channel_id=1, source_target_pairs={{0,384},{128,0},{256,128},{384,256},{1,385},{129,1},{257,129},{385... | collective-permute-start | bytes 1179656 | tf_op jit(solution)/shard_map/ppermute | solution.py:33
  177.4 3.6 %collective-permute-start.18 = (f32[96,1024]{1,0:T(8,128)S(1)}, f32[96,1024]{1,0:T(8,128)}, u32[]{:S(2)}, u32[]{:S(2)}) collective-permute-start(f32[96,1024]{1,0:T(8,128)S(1)} %get-tuple-element.25), channel_id=1, source_target_pairs={{0,256},{128,384},{256,0},{384,128},{1,257},{129,385},{257,1},{385... | collective-permute-start | bytes 1179656 | tf_op jit(solution)/shard_map/ppermute | solution.py:33
  185.8 4.5 %all-to-all-start.4 = ((f32[16,1,512]{2,1,0:T(1,128)}), f32[16,1,512]{2,1,0:T(1,128)S(1)}, u32[]{:S(2)}, u32[]{:S(2)}) async-start(f32[16,1,512]{2,1,0:T(1,128)} %reshape.512), calls=%async_computation.4 | async-start | bytes 65536 | tf_op jit(solution)/shard_map/all_to_all | solution.py:15
  192.9 8.8 %all-to-all-done.4 = f32[16,1,512]{2,1,0:T(1,128)S(1)} async-done(((f32[16,1,512]{2,1,0:T(1,128)}), f32[16,1,512]{2,1,0:T(1,128)S(1)}, u32[]{:S(2)}, u32[]{:S(2)}) %all-to-all-start.4) | async-done | bytes 32800 | tf_op jit(solution)/shard_map/all_to_all | solution.py:15
  202.7 4.8 %all-to-all-start.5 = ((f32[8,1,6144]{2,1,0:T(1,128)}), f32[8,1,6144]{2,1,0:T(1,128)S(1)}, u32[]{:S(2)}, u32[]{:S(2)}) async-start(f32[8,1,6144]{2,1,0:T(1,128)} %broadcast_in_dim.182), calls=%async_computation.5 | async-start | bytes 393216 | tf_op jit(solution)/shard_map/all_to_all | solution.py:15
  209.2 4.3 %all-to-all-done.5 = f32[8,1,6144]{2,1,0:T(1,128)S(1)} async-done(((f32[8,1,6144]{2,1,0:T(1,128)}), f32[8,1,6144]{2,1,0:T(1,128)S(1)}, u32[]{:S(2)}, u32[]{:S(2)}) %all-to-all-start.5) | async-done | bytes 196640 | tf_op jit(solution)/shard_map/all_to_all | solution.py:15
  (103 shorter events, 41.7 us)
Async XLA Ops:
  0.6 0.9 copy-start
  4.7 33.1 %all-to-all-start = ((f32[64,1,512]{2,1,0:T(1,128)}), f32[64,1,512]{2,1,0:T(1,128)S(1)}, u32[]{:S(2)}, u32[]{:S(2)}) async-start(f32[64,1,512]{2,1,0:T(1,128)} %copy.21), calls=%async_computation | async-start | bytes 262144 | tf_op jit(solution)/shard_map/all_to_all | solution.py:15
  26.3 16.8 %collective-permute-start.1 = (f32[96,1024]{1,0:T(8,128)}, f32[96,1024]{1,0:T(8,128)}, u32[]{:S(2)}, u32[]{:S(2)}) collective-permute-start(f32[96,1024]{1,0:T(8,128)} %get-tuple-element.29), channel_id=1, source_target_pairs={{0,128},{128,256},{256,384},{384,0},{1,129},{129,257},{257,385},{3... | collective-permute-start | bytes 1179656 | tf_op jit(solution)/shard_map/ppermute | solution.py:33
  29.2 20.1 %collective-permute-start.2 = (f32[96,1024]{1,0:T(8,128)}, f32[96,1024]{1,0:T(8,128)S(1)}, u32[]{:S(2)}, u32[]{:S(2)}) collective-permute-start(f32[96,1024]{1,0:T(8,128)} %get-tuple-element.31), channel_id=1, source_target_pairs={{0,256},{128,384},{256,0},{384,128},{1,257},{129,385},{257,1},{385... | collective-permute-start | bytes 1179656 | tf_op jit(solution)/shard_map/ppermute | solution.py:33
  33.7 23.2 %collective-permute-start.3 = (f32[96,1024]{1,0:T(8,128)}, f32[96,1024]{1,0:T(8,128)S(1)}, u32[]{:S(2)}, u32[]{:S(2)}) collective-permute-start(f32[96,1024]{1,0:T(8,128)} %get-tuple-element.28), channel_id=1, source_target_pairs={{0,384},{128,0},{256,128},{384,256},{1,385},{129,1},{257,129},{385... | collective-permute-start | bytes 1179656 | tf_op jit(solution)/shard_map/ppermute | solution.py:33
  38.6 11.4 %all-to-all-start.1 = ((f32[4,64,512]{2,1,0:T(8,128)}), f32[4,64,512]{2,1,0:T(8,128)S(1)}, u32[]{:S(2)}, u32[]{:S(2)}) async-start(f32[4,64,512]{2,1,0:T(8,128)} %broadcast_in_dim.159), calls=%async_computation.1 | async-start | bytes 1048576 | tf_op jit(solution)/shard_map/all_to_all | solution.py:15
  50.0 8.0 %collective-permute-start = (f32[256,512]{1,0:T(8,128)S(1)}, f32[256,512]{1,0:T(8,128)S(1)}, u32[]{:S(2)}, u32[]{:S(2)}) collective-permute-start(f32[256,512]{1,0:T(8,128)S(1)} %bitcast.54), channel_id=1, source_target_pairs={{0,1},{1,0},{2,3},{3,2},{4,5},{5,4},{6,7},{7,6},{8,9},{9,8},{10,11... | collective-permute-start | bytes 1572872 | tf_op jit(solution)/shard_map/ppermute | solution.py:64
  60.0 12.5 %collective-permute-start.6 = (f32[64,1024]{1,0:T(8,128)S(1)}, f32[64,1024]{1,0:T(8,128)S(1)}, u32[]{:S(2)}, u32[]{:S(2)}) collective-permute-start(f32[64,1024]{1,0:T(8,128)S(1)} %get-tuple-element.33), channel_id=1, source_target_pairs={{0,16},{1,113},{8,24},{9,121},{16,32},{17,1},{24,40},{25,9},{32,48... | collective-permute-start | bytes 786440 | tf_op jit(solution)/shard_map/ppermute | solution.py:29
  63.2 13.1 %collective-permute-start.5 = (f32[64,1024]{1,0:T(8,128)S(1)}, f32[64,1024]{1,0:T(8,128)S(1)}, u32[]{:S(2)}, u32[]{:S(2)}) collective-permute-start(f32[64,1024]{1,0:T(8,128)S(1)} %get-tuple-element.34), channel_id=1, source_target_pairs={{0,120},{8,0},{16,8},{24,16},{32,24},{40,32},{48,40},{56,48},{64,5... | collective-permute-start | bytes 786440 | tf_op jit(solution)/shard_map/ppermute | solution.py:23
  66.1 10.5 %collective-permute-start.4 = (f32[64,1024]{1,0:T(8,128)S(1)}, f32[64,1024]{1,0:T(8,128)S(1)}, u32[]{:S(2)}, u32[]{:S(2)}) collective-permute-start(f32[64,1024]{1,0:T(8,128)S(1)} %get-tuple-element.32), channel_id=1, source_target_pairs={{0,8},{8,16},{16,24},{24,32},{32,40},{40,48},{48,56},{56,64},{64,7... | collective-permute-start | bytes 786440 | tf_op jit(solution)/shard_map/ppermute | solution.py:23
  76.7 18.3 %collective-permute-start.9 = (f32[16,1024]{1,0:T(8,128)S(1)}, f32[16,1024]{1,0:T(8,128)S(1)}, u32[]{:S(2)}, u32[]{:S(2)}) collective-permute-start(f32[16,1024]{1,0:T(8,128)S(1)} %get-tuple-element.36), channel_id=1, source_target_pairs={{0,64},{8,72},{16,80},{24,88},{32,96},{40,104},{48,112},{56,120},{... | collective-permute-start | bytes 196616 | tf_op jit(solution)/shard_map/ppermute | solution.py:23
  85.7 14.4 %collective-permute-start.8 = (f32[16,1024]{1,0:T(8,128)S(1)}, f32[16,1024]{1,0:T(8,128)S(1)}, u32[]{:S(2)}, u32[]{:S(2)}) collective-permute-start(f32[16,1024]{1,0:T(8,128)S(1)} %get-tuple-element.37), channel_id=1, source_target_pairs={{0,96},{8,104},{16,112},{24,120},{32,0},{40,8},{48,16},{56,24},{64... | collective-permute-start | bytes 196616 | tf_op jit(solution)/shard_map/ppermute | solution.py:23
  89.1 11.1 %collective-permute-start.7 = (f32[16,1024]{1,0:T(8,128)S(1)}, f32[16,1024]{1,0:T(8,128)S(1)}, u32[]{:S(2)}, u32[]{:S(2)}) collective-permute-start(f32[16,1024]{1,0:T(8,128)S(1)} %get-tuple-element.35), channel_id=1, source_target_pairs={{0,32},{8,40},{16,48},{24,56},{32,64},{40,72},{48,80},{56,88},{64,... | collective-permute-start | bytes 196616 | tf_op jit(solution)/shard_map/ppermute | solution.py:23
  101.1 16.2 %all-to-all-start.2 = ((f32[32,3,16]{2,1,0:T(4,128)}), f32[32,3,16]{2,1,0:T(4,128)S(1)}, u32[]{:S(2)}, u32[]{:S(2)}) async-start(f32[32,3,16]{2,1,0:T(4,128)} %broadcast_in_dim.179), calls=%async_computation.2 | async-start | bytes 131072 | tf_op jit(solution)/shard_map/all_to_all | solution.py:15
  117.6 17.3 %collective-permute-start.10 = (f32[16,1024]{1,0:T(8,128)S(1)}, f32[16,1024]{1,0:T(8,128)S(1)}, u32[]{:S(2)}, u32[]{:S(2)}) collective-permute-start(f32[16,1024]{1,0:T(8,128)S(1)} %get-tuple-element.22), channel_id=1, source_target_pairs={{0,64},{8,72},{16,80},{24,88},{32,96},{40,104},{48,112},{56,120},{... | collective-permute-start | bytes 196616 | tf_op jit(solution)/shard_map/ppermute | solution.py:23
  125.7 13.7 %collective-permute-start.11 = (f32[16,1024]{1,0:T(8,128)S(1)}, f32[16,1024]{1,0:T(8,128)S(1)}, u32[]{:S(2)}, u32[]{:S(2)}) collective-permute-start(f32[16,1024]{1,0:T(8,128)S(1)} %get-tuple-element.22), channel_id=1, source_target_pairs={{0,96},{8,104},{16,112},{24,120},{32,0},{40,8},{48,16},{56,24},{64... | collective-permute-start | bytes 196616 | tf_op jit(solution)/shard_map/ppermute | solution.py:23
  129.5 13.0 %collective-permute-start.12 = (f32[16,1024]{1,0:T(8,128)S(1)}, f32[16,1024]{1,0:T(8,128)S(1)}, u32[]{:S(2)}, u32[]{:S(2)}) collective-permute-start(f32[16,1024]{1,0:T(8,128)S(1)} %get-tuple-element.22), channel_id=1, source_target_pairs={{0,32},{8,40},{16,48},{24,56},{32,64},{40,72},{48,80},{56,88},{64,... | collective-permute-start | bytes 196616 | tf_op jit(solution)/shard_map/ppermute | solution.py:23
  142.5 10.7 %collective-permute-start.13 = (f32[64,1024]{1,0:T(8,128)S(1)}, f32[64,1024]{1,0:T(8,128)S(1)}, u32[]{:S(2)}, u32[]{:S(2)}) collective-permute-start(f32[64,1024]{1,0:T(8,128)S(1)} %pad_maximum_fusion), channel_id=1, source_target_pairs={{0,120},{8,0},{16,8},{24,16},{32,24},{40,32},{48,40},{56,48},{64,5... | collective-permute-start | bytes 786440 | tf_op jit(solution)/shard_map/ppermute | solution.py:23
  144.4 14.0 %collective-permute-start.14 = (f32[64,1024]{1,0:T(8,128)S(1)}, f32[64,1024]{1,0:T(8,128)S(1)}, u32[]{:S(2)}, u32[]{:S(2)}) collective-permute-start(f32[64,1024]{1,0:T(8,128)S(1)} %pad_maximum_fusion), channel_id=1, source_target_pairs={{0,112},{1,17},{8,120},{9,25},{16,0},{17,33},{24,8},{25,41},{32,16... | collective-permute-start | bytes 786440 | tf_op jit(solution)/shard_map/ppermute | solution.py:29
  146.3 15.5 %collective-permute-start.15 = (f32[64,1024]{1,0:T(8,128)S(1)}, f32[64,1024]{1,0:T(8,128)S(1)}, u32[]{:S(2)}, u32[]{:S(2)}) collective-permute-start(f32[64,1024]{1,0:T(8,128)S(1)} %pad_maximum_fusion), channel_id=1, source_target_pairs={{0,8},{8,16},{16,24},{24,32},{32,40},{40,48},{48,56},{56,64},{64,7... | collective-permute-start | bytes 786440 | tf_op jit(solution)/shard_map/ppermute | solution.py:23
  164.3 19.6 %all-to-all-start.3 = ((f32[32,16,384]{2,1,0:T(8,128)}), f32[32,16,384]{2,1,0:T(8,128)}, u32[]{:S(2)}, u32[]{:S(2)}) async-start(f32[32,16,384]{2,1,0:T(8,128)} %bitcast.13), calls=%async_computation.3 | async-start | bytes 1572864 | tf_op jit(solution)/shard_map/all_to_all | solution.py:15
  170.4 21.4 %collective-permute-start.16 = (f32[96,1024]{1,0:T(8,128)S(1)}, f32[96,1024]{1,0:T(8,128)}, u32[]{:S(2)}, u32[]{:S(2)}) collective-permute-start(f32[96,1024]{1,0:T(8,128)S(1)} %get-tuple-element.27), channel_id=1, source_target_pairs={{0,128},{128,256},{256,384},{384,0},{1,129},{129,257},{257,385},{3... | collective-permute-start | bytes 1179656 | tf_op jit(solution)/shard_map/ppermute | solution.py:33
  173.8 19.1 %collective-permute-start.17 = (f32[96,1024]{1,0:T(8,128)S(1)}, f32[96,1024]{1,0:T(8,128)S(1)}, u32[]{:S(2)}, u32[]{:S(2)}) collective-permute-start(f32[96,1024]{1,0:T(8,128)S(1)} %get-tuple-element.26), channel_id=1, source_target_pairs={{0,384},{128,0},{256,128},{384,256},{1,385},{129,1},{257,129},{385... | collective-permute-start | bytes 1179656 | tf_op jit(solution)/shard_map/ppermute | solution.py:33
  177.4 30.1 %collective-permute-start.18 = (f32[96,1024]{1,0:T(8,128)S(1)}, f32[96,1024]{1,0:T(8,128)}, u32[]{:S(2)}, u32[]{:S(2)}) collective-permute-start(f32[96,1024]{1,0:T(8,128)S(1)} %get-tuple-element.25), channel_id=1, source_target_pairs={{0,256},{128,384},{256,0},{384,128},{1,257},{129,385},{257,1},{385... | collective-permute-start | bytes 1179656 | tf_op jit(solution)/shard_map/ppermute | solution.py:33
  185.8 16.0 %all-to-all-start.4 = ((f32[16,1,512]{2,1,0:T(1,128)}), f32[16,1,512]{2,1,0:T(1,128)S(1)}, u32[]{:S(2)}, u32[]{:S(2)}) async-start(f32[16,1,512]{2,1,0:T(1,128)} %reshape.512), calls=%async_computation.4 | async-start | bytes 65536 | tf_op jit(solution)/shard_map/all_to_all | solution.py:15
  202.7 10.7 %all-to-all-start.5 = ((f32[8,1,6144]{2,1,0:T(1,128)}), f32[8,1,6144]{2,1,0:T(1,128)S(1)}, u32[]{:S(2)}, u32[]{:S(2)}) async-start(f32[8,1,6144]{2,1,0:T(1,128)} %broadcast_in_dim.182), calls=%async_computation.5 | async-start | bytes 393216 | tf_op jit(solution)/shard_map/all_to_all | solution.py:15
  208.6 5.6 %copy-start.1 = (f32[96,4096]{1,0:T(8,128)}, f32[96,4096]{1,0:T(8,128)S(1)}, u32[]{:S(2)}) copy-start(f32[96,4096]{1,0:T(8,128)S(1)} %constant_dynamic-update-slice_fusion.7) | copy-start | bytes 4718596

commit v16 on v14

--- a/solution.py
+++ b/solution.py
@@ -46,7 +46,8 @@
     j, c = lax.axis_index(YC), lax.axis_index("c")
 
     row = lax.dynamic_slice(responses, (j, 0), (1, width)).reshape(4, 16, depth)
-    notes = jnp.pad(jnp.concatenate([targets, lengths, owners]).astype(jnp.float32), (0, META - 10))
+    notes = jnp.pad(targets, (0, META - 8)) + jnp.pad(lengths, (8, META - 9)) + jnp.pad(owners, (9, META - 10))
+    notes = notes.astype(jnp.float32)
     notes = jnp.broadcast_to(notes, (16, META))
     packed = jnp.concatenate([row.transpose(1, 0, 2).reshape(16, wide), notes], axis=1).reshape(1, 16, 1, wide + META)
     packed = jnp.broadcast_to(packed, (4, 16, 1, wide + META)).reshape(64, 1, wide + META)
@@ -118,7 +119,7 @@
     own = spread(grad, "h", 4).reshape(64, quarter)
     grads = jnp.concatenate([own, shift_z(own, -1), shift_far(own), shift_z(own, 1)], axis=0)
 
-    grad_rows = dot(grads, head, (1, 1), GRAD)
+    grad_rows = dot(grads, head, (1, 1))
     leaving = dot(deliver, grad_rows, (1, 0), GRAD).reshape(32, 16, wide)
     summed = jnp.sum(swap(leaving, XYC), axis=0)
 

time: 215 us -> 216 us (level)
  no operation moved by 1% of the time
where the time goes in v16:
time: 216 us; the launch traced here: 215 us
  starting transfers between devices  111 us (51%)
  waiting for transfers between devices  72 us (33%)
  local copies, waits for them, and re-layouts  16.7 us (8%)
  matrix products  8.44 us (4%)
  other arithmetic  3.59 us (2%)
  between operations  2.57 us (1%)
    all_to_all x8, starting transfers between devices, swap(): return lax.all_to_all(blocks, axes, split_axis=0, concat_axis=0, tiled=True)  63.7 us
    all_to_all x8, waiting for transfers between devices, swap(): return lax.all_to_all(blocks, axes, split_axis=0, concat_axis=0, tiled=True)  50.2 us
    ppermute x6, starting transfers between devices, shift_x(): return lax.ppermute(block, 'x', [(i, (i + step) % 4) for i in range(4)])  20.8 us
    ppermute x4, starting transfers between devices, shift_z(): return lax.ppermute(block, Z, [(i, (i + step) % 16) for i in range(16)])  14.9 us
    dot_general x7, matrix products, dot(): lax.dot_general(a, b, dims, precision=precision, preferred_element_type=j...  8.44 us
    ppermute x4, waiting for transfers between devices, shift_z(): return lax.ppermute(block, Z, [(i, (i + step) % 16) for i in range(16)])  8.2 us
    ppermute x2, waiting for transfers between devices, shift_far(): return lax.ppermute(block, ('h', 'l', 'c'), pairs)  7.81 us
    ppermute x1, starting transfers between devices, on_device(): slots_other = lax.ppermute(slots, 'c', [(0, 1), (1, 0)])  6.47 us
  transfers between devices with their start and end apart: 21, of which 15 were waited for; matrix products, arithmetic and copies ran while one was open for 8% of the time, Pallas kernels for 0%

profile of v16, /device:TPU:1, one launch (start us, length us, event | category | flops | bytes accessed | tf_op | source)
XLA Modules:
  0.0 214.6 jit_solution(9439323037151001358)
XLA Ops:
  4.7 19.1 %all-to-all-start = ((f32[64,1,512]{2,1,0:T(1,128)}), f32[64,1,512]{2,1,0:T(1,128)S(1)}, u32[]{:S(2)}, u32[]{:S(2)}) async-start(f32[64,1,512]{2,1,0:T(1,128)} %copy.21), calls=%async_computation | async-start | bytes 262144 | tf_op jit(solution)/shard_map/all_to_all | solution.py:15
  23.9 2.4 %constant_dynamic-slice_fusion = (f32[96,1024]{1,0:T(8,128)}, f32[96,1024]{1,0:T(8,128)}, f32[96,1024]{1,0:T(8,128)S(1)}, f32[96,1024]{1,0:T(8,128)}) fusion(f32[96,4096]{1,0:T(8,128)} %param.6, s32[]{:T(128)S(6)} %select_n.294, s32[]{:T(128)S(6)} %select_n.286, s32[]{:T(128)S(6)} %select_n.264, s32[]{:T(128)S(6)} %select_n.290), kind=kLoop, calls=%fused_computation.63 | loop fusion | bytes 3145744 | tf_op jit(solution)/shard_map/dynamic_slice | solution.py:56
  26.3 2.9 %collective-permute-start.1 = (f32[96,1024]{1,0:T(8,128)}, f32[96,1024]{1,0:T(8,128)}, u32[]{:S(2)}, u32[]{:S(2)}) collective-permute-start(f32[96,1024]{1,0:T(8,128)} %get-tuple-element.25), channel_id=1, source_target_pairs={{0,128},{128,256},{256,384},{384,0},{1,129},{129,257},{257,385},{3... | collective-permute-start | bytes 1179656 | tf_op jit(solution)/shard_map/ppermute | solution.py:32
  29.2 4.5 %collective-permute-start.2 = (f32[96,1024]{1,0:T(8,128)}, f32[96,1024]{1,0:T(8,128)S(1)}, u32[]{:S(2)}, u32[]{:S(2)}) collective-permute-start(f32[96,1024]{1,0:T(8,128)} %get-tuple-element.27), channel_id=1, source_target_pairs={{0,256},{128,384},{256,0},{384,128},{1,257},{129,385},{257,1},{385... | collective-permute-start | bytes 1179656 | tf_op jit(solution)/shard_map/ppermute | solution.py:32
  33.7 3.0 %collective-permute-start.3 = (f32[96,1024]{1,0:T(8,128)}, f32[96,1024]{1,0:T(8,128)S(1)}, u32[]{:S(2)}, u32[]{:S(2)}) collective-permute-start(f32[96,1024]{1,0:T(8,128)} %get-tuple-element.24), channel_id=1, source_target_pairs={{0,384},{128,0},{256,128},{384,256},{1,385},{129,1},{257,129},{385... | collective-permute-start | bytes 1179656 | tf_op jit(solution)/shard_map/ppermute | solution.py:32
  38.6 4.2 %all-to-all-start.1 = ((f32[4,64,512]{2,1,0:T(8,128)}), f32[4,64,512]{2,1,0:T(8,128)S(1)}, u32[]{:S(2)}, u32[]{:S(2)}) async-start(f32[4,64,512]{2,1,0:T(8,128)} %broadcast_in_dim.153), calls=%async_computation.1 | async-start | bytes 1048576 | tf_op jit(solution)/shard_map/all_to_all | solution.py:15
  44.1 5.2 %collective-permute-done.2 = f32[96,1024]{1,0:T(8,128)S(1)} collective-permute-done((f32[96,1024]{1,0:T(8,128)}, f32[96,1024]{1,0:T(8,128)S(1)}, u32[]{:S(2)}, u32[]{:S(2)}) %collective-permute-start.2) | collective-permute-done | bytes 393248 | tf_op jit(solution)/shard_map/ppermute | solution.py:32
  50.0 6.5 %collective-permute-start = (f32[256,512]{1,0:T(8,128)S(1)}, f32[256,512]{1,0:T(8,128)S(1)}, u32[]{:S(2)}, u32[]{:S(2)}) collective-permute-start(f32[256,512]{1,0:T(8,128)S(1)} %bitcast.54), channel_id=1, source_target_pairs={{0,1},{1,0},{2,3},{3,2},{4,5},{5,4},{6,7},{7,6},{8,9},{9,8},{10,11... | collective-permute-start | bytes 1572872 | tf_op jit(solution)/shard_map/ppermute | solution.py:64
  60.0 3.2 %collective-permute-start.6 = (f32[64,1024]{1,0:T(8,128)S(1)}, f32[64,1024]{1,0:T(8,128)S(1)}, u32[]{:S(2)}, u32[]{:S(2)}) collective-permute-start(f32[64,1024]{1,0:T(8,128)S(1)} %get-tuple-element.29), channel_id=1, source_target_pairs={{0,16},{1,113},{8,24},{9,121},{16,32},{17,1},{24,40},{25,9},{32,48... | collective-permute-start | bytes 786440 | tf_op jit(solution)/shard_map/ppermute | solution.py:28
  63.2 2.9 %collective-permute-start.5 = (f32[64,1024]{1,0:T(8,128)S(1)}, f32[64,1024]{1,0:T(8,128)S(1)}, u32[]{:S(2)}, u32[]{:S(2)}) collective-permute-start(f32[64,1024]{1,0:T(8,128)S(1)} %get-tuple-element.30), channel_id=1, source_target_pairs={{0,120},{8,0},{16,8},{24,16},{32,24},{40,32},{48,40},{56,48},{64,5... | collective-permute-start | bytes 786440 | tf_op jit(solution)/shard_map/ppermute | solution.py:23
  66.1 2.4 %collective-permute-start.4 = (f32[64,1024]{1,0:T(8,128)S(1)}, f32[64,1024]{1,0:T(8,128)S(1)}, u32[]{:S(2)}, u32[]{:S(2)}) collective-permute-start(f32[64,1024]{1,0:T(8,128)S(1)} %get-tuple-element.28), channel_id=1, source_target_pairs={{0,8},{8,16},{16,24},{24,32},{32,40},{40,48},{48,56},{56,64},{64,7... | collective-permute-start | bytes 786440 | tf_op jit(solution)/shard_map/ppermute | solution.py:23
  69.6 2.9 %collective-permute-done.6 = f32[64,1024]{1,0:T(8,128)S(1)} collective-permute-done((f32[64,1024]{1,0:T(8,128)S(1)}, f32[64,1024]{1,0:T(8,128)S(1)}, u32[]{:S(2)}, u32[]{:S(2)}) %collective-permute-start.6) | collective-permute-done | bytes 262176 | tf_op jit(solution)/shard_map/ppermute | solution.py:28
  72.4 3.9 %collective-permute-done.5 = f32[64,1024]{1,0:T(8,128)S(1)} collective-permute-done((f32[64,1024]{1,0:T(8,128)S(1)}, f32[64,1024]{1,0:T(8,128)S(1)}, u32[]{:S(2)}, u32[]{:S(2)}) %collective-permute-start.5) | collective-permute-done | bytes 262176 | tf_op jit(solution)/shard_map/ppermute | solution.py:23
  77.4 8.2 %all-to-all-start.2 = ((f32[4,16,1024]{2,1,0:T(8,128)}), f32[4,16,1024]{2,1,0:T(8,128)S(1)}, u32[]{:S(2)}, u32[]{:S(2)}) async-start(f32[4,16,1024]{2,1,0:T(8,128)} %bitcast.8), calls=%async_computation.2 | async-start | bytes 524288 | tf_op jit(solution)/shard_map/all_to_all | solution.py:15
  86.3 12.5 %all-to-all-done.2 = f32[4,16,1024]{2,1,0:T(8,128)S(1)} async-done(((f32[4,16,1024]{2,1,0:T(8,128)}), f32[4,16,1024]{2,1,0:T(8,128)S(1)}, u32[]{:S(2)}, u32[]{:S(2)}) %all-to-all-start.2) | async-done | bytes 262176 | tf_op jit(solution)/shard_map/all_to_all | solution.py:15
  99.8 12.4 %all-to-all-start.3 = ((f32[32,3,16]{2,1,0:T(4,128)}), f32[32,3,16]{2,1,0:T(4,128)S(1)}, u32[]{:S(2)}, u32[]{:S(2)}) async-start(f32[32,3,16]{2,1,0:T(4,128)} %broadcast_in_dim.171), calls=%async_computation.3 | async-start | bytes 131072 | tf_op jit(solution)/shard_map/all_to_all | solution.py:15
  112.2 7.4 %all-to-all-done.3 = f32[32,3,16]{2,1,0:T(4,128)S(1)} async-done(((f32[32,3,16]{2,1,0:T(4,128)}), f32[32,3,16]{2,1,0:T(4,128)S(1)}, u32[]{:S(2)}, u32[]{:S(2)}) %all-to-all-start.3) | async-done | bytes 6176 | tf_op jit(solution)/shard_map/all_to_all | solution.py:15
  120.5 3.8 %all-to-all-start.4 = ((f32[4,16,1024]{2,1,0:T(8,128)}), f32[4,16,1024]{2,1,0:T(8,128)S(1)}, u32[]{:S(2)}, u32[]{:S(2)}) async-start(f32[4,16,1024]{2,1,0:T(8,128)} %broadcast_in_dim.172), calls=%async_computation.4 | async-start | bytes 524288 | tf_op jit(solution)/shard_map/all_to_all | solution.py:15
  124.5 15.8 %all-to-all-done.4 = f32[4,16,1024]{2,1,0:T(8,128)S(1)} async-done(((f32[4,16,1024]{2,1,0:T(8,128)}), f32[4,16,1024]{2,1,0:T(8,128)S(1)}, u32[]{:S(2)}, u32[]{:S(2)}) %all-to-all-start.4) | async-done | bytes 262176 | tf_op jit(solution)/shard_map/all_to_all | solution.py:15
  140.2 6.3 %collective-permute-start.9 = (f32[64,1024]{1,0:T(8,128)S(1)}, f32[64,1024]{1,0:T(8,128)S(1)}, u32[]{:S(2)}, u32[]{:S(2)}) collective-permute-start(f32[64,1024]{1,0:T(8,128)S(1)} %bitcast.58), channel_id=1, source_target_pairs={{0,8},{8,16},{16,24},{24,32},{32,40},{40,48},{48,56},{56,64},{64,7... | collective-permute-start | bytes 786440 | tf_op jit(solution)/shard_map/ppermute | solution.py:23
  146.5 2.3 %collective-permute-start.8 = (f32[64,1024]{1,0:T(8,128)S(1)}, f32[64,1024]{1,0:T(8,128)S(1)}, u32[]{:S(2)}, u32[]{:S(2)}) collective-permute-start(f32[64,1024]{1,0:T(8,128)S(1)} %bitcast.59), channel_id=1, source_target_pairs={{0,16},{1,113},{8,24},{9,121},{16,32},{17,1},{24,40},{25,9},{32,48... | collective-permute-start | bytes 786440 | tf_op jit(solution)/shard_map/ppermute | solution.py:28
  148.8 3.4 %collective-permute-start.7 = (f32[64,1024]{1,0:T(8,128)S(1)}, f32[64,1024]{1,0:T(8,128)S(1)}, u32[]{:S(2)}, u32[]{:S(2)}) collective-permute-start(f32[64,1024]{1,0:T(8,128)S(1)} %bitcast.60), channel_id=1, source_target_pairs={{0,120},{8,0},{16,8},{24,16},{32,24},{40,32},{48,40},{56,48},{64,5... | collective-permute-start | bytes 786440 | tf_op jit(solution)/shard_map/ppermute | solution.py:23
  152.3 5.0 %collective-permute-done.8 = f32[64,1024]{1,0:T(8,128)S(1)} collective-permute-done((f32[64,1024]{1,0:T(8,128)S(1)}, f32[64,1024]{1,0:T(8,128)S(1)}, u32[]{:S(2)}, u32[]{:S(2)}) %collective-permute-start.8) | collective-permute-done | bytes 262176 | tf_op jit(solution)/shard_map/ppermute | solution.py:28
  157.3 3.9 %collective-permute-done.7 = f32[64,1024]{1,0:T(8,128)S(1)} collective-permute-done((f32[64,1024]{1,0:T(8,128)S(1)}, f32[64,1024]{1,0:T(8,128)S(1)}, u32[]{:S(2)}, u32[]{:S(2)}) %collective-permute-start.7) | collective-permute-done | bytes 262176 | tf_op jit(solution)/shard_map/ppermute | solution.py:23
  164.5 4.5 %all-to-all-start.5 = ((f32[32,16,384]{2,1,0:T(8,128)}), f32[32,16,384]{2,1,0:T(8,128)S(1)}, u32[]{:S(2)}, u32[]{:S(2)}) async-start(f32[32,16,384]{2,1,0:T(8,128)} %bitcast.15), calls=%async_computation.5 | async-start | bytes 1572864 | tf_op jit(solution)/shard_map/all_to_all | solution.py:15
  171.7 3.3 %collective-permute-start.10 = (f32[96,1024]{1,0:T(8,128)}, f32[96,1024]{1,0:T(8,128)}, u32[]{:S(2)}, u32[]{:S(2)}) collective-permute-start(f32[96,1024]{1,0:T(8,128)} %get-tuple-element.23), channel_id=1, source_target_pairs={{0,128},{128,256},{256,384},{384,0},{1,129},{129,257},{257,385},{3... | collective-permute-start | bytes 1179656 | tf_op jit(solution)/shard_map/ppermute | solution.py:32
  175.1 3.4 %collective-permute-start.11 = (f32[96,1024]{1,0:T(8,128)S(1)}, f32[96,1024]{1,0:T(8,128)}, u32[]{:S(2)}, u32[]{:S(2)}) collective-permute-start(f32[96,1024]{1,0:T(8,128)S(1)} %get-tuple-element.22), channel_id=1, source_target_pairs={{0,384},{128,0},{256,128},{384,256},{1,385},{129,1},{257,129},{385... | collective-permute-start | bytes 1179656 | tf_op jit(solution)/shard_map/ppermute | solution.py:32
  178.9 3.6 %collective-permute-start.12 = (f32[96,1024]{1,0:T(8,128)S(1)}, f32[96,1024]{1,0:T(8,128)}, u32[]{:S(2)}, u32[]{:S(2)}) collective-permute-start(f32[96,1024]{1,0:T(8,128)S(1)} %get-tuple-element.21), channel_id=1, source_target_pairs={{0,256},{128,384},{256,0},{384,128},{1,257},{129,385},{257,1},{385... | collective-permute-start | bytes 1179656 | tf_op jit(solution)/shard_map/ppermute | solution.py:32
  184.1 5.4 %all-to-all-start.6 = ((f32[16,1,512]{2,1,0:T(1,128)}), f32[16,1,512]{2,1,0:T(1,128)S(1)}, u32[]{:S(2)}, u32[]{:S(2)}) async-start(f32[16,1,512]{2,1,0:T(1,128)} %reshape.307), calls=%async_computation.6 | async-start | bytes 65536 | tf_op jit(solution)/shard_map/all_to_all | solution.py:15
  193.2 7.8 %all-to-all-done.6 = f32[16,1,512]{2,1,0:T(1,128)S(1)} async-done(((f32[16,1,512]{2,1,0:T(1,128)}), f32[16,1,512]{2,1,0:T(1,128)S(1)}, u32[]{:S(2)}, u32[]{:S(2)}) %all-to-all-start.6) | async-done | bytes 32800 | tf_op jit(solution)/shard_map/all_to_all | solution.py:15
  201.9 6.0 %all-to-all-start.7 = ((f32[8,1,6144]{2,1,0:T(1,128)}), f32[8,1,6144]{2,1,0:T(1,128)S(1)}, u32[]{:S(2)}, u32[]{:S(2)}) async-start(f32[8,1,6144]{2,1,0:T(1,128)} %broadcast_in_dim.175), calls=%async_computation.7 | async-start | bytes 393216 | tf_op jit(solution)/shard_map/all_to_all | solution.py:15
  209.6 4.3 %all-to-all-done.7 = f32[8,1,6144]{2,1,0:T(1,128)S(1)} async-done(((f32[8,1,6144]{2,1,0:T(1,128)}), f32[8,1,6144]{2,1,0:T(1,128)S(1)}, u32[]{:S(2)}, u32[]{:S(2)}) %all-to-all-start.7) | async-done | bytes 196640 | tf_op jit(solution)/shard_map/all_to_all | solution.py:15
  (93 shorter events, 29.8 us)
Async XLA Ops:
  0.6 0.9 copy-start
  4.7 33.1 %all-to-all-start = ((f32[64,1,512]{2,1,0:T(1,128)}), f32[64,1,512]{2,1,0:T(1,128)S(1)}, u32[]{:S(2)}, u32[]{:S(2)}) async-start(f32[64,1,512]{2,1,0:T(1,128)} %copy.21), calls=%async_computation | async-start | bytes 262144 | tf_op jit(solution)/shard_map/all_to_all | solution.py:15
  26.3 16.8 %collective-permute-start.1 = (f32[96,1024]{1,0:T(8,128)}, f32[96,1024]{1,0:T(8,128)}, u32[]{:S(2)}, u32[]{:S(2)}) collective-permute-start(f32[96,1024]{1,0:T(8,128)} %get-tuple-element.25), channel_id=1, source_target_pairs={{0,128},{128,256},{256,384},{384,0},{1,129},{129,257},{257,385},{3... | collective-permute-start | bytes 1179656 | tf_op jit(solution)/shard_map/ppermute | solution.py:32
  29.2 20.1 %collective-permute-start.2 = (f32[96,1024]{1,0:T(8,128)}, f32[96,1024]{1,0:T(8,128)S(1)}, u32[]{:S(2)}, u32[]{:S(2)}) collective-permute-start(f32[96,1024]{1,0:T(8,128)} %get-tuple-element.27), channel_id=1, source_target_pairs={{0,256},{128,384},{256,0},{384,128},{1,257},{129,385},{257,1},{385... | collective-permute-start | bytes 1179656 | tf_op jit(solution)/shard_map/ppermute | solution.py:32
  33.7 23.2 %collective-permute-start.3 = (f32[96,1024]{1,0:T(8,128)}, f32[96,1024]{1,0:T(8,128)S(1)}, u32[]{:S(2)}, u32[]{:S(2)}) collective-permute-start(f32[96,1024]{1,0:T(8,128)} %get-tuple-element.24), channel_id=1, source_target_pairs={{0,384},{128,0},{256,128},{384,256},{1,385},{129,1},{257,129},{385... | collective-permute-start | bytes 1179656 | tf_op jit(solution)/shard_map/ppermute | solution.py:32
  38.6 11.4 %all-to-all-start.1 = ((f32[4,64,512]{2,1,0:T(8,128)}), f32[4,64,512]{2,1,0:T(8,128)S(1)}, u32[]{:S(2)}, u32[]{:S(2)}) async-start(f32[4,64,512]{2,1,0:T(8,128)} %broadcast_in_dim.153), calls=%async_computation.1 | async-start | bytes 1048576 | tf_op jit(solution)/shard_map/all_to_all | solution.py:15
  50.0 8.0 %collective-permute-start = (f32[256,512]{1,0:T(8,128)S(1)}, f32[256,512]{1,0:T(8,128)S(1)}, u32[]{:S(2)}, u32[]{:S(2)}) collective-permute-start(f32[256,512]{1,0:T(8,128)S(1)} %bitcast.54), channel_id=1, source_target_pairs={{0,1},{1,0},{2,3},{3,2},{4,5},{5,4},{6,7},{7,6},{8,9},{9,8},{10,11... | collective-permute-start | bytes 1572872 | tf_op jit(solution)/shard_map/ppermute | solution.py:64
  60.0 12.4 %collective-permute-start.6 = (f32[64,1024]{1,0:T(8,128)S(1)}, f32[64,1024]{1,0:T(8,128)S(1)}, u32[]{:S(2)}, u32[]{:S(2)}) collective-permute-start(f32[64,1024]{1,0:T(8,128)S(1)} %get-tuple-element.29), channel_id=1, source_target_pairs={{0,16},{1,113},{8,24},{9,121},{16,32},{17,1},{24,40},{25,9},{32,48... | collective-permute-start | bytes 786440 | tf_op jit(solution)/shard_map/ppermute | solution.py:28
  63.2 13.1 %collective-permute-start.5 = (f32[64,1024]{1,0:T(8,128)S(1)}, f32[64,1024]{1,0:T(8,128)S(1)}, u32[]{:S(2)}, u32[]{:S(2)}) collective-permute-start(f32[64,1024]{1,0:T(8,128)S(1)} %get-tuple-element.30), channel_id=1, source_target_pairs={{0,120},{8,0},{16,8},{24,16},{32,24},{40,32},{48,40},{56,48},{64,5... | collective-permute-start | bytes 786440 | tf_op jit(solution)/shard_map/ppermute | solution.py:23
  66.1 10.6 %collective-permute-start.4 = (f32[64,1024]{1,0:T(8,128)S(1)}, f32[64,1024]{1,0:T(8,128)S(1)}, u32[]{:S(2)}, u32[]{:S(2)}) collective-permute-start(f32[64,1024]{1,0:T(8,128)S(1)} %get-tuple-element.28), channel_id=1, source_target_pairs={{0,8},{8,16},{16,24},{24,32},{32,40},{40,48},{48,56},{56,64},{64,7... | collective-permute-start | bytes 786440 | tf_op jit(solution)/shard_map/ppermute | solution.py:23
  77.4 21.3 %all-to-all-start.2 = ((f32[4,16,1024]{2,1,0:T(8,128)}), f32[4,16,1024]{2,1,0:T(8,128)S(1)}, u32[]{:S(2)}, u32[]{:S(2)}) async-start(f32[4,16,1024]{2,1,0:T(8,128)} %bitcast.8), calls=%async_computation.2 | async-start | bytes 524288 | tf_op jit(solution)/shard_map/all_to_all | solution.py:15
  99.8 19.8 %all-to-all-start.3 = ((f32[32,3,16]{2,1,0:T(4,128)}), f32[32,3,16]{2,1,0:T(4,128)S(1)}, u32[]{:S(2)}, u32[]{:S(2)}) async-start(f32[32,3,16]{2,1,0:T(4,128)} %broadcast_in_dim.171), calls=%async_computation.3 | async-start | bytes 131072 | tf_op jit(solution)/shard_map/all_to_all | solution.py:15
  120.5 19.7 %all-to-all-start.4 = ((f32[4,16,1024]{2,1,0:T(8,128)}), f32[4,16,1024]{2,1,0:T(8,128)S(1)}, u32[]{:S(2)}, u32[]{:S(2)}) async-start(f32[4,16,1024]{2,1,0:T(8,128)} %broadcast_in_dim.172), calls=%async_computation.4 | async-start | bytes 524288 | tf_op jit(solution)/shard_map/all_to_all | solution.py:15
  140.2 12.1 %collective-permute-start.9 = (f32[64,1024]{1,0:T(8,128)S(1)}, f32[64,1024]{1,0:T(8,128)S(1)}, u32[]{:S(2)}, u32[]{:S(2)}) collective-permute-start(f32[64,1024]{1,0:T(8,128)S(1)} %bitcast.58), channel_id=1, source_target_pairs={{0,8},{8,16},{16,24},{24,32},{32,40},{40,48},{48,56},{56,64},{64,7... | collective-permute-start | bytes 786440 | tf_op jit(solution)/shard_map/ppermute | solution.py:23
  146.5 10.8 %collective-permute-start.8 = (f32[64,1024]{1,0:T(8,128)S(1)}, f32[64,1024]{1,0:T(8,128)S(1)}, u32[]{:S(2)}, u32[]{:S(2)}) collective-permute-start(f32[64,1024]{1,0:T(8,128)S(1)} %bitcast.59), channel_id=1, source_target_pairs={{0,16},{1,113},{8,24},{9,121},{16,32},{17,1},{24,40},{25,9},{32,48... | collective-permute-start | bytes 786440 | tf_op jit(solution)/shard_map/ppermute | solution.py:28
  148.8 12.4 %collective-permute-start.7 = (f32[64,1024]{1,0:T(8,128)S(1)}, f32[64,1024]{1,0:T(8,128)S(1)}, u32[]{:S(2)}, u32[]{:S(2)}) collective-permute-start(f32[64,1024]{1,0:T(8,128)S(1)} %bitcast.60), channel_id=1, source_target_pairs={{0,120},{8,0},{16,8},{24,16},{32,24},{40,32},{48,40},{56,48},{64,5... | collective-permute-start | bytes 786440 | tf_op jit(solution)/shard_map/ppermute | solution.py:23
  157.3 7.2 %copy-start.2 = (f32[64,1024]{1,0:T(8,128)}, f32[64,1024]{1,0:T(8,128)S(1)}, u32[]{:S(2)}) copy-start(f32[64,1024]{1,0:T(8,128)S(1)} %collective-permute-done.8) | copy-start | bytes 786436
  161.2 3.3 %copy-start.3 = (f32[64,1024]{1,0:T(8,128)}, f32[64,1024]{1,0:T(8,128)S(1)}, u32[]{:S(2)}) copy-start(f32[64,1024]{1,0:T(8,128)S(1)} %collective-permute-done.7) | copy-start | bytes 786436
  164.5 18.9 %all-to-all-start.5 = ((f32[32,16,384]{2,1,0:T(8,128)}), f32[32,16,384]{2,1,0:T(8,128)S(1)}, u32[]{:S(2)}, u32[]{:S(2)}) async-start(f32[32,16,384]{2,1,0:T(8,128)} %bitcast.15), calls=%async_computation.5 | async-start | bytes 1572864 | tf_op jit(solution)/shard_map/all_to_all | solution.py:15
  171.7 19.3 %collective-permute-start.10 = (f32[96,1024]{1,0:T(8,128)}, f32[96,1024]{1,0:T(8,128)}, u32[]{:S(2)}, u32[]{:S(2)}) collective-permute-start(f32[96,1024]{1,0:T(8,128)} %get-tuple-element.23), channel_id=1, source_target_pairs={{0,128},{128,256},{256,384},{384,0},{1,129},{129,257},{257,385},{3... | collective-permute-start | bytes 1179656 | tf_op jit(solution)/shard_map/ppermute | solution.py:32
  175.1 17.1 %collective-permute-start.11 = (f32[96,1024]{1,0:T(8,128)S(1)}, f32[96,1024]{1,0:T(8,128)}, u32[]{:S(2)}, u32[]{:S(2)}) collective-permute-start(f32[96,1024]{1,0:T(8,128)S(1)} %get-tuple-element.22), channel_id=1, source_target_pairs={{0,384},{128,0},{256,128},{384,256},{1,385},{129,1},{257,129},{385... | collective-permute-start | bytes 1179656 | tf_op jit(solution)/shard_map/ppermute | solution.py:32
  178.9 29.0 %collective-permute-start.12 = (f32[96,1024]{1,0:T(8,128)S(1)}, f32[96,1024]{1,0:T(8,128)}, u32[]{:S(2)}, u32[]{:S(2)}) collective-permute-start(f32[96,1024]{1,0:T(8,128)S(1)} %get-tuple-element.21), channel_id=1, source_target_pairs={{0,256},{128,384},{256,0},{384,128},{1,257},{129,385},{257,1},{385... | collective-permute-start | bytes 1179656 | tf_op jit(solution)/shard_map/ppermute | solution.py:32
  184.1 16.8 %all-to-all-start.6 = ((f32[16,1,512]{2,1,0:T(1,128)}), f32[16,1,512]{2,1,0:T(1,128)S(1)}, u32[]{:S(2)}, u32[]{:S(2)}) async-start(f32[16,1,512]{2,1,0:T(1,128)} %reshape.307), calls=%async_computation.6 | async-start | bytes 65536 | tf_op jit(solution)/shard_map/all_to_all | solution.py:15
  201.9 11.9 %all-to-all-start.7 = ((f32[8,1,6144]{2,1,0:T(1,128)}), f32[8,1,6144]{2,1,0:T(1,128)S(1)}, u32[]{:S(2)}, u32[]{:S(2)}) async-start(f32[8,1,6144]{2,1,0:T(1,128)} %broadcast_in_dim.175), calls=%async_computation.7 | async-start | bytes 393216 | tf_op jit(solution)/shard_map/all_to_all | solution.py:15
  209.0 5.6 %copy-start.1 = (f32[96,4096]{1,0:T(8,128)}, f32[96,4096]{1,0:T(8,128)S(1)}, u32[]{:S(2)}) copy-start(f32[96,4096]{1,0:T(8,128)S(1)} %constant_dynamic-update-slice_fusion.2) | copy-start | bytes 4718596

commit v17 on v16

--- a/solution.py
+++ b/solution.py
@@ -101,7 +101,11 @@
     leave = dot(hidden[64:], head)
     stay = lax.optimization_barrier(dot(hidden[:64], head))
     block = stay + shift_z(leave[:64], 1) + shift_z(leave[128:], -1) + shift_far(leave[64:128])
-    logits = jnp.sum(swap(block.reshape(4, 16, quarter), "h"), axis=0)
+
+    def group(s):
+        return lax.dynamic_slice(block, ((h + s) % 4 * 16, 0), (16, quarter))
+
+    logits = group(0) + shift_z(group(1), 4) + shift_z(group(3), -4) + shift_z(group(2), 8)
 
     row_labels = lax.dynamic_slice(labels, (h * 16,), (16,))
     column = jnp.arange(quarter, dtype=jnp.int32) + j * columns + x * quarter

time: 216 us -> 216 us (level)
  starting transfers between devices: 111 us -> 118 us
  waiting for transfers between devices: 72 us -> 66.7 us
    ppermute x4 -> x7, starting transfers between devices: 14.9 us -> 30 us  [shift_z(): return lax.ppermute(block, Z, [(i, (i + step) % 16) for i in range(16)])]
    all_to_all x8 -> x7, waiting for transfers between devices: 50.2 us -> 39.5 us  [swap(): return lax.all_to_all(blocks, axes, split_axis=0, concat_axis=0, tiled=True)]
    ppermute x4 -> x7, waiting for transfers between devices: 8.2 us -> 18.9 us  [shift_z(): return lax.ppermute(block, Z, [(i, (i + step) % 16) for i in range(16)])]
    all_to_all x8 -> x7, starting transfers between devices: 63.7 us -> 55.3 us  [swap(): return lax.all_to_all(blocks, axes, split_axis=0, concat_axis=0, tiled=True)]
    ppermute x2, waiting for transfers between devices: 7.81 us -> 2.93 us  [shift_far(): return lax.ppermute(block, ('h', 'l', 'c'), pairs)]
  transfers between devices with their start and end apart: 21 -> 23, of which waited for: 15 -> 16; matrix products, arithmetic and copies ran while one was open for 8% -> 8% of each run, Pallas kernels for 0% -> 0%
where the time goes in v17:
time: 216 us; the launch traced here: 215 us
  starting transfers between devices  118 us (55%)
  waiting for transfers between devices  66.7 us (31%)
  local copies, waits for them, and re-layouts  16.8 us (8%)
  matrix products  8.43 us (4%)
  other arithmetic  2.88 us (1%)
  between operations  2.67 us (1%)
    all_to_all x7, starting transfers between devices, swap(): return lax.all_to_all(blocks, axes, split_axis=0, concat_axis=0, tiled=True)  55.3 us
    all_to_all x7, waiting for transfers between devices, swap(): return lax.all_to_all(blocks, axes, split_axis=0, concat_axis=0, tiled=True)  39.5 us
    ppermute x7, starting transfers between devices, shift_z(): return lax.ppermute(block, Z, [(i, (i + step) % 16) for i in range(16)])  30 us
    ppermute x6, starting transfers between devices, shift_x(): return lax.ppermute(block, 'x', [(i, (i + step) % 4) for i in range(4)])  20.8 us
    ppermute x7, waiting for transfers between devices, shift_z(): return lax.ppermute(block, Z, [(i, (i + step) % 16) for i in range(16)])  18.9 us
    dot_general x7, matrix products, dot(): lax.dot_general(a, b, dims, precision=precision, preferred_element_type=j...  8.43 us
    ppermute x1, starting transfers between devices, on_device(): slots_other = lax.ppermute(slots, 'c', [(0, 1), (1, 0)])  6.47 us
    ppermute x6, waiting for transfers between devices, shift_x(): return lax.ppermute(block, 'x', [(i, (i + step) % 4) for i in range(4)])  5.24 us
  transfers between devices with their start and end apart: 23, of which 16 were waited for; matrix products, arithmetic and copies ran while one was open for 8% of the time, Pallas kernels for 0%

profile of v17, /device:TPU:1, one launch (start us, length us, event | category | flops | bytes accessed | tf_op | source)
XLA Modules:
  0.0 215.2 jit_solution(2818400374312853688)
XLA Ops:
  4.7 19.1 %all-to-all-start = ((f32[64,1,512]{2,1,0:T(1,128)}), f32[64,1,512]{2,1,0:T(1,128)S(1)}, u32[]{:S(2)}, u32[]{:S(2)}) async-start(f32[64,1,512]{2,1,0:T(1,128)} %copy.21), calls=%async_computation | async-start | bytes 262144 | tf_op jit(solution)/shard_map/all_to_all | solution.py:15
  23.9 2.4 %constant_dynamic-slice_fusion.3 = (f32[96,1024]{1,0:T(8,128)}, f32[96,1024]{1,0:T(8,128)}, f32[96,1024]{1,0:T(8,128)S(1)}, f32[96,1024]{1,0:T(8,128)}) fusion(f32[96,4096]{1,0:T(8,128)} %param.6, s32[]{:T(128)S(6)} %select_n.322, s32[]{:T(128)S(6)} %select_n.314, s32[]{:T(128)S(6)} %select_n.292, s32[]{:T(128)S(6)} %select_n.318), kind=kLoop, calls=%fused_computation.66 | loop fusion | bytes 3145744 | tf_op jit(solution)/shard_map/dynamic_slice | solution.py:56
  26.3 2.9 %collective-permute-start.1 = (f32[96,1024]{1,0:T(8,128)}, f32[96,1024]{1,0:T(8,128)}, u32[]{:S(2)}, u32[]{:S(2)}) collective-permute-start(f32[96,1024]{1,0:T(8,128)} %get-tuple-element.27), channel_id=1, source_target_pairs={{0,128},{128,256},{256,384},{384,0},{1,129},{129,257},{257,385},{3... | collective-permute-start | bytes 1179656 | tf_op jit(solution)/shard_map/ppermute | solution.py:32
  29.2 4.5 %collective-permute-start.2 = (f32[96,1024]{1,0:T(8,128)}, f32[96,1024]{1,0:T(8,128)S(1)}, u32[]{:S(2)}, u32[]{:S(2)}) collective-permute-start(f32[96,1024]{1,0:T(8,128)} %get-tuple-element.29), channel_id=1, source_target_pairs={{0,256},{128,384},{256,0},{384,128},{1,257},{129,385},{257,1},{385... | collective-permute-start | bytes 1179656 | tf_op jit(solution)/shard_map/ppermute | solution.py:32
  33.7 3.0 %collective-permute-start.3 = (f32[96,1024]{1,0:T(8,128)}, f32[96,1024]{1,0:T(8,128)S(1)}, u32[]{:S(2)}, u32[]{:S(2)}) collective-permute-start(f32[96,1024]{1,0:T(8,128)} %get-tuple-element.26), channel_id=1, source_target_pairs={{0,384},{128,0},{256,128},{384,256},{1,385},{129,1},{257,129},{385... | collective-permute-start | bytes 1179656 | tf_op jit(solution)/shard_map/ppermute | solution.py:32
  38.6 4.2 %all-to-all-start.1 = ((f32[4,64,512]{2,1,0:T(8,128)}), f32[4,64,512]{2,1,0:T(8,128)S(1)}, u32[]{:S(2)}, u32[]{:S(2)}) async-start(f32[4,64,512]{2,1,0:T(8,128)} %broadcast_in_dim.153), calls=%async_computation.1 | async-start | bytes 1048576 | tf_op jit(solution)/shard_map/all_to_all | solution.py:15
  44.1 5.2 %collective-permute-done.2 = f32[96,1024]{1,0:T(8,128)S(1)} collective-permute-done((f32[96,1024]{1,0:T(8,128)}, f32[96,1024]{1,0:T(8,128)S(1)}, u32[]{:S(2)}, u32[]{:S(2)}) %collective-permute-start.2) | collective-permute-done | bytes 393248 | tf_op jit(solution)/shard_map/ppermute | solution.py:32
  50.0 6.5 %collective-permute-start = (f32[256,512]{1,0:T(8,128)S(1)}, f32[256,512]{1,0:T(8,128)S(1)}, u32[]{:S(2)}, u32[]{:S(2)}) collective-permute-start(f32[256,512]{1,0:T(8,128)S(1)} %bitcast.53), channel_id=1, source_target_pairs={{0,1},{1,0},{2,3},{3,2},{4,5},{5,4},{6,7},{7,6},{8,9},{9,8},{10,11... | collective-permute-start | bytes 1572872 | tf_op jit(solution)/shard_map/ppermute | solution.py:64
  60.0 3.2 %collective-permute-start.6 = (f32[64,1024]{1,0:T(8,128)S(1)}, f32[64,1024]{1,0:T(8,128)S(1)}, u32[]{:S(2)}, u32[]{:S(2)}) collective-permute-start(f32[64,1024]{1,0:T(8,128)S(1)} %get-tuple-element.31), channel_id=1, source_target_pairs={{0,16},{1,113},{8,24},{9,121},{16,32},{17,1},{24,40},{25,9},{32,48... | collective-permute-start | bytes 786440 | tf_op jit(solution)/shard_map/ppermute | solution.py:28
  63.2 2.9 %collective-permute-start.5 = (f32[64,1024]{1,0:T(8,128)S(1)}, f32[64,1024]{1,0:T(8,128)S(1)}, u32[]{:S(2)}, u32[]{:S(2)}) collective-permute-start(f32[64,1024]{1,0:T(8,128)S(1)} %get-tuple-element.32), channel_id=1, source_target_pairs={{0,120},{8,0},{16,8},{24,16},{32,24},{40,32},{48,40},{56,48},{64,5... | collective-permute-start | bytes 786440 | tf_op jit(solution)/shard_map/ppermute | solution.py:23
  66.1 2.3 %collective-permute-start.4 = (f32[64,1024]{1,0:T(8,128)S(1)}, f32[64,1024]{1,0:T(8,128)S(1)}, u32[]{:S(2)}, u32[]{:S(2)}) collective-permute-start(f32[64,1024]{1,0:T(8,128)S(1)} %get-tuple-element.30), channel_id=1, source_target_pairs={{0,8},{8,16},{16,24},{24,32},{32,40},{40,48},{48,56},{56,64},{64,7... | collective-permute-start | bytes 786440 | tf_op jit(solution)/shard_map/ppermute | solution.py:23
  69.5 2.9 %collective-permute-done.6 = f32[64,1024]{1,0:T(8,128)S(1)} collective-permute-done((f32[64,1024]{1,0:T(8,128)S(1)}, f32[64,1024]{1,0:T(8,128)S(1)}, u32[]{:S(2)}, u32[]{:S(2)}) %collective-permute-start.6) | collective-permute-done | bytes 262176 | tf_op jit(solution)/shard_map/ppermute | solution.py:28
  72.4 3.9 %collective-permute-done.5 = f32[64,1024]{1,0:T(8,128)S(1)} collective-permute-done((f32[64,1024]{1,0:T(8,128)S(1)}, f32[64,1024]{1,0:T(8,128)S(1)}, u32[]{:S(2)}, u32[]{:S(2)}) %collective-permute-start.5) | collective-permute-done | bytes 262176 | tf_op jit(solution)/shard_map/ppermute | solution.py:23
  76.8 9.1 %collective-permute-start.9 = (f32[16,1024]{1,0:T(8,128)S(1)}, f32[16,1024]{1,0:T(8,128)S(1)}, u32[]{:S(2)}, u32[]{:S(2)}) collective-permute-start(f32[16,1024]{1,0:T(8,128)S(1)} %get-tuple-element.34), channel_id=1, source_target_pairs={{0,64},{8,72},{16,80},{24,88},{32,96},{40,104},{48,112},{56,120},{... | collective-permute-start | bytes 196616 | tf_op jit(solution)/shard_map/ppermute | solution.py:23
  85.9 3.3 %collective-permute-start.8 = (f32[16,1024]{1,0:T(8,128)S(1)}, f32[16,1024]{1,0:T(8,128)S(1)}, u32[]{:S(2)}, u32[]{:S(2)}) collective-permute-start(f32[16,1024]{1,0:T(8,128)S(1)} %get-tuple-element.35), channel_id=1, source_target_pairs={{0,96},{8,104},{16,112},{24,120},{32,0},{40,8},{48,16},{56,24},{64... | collective-permute-start | bytes 196616 | tf_op jit(solution)/shard_map/ppermute | solution.py:23
  89.1 5.9 %collective-permute-start.7 = (f32[16,1024]{1,0:T(8,128)S(1)}, f32[16,1024]{1,0:T(8,128)S(1)}, u32[]{:S(2)}, u32[]{:S(2)}) collective-permute-start(f32[16,1024]{1,0:T(8,128)S(1)} %get-tuple-element.33), channel_id=1, source_target_pairs={{0,32},{8,40},{16,48},{24,56},{32,64},{40,72},{48,80},{56,88},{64,... | collective-permute-start | bytes 196616 | tf_op jit(solution)/shard_map/ppermute | solution.py:23
  95.3 4.8 %collective-permute-done.8 = f32[16,1024]{1,0:T(8,128)S(1)} collective-permute-done((f32[16,1024]{1,0:T(8,128)S(1)}, f32[16,1024]{1,0:T(8,128)S(1)}, u32[]{:S(2)}, u32[]{:S(2)}) %collective-permute-start.8) | collective-permute-done | bytes 65568 | tf_op jit(solution)/shard_map/ppermute | solution.py:23
  101.1 8.1 %all-to-all-start.2 = ((f32[32,3,16]{2,1,0:T(4,128)}), f32[32,3,16]{2,1,0:T(4,128)S(1)}, u32[]{:S(2)}, u32[]{:S(2)}) async-start(f32[32,3,16]{2,1,0:T(4,128)} %broadcast_in_dim.171), calls=%async_computation.2 | async-start | bytes 131072 | tf_op jit(solution)/shard_map/all_to_all | solution.py:15
  109.3 7.4 %all-to-all-done.2 = f32[32,3,16]{2,1,0:T(4,128)S(1)} async-done(((f32[32,3,16]{2,1,0:T(4,128)}), f32[32,3,16]{2,1,0:T(4,128)S(1)}, u32[]{:S(2)}, u32[]{:S(2)}) %all-to-all-start.2) | async-done | bytes 6176 | tf_op jit(solution)/shard_map/all_to_all | solution.py:15
  117.6 8.0 %all-to-all-start.3 = ((f32[4,16,1024]{2,1,0:T(8,128)}), f32[4,16,1024]{2,1,0:T(8,128)S(1)}, u32[]{:S(2)}, u32[]{:S(2)}) async-start(f32[4,16,1024]{2,1,0:T(8,128)} %broadcast_in_dim.172), calls=%async_computation.3 | async-start | bytes 524288 | tf_op jit(solution)/shard_map/all_to_all | solution.py:15
  125.7 17.7 %all-to-all-done.3 = f32[4,16,1024]{2,1,0:T(8,128)S(1)} async-done(((f32[4,16,1024]{2,1,0:T(8,128)}), f32[4,16,1024]{2,1,0:T(8,128)S(1)}, u32[]{:S(2)}, u32[]{:S(2)}) %all-to-all-start.3) | async-done | bytes 262176 | tf_op jit(solution)/shard_map/all_to_all | solution.py:15
  145.3 1.9 collective-permute-start.11
  147.3 4.6 %collective-permute-start.10 = (f32[64,1024]{1,0:T(8,128)S(1)}, f32[64,1024]{1,0:T(8,128)S(1)}, u32[]{:S(2)}, u32[]{:S(2)}) collective-permute-start(f32[64,1024]{1,0:T(8,128)S(1)} %bitcast.59), channel_id=1, source_target_pairs={{0,120},{8,0},{16,8},{24,16},{32,24},{40,32},{48,40},{56,48},{64,5... | collective-permute-start | bytes 786440 | tf_op jit(solution)/shard_map/ppermute | solution.py:23
  153.7 8.1 %collective-permute-done.10 = f32[64,1024]{1,0:T(8,128)S(1)} collective-permute-done((f32[64,1024]{1,0:T(8,128)S(1)}, f32[64,1024]{1,0:T(8,128)S(1)}, u32[]{:S(2)}, u32[]{:S(2)}) %collective-permute-start.10) | collective-permute-done | bytes 262176 | tf_op jit(solution)/shard_map/ppermute | solution.py:23
  165.1 3.9 %all-to-all-start.4 = ((f32[32,16,384]{2,1,0:T(8,128)}), f32[32,16,384]{2,1,0:T(8,128)S(1)}, u32[]{:S(2)}, u32[]{:S(2)}) async-start(f32[32,16,384]{2,1,0:T(8,128)} %bitcast.14), calls=%async_computation.4 | async-start | bytes 1572864 | tf_op jit(solution)/shard_map/all_to_all | solution.py:15
  171.9 3.5 %collective-permute-start.13 = (f32[96,1024]{1,0:T(8,128)}, f32[96,1024]{1,0:T(8,128)}, u32[]{:S(2)}, u32[]{:S(2)}) collective-permute-start(f32[96,1024]{1,0:T(8,128)} %get-tuple-element.25), channel_id=1, source_target_pairs={{0,128},{128,256},{256,384},{384,0},{1,129},{129,257},{257,385},{3... | collective-permute-start | bytes 1179656 | tf_op jit(solution)/shard_map/ppermute | solution.py:32
  175.4 3.2 %collective-permute-start.14 = (f32[96,1024]{1,0:T(8,128)}, f32[96,1024]{1,0:T(8,128)}, u32[]{:S(2)}, u32[]{:S(2)}) collective-permute-start(f32[96,1024]{1,0:T(8,128)} %get-tuple-element.24), channel_id=1, source_target_pairs={{0,384},{128,0},{256,128},{384,256},{1,385},{129,1},{257,129},{385... | collective-permute-start | bytes 1179656 | tf_op jit(solution)/shard_map/ppermute | solution.py:32
  179.1 3.6 %collective-permute-start.15 = (f32[96,1024]{1,0:T(8,128)S(1)}, f32[96,1024]{1,0:T(8,128)}, u32[]{:S(2)}, u32[]{:S(2)}) collective-permute-start(f32[96,1024]{1,0:T(8,128)S(1)} %get-tuple-element.23), channel_id=1, source_target_pairs={{0,256},{128,384},{256,0},{384,128},{1,257},{129,385},{257,1},{385... | collective-permute-start | bytes 1179656 | tf_op jit(solution)/shard_map/ppermute | solution.py:32
  184.1 5.8 %all-to-all-start.5 = ((f32[16,1,512]{2,1,0:T(1,128)}), f32[16,1,512]{2,1,0:T(1,128)S(1)}, u32[]{:S(2)}, u32[]{:S(2)}) async-start(f32[16,1,512]{2,1,0:T(1,128)} %reshape.250), calls=%async_computation.5 | async-start | bytes 65536 | tf_op jit(solution)/shard_map/all_to_all | solution.py:15
  193.6 7.8 %all-to-all-done.5 = f32[16,1,512]{2,1,0:T(1,128)S(1)} async-done(((f32[16,1,512]{2,1,0:T(1,128)}), f32[16,1,512]{2,1,0:T(1,128)S(1)}, u32[]{:S(2)}, u32[]{:S(2)}) %all-to-all-start.5) | async-done | bytes 32800 | tf_op jit(solution)/shard_map/all_to_all | solution.py:15
  202.4 6.2 %all-to-all-start.6 = ((f32[8,1,6144]{2,1,0:T(1,128)}), f32[8,1,6144]{2,1,0:T(1,128)S(1)}, u32[]{:S(2)}, u32[]{:S(2)}) async-start(f32[8,1,6144]{2,1,0:T(1,128)} %broadcast_in_dim.175), calls=%async_computation.6 | async-start | bytes 393216 | tf_op jit(solution)/shard_map/all_to_all | solution.py:15
  210.2 4.3 %all-to-all-done.6 = f32[8,1,6144]{2,1,0:T(1,128)S(1)} async-done(((f32[8,1,6144]{2,1,0:T(1,128)}), f32[8,1,6144]{2,1,0:T(1,128)S(1)}, u32[]{:S(2)}, u32[]{:S(2)}) %all-to-all-start.6) | async-done | bytes 196640 | tf_op jit(solution)/shard_map/all_to_all | solution.py:15
  (97 shorter events, 32.3 us)
Async XLA Ops:
  0.6 0.9 copy-start
  4.7 33.1 %all-to-all-start = ((f32[64,1,512]{2,1,0:T(1,128)}), f32[64,1,512]{2,1,0:T(1,128)S(1)}, u32[]{:S(2)}, u32[]{:S(2)}) async-start(f32[64,1,512]{2,1,0:T(1,128)} %copy.21), calls=%async_computation | async-start | bytes 262144 | tf_op jit(solution)/shard_map/all_to_all | solution.py:15
  26.3 16.8 %collective-permute-start.1 = (f32[96,1024]{1,0:T(8,128)}, f32[96,1024]{1,0:T(8,128)}, u32[]{:S(2)}, u32[]{:S(2)}) collective-permute-start(f32[96,1024]{1,0:T(8,128)} %get-tuple-element.27), channel_id=1, source_target_pairs={{0,128},{128,256},{256,384},{384,0},{1,129},{129,257},{257,385},{3... | collective-permute-start | bytes 1179656 | tf_op jit(solution)/shard_map/ppermute | solution.py:32
  29.2 20.1 %collective-permute-start.2 = (f32[96,1024]{1,0:T(8,128)}, f32[96,1024]{1,0:T(8,128)S(1)}, u32[]{:S(2)}, u32[]{:S(2)}) collective-permute-start(f32[96,1024]{1,0:T(8,128)} %get-tuple-element.29), channel_id=1, source_target_pairs={{0,256},{128,384},{256,0},{384,128},{1,257},{129,385},{257,1},{385... | collective-permute-start | bytes 1179656 | tf_op jit(solution)/shard_map/ppermute | solution.py:32
  33.7 23.2 %collective-permute-start.3 = (f32[96,1024]{1,0:T(8,128)}, f32[96,1024]{1,0:T(8,128)S(1)}, u32[]{:S(2)}, u32[]{:S(2)}) collective-permute-start(f32[96,1024]{1,0:T(8,128)} %get-tuple-element.26), channel_id=1, source_target_pairs={{0,384},{128,0},{256,128},{384,256},{1,385},{129,1},{257,129},{385... | collective-permute-start | bytes 1179656 | tf_op jit(solution)/shard_map/ppermute | solution.py:32
  38.6 11.4 %all-to-all-start.1 = ((f32[4,64,512]{2,1,0:T(8,128)}), f32[4,64,512]{2,1,0:T(8,128)S(1)}, u32[]{:S(2)}, u32[]{:S(2)}) async-start(f32[4,64,512]{2,1,0:T(8,128)} %broadcast_in_dim.153), calls=%async_computation.1 | async-start | bytes 1048576 | tf_op jit(solution)/shard_map/all_to_all | solution.py:15
  50.0 8.0 %collective-permute-start = (f32[256,512]{1,0:T(8,128)S(1)}, f32[256,512]{1,0:T(8,128)S(1)}, u32[]{:S(2)}, u32[]{:S(2)}) collective-permute-start(f32[256,512]{1,0:T(8,128)S(1)} %bitcast.53), channel_id=1, source_target_pairs={{0,1},{1,0},{2,3},{3,2},{4,5},{5,4},{6,7},{7,6},{8,9},{9,8},{10,11... | collective-permute-start | bytes 1572872 | tf_op jit(solution)/shard_map/ppermute | solution.py:64
  60.0 12.4 %collective-permute-start.6 = (f32[64,1024]{1,0:T(8,128)S(1)}, f32[64,1024]{1,0:T(8,128)S(1)}, u32[]{:S(2)}, u32[]{:S(2)}) collective-permute-start(f32[64,1024]{1,0:T(8,128)S(1)} %get-tuple-element.31), channel_id=1, source_target_pairs={{0,16},{1,113},{8,24},{9,121},{16,32},{17,1},{24,40},{25,9},{32,48... | collective-permute-start | bytes 786440 | tf_op jit(solution)/shard_map/ppermute | solution.py:28
  63.2 13.1 %collective-permute-start.5 = (f32[64,1024]{1,0:T(8,128)S(1)}, f32[64,1024]{1,0:T(8,128)S(1)}, u32[]{:S(2)}, u32[]{:S(2)}) collective-permute-start(f32[64,1024]{1,0:T(8,128)S(1)} %get-tuple-element.32), channel_id=1, source_target_pairs={{0,120},{8,0},{16,8},{24,16},{32,24},{40,32},{48,40},{56,48},{64,5... | collective-permute-start | bytes 786440 | tf_op jit(solution)/shard_map/ppermute | solution.py:23
  66.1 10.5 %collective-permute-start.4 = (f32[64,1024]{1,0:T(8,128)S(1)}, f32[64,1024]{1,0:T(8,128)S(1)}, u32[]{:S(2)}, u32[]{:S(2)}) collective-permute-start(f32[64,1024]{1,0:T(8,128)S(1)} %get-tuple-element.30), channel_id=1, source_target_pairs={{0,8},{8,16},{16,24},{24,32},{32,40},{40,48},{48,56},{56,64},{64,7... | collective-permute-start | bytes 786440 | tf_op jit(solution)/shard_map/ppermute | solution.py:23
  76.8 18.5 %collective-permute-start.9 = (f32[16,1024]{1,0:T(8,128)S(1)}, f32[16,1024]{1,0:T(8,128)S(1)}, u32[]{:S(2)}, u32[]{:S(2)}) collective-permute-start(f32[16,1024]{1,0:T(8,128)S(1)} %get-tuple-element.34), channel_id=1, source_target_pairs={{0,64},{8,72},{16,80},{24,88},{32,96},{40,104},{48,112},{56,120},{... | collective-permute-start | bytes 196616 | tf_op jit(solution)/shard_map/ppermute | solution.py:23
  85.9 14.3 %collective-permute-start.8 = (f32[16,1024]{1,0:T(8,128)S(1)}, f32[16,1024]{1,0:T(8,128)S(1)}, u32[]{:S(2)}, u32[]{:S(2)}) collective-permute-start(f32[16,1024]{1,0:T(8,128)S(1)} %get-tuple-element.35), channel_id=1, source_target_pairs={{0,96},{8,104},{16,112},{24,120},{32,0},{40,8},{48,16},{56,24},{64... | collective-permute-start | bytes 196616 | tf_op jit(solution)/shard_map/ppermute | solution.py:23
  89.1 11.0 %collective-permute-start.7 = (f32[16,1024]{1,0:T(8,128)S(1)}, f32[16,1024]{1,0:T(8,128)S(1)}, u32[]{:S(2)}, u32[]{:S(2)}) collective-permute-start(f32[16,1024]{1,0:T(8,128)S(1)} %get-tuple-element.33), channel_id=1, source_target_pairs={{0,32},{8,40},{16,48},{24,56},{32,64},{40,72},{48,80},{56,88},{64,... | collective-permute-start | bytes 196616 | tf_op jit(solution)/shard_map/ppermute | solution.py:23
  101.1 15.5 %all-to-all-start.2 = ((f32[32,3,16]{2,1,0:T(4,128)}), f32[32,3,16]{2,1,0:T(4,128)S(1)}, u32[]{:S(2)}, u32[]{:S(2)}) async-start(f32[32,3,16]{2,1,0:T(4,128)} %broadcast_in_dim.171), calls=%async_computation.2 | async-start | bytes 131072 | tf_op jit(solution)/shard_map/all_to_all | solution.py:15
  117.6 25.8 %all-to-all-start.3 = ((f32[4,16,1024]{2,1,0:T(8,128)}), f32[4,16,1024]{2,1,0:T(8,128)S(1)}, u32[]{:S(2)}, u32[]{:S(2)}) async-start(f32[4,16,1024]{2,1,0:T(8,128)} %broadcast_in_dim.172), calls=%async_computation.3 | async-start | bytes 524288 | tf_op jit(solution)/shard_map/all_to_all | solution.py:15
  143.4 10.3 %collective-permute-start.12 = (f32[64,1024]{1,0:T(8,128)S(1)}, f32[64,1024]{1,0:T(8,128)S(1)}, u32[]{:S(2)}, u32[]{:S(2)}) collective-permute-start(f32[64,1024]{1,0:T(8,128)S(1)} %bitcast.57), channel_id=1, source_target_pairs={{0,8},{8,16},{16,24},{24,32},{32,40},{40,48},{48,56},{56,64},{64,7... | collective-permute-start | bytes 786440 | tf_op jit(solution)/shard_map/ppermute | solution.py:23
  145.3 8.4 %collective-permute-start.11 = (f32[64,1024]{1,0:T(8,128)S(1)}, f32[64,1024]{1,0:T(8,128)S(1)}, u32[]{:S(2)}, u32[]{:S(2)}) collective-permute-start(f32[64,1024]{1,0:T(8,128)S(1)} %bitcast.58), channel_id=1, source_target_pairs={{0,16},{1,113},{8,24},{9,121},{16,32},{17,1},{24,40},{25,9},{32,48... | collective-permute-start | bytes 786440 | tf_op jit(solution)/shard_map/ppermute | solution.py:28
  147.3 14.6 %collective-permute-start.10 = (f32[64,1024]{1,0:T(8,128)S(1)}, f32[64,1024]{1,0:T(8,128)S(1)}, u32[]{:S(2)}, u32[]{:S(2)}) collective-permute-start(f32[64,1024]{1,0:T(8,128)S(1)} %bitcast.59), channel_id=1, source_target_pairs={{0,120},{8,0},{16,8},{24,16},{32,24},{40,32},{48,40},{56,48},{64,5... | collective-permute-start | bytes 786440 | tf_op jit(solution)/shard_map/ppermute | solution.py:23
  153.7 11.3 %copy-start.2 = (f32[64,1024]{1,0:T(8,128)}, f32[64,1024]{1,0:T(8,128)S(1)}, u32[]{:S(2)}) copy-start(f32[64,1024]{1,0:T(8,128)S(1)} %collective-permute-done.11) | copy-start | bytes 786436
  161.8 3.3 %copy-start.3 = (f32[64,1024]{1,0:T(8,128)}, f32[64,1024]{1,0:T(8,128)S(1)}, u32[]{:S(2)}) copy-start(f32[64,1024]{1,0:T(8,128)S(1)} %collective-permute-done.10) | copy-start | bytes 786436
  165.1 18.3 %all-to-all-start.4 = ((f32[32,16,384]{2,1,0:T(8,128)}), f32[32,16,384]{2,1,0:T(8,128)S(1)}, u32[]{:S(2)}, u32[]{:S(2)}) async-start(f32[32,16,384]{2,1,0:T(8,128)} %bitcast.14), calls=%async_computation.4 | async-start | bytes 1572864 | tf_op jit(solution)/shard_map/all_to_all | solution.py:15
  171.9 19.7 %collective-permute-start.13 = (f32[96,1024]{1,0:T(8,128)}, f32[96,1024]{1,0:T(8,128)}, u32[]{:S(2)}, u32[]{:S(2)}) collective-permute-start(f32[96,1024]{1,0:T(8,128)} %get-tuple-element.25), channel_id=1, source_target_pairs={{0,128},{128,256},{256,384},{384,0},{1,129},{129,257},{257,385},{3... | collective-permute-start | bytes 1179656 | tf_op jit(solution)/shard_map/ppermute | solution.py:32
  175.4 17.2 %collective-permute-start.14 = (f32[96,1024]{1,0:T(8,128)}, f32[96,1024]{1,0:T(8,128)}, u32[]{:S(2)}, u32[]{:S(2)}) collective-permute-start(f32[96,1024]{1,0:T(8,128)} %get-tuple-element.24), channel_id=1, source_target_pairs={{0,384},{128,0},{256,128},{384,256},{1,385},{129,1},{257,129},{385... | collective-permute-start | bytes 1179656 | tf_op jit(solution)/shard_map/ppermute | solution.py:32
  179.1 29.5 %collective-permute-start.15 = (f32[96,1024]{1,0:T(8,128)S(1)}, f32[96,1024]{1,0:T(8,128)}, u32[]{:S(2)}, u32[]{:S(2)}) collective-permute-start(f32[96,1024]{1,0:T(8,128)S(1)} %get-tuple-element.23), channel_id=1, source_target_pairs={{0,256},{128,384},{256,0},{384,128},{1,257},{129,385},{257,1},{385... | collective-permute-start | bytes 1179656 | tf_op jit(solution)/shard_map/ppermute | solution.py:32
  184.1 17.3 %all-to-all-start.5 = ((f32[16,1,512]{2,1,0:T(1,128)}), f32[16,1,512]{2,1,0:T(1,128)S(1)}, u32[]{:S(2)}, u32[]{:S(2)}) async-start(f32[16,1,512]{2,1,0:T(1,128)} %reshape.250), calls=%async_computation.5 | async-start | bytes 65536 | tf_op jit(solution)/shard_map/all_to_all | solution.py:15
  202.4 12.1 %all-to-all-start.6 = ((f32[8,1,6144]{2,1,0:T(1,128)}), f32[8,1,6144]{2,1,0:T(1,128)S(1)}, u32[]{:S(2)}, u32[]{:S(2)}) async-start(f32[8,1,6144]{2,1,0:T(1,128)} %broadcast_in_dim.175), calls=%async_computation.6 | async-start | bytes 393216 | tf_op jit(solution)/shard_map/all_to_all | solution.py:15
  209.6 5.6 %copy-start.1 = (f32[96,4096]{1,0:T(8,128)}, f32[96,4096]{1,0:T(8,128)S(1)}, u32[]{:S(2)}) copy-start(f32[96,4096]{1,0:T(8,128)S(1)} %constant_dynamic-update-slice_fusion.2) | copy-start | bytes 4718596

commit v18 on v16

--- a/solution.py
+++ b/solution.py
@@ -117,9 +117,11 @@
     grad = onehot - shifted * scale[:, None]
 
     own = spread(grad, "h", 4).reshape(64, quarter)
-    grads = jnp.concatenate([own, shift_z(own, -1), shift_far(own), shift_z(own, 1)], axis=0)
+    after, far, ahead = shift_z(own, -1), shift_far(own), shift_z(own, 1)
+    grads = jnp.concatenate([own, after, far, ahead], axis=0)
 
-    grad_rows = dot(grads, head, (1, 1))
+    early = lax.optimization_barrier(dot(jnp.concatenate([own, far, ahead], axis=0), head, (1, 1)))
+    grad_rows = jnp.concatenate([early[:64], dot(after, head, (1, 1)), early[64:]], axis=0)
     leaving = dot(deliver, grad_rows, (1, 0), GRAD).reshape(32, 16, wide)
     summed = jnp.sum(swap(leaving, XYC), axis=0)
 

time: 216 us -> 215 us (level)
    dot_general x7 -> x8, matrix products: 8.44 us -> 9.91 us  [dot(): lax.dot_general(a, b, dims, precision=precision, preferred_element_type=j...]
  transfers between devices with their start and end apart: 21 -> 21, of which waited for: 15 -> 15; matrix products, arithmetic and copies ran while one was open for 8% -> 9% of each run, Pallas kernels for 0% -> 0%
where the time goes in v18:
time: 215 us; the launch traced here: 214 us
  starting transfers between devices  111 us (52%)
  waiting for transfers between devices  70.5 us (33%)
  local copies, waits for them, and re-layouts  16.7 us (8%)
  matrix products  9.91 us (5%)
  other arithmetic  3.59 us (2%)
  between operations  2.6 us (1%)
    all_to_all x8, starting transfers between devices, swap(): return lax.all_to_all(blocks, axes, split_axis=0, concat_axis=0, tiled=True)  63.4 us
    all_to_all x8, waiting for transfers between devices, swap(): return lax.all_to_all(blocks, axes, split_axis=0, concat_axis=0, tiled=True)  50.5 us
    ppermute x6, starting transfers between devices, shift_x(): return lax.ppermute(block, 'x', [(i, (i + step) % 4) for i in range(4)])  20.6 us
    ppermute x4, starting transfers between devices, shift_z(): return lax.ppermute(block, Z, [(i, (i + step) % 16) for i in range(16)])  14.9 us
    dot_general x8, matrix products, dot(): lax.dot_general(a, b, dims, precision=precision, preferred_element_type=j...  9.91 us
    ppermute x2, waiting for transfers between devices, shift_far(): return lax.ppermute(block, ('h', 'l', 'c'), pairs)  7.94 us
    ppermute x1, starting transfers between devices, on_device(): slots_other = lax.ppermute(slots, 'c', [(0, 1), (1, 0)])  6.47 us
    ppermute x4, waiting for transfers between devices, shift_z(): return lax.ppermute(block, Z, [(i, (i + step) % 16) for i in range(16)])  6.27 us
  transfers between devices with their start and end apart: 21, of which 15 were waited for; matrix products, arithmetic and copies ran while one was open for 9% of the time, Pallas kernels for 0%

profile of v18, /device:TPU:1, one launch (start us, length us, event | category | flops | bytes accessed | tf_op | source)
XLA Modules:
  0.0 214.2 jit_solution(1820045942216455215)
XLA Ops:
  4.7 19.1 %all-to-all-start = ((f32[64,1,512]{2,1,0:T(1,128)}), f32[64,1,512]{2,1,0:T(1,128)S(1)}, u32[]{:S(2)}, u32[]{:S(2)}) async-start(f32[64,1,512]{2,1,0:T(1,128)} %copy.21), calls=%async_computation | async-start | bytes 262144 | tf_op jit(solution)/shard_map/all_to_all | solution.py:15
  23.9 2.4 %constant_dynamic-slice_fusion = (f32[96,1024]{1,0:T(8,128)}, f32[96,1024]{1,0:T(8,128)}, f32[96,1024]{1,0:T(8,128)S(1)}, f32[96,1024]{1,0:T(8,128)}) fusion(f32[96,4096]{1,0:T(8,128)} %param.6, s32[]{:T(128)S(6)} %select_n.294, s32[]{:T(128)S(6)} %select_n.286, s32[]{:T(128)S(6)} %select_n.264, s32[]{:T(128)S(6)} %select_n.290), kind=kLoop, calls=%fused_computation.79 | loop fusion | bytes 3145744 | tf_op jit(solution)/shard_map/dynamic_slice | solution.py:56
  26.3 2.9 %collective-permute-start.1 = (f32[96,1024]{1,0:T(8,128)}, f32[96,1024]{1,0:T(8,128)}, u32[]{:S(2)}, u32[]{:S(2)}) collective-permute-start(f32[96,1024]{1,0:T(8,128)} %get-tuple-element.25), channel_id=1, source_target_pairs={{0,128},{128,256},{256,384},{384,0},{1,129},{129,257},{257,385},{3... | collective-permute-start | bytes 1179656 | tf_op jit(solution)/shard_map/ppermute | solution.py:32
  29.2 4.5 %collective-permute-start.2 = (f32[96,1024]{1,0:T(8,128)}, f32[96,1024]{1,0:T(8,128)S(1)}, u32[]{:S(2)}, u32[]{:S(2)}) collective-permute-start(f32[96,1024]{1,0:T(8,128)} %get-tuple-element.27), channel_id=1, source_target_pairs={{0,256},{128,384},{256,0},{384,128},{1,257},{129,385},{257,1},{385... | collective-permute-start | bytes 1179656 | tf_op jit(solution)/shard_map/ppermute | solution.py:32
  33.7 3.0 %collective-permute-start.3 = (f32[96,1024]{1,0:T(8,128)}, f32[96,1024]{1,0:T(8,128)S(1)}, u32[]{:S(2)}, u32[]{:S(2)}) collective-permute-start(f32[96,1024]{1,0:T(8,128)} %get-tuple-element.24), channel_id=1, source_target_pairs={{0,384},{128,0},{256,128},{384,256},{1,385},{129,1},{257,129},{385... | collective-permute-start | bytes 1179656 | tf_op jit(solution)/shard_map/ppermute | solution.py:32
  38.6 4.2 %all-to-all-start.1 = ((f32[4,64,512]{2,1,0:T(8,128)}), f32[4,64,512]{2,1,0:T(8,128)S(1)}, u32[]{:S(2)}, u32[]{:S(2)}) async-start(f32[4,64,512]{2,1,0:T(8,128)} %broadcast_in_dim.153), calls=%async_computation.1 | async-start | bytes 1048576 | tf_op jit(solution)/shard_map/all_to_all | solution.py:15
  44.1 5.2 %collective-permute-done.2 = f32[96,1024]{1,0:T(8,128)S(1)} collective-permute-done((f32[96,1024]{1,0:T(8,128)}, f32[96,1024]{1,0:T(8,128)S(1)}, u32[]{:S(2)}, u32[]{:S(2)}) %collective-permute-start.2) | collective-permute-done | bytes 393248 | tf_op jit(solution)/shard_map/ppermute | solution.py:32
  50.0 6.5 %collective-permute-start = (f32[256,512]{1,0:T(8,128)S(1)}, f32[256,512]{1,0:T(8,128)S(1)}, u32[]{:S(2)}, u32[]{:S(2)}) collective-permute-start(f32[256,512]{1,0:T(8,128)S(1)} %bitcast.56), channel_id=1, source_target_pairs={{0,1},{1,0},{2,3},{3,2},{4,5},{5,4},{6,7},{7,6},{8,9},{9,8},{10,11... | collective-permute-start | bytes 1572872 | tf_op jit(solution)/shard_map/ppermute | solution.py:64
  60.0 3.2 %collective-permute-start.6 = (f32[64,1024]{1,0:T(8,128)S(1)}, f32[64,1024]{1,0:T(8,128)S(1)}, u32[]{:S(2)}, u32[]{:S(2)}) collective-permute-start(f32[64,1024]{1,0:T(8,128)S(1)} %get-tuple-element.29), channel_id=1, source_target_pairs={{0,16},{1,113},{8,24},{9,121},{16,32},{17,1},{24,40},{25,9},{32,48... | collective-permute-start | bytes 786440 | tf_op jit(solution)/shard_map/ppermute | solution.py:28
  63.2 2.9 %collective-permute-start.5 = (f32[64,1024]{1,0:T(8,128)S(1)}, f32[64,1024]{1,0:T(8,128)S(1)}, u32[]{:S(2)}, u32[]{:S(2)}) collective-permute-start(f32[64,1024]{1,0:T(8,128)S(1)} %get-tuple-element.30), channel_id=1, source_target_pairs={{0,120},{8,0},{16,8},{24,16},{32,24},{40,32},{48,40},{56,48},{64,5... | collective-permute-start | bytes 786440 | tf_op jit(solution)/shard_map/ppermute | solution.py:23
  66.1 2.4 %collective-permute-start.4 = (f32[64,1024]{1,0:T(8,128)S(1)}, f32[64,1024]{1,0:T(8,128)S(1)}, u32[]{:S(2)}, u32[]{:S(2)}) collective-permute-start(f32[64,1024]{1,0:T(8,128)S(1)} %get-tuple-element.28), channel_id=1, source_target_pairs={{0,8},{8,16},{16,24},{24,32},{32,40},{40,48},{48,56},{56,64},{64,7... | collective-permute-start | bytes 786440 | tf_op jit(solution)/shard_map/ppermute | solution.py:23
  69.6 2.9 %collective-permute-done.6 = f32[64,1024]{1,0:T(8,128)S(1)} collective-permute-done((f32[64,1024]{1,0:T(8,128)S(1)}, f32[64,1024]{1,0:T(8,128)S(1)}, u32[]{:S(2)}, u32[]{:S(2)}) %collective-permute-start.6) | collective-permute-done | bytes 262176 | tf_op jit(solution)/shard_map/ppermute | solution.py:28
  72.4 3.9 %collective-permute-done.5 = f32[64,1024]{1,0:T(8,128)S(1)} collective-permute-done((f32[64,1024]{1,0:T(8,128)S(1)}, f32[64,1024]{1,0:T(8,128)S(1)}, u32[]{:S(2)}, u32[]{:S(2)}) %collective-permute-start.5) | collective-permute-done | bytes 262176 | tf_op jit(solution)/shard_map/ppermute | solution.py:23
  77.4 8.2 %all-to-all-start.2 = ((f32[4,16,1024]{2,1,0:T(8,128)}), f32[4,16,1024]{2,1,0:T(8,128)S(1)}, u32[]{:S(2)}, u32[]{:S(2)}) async-start(f32[4,16,1024]{2,1,0:T(8,128)} %bitcast.8), calls=%async_computation.2 | async-start | bytes 524288 | tf_op jit(solution)/shard_map/all_to_all | solution.py:15
  86.3 12.5 %all-to-all-done.2 = f32[4,16,1024]{2,1,0:T(8,128)S(1)} async-done(((f32[4,16,1024]{2,1,0:T(8,128)}), f32[4,16,1024]{2,1,0:T(8,128)S(1)}, u32[]{:S(2)}, u32[]{:S(2)}) %all-to-all-start.2) | async-done | bytes 262176 | tf_op jit(solution)/shard_map/all_to_all | solution.py:15
  99.8 12.4 %all-to-all-start.3 = ((f32[32,3,16]{2,1,0:T(4,128)}), f32[32,3,16]{2,1,0:T(4,128)S(1)}, u32[]{:S(2)}, u32[]{:S(2)}) async-start(f32[32,3,16]{2,1,0:T(4,128)} %broadcast_in_dim.171), calls=%async_computation.3 | async-start | bytes 131072 | tf_op jit(solution)/shard_map/all_to_all | solution.py:15
  112.2 7.4 %all-to-all-done.3 = f32[32,3,16]{2,1,0:T(4,128)S(1)} async-done(((f32[32,3,16]{2,1,0:T(4,128)}), f32[32,3,16]{2,1,0:T(4,128)S(1)}, u32[]{:S(2)}, u32[]{:S(2)}) %all-to-all-start.3) | async-done | bytes 6176 | tf_op jit(solution)/shard_map/all_to_all | solution.py:15
  120.5 3.8 %all-to-all-start.4 = ((f32[4,16,1024]{2,1,0:T(8,128)}), f32[4,16,1024]{2,1,0:T(8,128)S(1)}, u32[]{:S(2)}, u32[]{:S(2)}) async-start(f32[4,16,1024]{2,1,0:T(8,128)} %broadcast_in_dim.172), calls=%async_computation.4 | async-start | bytes 524288 | tf_op jit(solution)/shard_map/all_to_all | solution.py:15
  124.5 15.8 %all-to-all-done.4 = f32[4,16,1024]{2,1,0:T(8,128)S(1)} async-done(((f32[4,16,1024]{2,1,0:T(8,128)}), f32[4,16,1024]{2,1,0:T(8,128)S(1)}, u32[]{:S(2)}, u32[]{:S(2)}) %all-to-all-start.4) | async-done | bytes 262176 | tf_op jit(solution)/shard_map/all_to_all | solution.py:15
  140.2 6.3 %collective-permute-start.8 = (f32[64,1024]{1,0:T(8,128)S(1)}, f32[64,1024]{1,0:T(8,128)S(1)}, u32[]{:S(2)}, u32[]{:S(2)}) collective-permute-start(f32[64,1024]{1,0:T(8,128)S(1)} %bitcast.60), channel_id=1, source_target_pairs={{0,8},{8,16},{16,24},{24,32},{32,40},{40,48},{48,56},{56,64},{64,7... | collective-permute-start | bytes 786440 | tf_op jit(solution)/shard_map/ppermute | solution.py:23
  146.5 2.3 %collective-permute-start.7 = (f32[64,1024]{1,0:T(8,128)S(1)}, f32[64,1024]{1,0:T(8,128)S(1)}, u32[]{:S(2)}, u32[]{:S(2)}) collective-permute-start(f32[64,1024]{1,0:T(8,128)S(1)} %bitcast.61), channel_id=1, source_target_pairs={{0,16},{1,113},{8,24},{9,121},{16,32},{17,1},{24,40},{25,9},{32,48... | collective-permute-start | bytes 786440 | tf_op jit(solution)/shard_map/ppermute | solution.py:28
  148.9 3.4 %collective-permute-start.9 = (f32[64,1024]{1,0:T(8,128)S(1)}, f32[64,1024]{1,0:T(8,128)S(1)}, u32[]{:S(2)}, u32[]{:S(2)}) collective-permute-start(f32[64,1024]{1,0:T(8,128)S(1)} %bitcast.62), channel_id=1, source_target_pairs={{0,120},{8,0},{16,8},{24,16},{32,24},{40,32},{48,40},{56,48},{64,5... | collective-permute-start | bytes 786440 | tf_op jit(solution)/shard_map/ppermute | solution.py:23
  152.3 5.1 %collective-permute-done.7 = f32[64,1024]{1,0:T(8,128)S(1)} collective-permute-done((f32[64,1024]{1,0:T(8,128)S(1)}, f32[64,1024]{1,0:T(8,128)S(1)}, u32[]{:S(2)}, u32[]{:S(2)}) %collective-permute-start.7) | collective-permute-done | bytes 262176 | tf_op jit(solution)/shard_map/ppermute | solution.py:28
  159.2 2.0 collective-permute-done.9
  164.2 6.0 %all-to-all-start.5 = ((f32[32,16,384]{2,1,0:T(8,128)}), f32[32,16,384]{2,1,0:T(8,128)S(1)}, u32[]{:S(2)}, u32[]{:S(2)}) async-start(f32[32,16,384]{2,1,0:T(8,128)} %bitcast.15), calls=%async_computation.5 | async-start | bytes 1572864 | tf_op jit(solution)/shard_map/all_to_all | solution.py:15
  172.9 3.3 %collective-permute-start.10 = (f32[96,1024]{1,0:T(8,128)}, f32[96,1024]{1,0:T(8,128)}, u32[]{:S(2)}, u32[]{:S(2)}) collective-permute-start(f32[96,1024]{1,0:T(8,128)} %get-tuple-element.23), channel_id=1, source_target_pairs={{0,128},{128,256},{256,384},{384,0},{1,129},{129,257},{257,385},{3... | collective-permute-start | bytes 1179656 | tf_op jit(solution)/shard_map/ppermute | solution.py:32
  176.3 3.2 %collective-permute-start.11 = (f32[96,1024]{1,0:T(8,128)S(1)}, f32[96,1024]{1,0:T(8,128)}, u32[]{:S(2)}, u32[]{:S(2)}) collective-permute-start(f32[96,1024]{1,0:T(8,128)S(1)} %get-tuple-element.22), channel_id=1, source_target_pairs={{0,384},{128,0},{256,128},{384,256},{1,385},{129,1},{257,129},{385... | collective-permute-start | bytes 1179656 | tf_op jit(solution)/shard_map/ppermute | solution.py:32
  179.9 3.6 %collective-permute-start.12 = (f32[96,1024]{1,0:T(8,128)S(1)}, f32[96,1024]{1,0:T(8,128)}, u32[]{:S(2)}, u32[]{:S(2)}) collective-permute-start(f32[96,1024]{1,0:T(8,128)S(1)} %get-tuple-element.21), channel_id=1, source_target_pairs={{0,256},{128,384},{256,0},{384,128},{1,257},{129,385},{257,1},{385... | collective-permute-start | bytes 1179656 | tf_op jit(solution)/shard_map/ppermute | solution.py:32
  185.3 3.9 %all-to-all-start.6 = ((f32[16,1,512]{2,1,0:T(1,128)}), f32[16,1,512]{2,1,0:T(1,128)S(1)}, u32[]{:S(2)}, u32[]{:S(2)}) async-start(f32[16,1,512]{2,1,0:T(1,128)} %reshape.307), calls=%async_computation.6 | async-start | bytes 65536 | tf_op jit(solution)/shard_map/all_to_all | solution.py:15
  192.9 7.9 %all-to-all-done.6 = f32[16,1,512]{2,1,0:T(1,128)S(1)} async-done(((f32[16,1,512]{2,1,0:T(1,128)}), f32[16,1,512]{2,1,0:T(1,128)S(1)}, u32[]{:S(2)}, u32[]{:S(2)}) %all-to-all-start.6) | async-done | bytes 32800 | tf_op jit(solution)/shard_map/all_to_all | solution.py:15
  201.8 5.8 %all-to-all-start.7 = ((f32[8,1,6144]{2,1,0:T(1,128)}), f32[8,1,6144]{2,1,0:T(1,128)S(1)}, u32[]{:S(2)}, u32[]{:S(2)}) async-start(f32[8,1,6144]{2,1,0:T(1,128)} %broadcast_in_dim.175), calls=%async_computation.7 | async-start | bytes 393216 | tf_op jit(solution)/shard_map/all_to_all | solution.py:15
  209.1 4.3 %all-to-all-done.7 = f32[8,1,6144]{2,1,0:T(1,128)S(1)} async-done(((f32[8,1,6144]{2,1,0:T(1,128)}), f32[8,1,6144]{2,1,0:T(1,128)S(1)}, u32[]{:S(2)}, u32[]{:S(2)}) %all-to-all-start.7) | async-done | bytes 196640 | tf_op jit(solution)/shard_map/all_to_all | solution.py:15
  (96 shorter events, 31.5 us)
Async XLA Ops:
  0.6 0.9 copy-start
  4.7 33.1 %all-to-all-start = ((f32[64,1,512]{2,1,0:T(1,128)}), f32[64,1,512]{2,1,0:T(1,128)S(1)}, u32[]{:S(2)}, u32[]{:S(2)}) async-start(f32[64,1,512]{2,1,0:T(1,128)} %copy.21), calls=%async_computation | async-start | bytes 262144 | tf_op jit(solution)/shard_map/all_to_all | solution.py:15
  26.3 16.8 %collective-permute-start.1 = (f32[96,1024]{1,0:T(8,128)}, f32[96,1024]{1,0:T(8,128)}, u32[]{:S(2)}, u32[]{:S(2)}) collective-permute-start(f32[96,1024]{1,0:T(8,128)} %get-tuple-element.25), channel_id=1, source_target_pairs={{0,128},{128,256},{256,384},{384,0},{1,129},{129,257},{257,385},{3... | collective-permute-start | bytes 1179656 | tf_op jit(solution)/shard_map/ppermute | solution.py:32
  29.2 20.1 %collective-permute-start.2 = (f32[96,1024]{1,0:T(8,128)}, f32[96,1024]{1,0:T(8,128)S(1)}, u32[]{:S(2)}, u32[]{:S(2)}) collective-permute-start(f32[96,1024]{1,0:T(8,128)} %get-tuple-element.27), channel_id=1, source_target_pairs={{0,256},{128,384},{256,0},{384,128},{1,257},{129,385},{257,1},{385... | collective-permute-start | bytes 1179656 | tf_op jit(solution)/shard_map/ppermute | solution.py:32
  33.7 23.2 %collective-permute-start.3 = (f32[96,1024]{1,0:T(8,128)}, f32[96,1024]{1,0:T(8,128)S(1)}, u32[]{:S(2)}, u32[]{:S(2)}) collective-permute-start(f32[96,1024]{1,0:T(8,128)} %get-tuple-element.24), channel_id=1, source_target_pairs={{0,384},{128,0},{256,128},{384,256},{1,385},{129,1},{257,129},{385... | collective-permute-start | bytes 1179656 | tf_op jit(solution)/shard_map/ppermute | solution.py:32
  38.6 11.4 %all-to-all-start.1 = ((f32[4,64,512]{2,1,0:T(8,128)}), f32[4,64,512]{2,1,0:T(8,128)S(1)}, u32[]{:S(2)}, u32[]{:S(2)}) async-start(f32[4,64,512]{2,1,0:T(8,128)} %broadcast_in_dim.153), calls=%async_computation.1 | async-start | bytes 1048576 | tf_op jit(solution)/shard_map/all_to_all | solution.py:15
  50.0 8.0 %collective-permute-start = (f32[256,512]{1,0:T(8,128)S(1)}, f32[256,512]{1,0:T(8,128)S(1)}, u32[]{:S(2)}, u32[]{:S(2)}) collective-permute-start(f32[256,512]{1,0:T(8,128)S(1)} %bitcast.56), channel_id=1, source_target_pairs={{0,1},{1,0},{2,3},{3,2},{4,5},{5,4},{6,7},{7,6},{8,9},{9,8},{10,11... | collective-permute-start | bytes 1572872 | tf_op jit(solution)/shard_map/ppermute | solution.py:64
  60.0 12.4 %collective-permute-start.6 = (f32[64,1024]{1,0:T(8,128)S(1)}, f32[64,1024]{1,0:T(8,128)S(1)}, u32[]{:S(2)}, u32[]{:S(2)}) collective-permute-start(f32[64,1024]{1,0:T(8,128)S(1)} %get-tuple-element.29), channel_id=1, source_target_pairs={{0,16},{1,113},{8,24},{9,121},{16,32},{17,1},{24,40},{25,9},{32,48... | collective-permute-start | bytes 786440 | tf_op jit(solution)/shard_map/ppermute | solution.py:28
  63.2 13.1 %collective-permute-start.5 = (f32[64,1024]{1,0:T(8,128)S(1)}, f32[64,1024]{1,0:T(8,128)S(1)}, u32[]{:S(2)}, u32[]{:S(2)}) collective-permute-start(f32[64,1024]{1,0:T(8,128)S(1)} %get-tuple-element.30), channel_id=1, source_target_pairs={{0,120},{8,0},{16,8},{24,16},{32,24},{40,32},{48,40},{56,48},{64,5... | collective-permute-start | bytes 786440 | tf_op jit(solution)/shard_map/ppermute | solution.py:23
  66.1 10.6 %collective-permute-start.4 = (f32[64,1024]{1,0:T(8,128)S(1)}, f32[64,1024]{1,0:T(8,128)S(1)}, u32[]{:S(2)}, u32[]{:S(2)}) collective-permute-start(f32[64,1024]{1,0:T(8,128)S(1)} %get-tuple-element.28), channel_id=1, source_target_pairs={{0,8},{8,16},{16,24},{24,32},{32,40},{40,48},{48,56},{56,64},{64,7... | collective-permute-start | bytes 786440 | tf_op jit(solution)/shard_map/ppermute | solution.py:23
  77.4 21.3 %all-to-all-start.2 = ((f32[4,16,1024]{2,1,0:T(8,128)}), f32[4,16,1024]{2,1,0:T(8,128)S(1)}, u32[]{:S(2)}, u32[]{:S(2)}) async-start(f32[4,16,1024]{2,1,0:T(8,128)} %bitcast.8), calls=%async_computation.2 | async-start | bytes 524288 | tf_op jit(solution)/shard_map/all_to_all | solution.py:15
  99.8 19.8 %all-to-all-start.3 = ((f32[32,3,16]{2,1,0:T(4,128)}), f32[32,3,16]{2,1,0:T(4,128)S(1)}, u32[]{:S(2)}, u32[]{:S(2)}) async-start(f32[32,3,16]{2,1,0:T(4,128)} %broadcast_in_dim.171), calls=%async_computation.3 | async-start | bytes 131072 | tf_op jit(solution)/shard_map/all_to_all | solution.py:15
  120.5 19.7 %all-to-all-start.4 = ((f32[4,16,1024]{2,1,0:T(8,128)}), f32[4,16,1024]{2,1,0:T(8,128)S(1)}, u32[]{:S(2)}, u32[]{:S(2)}) async-start(f32[4,16,1024]{2,1,0:T(8,128)} %broadcast_in_dim.172), calls=%async_computation.4 | async-start | bytes 524288 | tf_op jit(solution)/shard_map/all_to_all | solution.py:15
  140.2 12.1 %collective-permute-start.8 = (f32[64,1024]{1,0:T(8,128)S(1)}, f32[64,1024]{1,0:T(8,128)S(1)}, u32[]{:S(2)}, u32[]{:S(2)}) collective-permute-start(f32[64,1024]{1,0:T(8,128)S(1)} %bitcast.60), channel_id=1, source_target_pairs={{0,8},{8,16},{16,24},{24,32},{32,40},{40,48},{48,56},{56,64},{64,7... | collective-permute-start | bytes 786440 | tf_op jit(solution)/shard_map/ppermute | solution.py:23
  146.5 10.9 %collective-permute-start.7 = (f32[64,1024]{1,0:T(8,128)S(1)}, f32[64,1024]{1,0:T(8,128)S(1)}, u32[]{:S(2)}, u32[]{:S(2)}) collective-permute-start(f32[64,1024]{1,0:T(8,128)S(1)} %bitcast.61), channel_id=1, source_target_pairs={{0,16},{1,113},{8,24},{9,121},{16,32},{17,1},{24,40},{25,9},{32,48... | collective-permute-start | bytes 786440 | tf_op jit(solution)/shard_map/ppermute | solution.py:28
  148.9 12.3 %collective-permute-start.9 = (f32[64,1024]{1,0:T(8,128)S(1)}, f32[64,1024]{1,0:T(8,128)S(1)}, u32[]{:S(2)}, u32[]{:S(2)}) collective-permute-start(f32[64,1024]{1,0:T(8,128)S(1)} %bitcast.62), channel_id=1, source_target_pairs={{0,120},{8,0},{16,8},{24,16},{32,24},{40,32},{48,40},{56,48},{64,5... | collective-permute-start | bytes 786440 | tf_op jit(solution)/shard_map/ppermute | solution.py:23
  157.4 6.8 %copy-start.2 = (f32[64,1024]{1,0:T(8,128)}, f32[64,1024]{1,0:T(8,128)S(1)}, u32[]{:S(2)}) copy-start(f32[64,1024]{1,0:T(8,128)S(1)} %collective-permute-done.7) | copy-start | bytes 786436
  161.2 1.6 copy-start.3
  164.2 20.4 %all-to-all-start.5 = ((f32[32,16,384]{2,1,0:T(8,128)}), f32[32,16,384]{2,1,0:T(8,128)S(1)}, u32[]{:S(2)}, u32[]{:S(2)}) async-start(f32[32,16,384]{2,1,0:T(8,128)} %bitcast.15), calls=%async_computation.5 | async-start | bytes 1572864 | tf_op jit(solution)/shard_map/all_to_all | solution.py:15
  172.9 17.9 %collective-permute-start.10 = (f32[96,1024]{1,0:T(8,128)}, f32[96,1024]{1,0:T(8,128)}, u32[]{:S(2)}, u32[]{:S(2)}) collective-permute-start(f32[96,1024]{1,0:T(8,128)} %get-tuple-element.23), channel_id=1, source_target_pairs={{0,128},{128,256},{256,384},{384,0},{1,129},{129,257},{257,385},{3... | collective-permute-start | bytes 1179656 | tf_op jit(solution)/shard_map/ppermute | solution.py:32
  176.3 15.6 %collective-permute-start.11 = (f32[96,1024]{1,0:T(8,128)S(1)}, f32[96,1024]{1,0:T(8,128)}, u32[]{:S(2)}, u32[]{:S(2)}) collective-permute-start(f32[96,1024]{1,0:T(8,128)S(1)} %get-tuple-element.22), channel_id=1, source_target_pairs={{0,384},{128,0},{256,128},{384,256},{1,385},{129,1},{257,129},{385... | collective-permute-start | bytes 1179656 | tf_op jit(solution)/shard_map/ppermute | solution.py:32
  179.9 27.6 %collective-permute-start.12 = (f32[96,1024]{1,0:T(8,128)S(1)}, f32[96,1024]{1,0:T(8,128)}, u32[]{:S(2)}, u32[]{:S(2)}) collective-permute-start(f32[96,1024]{1,0:T(8,128)S(1)} %get-tuple-element.21), channel_id=1, source_target_pairs={{0,256},{128,384},{256,0},{384,128},{1,257},{129,385},{257,1},{385... | collective-permute-start | bytes 1179656 | tf_op jit(solution)/shard_map/ppermute | solution.py:32
  185.3 15.5 %all-to-all-start.6 = ((f32[16,1,512]{2,1,0:T(1,128)}), f32[16,1,512]{2,1,0:T(1,128)S(1)}, u32[]{:S(2)}, u32[]{:S(2)}) async-start(f32[16,1,512]{2,1,0:T(1,128)} %reshape.307), calls=%async_computation.6 | async-start | bytes 65536 | tf_op jit(solution)/shard_map/all_to_all | solution.py:15
  201.8 11.6 %all-to-all-start.7 = ((f32[8,1,6144]{2,1,0:T(1,128)}), f32[8,1,6144]{2,1,0:T(1,128)S(1)}, u32[]{:S(2)}, u32[]{:S(2)}) async-start(f32[8,1,6144]{2,1,0:T(1,128)} %broadcast_in_dim.175), calls=%async_computation.7 | async-start | bytes 393216 | tf_op jit(solution)/shard_map/all_to_all | solution.py:15
  208.6 5.6 %copy-start.1 = (f32[96,4096]{1,0:T(8,128)}, f32[96,4096]{1,0:T(8,128)S(1)}, u32[]{:S(2)}) copy-start(f32[96,4096]{1,0:T(8,128)S(1)} %constant_dynamic-update-slice_fusion.2) | copy-start | bytes 4718596
